TPU v7x, 256 devices: a whole 4x4x8 slice. The times are simulated.
256 devices in a mesh: row: 16 (over y_hi, x, core), col: 16 (over y_lo, z).
Axes of the slice: x: 4, y: 4 (y_hi: 2, y_lo: 2; y = y_hi * 2 + y_lo), z: 8, core: 2. Of those that a mesh axis runs over, the one named last changes fastest.
Arguments:
- pair: bfloat16 [96, 1536, 128], P('row', 'col'), may hold values from -6 to 6
- w_qkvg: bfloat16 [128, 256], replicated, may hold values from -0.5 to 0.5
- w_out: bfloat16 [64, 128], replicated, may hold values from -0.75 to 0.75
- bias: bfloat16 [2, 1536, 1536], P(None, 'col', 'row'), may hold values from -25 to 300
- chain_lengths: int32 [8], replicated, may hold values from 1 to 192, 960 in all
- d_pair_out: bfloat16 [96, 1536, 128], P('row', 'col'), may hold values from -6 to 6
Outputs:
- d_pair: bfloat16 [96, 1536, 128], P('row', 'col')
- d_bias: float32 [2, 1536, 1536], P(None, 'col', 'row')
Inputs may be any that keep to these rules, and one draw needn't show every extreme that they name: Chain c owns token slots c * 192 to (c + 1) * 192 - 1, of which the first chain_lengths[c] are valid; the lengths sum to 960, and some chain fills all its 192 slots.
All inputs are finite; a program needn't handle non-finite values.
Results may differ from a plain program's by a relative error of at most 0.023.
Values may be sent and summed in bfloat16 or wider, within the bound.
No kernel may reach another device: no remote copies, remote signals or barrier semaphores. Data moves between devices by JAX's collectives and lax.ppermute only.
A program may use at most 64 MiB of HBM per device.

v0:
```python
import math

import jax
import jax.numpy as jnp
from jax import lax
from jax.sharding import PartitionSpec as P

H = 2
DH = 32
CHAINS = 8


MASKED_SCORE = -1e30


def score_block(queries, block_kv, bias_block, valid_block):
    row_count, key_total = (block_kv.shape[0], block_kv.shape[1])
    head_total, head_size = (queries.shape[2], queries.shape[3])
    key_block = block_kv[..., : head_total * head_size].reshape(
        row_count, key_total, head_total, head_size
    )
    value_block = block_kv[..., head_total * head_size :].reshape(
        row_count, key_total, head_total, head_size
    )
    scores = jnp.einsum("ijhd,ikhd->ihjk", queries, key_block, preferred_element_type=jnp.float32)
    scores = scores + bias_block.astype(jnp.float32)[None]
    scores = jnp.where(valid_block[None, None, None, :], scores, MASKED_SCORE)
    return (scores, key_block, value_block)


def forward_block(carried, queries, block_kv, bias_block, valid_block):
    run_max, run_sum, accumulated = carried
    scores, key_block, value_block = score_block(queries, block_kv, bias_block, valid_block)
    new_max = jnp.maximum(run_max, jnp.max(scores, axis=3))
    factor = jnp.exp(run_max - new_max)
    exponent = jnp.exp(scores - new_max[..., None])
    run_sum = run_sum * factor + jnp.sum(exponent, axis=3)
    added = jnp.einsum(
        "ihjk,ikhd->ijhd",
        exponent,
        value_block.astype(jnp.float32),
        precision=lax.Precision.HIGHEST,
    )
    accumulated = accumulated * jnp.transpose(factor, (0, 2, 1))[..., None] + added
    return (new_max, run_sum, accumulated)


def backward_block(queries, d_attention, log_total, row_dot, block_kv, bias_block, valid_block):
    scores, key_block, value_block = score_block(queries, block_kv, bias_block, valid_block)
    weights = jnp.exp(scores - log_total[..., None])
    d_weights = jnp.einsum(
        "ijhd,ikhd->ihjk", d_attention, value_block, preferred_element_type=jnp.float32
    )
    d_scores = weights * (d_weights - row_dot[..., None])
    return (weights, d_scores, key_block)


def key_grads(queries, d_attention, weights, d_scores):
    d_keys = jnp.einsum(
        "ihjk,ijhd->kihd",
        d_scores.astype(jnp.bfloat16),
        queries,
        preferred_element_type=jnp.float32,
    )
    d_values = jnp.einsum(
        "ihjk,ijhd->kihd",
        weights.astype(jnp.bfloat16),
        d_attention,
        preferred_element_type=jnp.float32,
    )
    key_total, row_count = (d_keys.shape[0], d_keys.shape[1])
    return jnp.concatenate(
        [d_keys.reshape(key_total, row_count, -1), d_values.reshape(key_total, row_count, -1)],
        axis=2,
    )


def body(pair, w_qkvg, w_out, bias, chain_lengths, d_pair_out):
    row_count, col_count, channels = pair.shape
    head_span = H * DH
    score_scale = 1.0 / math.sqrt(DH)
    key_count = col_count * lax.axis_size("col")
    slot_size = key_count // CHAINS
    position = jnp.arange(key_count, dtype=jnp.int32)
    chosen = (position // slot_size)[:, None] == jnp.arange(CHAINS, dtype=jnp.int32)[None, :]
    chain_size = jnp.sum(jnp.where(chosen, chain_lengths[None, :], 0), axis=1)
    key_valid = position % slot_size < chain_size
    projected = jnp.einsum("ijc,cf->ijf", pair, w_qkvg, preferred_element_type=jnp.float32)
    queries = (
        (projected[..., :head_span] * score_scale)
        .astype(jnp.bfloat16)
        .reshape(row_count, col_count, H, DH)
    )
    key_value = projected[..., head_span : 3 * head_span].astype(jnp.bfloat16)
    gates = jax.nn.sigmoid(projected[..., 3 * head_span :])
    bias_all = lax.all_gather(bias, "row", axis=2, tiled=True)

    def block_starts(length):
        return jnp.arange(length // col_count, dtype=jnp.int32) * col_count

    initial = (
        jnp.full((row_count, H, col_count), MASKED_SCORE, jnp.float32),
        jnp.zeros((row_count, H, col_count), jnp.float32),
        jnp.zeros((row_count, col_count, H, DH), jnp.float32),
    )
    carried = initial
    pieces = lax.all_gather(key_value, "col", axis=1, tiled=True)

    def forward_advance(carried, offset):
        block_kv = lax.dynamic_slice_in_dim(pieces, offset, col_count, 1)
        bias_block = lax.dynamic_slice_in_dim(bias_all, offset, col_count, 2)
        valid_block = lax.dynamic_slice_in_dim(key_valid, offset, col_count, 0)
        return (forward_block(carried, queries, block_kv, bias_block, valid_block), None)

    carried, ignored = lax.scan(forward_advance, carried, block_starts(pieces.shape[1]))
    run_max, run_sum, accumulated = carried
    attention = (accumulated / jnp.transpose(run_sum, (0, 2, 1))[..., None]).reshape(
        row_count, col_count, head_span
    )
    log_total = run_max + jnp.log(run_sum)
    d_output = jnp.einsum("ijc,fc->ijf", d_pair_out, w_out, preferred_element_type=jnp.float32)
    d_attention = (d_output * gates).astype(jnp.bfloat16)
    row_dot = jnp.transpose(
        jnp.sum(
            (d_attention.astype(jnp.float32) * attention).reshape(row_count, col_count, H, DH),
            axis=3,
        ),
        (0, 2, 1),
    )
    d_gates = d_output * attention * gates * (1.0 - gates)
    d_attention_heads = d_attention.reshape(row_count, col_count, H, DH)
    start_state = (
        jnp.zeros((row_count, col_count, H, DH), jnp.float32),
        jnp.zeros((H, col_count, key_count), jnp.float32),
        jnp.zeros((key_count, row_count, 2 * head_span), jnp.float32),
    )
    carried = start_state
    backward_pieces = lax.all_gather(key_value, "col", axis=1, tiled=True)

    def backward_advance(carried, offset):
        d_queries, d_bias_rows, d_key_rows = carried
        block_kv = lax.dynamic_slice_in_dim(backward_pieces, offset, col_count, 1)
        bias_block = lax.dynamic_slice_in_dim(bias_all, offset, col_count, 2)
        valid_block = lax.dynamic_slice_in_dim(key_valid, offset, col_count, 0)
        weights, d_scores, key_block = backward_block(
            queries, d_attention_heads, log_total, row_dot, block_kv, bias_block, valid_block
        )
        d_queries = d_queries + jnp.einsum(
            "ihjk,ikhd->ijhd",
            d_scores.astype(jnp.bfloat16),
            key_block,
            preferred_element_type=jnp.float32,
        )
        d_bias_rows = lax.dynamic_update_slice_in_dim(
            d_bias_rows, jnp.sum(d_scores, axis=0), offset, 2
        )
        d_key_rows = lax.dynamic_update_slice_in_dim(
            d_key_rows, key_grads(queries, d_attention_heads, weights, d_scores), offset, 0
        )
        return ((d_queries, d_bias_rows, d_key_rows), None)

    carried, ignored = lax.scan(backward_advance, carried, block_starts(backward_pieces.shape[1]))
    d_queries, d_bias_rows, d_key_rows = carried
    d_key_value = lax.psum_scatter(
        d_key_rows.astype(jnp.bfloat16), "col", scatter_dimension=0, tiled=True
    ).astype(jnp.float32)
    d_bias = lax.psum_scatter(
        d_bias_rows.astype(jnp.bfloat16), "row", scatter_dimension=2, tiled=True
    ).astype(jnp.float32)
    d_key_value = jnp.transpose(d_key_value, (1, 0, 2))
    d_projected = jnp.concatenate(
        [d_queries.reshape(row_count, col_count, head_span) * score_scale, d_key_value, d_gates],
        axis=2,
    ).astype(jnp.bfloat16)
    d_pair = jnp.einsum(
        "ijf,cf->ijc", d_projected, w_qkvg, preferred_element_type=jnp.float32
    ).astype(jnp.bfloat16)
    return (d_pair, d_bias)


def solution(mesh):
    in_specs = (P("row", "col", None), P(), P(), P(None, "col", "row"), P(), P("row", "col", None))
    out_specs = (P("row", "col", None), P(None, "col", "row"))
    return jax.shard_map(body, mesh=mesh, in_specs=in_specs, out_specs=out_specs, check_vma=False)
```

profile of v0, /device:TPU:2, one launch (start us, length us, event | category | flops | bytes accessed | tf_op | source)
XLA Modules:
  0.0 504.6 jit_solution(11980293335710981370)
XLA Ops:
  11.4 25.3 %all_gather.8 = bf16[2,96,1536]{1,2,0:T(8,128)(2,1)} all-gather(bf16[2,96,96]{1,2,0:T(8,128)(2,1)S(1)} %copy.78), channel_id=1, replica_groups=mesh['row'=16,'col'=16] {'row'}, dimensions={2}, use_global_device_ids=true | all-gather | bytes 626688 | tf_op jit(solution)/shard_map/all_gather | solution.py:96
  36.7 48.9 %all-gather.2.cloned.1.call-done = bf16[6,1536,128]{2,1,0:T(8,128)(2,1)} async-done(((bf16[6,96,128]{2,1,0:T(8,128)(2,1)}), bf16[6,1536,128]{2,1,0:T(8,128)(2,1)}) %all-gather.2.cloned.1.call-update) | async-done | bytes 2359312 | tf_op jit(solution)/shard_map/all_gather | solution.py:138
  85.5 2.8 copy.81
  88.4 73.6 %while.30 = (s32[]{:T(128)}, f32[6,2,96]{2,1,0:T(2,128)S(1)}, f32[6,2,96]{2,1,0:T(2,128)S(1)}, f32[6,96,2,32]{1,3,2,0:T(8,128)S(1)}, s32[16]{0:T(128)S(1)}, /*in...) while((s32[]{:T(128)}, f32[6,2,96]{2,1,0:T(2,128)S(1)}, ...), condition=%wide.region_4.5_spmd.clone, body=%wide.region_1.4_spmd.clone.sunk | while | flops 50344712 | bytes 2396659 | solution.py:115
  166.9 178.2 %while.31 = (s32[]{:T(128)}, f32[6,96,2,32]{1,3,2,0:T(8,128)}, bf16[2,96,1536]{1,0,2:T(2,128)(2,1)}, bf16[1536,6,128]{2,0,1:T(8,128)(2,1)S(1)}, s32[16]{0:T(128)...) while((s32[]{:T(128)}, f32[6,96,2,32]{1,3,2,0:T(8,128)}, ...), condition=%wide.region_8.9_spmd.clone, body=%wide.region_6.8_spmd.clone.sunk | while | flops 36642824 | bytes 4580881 | solution.py:162
  173.8 2.6 dynamic_update_slice.10
  184.0 2.6 dynamic_update_slice.10
  195.2 2.6 dynamic_update_slice.10
  206.5 2.6 dynamic_update_slice.10
  217.7 2.6 dynamic_update_slice.10
  228.9 2.6 dynamic_update_slice.10
  240.1 2.6 dynamic_update_slice.10
  251.3 2.6 dynamic_update_slice.10
  262.5 2.6 dynamic_update_slice.10
  273.7 2.6 dynamic_update_slice.10
  284.9 2.6 dynamic_update_slice.10
  296.1 2.6 dynamic_update_slice.10
  307.3 2.6 dynamic_update_slice.10
  318.6 2.6 dynamic_update_slice.10
  329.8 2.6 dynamic_update_slice.10
  340.8 2.6 dynamic_update_slice.10
  345.2 3.3 reshape.73
  349.6 69.8 %reduce-scatter.7.cloned.1.call-done = bf16[96,192]{1,0:T(8,128)(2,1)} async-done(((bf16[1536,192]{1,0:T(8,128)(2,1)}), bf16[96,192]{1,0:T(8,128)(2,1)}) %reduce-scatter.7.cloned.1.call-update) | async-done | bytes 36880
  421.0 75.1 %reduce-scatter.5.cloned.1.call-done = bf16[96,6,128]{2,0,1:T(8,128)(2,1)} async-done(((bf16[1536,6,128]{2,0,1:T(8,128)(2,1)}), bf16[96,6,128]{2,0,1:T(8,128)(2,1)}) %reduce-scatter.5.cloned.1.call-update) | async-done | bytes 147472 | tf_op jit(solution)/shard_map/reduce_scatter | solution.py:164
  (436 shorter events, 160.4 us)
Async XLA Ops:
  7.2 0.9 copy-start
  7.2 3.1 copy-start.6
  7.2 4.1 copy-start.7
  7.2 78.3 %all-gather.2.cloned.1.call-start = ((), (), s32[]{:S(2)}) async-start(), calls=%async_computation.2 | async-start | bytes 2506752 | tf_op jit(solution)/shard_map/all_gather | solution.py:138
  9.9 409.4 %reduce-scatter.7.cloned.1.call-start = ((), (), s32[]{:S(2)}) async-start(), calls=%async_computation.4 | async-start | bytes 835584
  88.4 73.7 %copy-start.8 = (bf16[64,128]{1,0:T(8,128)(2,1)S(1)}, bf16[64,128]{1,0:T(8,128)(2,1)}, u32[]{:S(2)}) copy-start(bf16[64,128]{1,0:T(8,128)(2,1)} %param.12) | copy-start | bytes 49156
  162.0 2.4 copy-start.2
  345.2 3.4 copy-start.1
  345.2 4.0 copy-start.3
  345.2 4.2 copy-start.4
  348.4 147.7 %copy-start.5 = (bf16[128,256]{1,0:T(8,128)(2,1)S(1)}, bf16[128,256]{1,0:T(8,128)(2,1)}, u32[]{:S(2)}) copy-start(bf16[128,256]{1,0:T(8,128)(2,1)} %param.11) | copy-start | bytes 196612
  348.5 147.7 %reduce-scatter.5.cloned.1.call-start = ((), (), s32[]{:S(2)}) async-start(), calls=%async_computation.3 | async-start | bytes 2506752 | tf_op jit(solution)/shard_map/reduce_scatter | solution.py:164
Sparse Core Ops, SparseCore 0:
  10.4 75.0 all-gather.1
  348.6 70.7 reduce-scatter.6
  421.9 74.1 reduce-scatter.4
where the time goes:
time: 509 us; the launch traced here: 505 us
  waiting for transfers between devices  194 us (38%)
  local copies, waits for them, and re-layouts  111 us (22%)
  matrix products  63.9 us (13%)
  loops' own time  63.8 us (13%)
  other arithmetic  32.3 us (6%)
  blocking collectives  25.3 us (5%)
  between operations  14 us (3%)
    reduce_scatter x1, waiting for transfers between devices, body(): lax.psum_scatter(d_key_rows.astype(jnp.bfloat16), 'col', scatter_dimensio...  75.1 us
    unnamed x4, waiting for transfers between devices  70.5 us
    all_gather x1, waiting for transfers between devices, body(): backward_pieces = lax.all_gather(key_value, 'col', axis=1, tiled=True)  48.9 us
    dynamic_update_slice x48, local copies, waits for them, and re-layouts, backward_advance(): lax.dynamic_update_slice_in_dim(d_bias_rows, jnp.sum(d_scores, axis=0), o...  44.8 us
    another operation x1, loops' own time, body(): lax.scan(forward_advance, carried, block_starts(pieces.shape[1]))  31.9 us
    another operation x1, loops' own time, body(): lax.scan(backward_advance, carried, block_starts(backward_pieces.shape[1]))  31.9 us
    dot_general x16, matrix products, backward_advance(): jnp.einsum('ihjk,ikhd->ijhd', d_scores.astype(jnp.bfloat16), key_block, p...  27.8 us
    convert_element_type x32, other arithmetic, score_block(): scores = scores + bias_block.astype(jnp.float32)[None]  26.7 us
  transfers between devices with their start and end apart: 3, of which 3 were waited for; matrix products, arithmetic and copies ran while one was open for 1% of the time, Pallas kernels for 0%

commit v1 on v0

v1 whole, which is shorter than its diff:
```python
import functools
import math

import jax
import jax.numpy as jnp
from jax import lax
from jax.experimental import pallas as pl
from jax.experimental.pallas import tpu as pltpu
from jax.sharding import Mesh, PartitionSpec as P

H = 2
DH = 32
CHAINS = 8
SCALE = 1.0 / math.sqrt(DH)
MASKED_SCORE = -1e30
F32 = jnp.float32
BF16 = jnp.bfloat16

ROWS = 6
COLS = 96
RING = 8
HALF = RING * COLS
KEYS = 2 * HALF
WIDE = 128
SLOT = KEYS // CHAINS

NT = (((1,), (1,)), ((), ()))
NN = (((1,), (0,)), ((), ()))
TN = (((0,), (0,)), ((), ()))


def mm(a, b, dims):
    return lax.dot_general(a, b, dims, preferred_element_type=F32)


def params(limit=48 << 20):
    return pltpu.CompilerParams(vmem_limit_bytes=limit)


def cost(flops, size):
    return pl.CostEstimate(flops=flops, bytes_accessed=size, transcendentals=0)


def lanes(shape):
    return lax.broadcasted_iota(jnp.int32, shape, len(shape) - 1)


def head_weight(w, h):
    parts = [w[:, (part * H + h) * DH : (part * H + h + 1) * DH] for part in (1, 2, 0, 3)]
    return jnp.concatenate(parts, axis=1)


def project_kernel(pair_ref, grad_ref, w_ref, wout_ref, mine_ref, other_ref, gmine_ref, gother_ref):
    yl = lax.axis_index("yl")
    pair = pair_ref[...].reshape(ROWS * COLS, WIDE)
    grad = grad_ref[...].reshape(ROWS * COLS, WIDE)
    w = w_ref[...]
    wout = wout_ref[...]
    lane = lanes((ROWS * COLS, WIDE))
    for h in range(H):
        proj = mm(pair, head_weight(w, h), NN)
        rows = jnp.concatenate(
            [jnp.zeros((WIDE - DH, WIDE), BF16), wout[h * DH : (h + 1) * DH]], axis=0
        )
        d_out = mm(grad, rows, NT)
        gate = jax.nn.sigmoid(proj)
        payload = jnp.where(
            lane < 2 * DH, proj, jnp.where(lane < 3 * DH, proj * SCALE, d_out * gate)
        )
        payload = payload.astype(BF16).reshape(ROWS, COLS, WIDE)
        g = (d_out * gate * (1.0 - gate)).reshape(ROWS, COLS, WIDE)

        @pl.when(yl == h)
        def _():
            mine_ref[...] = payload
            gmine_ref[...] = g

        @pl.when(yl != h)
        def _():
            other_ref[...] = payload
            gother_ref[...] = g


def project(pair, grad, w, wout):
    shape = (ROWS, COLS, WIDE)
    return pl.pallas_call(
        project_kernel,
        out_shape=[
            jax.ShapeDtypeStruct(shape, BF16),
            jax.ShapeDtypeStruct(shape, BF16),
            jax.ShapeDtypeStruct(shape, F32),
            jax.ShapeDtypeStruct(shape, F32),
        ],
        compiler_params=params(),
        name="project",
    )(pair, grad, w, wout)


def pack_kernel(mine_ref, recv_ref, kv_ref, x0_ref, x1_ref):
    yl = lax.axis_index("yl")
    lane = lanes((COLS, WIDE))

    def write(i, a, b):
        x0_ref[i] = a
        x1_ref[i] = b
        moved = pltpu.roll(b.astype(F32), 2 * DH, 1)
        kv_ref[i] = jnp.where(lane < 2 * DH, a.astype(F32), moved).astype(BF16)

    for i in range(ROWS):

        @pl.when(yl == 0)
        def _():
            write(i, mine_ref[i], recv_ref[i])

        @pl.when(yl != 0)
        def _():
            write(i, recv_ref[i], mine_ref[i])


def pack(mine, recv):
    shape = jax.ShapeDtypeStruct((ROWS, COLS, WIDE), BF16)
    return pl.pallas_call(
        pack_kernel, out_shape=[shape] * 3, compiler_params=params(), name="pack"
    )(mine, recv)


def bias_kernel(len_ref, own_ref, oth_ref, out_ref):
    core = lax.axis_index("core")
    lane = lanes((1, SLOT))

    def write(even, odd):
        for yh in range(2):
            for x in range(4):
                valid = lane < len_ref[yh * 4 + x]
                lift = jnp.where(valid, 0.0, MASKED_SCORE)
                for yl in range(2):
                    both = jnp.concatenate(
                        [even[yh, x, yl].astype(F32), odd[yh, x, yl].astype(F32)], axis=1
                    )
                    start = yh * HALF + x * SLOT
                    out_ref[yl * COLS : (yl + 1) * COLS, start : start + SLOT] = both + lift

    @pl.when(core == 0)
    def _():
        write(own_ref, oth_ref)

    @pl.when(core != 0)
    def _():
        write(oth_ref, own_ref)


def bias_table(chain_lengths, own, oth):
    return pl.pallas_call(
        bias_kernel,
        out_shape=jax.ShapeDtypeStruct((2 * COLS, KEYS), F32),
        in_specs=[
            pl.BlockSpec(memory_space=pltpu.SMEM),
            pl.BlockSpec(memory_space=pltpu.VMEM),
            pl.BlockSpec(memory_space=pltpu.VMEM),
        ],
        compiler_params=params(),
        name="bias_table",
    )(chain_lengths, own, oth)


def masked(value, lane, part):
    keep = (lane >= part * DH) & (lane < (part + 1) * DH)
    return jnp.where(keep, value, jnp.zeros_like(value))


def main_kernel(x0_ref, x1_ref, bias_ref, *refs):
    kv_refs = refs[:RING]
    u_ref, dkv_refs, dbias_ref = refs[RING], refs[RING + 1 : 2 * RING + 1], refs[2 * RING + 1]
    kv_s, left, right, dkv_s = refs[2 * RING + 2 :]
    z = lax.axis_index("z")
    i = pl.program_id(0)
    for r in range(RING):
        start = pl.multiple_of(lax.rem(z + r, RING) * COLS, COLS)
        kv_s[pl.ds(start, COLS), :] = kv_refs[r][0]
    kv = kv_s[...]
    lane = lanes((COLS, WIDE))

    @pl.when(i == 0)
    def _():
        dbias_ref[...] = jnp.zeros_like(dbias_ref)

    for part, x_ref in enumerate((x0_ref, x1_ref)):
        x = x_ref[0]
        y = pltpu.roll(x.astype(F32), 2 * DH, 1).astype(BF16)
        q0, da0 = masked(y, lane, 0), masked(y, lane, 1)
        q1, da1 = masked(x, lane, 2), masked(x, lane, 3)
        rows = slice(part * COLS, (part + 1) * COLS)
        s0 = mm(q0, kv, NT) + bias_ref[rows, :HALF]
        s1 = mm(q1, kv, NT) + bias_ref[rows, HALF:]
        top = jnp.maximum(
            jnp.max(s0, axis=1, keepdims=True), jnp.max(s1, axis=1, keepdims=True)
        )
        e0 = jnp.exp(s0 - top)
        e1 = jnp.exp(s1 - top)
        total = jnp.sum(e0, axis=1, keepdims=True) + jnp.sum(e1, axis=1, keepdims=True)
        inverse = 1.0 / total
        p0 = e0 * inverse
        p1 = e1 * inverse
        p0b = p0.astype(BF16)
        p1b = p1.astype(BF16)
        pv0 = mm(p0b, kv, NN)
        pv1 = mm(p1b, kv, NN)
        dot = jnp.sum(pv0 * da0.astype(F32) + pv1 * da1.astype(F32), axis=1, keepdims=True)
        d0 = p0 * (mm(da0, kv, NT) - dot)
        d1 = p1 * (mm(da1, kv, NT) - dot)
        dbias_ref[rows, :HALF] += d0
        dbias_ref[rows, HALF:] += d1
        d0b = d0.astype(BF16)
        d1b = d1.astype(BF16)
        dk0 = mm(d0b, kv, NN)
        dk1 = mm(d1b, kv, NN)
        t0 = jnp.where(lane < DH, dk0, pv0)
        t1 = jnp.where(lane < 3 * DH, dk1, pv1)
        u = t0 + pltpu.roll(t1, 2 * DH, 1)
        u_ref[part, 0] = jnp.where(lane < DH, u * SCALE, u)
        base = part * COLS
        for slot, (l_val, r_val) in enumerate(((d0b, q0), (p0b, da0), (d1b, q1), (p1b, da1))):
            left[slot * 2 * COLS + base : slot * 2 * COLS + base + COLS, :] = l_val
            right[slot * 2 * COLS + base : slot * 2 * COLS + base + COLS, :] = r_val
    dkv_s[...] = mm(left[...], right[...], TN)
    for r in range(RING):
        start = pl.multiple_of(lax.rem(z + r, RING) * COLS, COLS)
        dkv_refs[r][0] = dkv_s[pl.ds(start, COLS), :].astype(BF16)


def main(x0, x1, bias, kvs):
    row = pl.BlockSpec((1, COLS, WIDE), lambda i: (i, 0, 0))
    table = pl.BlockSpec((2 * COLS, KEYS), lambda i: (0, 0))
    block = jax.ShapeDtypeStruct((ROWS, COLS, WIDE), BF16)
    out = pl.pallas_call(
        main_kernel,
        grid=(ROWS,),
        in_specs=[row, row, table] + [row] * RING,
        out_specs=[pl.BlockSpec((2, 1, COLS, WIDE), lambda i: (0, i, 0, 0))]
        + [row] * RING
        + [table],
        out_shape=[jax.ShapeDtypeStruct((2, ROWS, COLS, WIDE), F32)]
        + [block] * RING
        + [jax.ShapeDtypeStruct((2 * COLS, KEYS), F32)],
        scratch_shapes=[
            pltpu.VMEM((HALF, WIDE), BF16),
            pltpu.VMEM((8 * COLS, HALF), BF16),
            pltpu.VMEM((8 * COLS, WIDE), BF16),
            pltpu.VMEM((HALF, WIDE), F32),
        ],
        compiler_params=params(),
        name="main",
    )(x0, x1, bias, *kvs)
    return out[0], out[1 : RING + 1], out[RING + 1]


def split_kernel(table_ref, keep_ref, send_ref):
    core = lax.axis_index("core")
    for yh in range(2):
        for x in range(4):
            for b in range(2):
                start = yh * HALF + x * SLOT + b * COLS
                for yl in range(2):

                    @pl.when(core == b)
                    def _():
                        keep_ref[yh, x, yl] = table_ref[
                            yl * COLS : (yl + 1) * COLS, start : start + COLS
                        ]

                    @pl.when(core != b)
                    def _():
                        send_ref[yh, x, yl] = table_ref[
                            yl * COLS : (yl + 1) * COLS, start : start + COLS
                        ].astype(BF16)


def split_table(table):
    shape = (2, 4, 2, COLS, COLS)
    return pl.pallas_call(
        split_kernel,
        out_shape=[jax.ShapeDtypeStruct(shape, F32), jax.ShapeDtypeStruct(shape, BF16)],
        compiler_params=params(),
        name="split_table",
    )(table)


def finish_kernel(u_ref, a_ref, b_ref, c_ref, keep_ref, send_ref):
    yl = lax.axis_index("yl")
    lane = lanes((COLS, WIDE))
    for i in range(ROWS):
        dkv = a_ref[i].astype(F32) + b_ref[i].astype(F32) + c_ref[i].astype(F32)
        first = jnp.where(lane < 2 * DH, dkv, pltpu.roll(u_ref[0, i], 2 * DH, 1))
        second = jnp.where(
            lane < 2 * DH, pltpu.roll(dkv, 2 * DH, 1), pltpu.roll(u_ref[1, i], 2 * DH, 1)
        )

        @pl.when(yl == 0)
        def _():
            keep_ref[i] = first
            send_ref[i] = second.astype(BF16)

        @pl.when(yl != 0)
        def _():
            keep_ref[i] = second
            send_ref[i] = first.astype(BF16)


def finish(u, a, b, c):
    shape = (ROWS, COLS, WIDE)
    return pl.pallas_call(
        finish_kernel,
        out_shape=[jax.ShapeDtypeStruct(shape, F32), jax.ShapeDtypeStruct(shape, BF16)],
        compiler_params=params(),
        name="finish",
    )(u, a, b, c)


def output_kernel(keep_ref, recv_ref, gmine_ref, gother_ref, w_ref, out_ref):
    yl = lax.axis_index("yl")
    flat = (ROWS * COLS, WIDE)
    lane = lanes(flat)
    keep = keep_ref[...].reshape(flat)
    recv = recv_ref[...].reshape(flat).astype(F32)
    mine = jnp.where(lane < 3 * DH, keep, keep * gmine_ref[...].reshape(flat)).astype(BF16)
    other = jnp.where(lane < 3 * DH, recv, recv * gother_ref[...].reshape(flat)).astype(BF16)
    w = w_ref[...]
    w0, w1 = head_weight(w, 0), head_weight(w, 1)

    def write(a, b):
        out_ref[...] = (mm(a, w0, NT) + mm(b, w1, NT)).astype(BF16).reshape(ROWS, COLS, WIDE)

    @pl.when(yl == 0)
    def _():
        write(mine, other)

    @pl.when(yl != 0)
    def _():
        write(other, mine)


def output(keep, recv, gmine, gother, w):
    return pl.pallas_call(
        output_kernel,
        out_shape=jax.ShapeDtypeStruct((ROWS, COLS, WIDE), BF16),
        compiler_params=params(),
        name="output",
    )(keep, recv, gmine, gother, w)


def shift(value, step):
    return lax.ppermute(value, "z", [(z, (z + step) % RING) for z in range(RING)])


def swap(value, axis):
    return lax.ppermute(value, axis, [(0, 1), (1, 0)])


def added(a, b):
    return (a.astype(F32) + b.astype(F32)).astype(BF16)


def body(pair, w_qkvg, w_out, bias, chain_lengths, d_pair_out):
    peers = ("yh", "x", "yl")
    mine, other, gmine, gother = project(pair, d_pair_out, w_qkvg, w_out)
    recv = swap(other, "yl")
    wanted = jnp.broadcast_to(bias[None], (8,) + bias.shape).reshape(16, COLS, COLS)
    own = lax.all_to_all(wanted, peers, 0, 0, tiled=True)
    oth = swap(own, "core")
    blocks = (2, 4, 2, COLS, COLS)
    table = bias_table(chain_lengths, own.reshape(blocks), oth.reshape(blocks))
    kv, x0, x1 = pack(mine, recv)
    kvs = [kv] + [None] * (RING - 1)
    up = down = kv
    for r in range(1, 5):
        down = shift(down, -1)
        kvs[r] = down
        if r < 4:
            up = shift(up, 1)
            kvs[RING - r] = up
    u, dkvs, d_table = main(x0, x1, table, kvs)
    up = shift(dkvs[4], 1)
    up = shift(added(up, dkvs[3]), 1)
    down = shift(dkvs[5], -1)
    up = shift(added(up, dkvs[2]), 1)
    down = shift(added(down, dkvs[6]), -1)
    up = shift(added(up, dkvs[1]), 1)
    down = shift(added(down, dkvs[7]), -1)
    keep_table, send_table = split_table(d_table)
    summed = (keep_table + swap(send_table, "core").astype(F32)).astype(BF16)
    parts = lax.all_to_all(summed.reshape(16, COLS, COLS), peers, 0, 0, tiled=True)
    d_bias = jnp.sum(parts.reshape(8, H, COLS, COLS).astype(F32), axis=0)
    keep, send = finish(u, dkvs[0], up, down)
    d_pair = output(keep, swap(send, "yl"), gmine, gother, w_qkvg)
    return (d_pair, d_bias)


def solution(mesh):
    split = Mesh(mesh.devices.reshape(2, 4, 2, 2, RING), ("yh", "x", "core", "yl", "z"))
    row, col = ("yh", "x", "core"), ("yl", "z")
    in_specs = (P(row, col, None), P(), P(), P(None, col, row), P(), P(row, col, None))
    out_specs = (P(row, col, None), P(None, col, row))
    return jax.shard_map(body, mesh=split, in_specs=in_specs, out_specs=out_specs, check_vma=False)
```

time: 509 us -> 98.2 us (0.19)
  waiting for transfers between devices: 194 us -> 27.8 us
  local copies, waits for them, and re-layouts: 111 us -> 4.99 us
  matrix products: 63.9 us -> 0 us
  loops' own time: 63.8 us -> 0 us
  starting transfers between devices: 0.12 us -> 41.9 us
  other arithmetic: 32.3 us -> 1.77 us
  blocking collectives: 25.3 us -> 0 us
  Pallas kernels: 0 us -> 20.4 us
  between operations: 14 us -> 0.83 us
    reduce_scatter x1 -> x0, waiting for transfers between devices: 75.1 us -> none  [body(): lax.psum_scatter(d_key_rows.astype(jnp.bfloat16), 'col', scatter_dimensio...]
    unnamed x4 -> x0, waiting for transfers between devices: 70.5 us -> none
    dot_general x115 -> x0, matrix products: 63.9 us -> none  [the longest x16 27.8 us: backward_advance(): jnp.einsum('ihjk,ikhd->ijhd', d_scores.astype(jnp.bfloat16), key_block, p...]
    another operation x2 -> x0, loops' own time: 63.8 us -> none  [the longest x1 31.9 us: body(): lax.scan(forward_advance, carried, block_starts(pieces.shape[1]))]
    dynamic_update_slice x80 -> x0, local copies, waits for them, and re-layouts: 56 us -> none  [the longest x48 44.8 us: backward_advance(): lax.dynamic_update_slice_in_dim(d_bias_rows, jnp.sum(d_scores, axis=0), o...]
    all_gather x1 -> x0, waiting for transfers between devices: 48.9 us -> none  [body(): backward_pieces = lax.all_gather(key_value, 'col', axis=1, tiled=True)]
    ppermute x0 -> x18, starting transfers between devices: none -> 29 us  [the longest x14 25.7 us: shift(): lax.ppermute(value, 'z', [(z, (z + step) % RING) for z in range(RING)])]
    convert_element_type x34 -> x6, other arithmetic: 27.4 us -> 1.05 us  [the longest x1 0.84 us: body(): summed = (keep_table + swap(send_table, 'core').astype(F32)).astype(BF16)]
  transfers between devices with their start and end apart: 3 -> 20, of which waited for: 3 -> 8; matrix products, arithmetic and copies ran while one was open for 1% -> 3% of each run, Pallas kernels for 0% -> 4%
where the time goes in v1:
time: 98.2 us; the launch traced here: 97.7 us
  starting transfers between devices  41.9 us (43%)
  waiting for transfers between devices  27.8 us (28%)
  Pallas kernels  20.4 us (21%)
  local copies, waits for them, and re-layouts  4.99 us (5%)
  other arithmetic  1.77 us (2%)
    ppermute x14, starting transfers between devices, shift(): lax.ppermute(value, 'z', [(z, (z + step) % RING) for z in range(RING)])  25.7 us
    ppermute x14, waiting for transfers between devices, shift(): lax.ppermute(value, 'z', [(z, (z + step) % RING) for z in range(RING)])  16.8 us
    pallas_call x1, Pallas kernels, main(): pl.pallas_call(main_kernel, grid=(ROWS,), in_specs=[row, row, table] + [r...  14 us
    all_to_all x1, starting transfers between devices, body(): own = lax.all_to_all(wanted, peers, 0, 0, tiled=True)  7.48 us
    ppermute x4, waiting for transfers between devices, swap(): return lax.ppermute(value, axis, [(0, 1), (1, 0)])  6.95 us
    all_to_all x1, starting transfers between devices, body(): lax.all_to_all(summed.reshape(16, COLS, COLS), peers, 0, 0, tiled=True)  5.38 us
    all_to_all x1, waiting for transfers between devices, body(): own = lax.all_to_all(wanted, peers, 0, 0, tiled=True)  4 us
    unnamed x12, local copies, waits for them, and re-layouts  3.38 us
  transfers between devices with their start and end apart: 20, of which 8 were waited for; matrix products, arithmetic and copies ran while one was open for 3% of the time, Pallas kernels for 4%

profile of v1, /device:TPU:2, one launch (start us, length us, event | category | flops | bytes accessed | tf_op | source)
XLA Modules:
  0.0 97.7 jit_solution(3518055991339051594)
XLA Ops:
  1.5 0.9 copy-done.2
  4.7 1.7 %collective-permute-start = (bf16[6,96,128]{2,1,0:T(8,128)(2,1)S(1)}, bf16[6,96,128]{2,1,0:T(8,128)(2,1)S(1)}, u32[]{:S(2)}, u32[]{:S(2)}) collective-permute-start(bf16[6,96,128]{2,1,0:T(8,128)(2,1)S(1)} %get-tuple-element.24), channel_id=1, source_target_pairs={{0,8},{8,0},{1,9},{9,1},{2,10},{10,2},{3,11},{11,3},{4,12},{12,4},... | collective-permute-start | bytes 442376 | tf_op jit(solution)/shard_map/ppermute | solution.py:356
  6.3 4.0 %collective-permute-done.recv_ref = bf16[6,96,128]{2,1,0:T(8,128)(2,1)S(1)} collective-permute-done((bf16[6,96,128]{2,1,0:T(8,128)(2,1)S(1)}, bf16[6,96,128]{2,1,0:T(8,128)(2,1)S(1)}, u32[]{:S(2)}, u32[]{:S(2)}) %collective-permute-start) | collective-permute-done | bytes 147488 | tf_op jit(solution)/shard_map/ppermute | solution.py:356
  10.8 5.9 %collective-permute-start.2 = (bf16[6,96,128]{2,1,0:T(8,128)(2,1)S(1)}, bf16[6,96,128]{2,1,0:T(8,128)(2,1)S(1)}, u32[]{:S(2)}, u32[]{:S(2)}) collective-permute-start(bf16[6,96,128]{2,1,0:T(8,128)(2,1)S(1)} %get-tuple-element.27.refs_0_), channel_id=1, source_target_pairs={{0,7},{1,0},{2,1},{3,2},{4,3},{5,4},{6,5},{7,6},{8,15},{9,8},{10,9... | collective-permute-start | bytes 442376 | tf_op jit(solution)/shard_map/ppermute | solution.py:352
  16.7 1.6 %broadcast_in_dim.2 = bf16[8,2,96,96]{3,2,1,0:T(8,128)(2,1)} broadcast(bf16[2,96,96]{2,1,0:T(8,128)(2,1)} %param.9), dimensions={1,2,3} | broadcast | bytes 331776 | tf_op jit(solution)/shard_map/broadcast_in_dim | solution.py:367
  18.3 7.5 %all-to-all-start = ((bf16[16,96,96]{2,1,0:T(8,128)(2,1)}), bf16[16,96,96]{2,1,0:T(8,128)(2,1)S(1)}, u32[]{:S(2)}, u32[]{:S(2)}) async-start(bf16[16,96,96]{2,1,0:T(8,128)(2,1)} %bitcast), calls=%async_computation | async-start | bytes 786432 | tf_op jit(solution)/shard_map/all_to_all | solution.py:368
  25.8 3.2 %collective-permute-start.3 = (bf16[6,96,128]{2,1,0:T(8,128)(2,1)S(1)}, bf16[6,96,128]{2,1,0:T(8,128)(2,1)S(1)}, u32[]{:S(2)}, u32[]{:S(2)}) collective-permute-start(bf16[6,96,128]{2,1,0:T(8,128)(2,1)S(1)} %collective-permute-done.2.refs_1_), channel_id=1, source_target_pairs={{0,7},{1,0},{2,1},{3,2},{4,3},{5,4},{6,5},{7,6},{8,15},{9,8},{10,9... | collective-permute-start | bytes 442376 | tf_op jit(solution)/shard_map/ppermute | solution.py:352
  29.0 4.0 %all-to-all-done = bf16[16,96,96]{2,1,0:T(8,128)(2,1)S(1)} async-done(((bf16[16,96,96]{2,1,0:T(8,128)(2,1)}), bf16[16,96,96]{2,1,0:T(8,128)(2,1)S(1)}, u32[]{:S(2)}, u32[]{:S(2)}) %all-to-all-start) | async-done | bytes 294944 | tf_op jit(solution)/shard_map/all_to_all | solution.py:368
  33.1 3.2 %collective-permute-start.4 = (bf16[6,96,128]{2,1,0:T(8,128)(2,1)S(1)}, bf16[6,96,128]{2,1,0:T(8,128)(2,1)S(1)}, u32[]{:S(2)}, u32[]{:S(2)}) collective-permute-start(bf16[6,96,128]{2,1,0:T(8,128)(2,1)S(1)} %collective-permute-done.3.refs_2_), channel_id=1, source_target_pairs={{0,7},{1,0},{2,1},{3,2},{4,3},{5,4},{6,5},{7,6},{8,15},{9,8},{10,9... | collective-permute-start | bytes 442376 | tf_op jit(solution)/shard_map/ppermute | solution.py:352
  36.3 4.2 %collective-permute-done.7.refs_6_ = bf16[6,96,128]{2,1,0:T(8,128)(2,1)S(1)} collective-permute-done((bf16[6,96,128]{2,1,0:T(8,128)(2,1)S(1)}, bf16[6,96,128]{2,1,0:T(8,128)(2,1)S(1)}, u32[]{:S(2)}, u32[]{:S(2)}) %collective-permute-start.7) | collective-permute-done | bytes 147488 | tf_op jit(solution)/shard_map/ppermute | solution.py:352
  40.5 3.2 %collective-permute-start.5 = (bf16[6,96,128]{2,1,0:T(8,128)(2,1)S(1)}, bf16[6,96,128]{2,1,0:T(8,128)(2,1)S(1)}, u32[]{:S(2)}, u32[]{:S(2)}) collective-permute-start(bf16[6,96,128]{2,1,0:T(8,128)(2,1)S(1)} %collective-permute-done.4.refs_3_), channel_id=1, source_target_pairs={{0,7},{1,0},{2,1},{3,2},{4,3},{5,4},{6,5},{7,6},{8,15},{9,8},{10,9... | collective-permute-start | bytes 442376 | tf_op jit(solution)/shard_map/ppermute | solution.py:352
  43.8 1.3 %bias_table.1.bias_ref = f32[192,1536]{1,0:T(8,128)S(1)} custom-call(s32[8]{0:T(128)S(1)} %copy-done.5, bf16[2,4,2,96,96]{4,3,2,1,0:T(8,128)(2,1)S(1)} %bitcast.6, bf16[2,4,2,96,96]{4,3,2,1,0:T(8,128)(2,1)S(1)} %bitcast.7), custom_call_target="tpu_custom_call" | custom-call | tf_op jit(solution)/shard_map/bias_table/pallas_call | solution.py:153
  45.1 2.1 %collective-permute-done.8.refs_5_ = bf16[6,96,128]{2,1,0:T(8,128)(2,1)S(1)} collective-permute-done((bf16[6,96,128]{2,1,0:T(8,128)(2,1)S(1)}, bf16[6,96,128]{2,1,0:T(8,128)(2,1)S(1)}, u32[]{:S(2)}, u32[]{:S(2)}) %collective-permute-start.8) | collective-permute-done | bytes 147488 | tf_op jit(solution)/shard_map/ppermute | solution.py:352
  47.2 14.0 %main.1 = (f32[2,6,96,128]{3,2,1,0:T(8,128)S(1)}, bf16[6,96,128]{2,1,0:T(8,128)(2,1)S(1)}, bf16[6,96,128]{2,1,0:T(8,128)(2,1)S(1)}, bf16[6,96,128]{2,1,0:T(8,128...) custom-call(bf16[6,96,128]{2,1,0:T(8,128)(2,1)S(1)} %get-tuple-eleme, ...), custom_call_target="tpu_custom_call" | custom-call | tf_op jit(solution)/shard_map/main/pallas_call | solution.py:235
  61.4 3.2 %collective-permute-start.13 = (bf16[6,96,128]{2,1,0:T(8,128)(2,1)S(1)}, bf16[6,96,128]{2,1,0:T(8,128)(2,1)S(1)}, u32[]{:S(2)}, u32[]{:S(2)}) collective-permute-start(bf16[6,96,128]{2,1,0:T(8,128)(2,1)S(1)} %get-tuple-element.34), channel_id=1, source_target_pairs={{0,7},{1,0},{2,1},{3,2},{4,3},{5,4},{6,5},{7,6},{8,15},{9,8},{10,9... | collective-permute-start | bytes 442376 | tf_op jit(solution)/shard_map/ppermute | solution.py:352
  64.6 2.3 %split_table.1 = (f32[2,4,2,96,96]{4,3,2,1,0:T(8,128)S(1)}, bf16[2,4,2,96,96]{4,3,2,1,0:T(8,128)(2,1)S(1)}) custom-call(f32[192,1536]{1,0:T(8,128)S(1)} %get-tuple-element.41.table_ref), custom_call_target="tpu_custom_call" | custom-call | tf_op jit(solution)/shard_map/split_table/pallas_call | solution.py:280
  67.9 3.3 %collective-permute-start.14 = (bf16[6,96,128]{2,1,0:T(8,128)(2,1)S(1)}, bf16[6,96,128]{2,1,0:T(8,128)(2,1)S(1)}, u32[]{:S(2)}, u32[]{:S(2)}) collective-permute-start(bf16[6,96,128]{2,1,0:T(8,128)(2,1)S(1)} %add_convert_fusion.2), channel_id=1, source_target_pairs={{0,7},{1,0},{2,1},{3,2},{4,3},{5,4},{6,5},{7,6},{8,15},{9,8},{10,9... | collective-permute-start | bytes 442376 | tf_op jit(solution)/shard_map/ppermute | solution.py:352
  71.2 3.4 %collective-permute-done.10 = bf16[6,96,128]{2,1,0:T(8,128)(2,1)S(1)} collective-permute-done((bf16[6,96,128]{2,1,0:T(8,128)(2,1)S(1)}, bf16[6,96,128]{2,1,0:T(8,128)(2,1)S(1)}, u32[]{:S(2)}, u32[]{:S(2)}) %collective-permute-start.10) | collective-permute-done | bytes 147488 | tf_op jit(solution)/shard_map/ppermute | solution.py:352
  74.8 3.3 %collective-permute-start.15 = (bf16[6,96,128]{2,1,0:T(8,128)(2,1)S(1)}, bf16[6,96,128]{2,1,0:T(8,128)(2,1)S(1)}, u32[]{:S(2)}, u32[]{:S(2)}) collective-permute-start(bf16[6,96,128]{2,1,0:T(8,128)(2,1)S(1)} %add_convert_fusion.1), channel_id=1, source_target_pairs={{0,7},{1,0},{2,1},{3,2},{4,3},{5,4},{6,5},{7,6},{8,15},{9,8},{10,9... | collective-permute-start | bytes 442376 | tf_op jit(solution)/shard_map/ppermute | solution.py:352
  78.9 5.4 %all-to-all-start.1 = ((bf16[16,96,96]{2,1,0:T(8,128)(2,1)}), bf16[16,96,96]{2,1,0:T(8,128)(2,1)S(1)}, u32[]{:S(2)}, u32[]{:S(2)}) async-start(bf16[16,96,96]{2,1,0:T(8,128)(2,1)} %bitcast.3), calls=%async_computation.1 | async-start | bytes 786432 | tf_op jit(solution)/shard_map/all_to_all | solution.py:391
  84.5 6.3 %collective-permute-done.12.b_ref = bf16[6,96,128]{2,1,0:T(8,128)(2,1)S(1)} collective-permute-done((bf16[6,96,128]{2,1,0:T(8,128)(2,1)S(1)}, bf16[6,96,128]{2,1,0:T(8,128)(2,1)S(1)}, u32[]{:S(2)}, u32[]{:S(2)}) %collective-permute-start.12) | collective-permute-done | bytes 147488 | tf_op jit(solution)/shard_map/ppermute | solution.py:352
  91.4 1.6 %collective-permute-start.16 = (bf16[6,96,128]{2,1,0:T(8,128)(2,1)S(1)}, bf16[6,96,128]{2,1,0:T(8,128)(2,1)S(1)}, u32[]{:S(2)}, u32[]{:S(2)}) collective-permute-start(bf16[6,96,128]{2,1,0:T(8,128)(2,1)S(1)} %get-tuple-element.38), channel_id=1, source_target_pairs={{0,8},{8,0},{1,9},{9,1},{2,10},{10,2},{3,11},{11,3},{4,12},{12,4},... | collective-permute-start | bytes 442376 | tf_op jit(solution)/shard_map/ppermute | solution.py:356
  93.7 2.9 %collective-permute-done.16.recv_ref = bf16[6,96,128]{2,1,0:T(8,128)(2,1)S(1)} collective-permute-done((bf16[6,96,128]{2,1,0:T(8,128)(2,1)S(1)}, bf16[6,96,128]{2,1,0:T(8,128)(2,1)S(1)}, u32[]{:S(2)}, u32[]{:S(2)}) %collective-permute-start.16) | collective-permute-done | bytes 147488 | tf_op jit(solution)/shard_map/ppermute | solution.py:356
  96.7 1.0 %output.1 = bf16[6,96,128]{2,1,0:T(8,128)(2,1)} custom-call(f32[6,96,128]{2,1,0:T(8,128)S(1)} %get-tuple-element.37.keep_ref, bf16[6,96,128]{2,1,0:T(8,128)(2,1)S(1)} %collective-permute-done.16.recv_ref, f32[6,96,128]{2,1,0:T(8,128)S(1)} %get-tuple-element.39.gmine_ref, f32[6,96,128]{2,1,0:T(8,128)S(1)} %get-tuple-element.40.gother_ref, ...), custom_call_target="tpu_custom_call" | custom-call | tf_op jit(solution)/shard_map/output/pallas_call | solution.py:343
  (43 shorter events, 7.2 us)
Async XLA Ops:
  1.5 0.9 copy-start.2
  2.4 0.9 copy-start.3
  4.0 39.8 %copy-start.5 = (s32[8]{0:T(128)S(1)}, s32[8]{0:T(128)}, u32[]{:S(2)}) copy-start(s32[8]{0:T(128)} %len_ref.1) | copy-start | bytes 100
  4.7 5.7 %collective-permute-start = (bf16[6,96,128]{2,1,0:T(8,128)(2,1)S(1)}, bf16[6,96,128]{2,1,0:T(8,128)(2,1)S(1)}, u32[]{:S(2)}, u32[]{:S(2)}) collective-permute-start(bf16[6,96,128]{2,1,0:T(8,128)(2,1)S(1)} %get-tuple-element.24), channel_id=1, source_target_pairs={{0,8},{8,0},{1,9},{9,1},{2,10},{10,2},{3,11},{11,3},{4,12},{12,4},... | collective-permute-start | bytes 442376 | tf_op jit(solution)/shard_map/ppermute | solution.py:356
  10.8 15.0 %collective-permute-start.2 = (bf16[6,96,128]{2,1,0:T(8,128)(2,1)S(1)}, bf16[6,96,128]{2,1,0:T(8,128)(2,1)S(1)}, u32[]{:S(2)}, u32[]{:S(2)}) collective-permute-start(bf16[6,96,128]{2,1,0:T(8,128)(2,1)S(1)} %get-tuple-element.27.refs_0_), channel_id=1, source_target_pairs={{0,7},{1,0},{2,1},{3,2},{4,3},{5,4},{6,5},{7,6},{8,15},{9,8},{10,9... | collective-permute-start | bytes 442376 | tf_op jit(solution)/shard_map/ppermute | solution.py:352
  18.3 14.7 %all-to-all-start = ((bf16[16,96,96]{2,1,0:T(8,128)(2,1)}), bf16[16,96,96]{2,1,0:T(8,128)(2,1)S(1)}, u32[]{:S(2)}, u32[]{:S(2)}) async-start(bf16[16,96,96]{2,1,0:T(8,128)(2,1)} %bitcast), calls=%async_computation | async-start | bytes 786432 | tf_op jit(solution)/shard_map/all_to_all | solution.py:368
  25.8 7.2 %collective-permute-start.6 = (bf16[6,96,128]{2,1,0:T(8,128)(2,1)S(1)}, bf16[6,96,128]{2,1,0:T(8,128)(2,1)S(1)}, u32[]{:S(2)}, u32[]{:S(2)}) collective-permute-start(bf16[6,96,128]{2,1,0:T(8,128)(2,1)S(1)} %get-tuple-element.27.refs_0_), channel_id=1, source_target_pairs={{0,1},{1,2},{2,3},{3,4},{4,5},{5,6},{6,7},{7,0},{8,9},{9,10},{10,1... | collective-permute-start | bytes 442376 | tf_op jit(solution)/shard_map/ppermute | solution.py:352
  25.8 7.2 %collective-permute-start.3 = (bf16[6,96,128]{2,1,0:T(8,128)(2,1)S(1)}, bf16[6,96,128]{2,1,0:T(8,128)(2,1)S(1)}, u32[]{:S(2)}, u32[]{:S(2)}) collective-permute-start(bf16[6,96,128]{2,1,0:T(8,128)(2,1)S(1)} %collective-permute-done.2.refs_1_), channel_id=1, source_target_pairs={{0,7},{1,0},{2,1},{3,2},{4,3},{5,4},{6,5},{7,6},{8,15},{9,8},{10,9... | collective-permute-start | bytes 442376 | tf_op jit(solution)/shard_map/ppermute | solution.py:352
  33.0 10.7 %collective-permute-start.1 = (bf16[16,96,96]{2,1,0:T(8,128)(2,1)S(1)}, bf16[16,96,96]{2,1,0:T(8,128)(2,1)S(1)}, u32[]{:S(2)}, u32[]{:S(2)}) collective-permute-start(bf16[16,96,96]{2,1,0:T(8,128)(2,1)S(1)} %all-to-all-done), channel_id=1, source_target_pairs={{0,16},{16,0},{1,17},{17,1},{2,18},{18,2},{3,19},{19,3},{4,20},{20... | collective-permute-start | bytes 884744 | tf_op jit(solution)/shard_map/ppermute | solution.py:356
  33.0 7.5 %collective-permute-start.7 = (bf16[6,96,128]{2,1,0:T(8,128)(2,1)S(1)}, bf16[6,96,128]{2,1,0:T(8,128)(2,1)S(1)}, u32[]{:S(2)}, u32[]{:S(2)}) collective-permute-start(bf16[6,96,128]{2,1,0:T(8,128)(2,1)S(1)} %collective-permute-done.6.refs_7_), channel_id=1, source_target_pairs={{0,1},{1,2},{2,3},{3,4},{4,5},{5,6},{6,7},{7,0},{8,9},{9,10},{10,1... | collective-permute-start | bytes 442376 | tf_op jit(solution)/shard_map/ppermute | solution.py:352
  33.1 7.5 %collective-permute-start.4 = (bf16[6,96,128]{2,1,0:T(8,128)(2,1)S(1)}, bf16[6,96,128]{2,1,0:T(8,128)(2,1)S(1)}, u32[]{:S(2)}, u32[]{:S(2)}) collective-permute-start(bf16[6,96,128]{2,1,0:T(8,128)(2,1)S(1)} %collective-permute-done.3.refs_2_), channel_id=1, source_target_pairs={{0,7},{1,0},{2,1},{3,2},{4,3},{5,4},{6,5},{7,6},{8,15},{9,8},{10,9... | collective-permute-start | bytes 442376 | tf_op jit(solution)/shard_map/ppermute | solution.py:352
  40.5 6.7 %collective-permute-start.8 = (bf16[6,96,128]{2,1,0:T(8,128)(2,1)S(1)}, bf16[6,96,128]{2,1,0:T(8,128)(2,1)S(1)}, u32[]{:S(2)}, u32[]{:S(2)}) collective-permute-start(bf16[6,96,128]{2,1,0:T(8,128)(2,1)S(1)} %collective-permute-done.7.refs_6_), channel_id=1, source_target_pairs={{0,1},{1,2},{2,3},{3,4},{4,5},{5,6},{6,7},{7,0},{8,9},{9,10},{10,1... | collective-permute-start | bytes 442376 | tf_op jit(solution)/shard_map/ppermute | solution.py:352
  40.5 6.7 %collective-permute-start.5 = (bf16[6,96,128]{2,1,0:T(8,128)(2,1)S(1)}, bf16[6,96,128]{2,1,0:T(8,128)(2,1)S(1)}, u32[]{:S(2)}, u32[]{:S(2)}) collective-permute-start(bf16[6,96,128]{2,1,0:T(8,128)(2,1)S(1)} %collective-permute-done.4.refs_3_), channel_id=1, source_target_pairs={{0,7},{1,0},{2,1},{3,2},{4,3},{5,4},{6,5},{7,6},{8,15},{9,8},{10,9... | collective-permute-start | bytes 442376 | tf_op jit(solution)/shard_map/ppermute | solution.py:352
  61.3 6.4 %collective-permute-start.9 = (bf16[6,96,128]{2,1,0:T(8,128)(2,1)S(1)}, bf16[6,96,128]{2,1,0:T(8,128)(2,1)S(1)}, u32[]{:S(2)}, u32[]{:S(2)}) collective-permute-start(bf16[6,96,128]{2,1,0:T(8,128)(2,1)S(1)} %get-tuple-element.30), channel_id=1, source_target_pairs={{0,1},{1,2},{2,3},{3,4},{4,5},{5,6},{6,7},{7,0},{8,9},{9,10},{10,1... | collective-permute-start | bytes 442376 | tf_op jit(solution)/shard_map/ppermute | solution.py:352
  61.4 6.5 %collective-permute-start.13 = (bf16[6,96,128]{2,1,0:T(8,128)(2,1)S(1)}, bf16[6,96,128]{2,1,0:T(8,128)(2,1)S(1)}, u32[]{:S(2)}, u32[]{:S(2)}) collective-permute-start(bf16[6,96,128]{2,1,0:T(8,128)(2,1)S(1)} %get-tuple-element.34), channel_id=1, source_target_pairs={{0,7},{1,0},{2,1},{3,2},{4,3},{5,4},{6,5},{7,6},{8,15},{9,8},{10,9... | collective-permute-start | bytes 442376 | tf_op jit(solution)/shard_map/ppermute | solution.py:352
  66.9 11.2 %collective-permute-start.17 = (bf16[2,4,2,96,96]{4,3,2,1,0:T(8,128)(2,1)S(1)}, bf16[2,4,2,96,96]{4,3,2,1,0:T(8,128)(2,1)S(1)}, u32[]{:S(2)}, u32[]{:S(2)}) collective-permute-start(bf16[2,4,2,96,96]{4,3,2,1,0:T(8,128)(2,1)S(1)} %get-tuple-element.43), channel_id=1, source_target_pairs={{0,16},{16,0},{1,17},{17,1},{2,18},{18,2},{3,19},{19,3},{4,20},{20... | collective-permute-start | bytes 884744 | tf_op jit(solution)/shard_map/ppermute | solution.py:356
  67.7 6.8 %collective-permute-start.10 = (bf16[6,96,128]{2,1,0:T(8,128)(2,1)S(1)}, bf16[6,96,128]{2,1,0:T(8,128)(2,1)S(1)}, u32[]{:S(2)}, u32[]{:S(2)}) collective-permute-start(bf16[6,96,128]{2,1,0:T(8,128)(2,1)S(1)} %add_convert_fusion.5), channel_id=1, source_target_pairs={{0,1},{1,2},{2,3},{3,4},{4,5},{5,6},{6,7},{7,0},{8,9},{9,10},{10,1... | collective-permute-start | bytes 442376 | tf_op jit(solution)/shard_map/ppermute | solution.py:352
  67.9 6.8 %collective-permute-start.14 = (bf16[6,96,128]{2,1,0:T(8,128)(2,1)S(1)}, bf16[6,96,128]{2,1,0:T(8,128)(2,1)S(1)}, u32[]{:S(2)}, u32[]{:S(2)}) collective-permute-start(bf16[6,96,128]{2,1,0:T(8,128)(2,1)S(1)} %add_convert_fusion.2), channel_id=1, source_target_pairs={{0,7},{1,0},{2,1},{3,2},{4,3},{5,4},{6,5},{7,6},{8,15},{9,8},{10,9... | collective-permute-start | bytes 442376 | tf_op jit(solution)/shard_map/ppermute | solution.py:352
  74.6 9.7 %collective-permute-start.11 = (bf16[6,96,128]{2,1,0:T(8,128)(2,1)S(1)}, bf16[6,96,128]{2,1,0:T(8,128)(2,1)S(1)}, u32[]{:S(2)}, u32[]{:S(2)}) collective-permute-start(bf16[6,96,128]{2,1,0:T(8,128)(2,1)S(1)} %add_convert_fusion.4), channel_id=1, source_target_pairs={{0,1},{1,2},{2,3},{3,4},{4,5},{5,6},{6,7},{7,0},{8,9},{9,10},{10,1... | collective-permute-start | bytes 442376 | tf_op jit(solution)/shard_map/ppermute | solution.py:352
  74.8 9.7 %collective-permute-start.15 = (bf16[6,96,128]{2,1,0:T(8,128)(2,1)S(1)}, bf16[6,96,128]{2,1,0:T(8,128)(2,1)S(1)}, u32[]{:S(2)}, u32[]{:S(2)}) collective-permute-start(bf16[6,96,128]{2,1,0:T(8,128)(2,1)S(1)} %add_convert_fusion.1), channel_id=1, source_target_pairs={{0,7},{1,0},{2,1},{3,2},{4,3},{5,4},{6,5},{7,6},{8,15},{9,8},{10,9... | collective-permute-start | bytes 442376 | tf_op jit(solution)/shard_map/ppermute | solution.py:352
  78.9 14.1 %all-to-all-start.1 = ((bf16[16,96,96]{2,1,0:T(8,128)(2,1)}), bf16[16,96,96]{2,1,0:T(8,128)(2,1)S(1)}, u32[]{:S(2)}, u32[]{:S(2)}) async-start(bf16[16,96,96]{2,1,0:T(8,128)(2,1)} %bitcast.3), calls=%async_computation.1 | async-start | bytes 786432 | tf_op jit(solution)/shard_map/all_to_all | solution.py:391
  84.3 12.4 %copy-start.1 = (bf16[128,256]{1,0:T(8,128)(2,1)S(1)}, bf16[128,256]{1,0:T(8,128)(2,1)}, u32[]{:S(2)}) copy-start(bf16[128,256]{1,0:T(8,128)(2,1)} %w_ref.3) | copy-start | bytes 196612
  84.4 6.4 %collective-permute-start.12 = (bf16[6,96,128]{2,1,0:T(8,128)(2,1)S(1)}, bf16[6,96,128]{2,1,0:T(8,128)(2,1)S(1)}, u32[]{:S(2)}, u32[]{:S(2)}) collective-permute-start(bf16[6,96,128]{2,1,0:T(8,128)(2,1)S(1)} %add_convert_fusion.3), channel_id=1, source_target_pairs={{0,1},{1,2},{2,3},{3,4},{4,5},{5,6},{6,7},{7,0},{8,9},{9,10},{10,1... | collective-permute-start | bytes 442376 | tf_op jit(solution)/shard_map/ppermute | solution.py:352
  91.4 5.2 %collective-permute-start.16 = (bf16[6,96,128]{2,1,0:T(8,128)(2,1)S(1)}, bf16[6,96,128]{2,1,0:T(8,128)(2,1)S(1)}, u32[]{:S(2)}, u32[]{:S(2)}) collective-permute-start(bf16[6,96,128]{2,1,0:T(8,128)(2,1)S(1)} %get-tuple-element.38), channel_id=1, source_target_pairs={{0,8},{8,0},{1,9},{9,1},{2,10},{10,2},{3,11},{11,3},{4,12},{12,4},... | collective-permute-start | bytes 442376 | tf_op jit(solution)/shard_map/ppermute | solution.py:356
  (2 other events, 1.6 us)

commit v2 on v1

v2 whole, which is shorter than its diff:
```python
import functools
import math

import jax
import jax.numpy as jnp
from jax import lax
from jax.experimental import pallas as pl
from jax.experimental.pallas import tpu as pltpu
from jax.sharding import Mesh, PartitionSpec as P

H = 2
DH = 32
CHAINS = 8
SCALE = 1.0 / math.sqrt(DH)
MASKED_SCORE = -1e30
F32 = jnp.float32
BF16 = jnp.bfloat16

ROWS = 6
COLS = 96
RING = 8
HALF = RING * COLS
KEYS = 2 * HALF
WIDE = 128
CHUNK = 4 * COLS
CHUNKS = ((0, 1), (2, 7), (3, 6), (4, 5))
LAST = len(CHUNKS) - 1
M_LANE = 64
SLOT = KEYS // CHAINS

NT = (((1,), (1,)), ((), ()))
NN = (((1,), (0,)), ((), ()))
TN = (((0,), (0,)), ((), ()))


def mm(a, b, dims):
    return lax.dot_general(a, b, dims, preferred_element_type=F32)


def params(limit=48 << 20):
    return pltpu.CompilerParams(vmem_limit_bytes=limit)


def cost(us):
    return pl.CostEstimate(flops=0, bytes_accessed=int(us * 3e6), transcendentals=0)


def lanes(shape):
    return lax.broadcasted_iota(jnp.int32, shape, len(shape) - 1)


def head_weight(w, h):
    parts = [w[:, (part * H + h) * DH : (part * H + h + 1) * DH] for part in (1, 2, 0, 3)]
    return jnp.concatenate(parts, axis=1)


def project_kernel(
    pair_hbm, grad_hbm, w_hbm, wout_hbm, mine_ref, other_ref, gmine_ref, gother_ref,
    pair_s, grad_s, w_s, wout_s, sem,
):
    yl = lax.axis_index("yl")
    pairs = ((w_hbm, w_s), (wout_hbm, wout_s), (pair_hbm, pair_s), (grad_hbm, grad_s))
    copies = [pltpu.make_async_copy(a, b, sem.at[n]) for n, (a, b) in enumerate(pairs)]
    for copy in copies:
        copy.start()
    for copy in copies:
        copy.wait()
    pair = pair_s[...].reshape(ROWS * COLS, WIDE)
    grad = grad_s[...].reshape(ROWS * COLS, WIDE)
    w = w_s[...]
    wout = wout_s[...]
    lane = lanes((ROWS * COLS, WIDE))
    for h in range(H):
        proj = mm(pair, head_weight(w, h), NN)
        rows = jnp.concatenate(
            [jnp.zeros((WIDE - DH, WIDE), BF16), wout[h * DH : (h + 1) * DH]], axis=0
        )
        d_out = mm(grad, rows, NT)
        gate = jax.nn.sigmoid(proj)
        payload = jnp.where(
            lane < 2 * DH, proj, jnp.where(lane < 3 * DH, proj * SCALE, d_out * gate)
        )
        payload = payload.astype(BF16).reshape(ROWS, COLS, WIDE)
        g = (d_out * gate * (1.0 - gate)).reshape(ROWS, COLS, WIDE)

        @pl.when(yl == h)
        def _():
            mine_ref[...] = payload
            gmine_ref[...] = g

        @pl.when(yl != h)
        def _():
            other_ref[...] = payload
            gother_ref[...] = g


def project(pair, grad, w, wout):
    shape = (ROWS, COLS, WIDE)
    return pl.pallas_call(
        project_kernel,
        in_specs=[pl.BlockSpec(memory_space=pl.ANY)] * 4,
        out_shape=[
            jax.ShapeDtypeStruct(shape, BF16),
            jax.ShapeDtypeStruct(shape, BF16),
            jax.ShapeDtypeStruct(shape, F32),
            jax.ShapeDtypeStruct(shape, F32),
        ],
        scratch_shapes=[
            pltpu.VMEM(shape, BF16),
            pltpu.VMEM(shape, BF16),
            pltpu.VMEM(w.shape, BF16),
            pltpu.VMEM(wout.shape, BF16),
            pltpu.SemaphoreType.DMA((4,)),
        ],
        compiler_params=params(),
        cost_estimate=cost(2.0),
        name="project",
    )(pair, grad, w, wout)


def pack_kernel(mine_ref, recv_ref, kv_ref, q_ref, da_ref):
    yl = lax.axis_index("yl")
    lane = lanes((COLS, WIDE))

    def write(i, a, b):
        a, b = a.astype(F32), b.astype(F32)
        kv_ref[i] = jnp.where(lane < 2 * DH, a, pltpu.roll(b, 2 * DH, 1)).astype(BF16)
        for part, x in enumerate((a, b)):
            y = pltpu.roll(x, 2 * DH, 1)
            rows = slice(part * COLS, (part + 1) * COLS)
            q_ref[i, rows] = jnp.where(lane < DH, y, 0.0).astype(BF16)
            da_ref[i, rows] = jnp.where((lane >= DH) & (lane < 2 * DH), y, 0.0).astype(BF16)

    for i in range(ROWS):

        @pl.when(yl == 0)
        def _():
            write(i, mine_ref[i], recv_ref[i])

        @pl.when(yl != 0)
        def _():
            write(i, recv_ref[i], mine_ref[i])


def pack(mine, recv):
    block = jax.ShapeDtypeStruct((ROWS, COLS, WIDE), BF16)
    both = jax.ShapeDtypeStruct((ROWS, 2 * COLS, WIDE), BF16)
    return pl.pallas_call(
        pack_kernel,
        out_shape=[block, both, both],
        compiler_params=params(),
        cost_estimate=cost(0.6),
        name="pack",
    )(mine, recv)


def bias_kernel(len_ref, own_ref, oth_ref, out_ref):
    core = lax.axis_index("core")
    z = lax.axis_index("z")
    lane = lanes((1, COLS))
    for c, pair in enumerate(CHUNKS):
        for n, r in enumerate(pair):
            at = lax.rem(z + r, RING)
            x, odd = at // 2, lax.rem(at, 2)
            for yh in range(2):
                start = (yh * 2 + n) * COLS
                valid = lane + odd * COLS < len_ref[yh * 4 + x]
                lift = jnp.where(valid, 0.0, MASKED_SCORE)
                for yl in range(2):
                    rows = slice(yl * COLS, (yl + 1) * COLS)
                    both = jnp.where(odd == core, own_ref[yh, x, yl], oth_ref[yh, x, yl])
                    out_ref[c, rows, start : start + COLS] = both.astype(F32) + lift


def bias_table(chain_lengths, own, oth):
    return pl.pallas_call(
        bias_kernel,
        out_shape=jax.ShapeDtypeStruct((len(CHUNKS), 2 * COLS, CHUNK), F32),
        in_specs=[
            pl.BlockSpec(memory_space=pltpu.SMEM),
            pl.BlockSpec(memory_space=pltpu.VMEM),
            pl.BlockSpec(memory_space=pltpu.VMEM),
        ],
        compiler_params=params(),
        cost_estimate=cost(1.5),
        name="bias_table",
    )(chain_lengths, own, oth)


def stack(a, b):
    two = jnp.concatenate([a, b], axis=0)
    moved = pltpu.roll(two.astype(F32), 2 * DH, 1).astype(BF16)
    return jnp.concatenate([two, moved], axis=0)


def unstack(value):
    moved = pltpu.roll(value[2 * COLS :], 2 * DH, 1)
    both = (value[: 2 * COLS] + moved).astype(BF16)
    return both[:COLS], both[COLS:]


def column(state, n):
    return state[:, M_LANE + n : M_LANE + n + 1]


def score_step(c, q, kv, bias, state):
    lane = lanes((2 * COLS, WIDE))
    s = mm(q, kv, NT) + bias
    top = jnp.max(s, axis=1, keepdims=True)
    if c > 0:
        old = column(state, c)
        top = jnp.maximum(top, old)
        fade = jnp.exp(old - top)
    e = jnp.exp(s - top)
    total = jnp.sum(e, axis=1, keepdims=True)
    acc = mm(e.astype(BF16), kv, NN)
    if c > 0:
        total = total + column(state, 0) * fade
        acc = acc + state * fade
    acc = jnp.where(lane < M_LANE, acc, jnp.where(lane == M_LANE, total, 0.0))
    for n in range(c):
        acc = jnp.where(lane == M_LANE + 1 + n, column(state, 1 + n), acc)
    acc = jnp.where(lane == M_LANE + 1 + c, top, acc)
    return e, acc, top, total


def forward_kernel(c, q_ref, a_ref, b_ref, bias_ref, *refs):
    state = refs[0][0] if c > 0 else None
    e_ref, state_ref = refs[-2:]
    e, acc, _, _ = score_step(c, q_ref[0], stack(a_ref[0], b_ref[0]), bias_ref[0], state)
    e_ref[0] = e
    state_ref[0] = acc


ROW = pl.BlockSpec((1, COLS, WIDE), lambda i: (i, 0, 0))
ROW2 = pl.BlockSpec((1, 2 * COLS, WIDE), lambda i: (i, 0, 0))
ROWE = pl.BlockSpec((1, 2 * COLS, CHUNK), lambda i: (i, 0, 0))
TABLE = pl.BlockSpec((2 * COLS, CHUNK), lambda i: (0, 0))
BLOCK = jax.ShapeDtypeStruct((ROWS, COLS, WIDE), BF16)
STATE = jax.ShapeDtypeStruct((ROWS, 2 * COLS, WIDE), F32)


def table_of(c):
    return pl.BlockSpec((1, 2 * COLS, CHUNK), lambda i: (c, 0, 0))


def forward(c, q, kvs, bias, state):
    a, b = CHUNKS[c]
    more = [] if c == 0 else [state]
    return pl.pallas_call(
        functools.partial(forward_kernel, c),
        grid=(ROWS,),
        in_specs=[ROW2, ROW, ROW, table_of(c)] + [ROW2] * len(more),
        out_specs=[ROWE, ROW2],
        out_shape=[jax.ShapeDtypeStruct((ROWS, 2 * COLS, CHUNK), F32), STATE],
        compiler_params=params(),
        cost_estimate=cost(2.0),
        name=f"forward_{c}",
    )(q, kvs[a], kvs[b], bias, *more)


def gradient_step(p, q, da, kv, dot, left, right):
    d = p * (mm(da, kv, NT) - dot)
    low = d.astype(BF16)
    left[: 2 * COLS, :] = low
    left[2 * COLS :, :] = p.astype(BF16)
    dq = mm(low, kv, NN)
    return d, dq, mm(left[...], right[...], TN)


def turn_kernel(q_ref, da_ref, a_ref, b_ref, bias_ref, state_ref, *refs):
    out_ref, da_out, db_out, table_ref, left, right = refs
    i = pl.program_id(0)
    q, da = q_ref[0], da_ref[0]
    kv = stack(a_ref[0], b_ref[0])
    e, acc, top, total = score_step(LAST, q, kv, bias_ref[0], state_ref[0])
    inverse = 1.0 / total
    acc = acc * inverse
    dot = jnp.sum(acc * da.astype(F32), axis=1, keepdims=True)
    right[: 2 * COLS, :] = q
    right[2 * COLS :, :] = da
    d, dq, dkv = gradient_step(e * inverse, q, da, kv, dot, left, right)

    @pl.when(i == 0)
    def _():
        table_ref[...] = d

    @pl.when(i != 0)
    def _():
        table_ref[...] += d

    da_out[0], db_out[0] = unstack(dkv)
    lane = lanes((2 * COLS, WIDE))
    out = jnp.where(lane < DH, dq, acc)
    out = jnp.where(lane == M_LANE, dot, out)
    for c in range(LAST):
        factor = jnp.exp(column(state_ref[0], 1 + c) - top) * inverse
        out = jnp.where(lane == M_LANE + 1 + c, factor, out)
    out_ref[0] = out


def turn(q, da, kvs, bias, state):
    a, b = CHUNKS[LAST]
    return pl.pallas_call(
        turn_kernel,
        grid=(ROWS,),
        in_specs=[ROW2, ROW2, ROW, ROW, table_of(LAST), ROW2],
        out_specs=[ROW2, ROW, ROW, TABLE],
        out_shape=[STATE, BLOCK, BLOCK, jax.ShapeDtypeStruct((2 * COLS, CHUNK), F32)],
        scratch_shapes=[pltpu.VMEM((CHUNK, CHUNK), BF16), pltpu.VMEM((CHUNK, WIDE), BF16)],
        compiler_params=params(),
        cost_estimate=cost(4.0),
        name="turn",
    )(q, da, kvs[a], kvs[b], bias, state)


def backward_kernel(q_ref, da_ref, state_ref, table_ref, *refs):
    n = LAST
    kv_refs, e_refs = refs[: 2 * n], refs[2 * n : 3 * n]
    u_ref, dkv_refs = refs[3 * n], refs[3 * n + 1 : 5 * n + 1]
    keep_ref, send_ref = refs[5 * n + 1 : 5 * n + 3]
    left, right, sums = refs[5 * n + 3 :]
    i = pl.program_id(0)
    q, da, state = q_ref[0], da_ref[0], state_ref[0]
    dot = column(state, 0)
    right[: 2 * COLS, :] = q
    right[2 * COLS :, :] = da

    @pl.when(i == 0)
    def _():
        sums[...] = jnp.zeros_like(sums)

    u = state
    lane = lanes((2 * COLS, WIDE))
    for c in range(n):
        kv = stack(kv_refs[2 * c][0], kv_refs[2 * c + 1][0])
        p = e_refs[c][0] * column(state, 1 + c)
        d, dq, dkv = gradient_step(p, q, da, kv, dot, left.at[c], right)
        sums[c] += d
        u = jnp.where(lane < DH, u + dq, u)
        dkv_refs[2 * c][0], dkv_refs[2 * c + 1][0] = unstack(dkv)
    u = jnp.where(lane < DH, u * SCALE, u)
    u_ref[0, 0] = u[:COLS]
    u_ref[1, 0] = u[COLS:]

    @pl.when(i == ROWS - 1)
    def _():
        core = lax.axis_index("core")
        z = lax.axis_index("z")
        for c, pair in enumerate(CHUNKS):
            table = table_ref if c == LAST else sums.at[c]
            for m, r in enumerate(pair):
                at = lax.rem(z + r, RING)
                x, odd = at // 2, lax.rem(at, 2)
                for yh in range(2):
                    start = (yh * 2 + m) * COLS
                    for yl in range(2):
                        rows = slice(yl * COLS, (yl + 1) * COLS)
                        piece = table[rows, start : start + COLS]

                        @pl.when(odd == core)
                        def _():
                            keep_ref[yh, x, yl] = piece

                        @pl.when(odd != core)
                        def _():
                            send_ref[yh, x, yl] = piece.astype(BF16)


def backward(q, da, state, table, kvs, es):
    order = [r for pair in CHUNKS[:LAST] for r in pair]
    blocks = (2, 4, 2, COLS, COLS)
    whole = pl.BlockSpec(blocks, lambda i: (0, 0, 0, 0, 0))
    out = pl.pallas_call(
        backward_kernel,
        grid=(ROWS,),
        in_specs=[ROW2, ROW2, ROW2, TABLE] + [ROW] * len(order) + [ROWE] * LAST,
        out_specs=[pl.BlockSpec((2, 1, COLS, WIDE), lambda i: (0, i, 0, 0))]
        + [ROW] * len(order)
        + [whole, whole],
        out_shape=[jax.ShapeDtypeStruct((2, ROWS, COLS, WIDE), F32)]
        + [BLOCK] * len(order)
        + [jax.ShapeDtypeStruct(blocks, F32), jax.ShapeDtypeStruct(blocks, BF16)],
        scratch_shapes=[
            pltpu.VMEM((LAST, CHUNK, CHUNK), BF16),
            pltpu.VMEM((CHUNK, WIDE), BF16),
            pltpu.VMEM((LAST, 2 * COLS, CHUNK), F32),
        ],
        compiler_params=params(),
        cost_estimate=cost(6.0),
        name="backward",
    )(q, da, state, table, *[kvs[r] for r in order], *es)
    return out[0], dict(zip(order, out[1 : len(order) + 1])), out[-2], out[-1]


def finish_kernel(u_ref, a_ref, b_ref, c_ref, keep_ref, send_ref):
    yl = lax.axis_index("yl")
    lane = lanes((COLS, WIDE))
    for i in range(ROWS):
        dkv = a_ref[i].astype(F32) + b_ref[i].astype(F32) + c_ref[i].astype(F32)
        first = jnp.where(lane < 2 * DH, dkv, pltpu.roll(u_ref[0, i], 2 * DH, 1))
        second = jnp.where(
            lane < 2 * DH, pltpu.roll(dkv, 2 * DH, 1), pltpu.roll(u_ref[1, i], 2 * DH, 1)
        )

        @pl.when(yl == 0)
        def _():
            keep_ref[i] = first
            send_ref[i] = second.astype(BF16)

        @pl.when(yl != 0)
        def _():
            keep_ref[i] = second
            send_ref[i] = first.astype(BF16)


def finish(u, a, b, c):
    shape = (ROWS, COLS, WIDE)
    return pl.pallas_call(
        finish_kernel,
        out_shape=[jax.ShapeDtypeStruct(shape, F32), jax.ShapeDtypeStruct(shape, BF16)],
        compiler_params=params(),
        name="finish",
    )(u, a, b, c)


def output_kernel(keep_ref, recv_ref, gmine_ref, gother_ref, w_ref, out_ref):
    yl = lax.axis_index("yl")
    flat = (ROWS * COLS, WIDE)
    lane = lanes(flat)
    keep = keep_ref[...].reshape(flat)
    recv = recv_ref[...].reshape(flat).astype(F32)
    mine = jnp.where(lane < 3 * DH, keep, keep * gmine_ref[...].reshape(flat)).astype(BF16)
    other = jnp.where(lane < 3 * DH, recv, recv * gother_ref[...].reshape(flat)).astype(BF16)
    w = w_ref[...]
    w0, w1 = head_weight(w, 0), head_weight(w, 1)

    def write(a, b):
        out_ref[...] = (mm(a, w0, NT) + mm(b, w1, NT)).astype(BF16).reshape(ROWS, COLS, WIDE)

    @pl.when(yl == 0)
    def _():
        write(mine, other)

    @pl.when(yl != 0)
    def _():
        write(other, mine)


def output(keep, recv, gmine, gother, w):
    return pl.pallas_call(
        output_kernel,
        out_shape=jax.ShapeDtypeStruct((ROWS, COLS, WIDE), BF16),
        compiler_params=params(),
        name="output",
    )(keep, recv, gmine, gother, w)


def shift(value, step):
    return lax.ppermute(value, "z", [(z, (z + step) % RING) for z in range(RING)])


def swap(value, axis):
    return lax.ppermute(value, axis, [(0, 1), (1, 0)])


def added(a, b):
    return (a.astype(F32) + b.astype(F32)).astype(BF16)


def body(pair, w_qkvg, w_out, bias, chain_lengths, d_pair_out):
    peers = ("yh", "x", "yl")
    wanted = jnp.broadcast_to(bias[None], (8,) + bias.shape).reshape(16, COLS, COLS)
    mine, other, gmine, gother = project(pair, d_pair_out, w_qkvg, w_out)
    recv = swap(other, "yl")
    own = lax.all_to_all(wanted, peers, 0, 0, tiled=True)
    kv, q, da = pack(mine, recv)
    oth = swap(own, "core")
    blocks = (2, 4, 2, COLS, COLS)
    table = bias_table(chain_lengths, own.reshape(blocks), oth.reshape(blocks))
    kvs = [kv] + [None] * (RING - 1)
    up = down = kv
    for r in range(1, 5):
        down = shift(down, -1)
        kvs[r] = down
        if r < 4:
            up = shift(up, 1)
            kvs[RING - r] = up
    es, state = [], None
    for c in range(LAST):
        e, state = forward(c, q, kvs, table, state)
        es.append(e)
    state, d4, d5, d_last = turn(q, da, kvs, table, state)
    up = shift(d4, 1)
    down = shift(d5, -1)
    u, dkvs, keep_table, send_table = backward(q, da, state, d_last, kvs, es)
    up = shift(added(up, dkvs[3]), 1)
    down = shift(added(down, dkvs[6]), -1)
    up = shift(added(up, dkvs[2]), 1)
    down = shift(added(down, dkvs[7]), -1)
    up = shift(added(up, dkvs[1]), 1)
    summed = (keep_table + swap(send_table, "core").astype(F32)).astype(BF16)
    parts = lax.all_to_all(summed.reshape(16, COLS, COLS), peers, 0, 0, tiled=True)
    d_bias = jnp.sum(parts.reshape(8, H, COLS, COLS).astype(F32), axis=0)
    keep, send = finish(u, dkvs[0], up, down)
    d_pair = output(keep, swap(send, "yl"), gmine, gother, w_qkvg)
    return (d_pair, d_bias)


def solution(mesh):
    split = Mesh(mesh.devices.reshape(2, 4, 2, 2, RING), ("yh", "x", "core", "yl", "z"))
    row, col = ("yh", "x", "core"), ("yl", "z")
    in_specs = (P(row, col, None), P(), P(), P(None, col, row), P(), P(row, col, None))
    out_specs = (P(row, col, None), P(None, col, row))
    return jax.shard_map(body, mesh=split, in_specs=in_specs, out_specs=out_specs, check_vma=False)
```

time: 98.2 us -> 115 us (1.17)
  Pallas kernels: 20.4 us -> 35.3 us
  local copies, waits for them, and re-layouts: 4.99 us -> 8.6 us
  waiting for transfers between devices: 27.8 us -> 25.6 us
    pallas_call x5 -> x8, Pallas kernels: 18.8 us -> 33.6 us  [the longest x3 11.4 us: forward(): pl.pallas_call(functools.partial(forward_kernel, c), grid=(ROWS,), in_spe...]
    unnamed x12 -> x18, local copies, waits for them, and re-layouts: 3.38 us -> 7.01 us
    ppermute x14, waiting for transfers between devices: 16.8 us -> 14.7 us  [shift(): lax.ppermute(value, 'z', [(z, (z + step) % RING) for z in range(RING)])]
  transfers between devices with their start and end apart: 20 -> 20, of which waited for: 8 -> 6; matrix products, arithmetic and copies ran while one was open for 3% -> 3% of each run, Pallas kernels for 4% -> 21%
where the time goes in v2:
time: 115 us; the launch traced here: 114 us
  starting transfers between devices  42.3 us (37%)
  Pallas kernels  35.3 us (31%)
  waiting for transfers between devices  25.6 us (22%)
  local copies, waits for them, and re-layouts  8.6 us (7%)
  other arithmetic  1.76 us (2%)
    ppermute x14, starting transfers between devices, shift(): lax.ppermute(value, 'z', [(z, (z + step) % RING) for z in range(RING)])  25.8 us
    ppermute x14, waiting for transfers between devices, shift(): lax.ppermute(value, 'z', [(z, (z + step) % RING) for z in range(RING)])  14.7 us
    pallas_call x3, Pallas kernels, forward(): pl.pallas_call(functools.partial(forward_kernel, c), grid=(ROWS,), in_spe...  11.4 us
    pallas_call x1, Pallas kernels, backward(): pl.pallas_call(backward_kernel, grid=(ROWS,), in_specs=[ROW2, ROW2, ROW2,...  10.5 us
    pallas_call x1, Pallas kernels, turn(): pl.pallas_call(turn_kernel, grid=(ROWS,), in_specs=[ROW2, ROW2, ROW, ROW,...  9.12 us
    all_to_all x1, starting transfers between devices, body(): own = lax.all_to_all(wanted, peers, 0, 0, tiled=True)  7.48 us
    unnamed x18, local copies, waits for them, and re-layouts  7.01 us
    ppermute x4, waiting for transfers between devices, swap(): return lax.ppermute(value, axis, [(0, 1), (1, 0)])  6.96 us
  transfers between devices with their start and end apart: 20, of which 6 were waited for; matrix products, arithmetic and copies ran while one was open for 3% of the time, Pallas kernels for 21%

profile of v2, /device:TPU:2, one launch (start us, length us, event | category | flops | bytes accessed | tf_op | source)
XLA Modules:
  0.0 114.5 jit_solution(4930764565788958125)
XLA Ops:
  5.2 1.7 %collective-permute-start = (bf16[6,96,128]{2,1,0:T(8,128)(2,1)S(1)}, bf16[6,96,128]{2,1,0:T(8,128)(2,1)S(1)}, u32[]{:S(2)}, u32[]{:S(2)}) collective-permute-start(bf16[6,96,128]{2,1,0:T(8,128)(2,1)S(1)} %get-tuple-element.31), channel_id=1, source_target_pairs={{0,8},{8,0},{1,9},{9,1},{2,10},{10,2},{3,11},{11,3},{4,12},{12,4},... | collective-permute-start | bytes 442376 | tf_op jit(solution)/shard_map/ppermute | solution.py:464
  6.8 4.0 %collective-permute-done.recv_ref = bf16[6,96,128]{2,1,0:T(8,128)(2,1)S(1)} collective-permute-done((bf16[6,96,128]{2,1,0:T(8,128)(2,1)S(1)}, bf16[6,96,128]{2,1,0:T(8,128)(2,1)S(1)}, u32[]{:S(2)}, u32[]{:S(2)}) %collective-permute-start) | collective-permute-done | bytes 147488 | tf_op jit(solution)/shard_map/ppermute | solution.py:464
  11.4 5.9 %collective-permute-start.1 = (bf16[6,96,128]{2,1,0:T(8,128)(2,1)S(1)}, bf16[6,96,128]{2,1,0:T(8,128)(2,1)S(1)}, u32[]{:S(2)}, u32[]{:S(2)}) collective-permute-start(bf16[6,96,128]{2,1,0:T(8,128)(2,1)S(1)} %get-tuple-element.34.a_ref.refs_0_), channel_id=1, source_target_pairs={{0,7},{1,0},{2,1},{3,2},{4,3},{5,4},{6,5},{7,6},{8,15},{9,8},{10,9... | collective-permute-start | bytes 442376 | tf_op jit(solution)/shard_map/ppermute | solution.py:460
  17.3 1.6 %broadcast_in_dim.2 = bf16[8,2,96,96]{3,2,1,0:T(8,128)(2,1)} broadcast(bf16[2,96,96]{2,1,0:T(8,128)(2,1)} %param.9), dimensions={1,2,3} | broadcast | bytes 331776 | tf_op jit(solution)/shard_map/broadcast_in_dim | solution.py:473
  18.9 7.5 %all-to-all-start = ((bf16[16,96,96]{2,1,0:T(8,128)(2,1)}), bf16[16,96,96]{2,1,0:T(8,128)(2,1)S(1)}, u32[]{:S(2)}, u32[]{:S(2)}) async-start(bf16[16,96,96]{2,1,0:T(8,128)(2,1)} %bitcast), calls=%async_computation | async-start | bytes 786432 | tf_op jit(solution)/shard_map/all_to_all | solution.py:476
  26.4 3.2 %collective-permute-start.2 = (bf16[6,96,128]{2,1,0:T(8,128)(2,1)S(1)}, bf16[6,96,128]{2,1,0:T(8,128)(2,1)S(1)}, u32[]{:S(2)}, u32[]{:S(2)}) collective-permute-start(bf16[6,96,128]{2,1,0:T(8,128)(2,1)S(1)} %collective-permute-done.1.b_ref.refs_1_), channel_id=1, source_target_pairs={{0,7},{1,0},{2,1},{3,2},{4,3},{5,4},{6,5},{7,6},{8,15},{9,8},{10,9... | collective-permute-start | bytes 442376 | tf_op jit(solution)/shard_map/ppermute | solution.py:460
  29.6 4.0 %all-to-all-done = bf16[16,96,96]{2,1,0:T(8,128)(2,1)S(1)} async-done(((bf16[16,96,96]{2,1,0:T(8,128)(2,1)}), bf16[16,96,96]{2,1,0:T(8,128)(2,1)S(1)}, u32[]{:S(2)}, u32[]{:S(2)}) %all-to-all-start) | async-done | bytes 294944 | tf_op jit(solution)/shard_map/all_to_all | solution.py:476
  33.6 3.2 %collective-permute-start.3 = (bf16[6,96,128]{2,1,0:T(8,128)(2,1)S(1)}, bf16[6,96,128]{2,1,0:T(8,128)(2,1)S(1)}, u32[]{:S(2)}, u32[]{:S(2)}) collective-permute-start(bf16[6,96,128]{2,1,0:T(8,128)(2,1)S(1)} %collective-permute-done.2.a_ref.refs_2_), channel_id=1, source_target_pairs={{0,7},{1,0},{2,1},{3,2},{4,3},{5,4},{6,5},{7,6},{8,15},{9,8},{10,9... | collective-permute-start | bytes 442376 | tf_op jit(solution)/shard_map/ppermute | solution.py:460
  36.9 4.2 %collective-permute-done.6.b_ref.refs_5_ = bf16[6,96,128]{2,1,0:T(8,128)(2,1)S(1)} collective-permute-done((bf16[6,96,128]{2,1,0:T(8,128)(2,1)S(1)}, bf16[6,96,128]{2,1,0:T(8,128)(2,1)S(1)}, u32[]{:S(2)}, u32[]{:S(2)}) %collective-permute-start.6) | collective-permute-done | bytes 147488 | tf_op jit(solution)/shard_map/ppermute | solution.py:460
  41.1 3.2 %collective-permute-start.4 = (bf16[6,96,128]{2,1,0:T(8,128)(2,1)S(1)}, bf16[6,96,128]{2,1,0:T(8,128)(2,1)S(1)}, u32[]{:S(2)}, u32[]{:S(2)}) collective-permute-start(bf16[6,96,128]{2,1,0:T(8,128)(2,1)S(1)} %collective-permute-done.3.a_ref.refs_4_), channel_id=1, source_target_pairs={{0,7},{1,0},{2,1},{3,2},{4,3},{5,4},{6,5},{7,6},{8,15},{9,8},{10,9... | collective-permute-start | bytes 442376 | tf_op jit(solution)/shard_map/ppermute | solution.py:460
  45.3 3.1 %forward_0.1 = (f32[6,192,384]{2,1,0:T(8,128)S(1)}, f32[6,192,128]{2,1,0:T(8,128)S(1)}) custom-call(bf16[6,192,128]{2,1,0:T(8,128)(2,1)S(1)} %get-tuple-element.32.q_ref, bf16[6,96,128]{2,1,0:T(8,128)(2,1)S(1)} %get-tuple-element.34.a_ref.refs_0_, bf16[6,96,128]{2,1,0:T(8,128)(2,1)S(1)} %collective-permute-done.1.b_ref.refs_1_, ...), custom_call_target="tpu_custom_call" | custom-call | bytes 6000000 | tf_op jit(solution)/shard_map/forward_0/pallas_call | solution.py:250
  48.4 1.2 %copy-done = f32[6,192,384]{2,1,0:T(8,128)} copy-done((f32[6,192,384]{2,1,0:T(8,128)}, f32[6,192,384]{2,1,0:T(8,128)S(1)}, u32[]{:S(2)}) %copy-start) | copy-done | bytes 1769496
  49.6 4.2 %forward_1.1 = (f32[6,192,384]{2,1,0:T(8,128)S(1)}, f32[6,192,128]{2,1,0:T(8,128)S(1)}) custom-call(bf16[6,192,128]{2,1,0:T(8,128)(2,1)S(1)} %get-tuple-element.32.q_ref, bf16[6,96,128]{2,1,0:T(8,128)(2,1)S(1)} %collective-permute-done.2.a_ref.refs_2_, bf16[6,96,128]{2,1,0:T(8,128)(2,1)S(1)} %collective-permute-done.5.b_ref.refs_3_, ...), custom_call_target="tpu_custom_call" | custom-call | bytes 6000000 | tf_op jit(solution)/shard_map/forward_1/pallas_call | solution.py:250
  55.0 4.2 %forward_2.1 = (f32[6,192,384]{2,1,0:T(8,128)S(1)}, f32[6,192,128]{2,1,0:T(8,128)S(1)}) custom-call(bf16[6,192,128]{2,1,0:T(8,128)(2,1)S(1)} %get-tuple-element.32.q_ref, bf16[6,96,128]{2,1,0:T(8,128)(2,1)S(1)} %collective-permute-done.3.a_ref.refs_4_, bf16[6,96,128]{2,1,0:T(8,128)(2,1)S(1)} %collective-permute-done.6.b_ref.refs_5_, ...), custom_call_target="tpu_custom_call" | custom-call | bytes 6000000 | tf_op jit(solution)/shard_map/forward_2/pallas_call | solution.py:250
  60.4 9.1 %turn.1 = (f32[6,192,128]{2,1,0:T(8,128)S(1)}, bf16[6,96,128]{2,1,0:T(8,128)(2,1)S(1)}, bf16[6,96,128]{2,1,0:T(8,128)(2,1)S(1)}, f32[192,384]{1,0:T(8,128)S(1)}) custom-call(bf16[6,192,128]{2,1,0:T(8,128)(2,1)S(1)} %get-tuple-element.32.q_ref, bf16[6,192,128]{2,1,0:T(8,128)(2,1)S(1)} %get-tuple-element.33.da_ref, ...), custom_call_target="tpu_custom_call" | custom-call | bytes 12000000 | tf_op jit(solution)/shard_map/turn/pallas_call | solution.py:304
  69.6 3.2 %collective-permute-start.13 = (bf16[6,96,128]{2,1,0:T(8,128)(2,1)S(1)}, bf16[6,96,128]{2,1,0:T(8,128)(2,1)S(1)}, u32[]{:S(2)}, u32[]{:S(2)}) collective-permute-start(bf16[6,96,128]{2,1,0:T(8,128)(2,1)S(1)} %get-tuple-element.49), channel_id=1, source_target_pairs={{0,7},{1,0},{2,1},{3,2},{4,3},{5,4},{6,5},{7,6},{8,15},{9,8},{10,9... | collective-permute-start | bytes 442376 | tf_op jit(solution)/shard_map/ppermute | solution.py:460
  72.9 10.5 %backward.1 = (f32[2,6,96,128]{3,2,1,0:T(8,128)S(1)}, bf16[6,96,128]{2,1,0:T(8,128)(2,1)S(1)}, bf16[6,96,128]{2,1,0:T(8,128)(2,1)S(1)}, bf16[6,96,128]{2,1,0:T(8...) custom-call(bf16[6,192,128]{2,1,0:T(8,128)(2,1)S(1)} %get-tuple-elem, ...), custom_call_target="tpu_custom_call" | custom-call | bytes 18000000 | tf_op jit(solution)/shard_map/backward/pallas_call | solution.py:374
  83.6 3.3 %collective-permute-start.14 = (bf16[6,96,128]{2,1,0:T(8,128)(2,1)S(1)}, bf16[6,96,128]{2,1,0:T(8,128)(2,1)S(1)}, u32[]{:S(2)}, u32[]{:S(2)}) collective-permute-start(bf16[6,96,128]{2,1,0:T(8,128)(2,1)S(1)} %add_convert_fusion.2), channel_id=1, source_target_pairs={{0,7},{1,0},{2,1},{3,2},{4,3},{5,4},{6,5},{7,6},{8,15},{9,8},{10,9... | collective-permute-start | bytes 442376 | tf_op jit(solution)/shard_map/ppermute | solution.py:460
  86.9 4.1 %collective-permute-done.10 = bf16[6,96,128]{2,1,0:T(8,128)(2,1)S(1)} collective-permute-done((bf16[6,96,128]{2,1,0:T(8,128)(2,1)S(1)}, bf16[6,96,128]{2,1,0:T(8,128)(2,1)S(1)}, u32[]{:S(2)}, u32[]{:S(2)}) %collective-permute-start.10) | collective-permute-done | bytes 147488 | tf_op jit(solution)/shard_map/ppermute | solution.py:460
  91.2 3.3 %collective-permute-start.15 = (bf16[6,96,128]{2,1,0:T(8,128)(2,1)S(1)}, bf16[6,96,128]{2,1,0:T(8,128)(2,1)S(1)}, u32[]{:S(2)}, u32[]{:S(2)}) collective-permute-start(bf16[6,96,128]{2,1,0:T(8,128)(2,1)S(1)} %add_convert_fusion.1), channel_id=1, source_target_pairs={{0,7},{1,0},{2,1},{3,2},{4,3},{5,4},{6,5},{7,6},{8,15},{9,8},{10,9... | collective-permute-start | bytes 442376 | tf_op jit(solution)/shard_map/ppermute | solution.py:460
  95.3 5.7 %all-to-all-start.1 = ((bf16[16,96,96]{2,1,0:T(8,128)(2,1)}), bf16[16,96,96]{2,1,0:T(8,128)(2,1)S(1)}, u32[]{:S(2)}, u32[]{:S(2)}) async-start(bf16[16,96,96]{2,1,0:T(8,128)(2,1)} %bitcast.3), calls=%async_computation.1 | async-start | bytes 786432 | tf_op jit(solution)/shard_map/all_to_all | solution.py:503
  101.2 6.3 %collective-permute-done.12.b_ref = bf16[6,96,128]{2,1,0:T(8,128)(2,1)S(1)} collective-permute-done((bf16[6,96,128]{2,1,0:T(8,128)(2,1)S(1)}, bf16[6,96,128]{2,1,0:T(8,128)(2,1)S(1)}, u32[]{:S(2)}, u32[]{:S(2)}) %collective-permute-start.12) | collective-permute-done | bytes 147488 | tf_op jit(solution)/shard_map/ppermute | solution.py:460
  108.2 1.6 %collective-permute-start.16 = (bf16[6,96,128]{2,1,0:T(8,128)(2,1)S(1)}, bf16[6,96,128]{2,1,0:T(8,128)(2,1)S(1)}, u32[]{:S(2)}, u32[]{:S(2)}) collective-permute-start(bf16[6,96,128]{2,1,0:T(8,128)(2,1)S(1)} %get-tuple-element.53), channel_id=1, source_target_pairs={{0,8},{8,0},{1,9},{9,1},{2,10},{10,2},{3,11},{11,3},{4,12},{12,4},... | collective-permute-start | bytes 442376 | tf_op jit(solution)/shard_map/ppermute | solution.py:464
  110.5 2.9 %collective-permute-done.16.recv_ref = bf16[6,96,128]{2,1,0:T(8,128)(2,1)S(1)} collective-permute-done((bf16[6,96,128]{2,1,0:T(8,128)(2,1)S(1)}, bf16[6,96,128]{2,1,0:T(8,128)(2,1)S(1)}, u32[]{:S(2)}, u32[]{:S(2)}) %collective-permute-start.16) | collective-permute-done | bytes 147488 | tf_op jit(solution)/shard_map/ppermute | solution.py:464
  (52 shorter events, 12.3 us)
Async XLA Ops:
  4.0 40.3 %copy-start.8 = (s32[8]{0:T(128)S(1)}, s32[8]{0:T(128)}, u32[]{:S(2)}) copy-start(s32[8]{0:T(128)} %len_ref.1) | copy-start | bytes 100
  5.2 5.7 %collective-permute-start = (bf16[6,96,128]{2,1,0:T(8,128)(2,1)S(1)}, bf16[6,96,128]{2,1,0:T(8,128)(2,1)S(1)}, u32[]{:S(2)}, u32[]{:S(2)}) collective-permute-start(bf16[6,96,128]{2,1,0:T(8,128)(2,1)S(1)} %get-tuple-element.31), channel_id=1, source_target_pairs={{0,8},{8,0},{1,9},{9,1},{2,10},{10,2},{3,11},{11,3},{4,12},{12,4},... | collective-permute-start | bytes 442376 | tf_op jit(solution)/shard_map/ppermute | solution.py:464
  11.4 15.0 %collective-permute-start.1 = (bf16[6,96,128]{2,1,0:T(8,128)(2,1)S(1)}, bf16[6,96,128]{2,1,0:T(8,128)(2,1)S(1)}, u32[]{:S(2)}, u32[]{:S(2)}) collective-permute-start(bf16[6,96,128]{2,1,0:T(8,128)(2,1)S(1)} %get-tuple-element.34.a_ref.refs_0_), channel_id=1, source_target_pairs={{0,7},{1,0},{2,1},{3,2},{4,3},{5,4},{6,5},{7,6},{8,15},{9,8},{10,9... | collective-permute-start | bytes 442376 | tf_op jit(solution)/shard_map/ppermute | solution.py:460
  18.9 14.7 %all-to-all-start = ((bf16[16,96,96]{2,1,0:T(8,128)(2,1)}), bf16[16,96,96]{2,1,0:T(8,128)(2,1)S(1)}, u32[]{:S(2)}, u32[]{:S(2)}) async-start(bf16[16,96,96]{2,1,0:T(8,128)(2,1)} %bitcast), calls=%async_computation | async-start | bytes 786432 | tf_op jit(solution)/shard_map/all_to_all | solution.py:476
  26.4 7.2 %collective-permute-start.5 = (bf16[6,96,128]{2,1,0:T(8,128)(2,1)S(1)}, bf16[6,96,128]{2,1,0:T(8,128)(2,1)S(1)}, u32[]{:S(2)}, u32[]{:S(2)}) collective-permute-start(bf16[6,96,128]{2,1,0:T(8,128)(2,1)S(1)} %get-tuple-element.34.a_ref.refs_0_), channel_id=1, source_target_pairs={{0,1},{1,2},{2,3},{3,4},{4,5},{5,6},{6,7},{7,0},{8,9},{9,10},{10,1... | collective-permute-start | bytes 442376 | tf_op jit(solution)/shard_map/ppermute | solution.py:460
  26.4 7.2 %collective-permute-start.2 = (bf16[6,96,128]{2,1,0:T(8,128)(2,1)S(1)}, bf16[6,96,128]{2,1,0:T(8,128)(2,1)S(1)}, u32[]{:S(2)}, u32[]{:S(2)}) collective-permute-start(bf16[6,96,128]{2,1,0:T(8,128)(2,1)S(1)} %collective-permute-done.1.b_ref.refs_1_), channel_id=1, source_target_pairs={{0,7},{1,0},{2,1},{3,2},{4,3},{5,4},{6,5},{7,6},{8,15},{9,8},{10,9... | collective-permute-start | bytes 442376 | tf_op jit(solution)/shard_map/ppermute | solution.py:460
  33.6 10.7 %collective-permute-start.8 = (bf16[16,96,96]{2,1,0:T(8,128)(2,1)S(1)}, bf16[16,96,96]{2,1,0:T(8,128)(2,1)S(1)}, u32[]{:S(2)}, u32[]{:S(2)}) collective-permute-start(bf16[16,96,96]{2,1,0:T(8,128)(2,1)S(1)} %all-to-all-done), channel_id=1, source_target_pairs={{0,16},{16,0},{1,17},{17,1},{2,18},{18,2},{3,19},{19,3},{4,20},{20... | collective-permute-start | bytes 884744 | tf_op jit(solution)/shard_map/ppermute | solution.py:464
  33.6 7.5 %collective-permute-start.6 = (bf16[6,96,128]{2,1,0:T(8,128)(2,1)S(1)}, bf16[6,96,128]{2,1,0:T(8,128)(2,1)S(1)}, u32[]{:S(2)}, u32[]{:S(2)}) collective-permute-start(bf16[6,96,128]{2,1,0:T(8,128)(2,1)S(1)} %collective-permute-done.5.b_ref.refs_3_), channel_id=1, source_target_pairs={{0,1},{1,2},{2,3},{3,4},{4,5},{5,6},{6,7},{7,0},{8,9},{9,10},{10,1... | collective-permute-start | bytes 442376 | tf_op jit(solution)/shard_map/ppermute | solution.py:460
  33.6 7.5 %collective-permute-start.3 = (bf16[6,96,128]{2,1,0:T(8,128)(2,1)S(1)}, bf16[6,96,128]{2,1,0:T(8,128)(2,1)S(1)}, u32[]{:S(2)}, u32[]{:S(2)}) collective-permute-start(bf16[6,96,128]{2,1,0:T(8,128)(2,1)S(1)} %collective-permute-done.2.a_ref.refs_2_), channel_id=1, source_target_pairs={{0,7},{1,0},{2,1},{3,2},{4,3},{5,4},{6,5},{7,6},{8,15},{9,8},{10,9... | collective-permute-start | bytes 442376 | tf_op jit(solution)/shard_map/ppermute | solution.py:460
  41.1 19.3 %collective-permute-start.7 = (bf16[6,96,128]{2,1,0:T(8,128)(2,1)S(1)}, bf16[6,96,128]{2,1,0:T(8,128)(2,1)S(1)}, u32[]{:S(2)}, u32[]{:S(2)}) collective-permute-start(bf16[6,96,128]{2,1,0:T(8,128)(2,1)S(1)} %collective-permute-done.6.b_ref.refs_5_), channel_id=1, source_target_pairs={{0,1},{1,2},{2,3},{3,4},{4,5},{5,6},{6,7},{7,0},{8,9},{9,10},{10,1... | collective-permute-start | bytes 442376 | tf_op jit(solution)/shard_map/ppermute | solution.py:460
  41.1 19.3 %collective-permute-start.4 = (bf16[6,96,128]{2,1,0:T(8,128)(2,1)S(1)}, bf16[6,96,128]{2,1,0:T(8,128)(2,1)S(1)}, u32[]{:S(2)}, u32[]{:S(2)}) collective-permute-start(bf16[6,96,128]{2,1,0:T(8,128)(2,1)S(1)} %collective-permute-done.3.a_ref.refs_4_), channel_id=1, source_target_pairs={{0,7},{1,0},{2,1},{3,2},{4,3},{5,4},{6,5},{7,6},{8,15},{9,8},{10,9... | collective-permute-start | bytes 442376 | tf_op jit(solution)/shard_map/ppermute | solution.py:460
  48.4 1.2 %copy-start = (f32[6,192,384]{2,1,0:T(8,128)}, f32[6,192,384]{2,1,0:T(8,128)S(1)}, u32[]{:S(2)}) copy-start(f32[6,192,384]{2,1,0:T(8,128)S(1)} %get-tuple-element.40.refs_6_) | copy-start | bytes 5308420
  59.2 1.2 %copy-start.2 = (f32[6,192,384]{2,1,0:T(8,128)}, f32[6,192,384]{2,1,0:T(8,128)S(1)}, u32[]{:S(2)}) copy-start(f32[6,192,384]{2,1,0:T(8,128)S(1)} %get-tuple-element.42.refs_8_) | copy-start | bytes 5308420
  69.5 13.9 %collective-permute-start.9 = (bf16[6,96,128]{2,1,0:T(8,128)(2,1)S(1)}, bf16[6,96,128]{2,1,0:T(8,128)(2,1)S(1)}, u32[]{:S(2)}, u32[]{:S(2)}) collective-permute-start(bf16[6,96,128]{2,1,0:T(8,128)(2,1)S(1)} %get-tuple-element.45), channel_id=1, source_target_pairs={{0,1},{1,2},{2,3},{3,4},{4,5},{5,6},{6,7},{7,0},{8,9},{9,10},{10,1... | collective-permute-start | bytes 442376 | tf_op jit(solution)/shard_map/ppermute | solution.py:460
  69.6 14.0 %collective-permute-start.13 = (bf16[6,96,128]{2,1,0:T(8,128)(2,1)S(1)}, bf16[6,96,128]{2,1,0:T(8,128)(2,1)S(1)}, u32[]{:S(2)}, u32[]{:S(2)}) collective-permute-start(bf16[6,96,128]{2,1,0:T(8,128)(2,1)S(1)} %get-tuple-element.49), channel_id=1, source_target_pairs={{0,7},{1,0},{2,1},{3,2},{4,3},{5,4},{6,5},{7,6},{8,15},{9,8},{10,9... | collective-permute-start | bytes 442376 | tf_op jit(solution)/shard_map/ppermute | solution.py:460
  83.3 11.2 %collective-permute-start.17 = (bf16[2,4,2,96,96]{4,3,2,1,0:T(8,128)(2,1)S(1)}, bf16[2,4,2,96,96]{4,3,2,1,0:T(8,128)(2,1)S(1)}, u32[]{:S(2)}, u32[]{:S(2)}) collective-permute-start(bf16[2,4,2,96,96]{4,3,2,1,0:T(8,128)(2,1)S(1)} %get-tuple-element.57), channel_id=1, source_target_pairs={{0,16},{16,0},{1,17},{17,1},{2,18},{18,2},{3,19},{19,3},{4,20},{20... | collective-permute-start | bytes 884744 | tf_op jit(solution)/shard_map/ppermute | solution.py:464
  83.5 7.5 %collective-permute-start.10 = (bf16[6,96,128]{2,1,0:T(8,128)(2,1)S(1)}, bf16[6,96,128]{2,1,0:T(8,128)(2,1)S(1)}, u32[]{:S(2)}, u32[]{:S(2)}) collective-permute-start(bf16[6,96,128]{2,1,0:T(8,128)(2,1)S(1)} %add_convert_fusion.5), channel_id=1, source_target_pairs={{0,1},{1,2},{2,3},{3,4},{4,5},{5,6},{6,7},{7,0},{8,9},{9,10},{10,1... | collective-permute-start | bytes 442376 | tf_op jit(solution)/shard_map/ppermute | solution.py:460
  83.6 7.5 %collective-permute-start.14 = (bf16[6,96,128]{2,1,0:T(8,128)(2,1)S(1)}, bf16[6,96,128]{2,1,0:T(8,128)(2,1)S(1)}, u32[]{:S(2)}, u32[]{:S(2)}) collective-permute-start(bf16[6,96,128]{2,1,0:T(8,128)(2,1)S(1)} %add_convert_fusion.2), channel_id=1, source_target_pairs={{0,7},{1,0},{2,1},{3,2},{4,3},{5,4},{6,5},{7,6},{8,15},{9,8},{10,9... | collective-permute-start | bytes 442376 | tf_op jit(solution)/shard_map/ppermute | solution.py:460
  91.1 10.0 %collective-permute-start.11 = (bf16[6,96,128]{2,1,0:T(8,128)(2,1)S(1)}, bf16[6,96,128]{2,1,0:T(8,128)(2,1)S(1)}, u32[]{:S(2)}, u32[]{:S(2)}) collective-permute-start(bf16[6,96,128]{2,1,0:T(8,128)(2,1)S(1)} %add_convert_fusion.4), channel_id=1, source_target_pairs={{0,1},{1,2},{2,3},{3,4},{4,5},{5,6},{6,7},{7,0},{8,9},{9,10},{10,1... | collective-permute-start | bytes 442376 | tf_op jit(solution)/shard_map/ppermute | solution.py:460
  91.2 10.0 %collective-permute-start.15 = (bf16[6,96,128]{2,1,0:T(8,128)(2,1)S(1)}, bf16[6,96,128]{2,1,0:T(8,128)(2,1)S(1)}, u32[]{:S(2)}, u32[]{:S(2)}) collective-permute-start(bf16[6,96,128]{2,1,0:T(8,128)(2,1)S(1)} %add_convert_fusion.1), channel_id=1, source_target_pairs={{0,7},{1,0},{2,1},{3,2},{4,3},{5,4},{6,5},{7,6},{8,15},{9,8},{10,9... | collective-permute-start | bytes 442376 | tf_op jit(solution)/shard_map/ppermute | solution.py:460
  95.3 18.1 %copy-start.4 = (bf16[128,256]{1,0:T(8,128)(2,1)S(1)}, bf16[128,256]{1,0:T(8,128)(2,1)}, u32[]{:S(2)}) copy-start(bf16[128,256]{1,0:T(8,128)(2,1)} %w_ref.1) | copy-start | bytes 196612
  95.3 14.4 %all-to-all-start.1 = ((bf16[16,96,96]{2,1,0:T(8,128)(2,1)}), bf16[16,96,96]{2,1,0:T(8,128)(2,1)S(1)}, u32[]{:S(2)}, u32[]{:S(2)}) async-start(bf16[16,96,96]{2,1,0:T(8,128)(2,1)} %bitcast.3), calls=%async_computation.1 | async-start | bytes 786432 | tf_op jit(solution)/shard_map/all_to_all | solution.py:503
  101.1 6.4 %collective-permute-start.12 = (bf16[6,96,128]{2,1,0:T(8,128)(2,1)S(1)}, bf16[6,96,128]{2,1,0:T(8,128)(2,1)S(1)}, u32[]{:S(2)}, u32[]{:S(2)}) collective-permute-start(bf16[6,96,128]{2,1,0:T(8,128)(2,1)S(1)} %add_convert_fusion.3), channel_id=1, source_target_pairs={{0,1},{1,2},{2,3},{3,4},{4,5},{5,6},{6,7},{7,0},{8,9},{9,10},{10,1... | collective-permute-start | bytes 442376 | tf_op jit(solution)/shard_map/ppermute | solution.py:460
  108.2 5.2 %collective-permute-start.16 = (bf16[6,96,128]{2,1,0:T(8,128)(2,1)S(1)}, bf16[6,96,128]{2,1,0:T(8,128)(2,1)S(1)}, u32[]{:S(2)}, u32[]{:S(2)}) collective-permute-start(bf16[6,96,128]{2,1,0:T(8,128)(2,1)S(1)} %get-tuple-element.53), channel_id=1, source_target_pairs={{0,8},{8,0},{1,9},{9,1},{2,10},{10,2},{3,11},{11,3},{4,12},{12,4},... | collective-permute-start | bytes 442376 | tf_op jit(solution)/shard_map/ppermute | solution.py:464
  (5 other events, 4.6 us)

commit v3 on v2

v3 whole, which is shorter than its diff:
```python
import functools
import math

import jax
import jax.numpy as jnp
from jax import lax
from jax.experimental import pallas as pl
from jax.experimental.pallas import tpu as pltpu
from jax.sharding import Mesh, PartitionSpec as P

H = 2
DH = 32
CHAINS = 8
SCALE = 1.0 / math.sqrt(DH)
MASKED_SCORE = -1e30
F32 = jnp.float32
BF16 = jnp.bfloat16

ROWS = 6
COLS = 96
RING = 8
HALF = RING * COLS
KEYS = 2 * HALF
WIDE = 128
EARLY = (0, 1, 7, 2, 6, 3)
LATE = (4, 5)
NE, NL = len(EARLY) * COLS, len(LATE) * COLS
SLOT = KEYS // CHAINS

NT = (((1,), (1,)), ((), ()))
NN = (((1,), (0,)), ((), ()))
TN = (((0,), (0,)), ((), ()))


def mm(a, b, dims):
    return lax.dot_general(a, b, dims, preferred_element_type=F32)


def params(limit=32 << 20):
    return pltpu.CompilerParams(vmem_limit_bytes=limit)


def cost(us):
    return pl.CostEstimate(flops=0, bytes_accessed=int(us * 3e6), transcendentals=0)


def lanes(shape):
    return lax.broadcasted_iota(jnp.int32, shape, len(shape) - 1)


def head_weight(w, h):
    parts = [w[:, (part * H + h) * DH : (part * H + h + 1) * DH] for part in (1, 2, 0, 3)]
    return jnp.concatenate(parts, axis=1)


def project_kernel(
    pair_hbm, grad_hbm, w_hbm, wout_hbm, mine_ref, other_ref, gmine_ref, gother_ref,
    pair_s, grad_s, w_s, wout_s, sem,
):
    yl = lax.axis_index("yl")
    pairs = ((w_hbm, w_s), (wout_hbm, wout_s), (pair_hbm, pair_s), (grad_hbm, grad_s))
    copies = [pltpu.make_async_copy(a, b, sem.at[n]) for n, (a, b) in enumerate(pairs)]
    for copy in copies:
        copy.start()
    for copy in copies:
        copy.wait()
    pair = pair_s[...].reshape(ROWS * COLS, WIDE)
    grad = grad_s[...].reshape(ROWS * COLS, WIDE)
    w = w_s[...]
    wout = wout_s[...]
    lane = lanes((ROWS * COLS, WIDE))
    for h in range(H):
        proj = mm(pair, head_weight(w, h), NN)
        rows = jnp.concatenate(
            [jnp.zeros((WIDE - DH, WIDE), BF16), wout[h * DH : (h + 1) * DH]], axis=0
        )
        d_out = mm(grad, rows, NT)
        gate = jax.nn.sigmoid(proj)
        payload = jnp.where(
            lane < 2 * DH, proj, jnp.where(lane < 3 * DH, proj * SCALE, d_out * gate)
        )
        payload = payload.astype(BF16).reshape(ROWS, COLS, WIDE)
        g = (d_out * gate * (1.0 - gate)).reshape(ROWS, COLS, WIDE)

        @pl.when(yl == h)
        def _():
            mine_ref[...] = payload
            gmine_ref[...] = g

        @pl.when(yl != h)
        def _():
            other_ref[...] = payload
            gother_ref[...] = g


def project(pair, grad, w, wout):
    shape = (ROWS, COLS, WIDE)
    return pl.pallas_call(
        project_kernel,
        in_specs=[pl.BlockSpec(memory_space=pltpu.HBM)] * 4,
        out_shape=[
            jax.ShapeDtypeStruct(shape, BF16),
            jax.ShapeDtypeStruct(shape, BF16),
            jax.ShapeDtypeStruct(shape, F32),
            jax.ShapeDtypeStruct(shape, F32),
        ],
        scratch_shapes=[
            pltpu.VMEM(shape, BF16),
            pltpu.VMEM(shape, BF16),
            pltpu.VMEM(w.shape, BF16),
            pltpu.VMEM(wout.shape, BF16),
            pltpu.SemaphoreType.DMA((4,)),
        ],
        compiler_params=params(60 << 20),
        cost_estimate=cost(2.0),
        name="project",
    )(pair, grad, w, wout)


def pack_kernel(mine_ref, recv_ref, kv_ref, q_ref, da_ref, qt_ref, dat_ref):
    yl = lax.axis_index("yl")
    lane = lanes((COLS, WIDE))

    def write(i, a, b):
        a, b = a.astype(F32), b.astype(F32)
        kv_ref[i] = jnp.where(lane < 2 * DH, a, pltpu.roll(b, 2 * DH, 1)).astype(BF16)
        for part, x in enumerate((a, b)):
            y = pltpu.roll(x, 2 * DH, 1)
            rows = slice(part * COLS, (part + 1) * COLS)
            q_ref[i, rows] = jnp.where(lane < DH, y, 0.0).astype(BF16)
            da_ref[i, rows] = jnp.where((lane >= DH) & (lane < 2 * DH), y, 0.0).astype(BF16)
        turned = jnp.concatenate([a, b], axis=0).T
        qt_ref[i] = turned[2 * DH : 3 * DH].astype(BF16)
        dat_ref[i] = turned[3 * DH :].astype(BF16)

    for i in range(ROWS):

        @pl.when(yl == 0)
        def _():
            write(i, mine_ref[i], recv_ref[i])

        @pl.when(yl != 0)
        def _():
            write(i, recv_ref[i], mine_ref[i])


BLOCK = jax.ShapeDtypeStruct((ROWS, COLS, WIDE), BF16)
STATE = jax.ShapeDtypeStruct((ROWS, 2 * COLS, WIDE), F32)


def pack(mine, recv):
    both = jax.ShapeDtypeStruct((ROWS, 2 * COLS, WIDE), BF16)
    turned = jax.ShapeDtypeStruct((ROWS, DH, 2 * COLS), BF16)
    return pl.pallas_call(
        pack_kernel,
        out_shape=[BLOCK, both, both, turned, turned],
        compiler_params=params(),
        cost_estimate=cost(0.6),
        name="pack",
    )(mine, recv)


def bias_kernel(len_ref, own_ref, oth_ref, early_ref, late_ref):
    core = lax.axis_index("core")
    z = lax.axis_index("z")
    lane = lanes((1, COLS))
    for order, out_ref in ((EARLY, early_ref), (LATE, late_ref)):
        for n, r in enumerate(order):
            at = lax.rem(z + r, RING)
            x, odd = at // 2, lax.rem(at, 2)
            for yh in range(2):
                start = (yh * len(order) + n) * COLS
                valid = lane + odd * COLS < len_ref[yh * 4 + x]
                lift = jnp.where(valid, 0.0, MASKED_SCORE)
                for yl in range(2):
                    rows = slice(yl * COLS, (yl + 1) * COLS)
                    both = jnp.where(odd == core, own_ref[yh, x, yl], oth_ref[yh, x, yl])
                    out_ref[rows, start : start + COLS] = both.astype(F32) + lift


def bias_tables(chain_lengths, own, oth):
    return pl.pallas_call(
        bias_kernel,
        out_shape=[
            jax.ShapeDtypeStruct((2 * COLS, 2 * NE), F32),
            jax.ShapeDtypeStruct((2 * COLS, 2 * NL), F32),
        ],
        in_specs=[
            pl.BlockSpec(memory_space=pltpu.SMEM),
            pl.BlockSpec(memory_space=pltpu.VMEM),
            pl.BlockSpec(memory_space=pltpu.VMEM),
        ],
        compiler_params=params(),
        cost_estimate=cost(1.5),
        name="bias_tables",
    )(chain_lengths, own, oth)


def stack(refs, i):
    one = jnp.concatenate([ref[i] for ref in refs], axis=0)
    moved = pltpu.roll(one.astype(F32), 2 * DH, 1).astype(BF16)
    return jnp.concatenate([one, moved], axis=0)


def key_gradients(qt, dat, low, p_low, dkv_refs, i):
    dk = mm(qt, low, NN)
    dv = mm(dat, p_low, NN)
    half = dk.shape[1] // 2
    dkv = jnp.concatenate([dk[:, :half], dv[:, :half], dk[:, half:], dv[:, half:]], axis=0).T
    for n, ref in enumerate(dkv_refs):
        ref[i] = dkv[n * COLS : (n + 1) * COLS].astype(BF16)


def early_kernel(q_ref, bias_ref, *refs):
    n = len(EARLY)
    kv_refs, (e_ref, state_ref) = refs[:n], refs[n:]
    lane = lanes((2 * COLS, WIDE))
    for i in range(ROWS):
        kv = stack(kv_refs, i)
        s = mm(q_ref[i], kv, NT) + bias_ref[...]
        top = jnp.max(s, axis=1, keepdims=True)
        e = jnp.exp(s - top)
        total = jnp.sum(e, axis=1, keepdims=True)
        low = e.astype(BF16)
        e_ref[i] = low
        acc = mm(low, kv, NN)
        acc = jnp.where(lane < 2 * DH, acc, jnp.where(lane == 2 * DH, total, top))
        state_ref[i] = acc


def early(q, bias, kvs):
    return pl.pallas_call(
        early_kernel,
        out_shape=[jax.ShapeDtypeStruct((ROWS, 2 * COLS, 2 * NE), BF16), STATE],
        compiler_params=params(),
        cost_estimate=cost(4.0),
        name="early",
    )(q, bias, *[kvs[r] for r in EARLY])


def turn_kernel(q_ref, da_ref, qt_ref, dat_ref, bias_ref, state_ref, *refs):
    n = len(LATE)
    kv_refs, out_ref, dkv_refs, table_ref = refs[:n], refs[n], refs[n + 1 : 2 * n + 1], refs[-1]
    lane = lanes((2 * COLS, WIDE))
    for i in range(ROWS):
        q, da, state = q_ref[i], da_ref[i], state_ref[i]
        kv = stack(kv_refs, i)
        s = mm(q, kv, NT) + bias_ref[...]
        old = state[:, 2 * DH + 1 : 2 * DH + 2]
        top = jnp.maximum(jnp.max(s, axis=1, keepdims=True), old)
        fade = jnp.exp(old - top)
        e = jnp.exp(s - top)
        total = jnp.sum(e, axis=1, keepdims=True) + state[:, 2 * DH : 2 * DH + 1] * fade
        inverse = 1.0 / total
        factor = fade * inverse
        p = e * inverse
        p_low = p.astype(BF16)
        acc = mm(p_low, kv, NN) + state * factor
        dot = jnp.sum(jnp.where(lane < 2 * DH, acc * da.astype(F32), 0.0), axis=1, keepdims=True)
        d = p * (mm(da, kv, NT) - dot)
        if i == 0:
            table_ref[...] = d
        else:
            table_ref[...] += d
        low = d.astype(BF16)
        dq = mm(low, kv, NN)
        key_gradients(qt_ref[i], dat_ref[i], low, p_low, dkv_refs, i)
        out = jnp.where(lane < DH, dq, acc)
        out_ref[i] = jnp.where(
            lane < 2 * DH, out, jnp.where(lane == 2 * DH, dot, factor)
        )


def turn(q, da, qt, dat, bias, state, kvs):
    return pl.pallas_call(
        turn_kernel,
        out_shape=[STATE]
        + [BLOCK] * len(LATE)
        + [jax.ShapeDtypeStruct((2 * COLS, 2 * NL), F32)],
        compiler_params=params(),
        cost_estimate=cost(4.0),
        name="turn",
    )(q, da, qt, dat, bias, state, *[kvs[r] for r in LATE])


def backward_kernel(q_ref, da_ref, qt_ref, dat_ref, state_ref, e_ref, late_ref, *refs):
    n = len(EARLY)
    kv_refs, u_ref, dkv_refs = refs[:n], refs[n], refs[n + 1 : 2 * n + 1]
    keep_ref, send_ref, table_ref = refs[2 * n + 1 :]
    lane = lanes((2 * COLS, WIDE))
    for i in range(ROWS):
        da, state = da_ref[i], state_ref[i]
        dot = state[:, 2 * DH : 2 * DH + 1]
        factor = state[:, 2 * DH + 1 : 2 * DH + 2]
        kv = stack(kv_refs, i)
        p = e_ref[i].astype(F32) * factor
        d = p * (mm(da, kv, NT) - dot)
        if i == 0:
            table_ref[...] = d
        else:
            table_ref[...] += d
        low = d.astype(BF16)
        u = jnp.where(lane < DH, (state + mm(low, kv, NN)) * SCALE, state)
        u_ref[0, i] = u[:COLS]
        u_ref[1, i] = u[COLS:]
        key_gradients(qt_ref[i], dat_ref[i], low, p.astype(BF16), dkv_refs, i)
    core = lax.axis_index("core")
    z = lax.axis_index("z")
    for order, table in ((EARLY, table_ref), (LATE, late_ref)):
        for m, r in enumerate(order):
            at = lax.rem(z + r, RING)
            x, odd = at // 2, lax.rem(at, 2)
            for yh in range(2):
                start = (yh * len(order) + m) * COLS
                for yl in range(2):
                    piece = table[yl * COLS : (yl + 1) * COLS, start : start + COLS]

                    @pl.when(odd == core)
                    def _():
                        keep_ref[yh, x, yl] = piece

                    @pl.when(odd != core)
                    def _():
                        send_ref[yh, x, yl] = piece.astype(BF16)


def backward(q, da, qt, dat, state, e, late, kvs):
    n = len(EARLY)
    blocks = (2, 4, 2, COLS, COLS)
    out = pl.pallas_call(
        backward_kernel,
        out_shape=[jax.ShapeDtypeStruct((2, ROWS, COLS, WIDE), F32)]
        + [BLOCK] * n
        + [jax.ShapeDtypeStruct(blocks, F32), jax.ShapeDtypeStruct(blocks, BF16)],
        scratch_shapes=[pltpu.VMEM((2 * COLS, 2 * NE), F32)],
        compiler_params=params(),
        cost_estimate=cost(5.0),
        name="backward",
    )(q, da, qt, dat, state, e, late, *[kvs[r] for r in EARLY])
    return out[0], dict(zip(EARLY, out[1 : n + 1])), out[-2], out[-1]


def finish_kernel(u_ref, a_ref, b_ref, c_ref, keep_ref, send_ref):
    yl = lax.axis_index("yl")
    lane = lanes((COLS, WIDE))
    for i in range(ROWS):
        dkv = a_ref[i].astype(F32) + b_ref[i].astype(F32) + c_ref[i].astype(F32)
        first = jnp.where(lane < 2 * DH, dkv, pltpu.roll(u_ref[0, i], 2 * DH, 1))
        second = jnp.where(
            lane < 2 * DH, pltpu.roll(dkv, 2 * DH, 1), pltpu.roll(u_ref[1, i], 2 * DH, 1)
        )

        @pl.when(yl == 0)
        def _():
            keep_ref[i] = first
            send_ref[i] = second.astype(BF16)

        @pl.when(yl != 0)
        def _():
            keep_ref[i] = second
            send_ref[i] = first.astype(BF16)


def finish(u, a, b, c):
    shape = (ROWS, COLS, WIDE)
    return pl.pallas_call(
        finish_kernel,
        out_shape=[jax.ShapeDtypeStruct(shape, F32), jax.ShapeDtypeStruct(shape, BF16)],
        compiler_params=params(),
        name="finish",
    )(u, a, b, c)


def output_kernel(keep_ref, recv_ref, gmine_ref, gother_ref, w_ref, out_ref):
    yl = lax.axis_index("yl")
    flat = (ROWS * COLS, WIDE)
    lane = lanes(flat)
    keep = keep_ref[...].reshape(flat)
    recv = recv_ref[...].reshape(flat).astype(F32)
    mine = jnp.where(lane < 3 * DH, keep, keep * gmine_ref[...].reshape(flat)).astype(BF16)
    other = jnp.where(lane < 3 * DH, recv, recv * gother_ref[...].reshape(flat)).astype(BF16)
    w = w_ref[...]
    w0, w1 = head_weight(w, 0), head_weight(w, 1)

    def write(a, b):
        out_ref[...] = (mm(a, w0, NT) + mm(b, w1, NT)).astype(BF16).reshape(ROWS, COLS, WIDE)

    @pl.when(yl == 0)
    def _():
        write(mine, other)

    @pl.when(yl != 0)
    def _():
        write(other, mine)


def output(keep, recv, gmine, gother, w):
    return pl.pallas_call(
        output_kernel,
        out_shape=jax.ShapeDtypeStruct((ROWS, COLS, WIDE), BF16),
        compiler_params=params(),
        name="output",
    )(keep, recv, gmine, gother, w)


def shift(value, step):
    return lax.ppermute(value, "z", [(z, (z + step) % RING) for z in range(RING)])


def swap(value, axis):
    return lax.ppermute(value, axis, [(0, 1), (1, 0)])


def added(a, b):
    return (a.astype(F32) + b.astype(F32)).astype(BF16)


def body(pair, w_qkvg, w_out, bias, chain_lengths, d_pair_out):
    peers = ("yh", "x", "yl")
    wanted = jnp.broadcast_to(bias[None], (8,) + bias.shape).reshape(16, COLS, COLS)
    mine, other, gmine, gother = project(pair, d_pair_out, w_qkvg, w_out)
    recv = swap(other, "yl")
    own = lax.all_to_all(wanted, peers, 0, 0, tiled=True)
    kv, q, da, qt, dat = pack(mine, recv)
    oth = swap(own, "core")
    blocks = (2, 4, 2, COLS, COLS)
    bias_early, bias_late = bias_tables(
        chain_lengths, own.reshape(blocks), oth.reshape(blocks)
    )
    kvs = [kv] + [None] * (RING - 1)
    up = down = kv
    for r in range(1, 5):
        down = shift(down, -1)
        kvs[r] = down
        if r < 4:
            up = shift(up, 1)
            kvs[RING - r] = up
    e, state = early(q, bias_early, kvs)
    state, d4, d5, d_late = turn(q, da, qt, dat, bias_late, state, kvs)
    up = shift(d4, 1)
    down = shift(d5, -1)
    u, dkvs, keep_table, send_table = backward(q, da, qt, dat, state, e, d_late, kvs)
    up = shift(added(up, dkvs[3]), 1)
    down = shift(added(down, dkvs[6]), -1)
    up = shift(added(up, dkvs[2]), 1)
    down = shift(added(down, dkvs[7]), -1)
    up = shift(added(up, dkvs[1]), 1)
    summed = (keep_table + swap(send_table, "core").astype(F32)).astype(BF16)
    parts = lax.all_to_all(summed.reshape(16, COLS, COLS), peers, 0, 0, tiled=True)
    d_bias = jnp.sum(parts.reshape(8, H, COLS, COLS).astype(F32), axis=0)
    keep, send = finish(u, dkvs[0], up, down)
    d_pair = output(keep, swap(send, "yl"), gmine, gother, w_qkvg)
    return (d_pair, d_bias)


def solution(mesh):
    split = Mesh(mesh.devices.reshape(2, 4, 2, 2, RING), ("yh", "x", "core", "yl", "z"))
    row, col = ("yh", "x", "core"), ("yl", "z")
    in_specs = (P(row, col, None), P(), P(), P(None, col, row), P(), P(row, col, None))
    out_specs = (P(row, col, None), P(None, col, row))
    return jax.shard_map(body, mesh=split, in_specs=in_specs, out_specs=out_specs, check_vma=False)
```

time: 115 us -> 94.5 us (0.82)
  Pallas kernels: 35.3 us -> 20.4 us
  local copies, waits for them, and re-layouts: 8.6 us -> 3.19 us
    pallas_call x8 -> x6, Pallas kernels: 33.6 us -> 18.7 us  [the longest x1 5.69 us: turn(): pl.pallas_call(turn_kernel, out_shape=[STATE] + [BLOCK] * len(LATE) + [ja...]
    unnamed x18 -> x10, local copies, waits for them, and re-layouts: 7.01 us -> 1.58 us
  transfers between devices with their start and end apart: 20 -> 20, of which waited for: 6 -> 6; matrix products, arithmetic and copies ran while one was open for 3% -> 4% of each run, Pallas kernels for 21% -> 11%
where the time goes in v3:
time: 94.5 us; the launch traced here: 94.1 us
  starting transfers between devices  42.1 us (45%)
  waiting for transfers between devices  25.8 us (27%)
  Pallas kernels  20.4 us (22%)
  local copies, waits for them, and re-layouts  3.19 us (3%)
  other arithmetic  1.77 us (2%)
    ppermute x14, starting transfers between devices, shift(): lax.ppermute(value, 'z', [(z, (z + step) % RING) for z in range(RING)])  25.8 us
    ppermute x14, waiting for transfers between devices, shift(): lax.ppermute(value, 'z', [(z, (z + step) % RING) for z in range(RING)])  14.6 us
    all_to_all x1, starting transfers between devices, body(): own = lax.all_to_all(wanted, peers, 0, 0, tiled=True)  7.48 us
    ppermute x4, waiting for transfers between devices, swap(): return lax.ppermute(value, axis, [(0, 1), (1, 0)])  7.17 us
    pallas_call x1, Pallas kernels, turn(): pl.pallas_call(turn_kernel, out_shape=[STATE] + [BLOCK] * len(LATE) + [ja...  5.69 us
    all_to_all x1, starting transfers between devices, body(): lax.all_to_all(summed.reshape(16, COLS, COLS), peers, 0, 0, tiled=True)  5.61 us
    pallas_call x1, Pallas kernels, backward(): pl.pallas_call(backward_kernel, out_shape=[jax.ShapeDtypeStruct((2, ROWS,...  5.35 us
    all_to_all x1, waiting for transfers between devices, body(): own = lax.all_to_all(wanted, peers, 0, 0, tiled=True)  4 us
  transfers between devices with their start and end apart: 20, of which 6 were waited for; matrix products, arithmetic and copies ran while one was open for 4% of the time, Pallas kernels for 11%

profile of v3, /device:TPU:2, one launch (start us, length us, event | category | flops | bytes accessed | tf_op | source)
XLA Modules:
  0.0 94.1 jit_solution(4263831464001808049)
XLA Ops:
  0.6 2.6 %project.1 = (bf16[6,96,128]{2,1,0:T(8,128)(2,1)}, bf16[6,96,128]{2,1,0:T(8,128)(2,1)}, f32[6,96,128]{2,1,0:T(8,128)}, f32[6,96,128]{2,1,0:T(8,128)}) custom-call(bf16[6,96,128]{2,1,0:T(8,128)(2,1)} %pair_hbm.1, bf16[6,96,128]{2,1,0:T(8,128)(2,1)} %grad_hbm.1, bf16[128,256]{1,0:T(8,128)(2,1)} %w_ref.1, bf16[64,128]{1,0:T(8,128)(2,1)} %wout_hbm.1), custom_call_target="tpu_custom_call" | custom-call | bytes 6000000 | tf_op jit(solution)/shard_map/project/pallas_call | solution.py:98
  3.3 1.7 %collective-permute-start = (bf16[6,96,128]{2,1,0:T(8,128)(2,1)}, bf16[6,96,128]{2,1,0:T(8,128)(2,1)S(1)}, u32[]{:S(2)}, u32[]{:S(2)}) collective-permute-start(bf16[6,96,128]{2,1,0:T(8,128)(2,1)} %get-tuple-element.31), channel_id=1, source_target_pairs={{0,8},{8,0},{1,9},{9,1},{2,10},{10,2},{3,11},{11,3},{4,12},{12,4},... | collective-permute-start | bytes 442376 | tf_op jit(solution)/shard_map/ppermute | solution.py:411
  4.9 4.2 %collective-permute-done.recv_ref = bf16[6,96,128]{2,1,0:T(8,128)(2,1)S(1)} collective-permute-done((bf16[6,96,128]{2,1,0:T(8,128)(2,1)}, bf16[6,96,128]{2,1,0:T(8,128)(2,1)S(1)}, u32[]{:S(2)}, u32[]{:S(2)}) %collective-permute-start) | collective-permute-done | bytes 147488 | tf_op jit(solution)/shard_map/ppermute | solution.py:411
  10.9 5.9 %collective-permute-start.2 = (bf16[6,96,128]{2,1,0:T(8,128)(2,1)S(1)}, bf16[6,96,128]{2,1,0:T(8,128)(2,1)S(1)}, u32[]{:S(2)}, u32[]{:S(2)}) collective-permute-start(bf16[6,96,128]{2,1,0:T(8,128)(2,1)S(1)} %get-tuple-element.38.refs_0_), channel_id=1, source_target_pairs={{0,7},{1,0},{2,1},{3,2},{4,3},{5,4},{6,5},{7,6},{8,15},{9,8},{10,9... | collective-permute-start | bytes 442376 | tf_op jit(solution)/shard_map/ppermute | solution.py:407
  16.8 1.6 %broadcast_in_dim.2 = bf16[8,2,96,96]{3,2,1,0:T(8,128)(2,1)} broadcast(bf16[2,96,96]{2,1,0:T(8,128)(2,1)} %param.9), dimensions={1,2,3} | broadcast | bytes 331776 | tf_op jit(solution)/shard_map/broadcast_in_dim | solution.py:420
  18.4 7.5 %all-to-all-start = ((bf16[16,96,96]{2,1,0:T(8,128)(2,1)}), bf16[16,96,96]{2,1,0:T(8,128)(2,1)S(1)}, u32[]{:S(2)}, u32[]{:S(2)}) async-start(bf16[16,96,96]{2,1,0:T(8,128)(2,1)} %bitcast), calls=%async_computation | async-start | bytes 786432 | tf_op jit(solution)/shard_map/all_to_all | solution.py:423
  25.9 3.2 %collective-permute-start.4 = (bf16[6,96,128]{2,1,0:T(8,128)(2,1)S(1)}, bf16[6,96,128]{2,1,0:T(8,128)(2,1)S(1)}, u32[]{:S(2)}, u32[]{:S(2)}) collective-permute-start(bf16[6,96,128]{2,1,0:T(8,128)(2,1)S(1)} %collective-permute-done.2.refs_1_), channel_id=1, source_target_pairs={{0,7},{1,0},{2,1},{3,2},{4,3},{5,4},{6,5},{7,6},{8,15},{9,8},{10,9... | collective-permute-start | bytes 442376 | tf_op jit(solution)/shard_map/ppermute | solution.py:407
  29.1 4.0 %all-to-all-done = bf16[16,96,96]{2,1,0:T(8,128)(2,1)S(1)} async-done(((bf16[16,96,96]{2,1,0:T(8,128)(2,1)}), bf16[16,96,96]{2,1,0:T(8,128)(2,1)S(1)}, u32[]{:S(2)}, u32[]{:S(2)}) %all-to-all-start) | async-done | bytes 294944 | tf_op jit(solution)/shard_map/all_to_all | solution.py:423
  33.2 3.2 %collective-permute-start.6 = (bf16[6,96,128]{2,1,0:T(8,128)(2,1)S(1)}, bf16[6,96,128]{2,1,0:T(8,128)(2,1)S(1)}, u32[]{:S(2)}, u32[]{:S(2)}) collective-permute-start(bf16[6,96,128]{2,1,0:T(8,128)(2,1)S(1)} %collective-permute-done.4.refs_3_), channel_id=1, source_target_pairs={{0,7},{1,0},{2,1},{3,2},{4,3},{5,4},{6,5},{7,6},{8,15},{9,8},{10,9... | collective-permute-start | bytes 442376 | tf_op jit(solution)/shard_map/ppermute | solution.py:407
  36.4 4.2 %collective-permute-done.5.refs_4_ = bf16[6,96,128]{2,1,0:T(8,128)(2,1)S(1)} collective-permute-done((bf16[6,96,128]{2,1,0:T(8,128)(2,1)S(1)}, bf16[6,96,128]{2,1,0:T(8,128)(2,1)S(1)}, u32[]{:S(2)}, u32[]{:S(2)}) %collective-permute-start.5) | collective-permute-done | bytes 147488 | tf_op jit(solution)/shard_map/ppermute | solution.py:407
  40.6 3.2 %collective-permute-start.7 = (bf16[6,96,128]{2,1,0:T(8,128)(2,1)S(1)}, bf16[6,96,128]{2,1,0:T(8,128)(2,1)S(1)}, u32[]{:S(2)}, u32[]{:S(2)}) collective-permute-start(bf16[6,96,128]{2,1,0:T(8,128)(2,1)S(1)} %collective-permute-done.6.refs_5_), channel_id=1, source_target_pairs={{0,7},{1,0},{2,1},{3,2},{4,3},{5,4},{6,5},{7,6},{8,15},{9,8},{10,9... | collective-permute-start | bytes 442376 | tf_op jit(solution)/shard_map/ppermute | solution.py:407
  44.5 1.0 %bias_tables.1 = (f32[192,1152]{1,0:T(8,128)S(1)}, f32[192,384]{1,0:T(8,128)S(1)}) custom-call(s32[8]{0:T(128)S(1)} %copy-done.4, bf16[2,4,2,96,96]{4,3,2,1,0:T(8,128)(2,1)S(1)} %bitcast.6, bf16[2,4,2,96,96]{4,3,2,1,0:T(8,128)(2,1)S(1)} %bitcast.7), custom_call_target="tpu_custom_call" | custom-call | bytes 4500000 | tf_op jit(solution)/shard_map/bias_tables/pallas_call | solution.py:182
  45.5 3.3 %early.1 = (bf16[6,192,1152]{2,1,0:T(8,128)(2,1)S(1)}, f32[6,192,128]{2,1,0:T(8,128)S(1)}) custom-call(bf16[6,192,128]{2,1,0:T(8,128)(2,1)S(1)} %get-tuple-element.32.q_ref, f32[192,1152]{1,0:T(8,128)S(1)} %get-tuple-element.37.bias_ref, bf16[6,96,128]{2,1,0:T(8,128)(2,1)S(1)} %get-tuple-element.38.refs_0_, ...), custom_call_target="tpu_custom_call" | custom-call | bytes 12000000 | tf_op jit(solution)/shard_map/early/pallas_call | solution.py:232
  48.8 5.7 %turn.1 = (f32[6,192,128]{2,1,0:T(8,128)S(1)}, bf16[6,96,128]{2,1,0:T(8,128)(2,1)S(1)}, bf16[6,96,128]{2,1,0:T(8,128)(2,1)S(1)}, f32[192,384]{1,0:T(8,128)S(1)}) custom-call(bf16[6,192,128]{2,1,0:T(8,128)(2,1)S(1)} %get-tuple-element.32.q_ref, bf16[6,192,128]{2,1,0:T(8,128)(2,1)S(1)} %get-tuple-element.33.da_ref, ...), custom_call_target="tpu_custom_call" | custom-call | bytes 12000000 | tf_op jit(solution)/shard_map/turn/pallas_call | solution.py:275
  54.6 3.2 %collective-permute-start.13 = (bf16[6,96,128]{2,1,0:T(8,128)(2,1)S(1)}, bf16[6,96,128]{2,1,0:T(8,128)(2,1)S(1)}, u32[]{:S(2)}, u32[]{:S(2)}) collective-permute-start(bf16[6,96,128]{2,1,0:T(8,128)(2,1)S(1)} %get-tuple-element.49), channel_id=1, source_target_pairs={{0,7},{1,0},{2,1},{3,2},{4,3},{5,4},{6,5},{7,6},{8,15},{9,8},{10,9... | collective-permute-start | bytes 442376 | tf_op jit(solution)/shard_map/ppermute | solution.py:407
  57.8 5.3 %backward.1 = (f32[2,6,96,128]{3,2,1,0:T(8,128)S(1)}, bf16[6,96,128]{2,1,0:T(8,128)(2,1)S(1)}, bf16[6,96,128]{2,1,0:T(8,128)(2,1)S(1)}, bf16[6,96,128]{2,1,0:T(8...) custom-call(bf16[6,192,128]{2,1,0:T(8,128)(2,1)S(1)} %get-tuple-elem, ...), custom_call_target="tpu_custom_call" | custom-call | bytes 15000000 | tf_op jit(solution)/shard_map/backward/pallas_call | solution.py:330
  63.4 3.3 %collective-permute-start.14 = (bf16[6,96,128]{2,1,0:T(8,128)(2,1)S(1)}, bf16[6,96,128]{2,1,0:T(8,128)(2,1)S(1)}, u32[]{:S(2)}, u32[]{:S(2)}) collective-permute-start(bf16[6,96,128]{2,1,0:T(8,128)(2,1)S(1)} %add_convert_fusion.2), channel_id=1, source_target_pairs={{0,7},{1,0},{2,1},{3,2},{4,3},{5,4},{6,5},{7,6},{8,15},{9,8},{10,9... | collective-permute-start | bytes 442376 | tf_op jit(solution)/shard_map/ppermute | solution.py:407
  66.7 4.1 %collective-permute-done.10 = bf16[6,96,128]{2,1,0:T(8,128)(2,1)S(1)} collective-permute-done((bf16[6,96,128]{2,1,0:T(8,128)(2,1)S(1)}, bf16[6,96,128]{2,1,0:T(8,128)(2,1)S(1)}, u32[]{:S(2)}, u32[]{:S(2)}) %collective-permute-start.10) | collective-permute-done | bytes 147488 | tf_op jit(solution)/shard_map/ppermute | solution.py:407
  71.0 3.3 %collective-permute-start.15 = (bf16[6,96,128]{2,1,0:T(8,128)(2,1)S(1)}, bf16[6,96,128]{2,1,0:T(8,128)(2,1)S(1)}, u32[]{:S(2)}, u32[]{:S(2)}) collective-permute-start(bf16[6,96,128]{2,1,0:T(8,128)(2,1)S(1)} %add_convert_fusion.1), channel_id=1, source_target_pairs={{0,7},{1,0},{2,1},{3,2},{4,3},{5,4},{6,5},{7,6},{8,15},{9,8},{10,9... | collective-permute-start | bytes 442376 | tf_op jit(solution)/shard_map/ppermute | solution.py:407
  75.1 5.6 %all-to-all-start.1 = ((bf16[16,96,96]{2,1,0:T(8,128)(2,1)}), bf16[16,96,96]{2,1,0:T(8,128)(2,1)S(1)}, u32[]{:S(2)}, u32[]{:S(2)}) async-start(bf16[16,96,96]{2,1,0:T(8,128)(2,1)} %bitcast.3), calls=%async_computation.1 | async-start | bytes 786432 | tf_op jit(solution)/shard_map/all_to_all | solution.py:449
  80.9 6.3 %collective-permute-done.12.b_ref = bf16[6,96,128]{2,1,0:T(8,128)(2,1)S(1)} collective-permute-done((bf16[6,96,128]{2,1,0:T(8,128)(2,1)S(1)}, bf16[6,96,128]{2,1,0:T(8,128)(2,1)S(1)}, u32[]{:S(2)}, u32[]{:S(2)}) %collective-permute-start.12) | collective-permute-done | bytes 147488 | tf_op jit(solution)/shard_map/ppermute | solution.py:407
  87.8 1.6 %collective-permute-start.16 = (bf16[6,96,128]{2,1,0:T(8,128)(2,1)S(1)}, bf16[6,96,128]{2,1,0:T(8,128)(2,1)S(1)}, u32[]{:S(2)}, u32[]{:S(2)}) collective-permute-start(bf16[6,96,128]{2,1,0:T(8,128)(2,1)S(1)} %get-tuple-element.53), channel_id=1, source_target_pairs={{0,8},{8,0},{1,9},{9,1},{2,10},{10,2},{3,11},{11,3},{4,12},{12,4},... | collective-permute-start | bytes 442376 | tf_op jit(solution)/shard_map/ppermute | solution.py:411
  90.1 2.9 %collective-permute-done.16.recv_ref = bf16[6,96,128]{2,1,0:T(8,128)(2,1)S(1)} collective-permute-done((bf16[6,96,128]{2,1,0:T(8,128)(2,1)S(1)}, bf16[6,96,128]{2,1,0:T(8,128)(2,1)S(1)}, u32[]{:S(2)}, u32[]{:S(2)}) %collective-permute-start.16) | collective-permute-done | bytes 147488 | tf_op jit(solution)/shard_map/ppermute | solution.py:411
  93.1 1.1 %output.1 = bf16[6,96,128]{2,1,0:T(8,128)(2,1)} custom-call(f32[6,96,128]{2,1,0:T(8,128)S(1)} %get-tuple-element.52.keep_ref, bf16[6,96,128]{2,1,0:T(8,128)(2,1)S(1)} %collective-permute-done.16.recv_ref, f32[6,96,128]{2,1,0:T(8,128)S(1)} %copy-done, f32[6,96,128]{2,1,0:T(8,128)S(1)} %copy-done.1, bf16[128,256]{1,0:T(8,128)(2,1)S(1)} %copy-done.2), custom_call_target="tpu_custom_call" | custom-call | tf_op jit(solution)/shard_map/output/pallas_call | solution.py:398
  (42 shorter events, 5.2 us)
Async XLA Ops:
  3.3 5.9 %collective-permute-start = (bf16[6,96,128]{2,1,0:T(8,128)(2,1)}, bf16[6,96,128]{2,1,0:T(8,128)(2,1)S(1)}, u32[]{:S(2)}, u32[]{:S(2)}) collective-permute-start(bf16[6,96,128]{2,1,0:T(8,128)(2,1)} %get-tuple-element.31), channel_id=1, source_target_pairs={{0,8},{8,0},{1,9},{9,1},{2,10},{10,2},{3,11},{11,3},{4,12},{12,4},... | collective-permute-start | bytes 442376 | tf_op jit(solution)/shard_map/ppermute | solution.py:411
  9.2 0.9 copy-start.3
  10.9 15.0 %collective-permute-start.2 = (bf16[6,96,128]{2,1,0:T(8,128)(2,1)S(1)}, bf16[6,96,128]{2,1,0:T(8,128)(2,1)S(1)}, u32[]{:S(2)}, u32[]{:S(2)}) collective-permute-start(bf16[6,96,128]{2,1,0:T(8,128)(2,1)S(1)} %get-tuple-element.38.refs_0_), channel_id=1, source_target_pairs={{0,7},{1,0},{2,1},{3,2},{4,3},{5,4},{6,5},{7,6},{8,15},{9,8},{10,9... | collective-permute-start | bytes 442376 | tf_op jit(solution)/shard_map/ppermute | solution.py:407
  18.4 14.7 %all-to-all-start = ((bf16[16,96,96]{2,1,0:T(8,128)(2,1)}), bf16[16,96,96]{2,1,0:T(8,128)(2,1)S(1)}, u32[]{:S(2)}, u32[]{:S(2)}) async-start(bf16[16,96,96]{2,1,0:T(8,128)(2,1)} %bitcast), calls=%async_computation | async-start | bytes 786432 | tf_op jit(solution)/shard_map/all_to_all | solution.py:423
  25.9 7.2 %collective-permute-start.3 = (bf16[6,96,128]{2,1,0:T(8,128)(2,1)S(1)}, bf16[6,96,128]{2,1,0:T(8,128)(2,1)S(1)}, u32[]{:S(2)}, u32[]{:S(2)}) collective-permute-start(bf16[6,96,128]{2,1,0:T(8,128)(2,1)S(1)} %get-tuple-element.38.refs_0_), channel_id=1, source_target_pairs={{0,1},{1,2},{2,3},{3,4},{4,5},{5,6},{6,7},{7,0},{8,9},{9,10},{10,1... | collective-permute-start | bytes 442376 | tf_op jit(solution)/shard_map/ppermute | solution.py:407
  25.9 7.2 %collective-permute-start.4 = (bf16[6,96,128]{2,1,0:T(8,128)(2,1)S(1)}, bf16[6,96,128]{2,1,0:T(8,128)(2,1)S(1)}, u32[]{:S(2)}, u32[]{:S(2)}) collective-permute-start(bf16[6,96,128]{2,1,0:T(8,128)(2,1)S(1)} %collective-permute-done.2.refs_1_), channel_id=1, source_target_pairs={{0,7},{1,0},{2,1},{3,2},{4,3},{5,4},{6,5},{7,6},{8,15},{9,8},{10,9... | collective-permute-start | bytes 442376 | tf_op jit(solution)/shard_map/ppermute | solution.py:407
  33.1 10.7 %collective-permute-start.1 = (bf16[16,96,96]{2,1,0:T(8,128)(2,1)S(1)}, bf16[16,96,96]{2,1,0:T(8,128)(2,1)S(1)}, u32[]{:S(2)}, u32[]{:S(2)}) collective-permute-start(bf16[16,96,96]{2,1,0:T(8,128)(2,1)S(1)} %all-to-all-done), channel_id=1, source_target_pairs={{0,16},{16,0},{1,17},{17,1},{2,18},{18,2},{3,19},{19,3},{4,20},{20... | collective-permute-start | bytes 884744 | tf_op jit(solution)/shard_map/ppermute | solution.py:411
  33.2 7.5 %collective-permute-start.5 = (bf16[6,96,128]{2,1,0:T(8,128)(2,1)S(1)}, bf16[6,96,128]{2,1,0:T(8,128)(2,1)S(1)}, u32[]{:S(2)}, u32[]{:S(2)}) collective-permute-start(bf16[6,96,128]{2,1,0:T(8,128)(2,1)S(1)} %collective-permute-done.3.refs_2_), channel_id=1, source_target_pairs={{0,1},{1,2},{2,3},{3,4},{4,5},{5,6},{6,7},{7,0},{8,9},{9,10},{10,1... | collective-permute-start | bytes 442376 | tf_op jit(solution)/shard_map/ppermute | solution.py:407
  33.2 7.5 %collective-permute-start.6 = (bf16[6,96,128]{2,1,0:T(8,128)(2,1)S(1)}, bf16[6,96,128]{2,1,0:T(8,128)(2,1)S(1)}, u32[]{:S(2)}, u32[]{:S(2)}) collective-permute-start(bf16[6,96,128]{2,1,0:T(8,128)(2,1)S(1)} %collective-permute-done.4.refs_3_), channel_id=1, source_target_pairs={{0,7},{1,0},{2,1},{3,2},{4,3},{5,4},{6,5},{7,6},{8,15},{9,8},{10,9... | collective-permute-start | bytes 442376 | tf_op jit(solution)/shard_map/ppermute | solution.py:407
  40.6 8.1 %collective-permute-start.8 = (bf16[6,96,128]{2,1,0:T(8,128)(2,1)S(1)}, bf16[6,96,128]{2,1,0:T(8,128)(2,1)S(1)}, u32[]{:S(2)}, u32[]{:S(2)}) collective-permute-start(bf16[6,96,128]{2,1,0:T(8,128)(2,1)S(1)} %collective-permute-done.5.refs_4_), channel_id=1, source_target_pairs={{0,1},{1,2},{2,3},{3,4},{4,5},{5,6},{6,7},{7,0},{8,9},{9,10},{10,1... | collective-permute-start | bytes 442376 | tf_op jit(solution)/shard_map/ppermute | solution.py:407
  40.6 8.1 %collective-permute-start.7 = (bf16[6,96,128]{2,1,0:T(8,128)(2,1)S(1)}, bf16[6,96,128]{2,1,0:T(8,128)(2,1)S(1)}, u32[]{:S(2)}, u32[]{:S(2)}) collective-permute-start(bf16[6,96,128]{2,1,0:T(8,128)(2,1)S(1)} %collective-permute-done.6.refs_5_), channel_id=1, source_target_pairs={{0,7},{1,0},{2,1},{3,2},{4,3},{5,4},{6,5},{7,6},{8,15},{9,8},{10,9... | collective-permute-start | bytes 442376 | tf_op jit(solution)/shard_map/ppermute | solution.py:407
  54.5 8.7 %collective-permute-start.9 = (bf16[6,96,128]{2,1,0:T(8,128)(2,1)S(1)}, bf16[6,96,128]{2,1,0:T(8,128)(2,1)S(1)}, u32[]{:S(2)}, u32[]{:S(2)}) collective-permute-start(bf16[6,96,128]{2,1,0:T(8,128)(2,1)S(1)} %get-tuple-element.45), channel_id=1, source_target_pairs={{0,1},{1,2},{2,3},{3,4},{4,5},{5,6},{6,7},{7,0},{8,9},{9,10},{10,1... | collective-permute-start | bytes 442376 | tf_op jit(solution)/shard_map/ppermute | solution.py:407
  54.6 8.8 %collective-permute-start.13 = (bf16[6,96,128]{2,1,0:T(8,128)(2,1)S(1)}, bf16[6,96,128]{2,1,0:T(8,128)(2,1)S(1)}, u32[]{:S(2)}, u32[]{:S(2)}) collective-permute-start(bf16[6,96,128]{2,1,0:T(8,128)(2,1)S(1)} %get-tuple-element.49), channel_id=1, source_target_pairs={{0,7},{1,0},{2,1},{3,2},{4,3},{5,4},{6,5},{7,6},{8,15},{9,8},{10,9... | collective-permute-start | bytes 442376 | tf_op jit(solution)/shard_map/ppermute | solution.py:407
  63.1 11.1 %collective-permute-start.17 = (bf16[2,4,2,96,96]{4,3,2,1,0:T(8,128)(2,1)S(1)}, bf16[2,4,2,96,96]{4,3,2,1,0:T(8,128)(2,1)S(1)}, u32[]{:S(2)}, u32[]{:S(2)}) collective-permute-start(bf16[2,4,2,96,96]{4,3,2,1,0:T(8,128)(2,1)S(1)} %get-tuple-element.57), channel_id=1, source_target_pairs={{0,16},{16,0},{1,17},{17,1},{2,18},{18,2},{3,19},{19,3},{4,20},{20... | collective-permute-start | bytes 884744 | tf_op jit(solution)/shard_map/ppermute | solution.py:411
  63.3 7.5 %collective-permute-start.10 = (bf16[6,96,128]{2,1,0:T(8,128)(2,1)S(1)}, bf16[6,96,128]{2,1,0:T(8,128)(2,1)S(1)}, u32[]{:S(2)}, u32[]{:S(2)}) collective-permute-start(bf16[6,96,128]{2,1,0:T(8,128)(2,1)S(1)} %add_convert_fusion.5), channel_id=1, source_target_pairs={{0,1},{1,2},{2,3},{3,4},{4,5},{5,6},{6,7},{7,0},{8,9},{9,10},{10,1... | collective-permute-start | bytes 442376 | tf_op jit(solution)/shard_map/ppermute | solution.py:407
  63.4 29.7 %copy-start = (f32[6,96,128]{2,1,0:T(8,128)S(1)}, f32[6,96,128]{2,1,0:T(8,128)}, u32[]{:S(2)}) copy-start(f32[6,96,128]{2,1,0:T(8,128)} %get-tuple-element.54.gmine_ref) | copy-start | bytes 884740
  63.4 29.7 %copy-start.1 = (f32[6,96,128]{2,1,0:T(8,128)S(1)}, f32[6,96,128]{2,1,0:T(8,128)}, u32[]{:S(2)}) copy-start(f32[6,96,128]{2,1,0:T(8,128)} %get-tuple-element.55.gother_ref) | copy-start | bytes 884740
  63.4 29.7 %copy-start.2 = (bf16[128,256]{1,0:T(8,128)(2,1)S(1)}, bf16[128,256]{1,0:T(8,128)(2,1)}, u32[]{:S(2)}) copy-start(bf16[128,256]{1,0:T(8,128)(2,1)} %w_ref.1) | copy-start | bytes 196612
  63.4 7.5 %collective-permute-start.14 = (bf16[6,96,128]{2,1,0:T(8,128)(2,1)S(1)}, bf16[6,96,128]{2,1,0:T(8,128)(2,1)S(1)}, u32[]{:S(2)}, u32[]{:S(2)}) collective-permute-start(bf16[6,96,128]{2,1,0:T(8,128)(2,1)S(1)} %add_convert_fusion.2), channel_id=1, source_target_pairs={{0,7},{1,0},{2,1},{3,2},{4,3},{5,4},{6,5},{7,6},{8,15},{9,8},{10,9... | collective-permute-start | bytes 442376 | tf_op jit(solution)/shard_map/ppermute | solution.py:407
  70.8 9.9 %collective-permute-start.11 = (bf16[6,96,128]{2,1,0:T(8,128)(2,1)S(1)}, bf16[6,96,128]{2,1,0:T(8,128)(2,1)S(1)}, u32[]{:S(2)}, u32[]{:S(2)}) collective-permute-start(bf16[6,96,128]{2,1,0:T(8,128)(2,1)S(1)} %add_convert_fusion.4), channel_id=1, source_target_pairs={{0,1},{1,2},{2,3},{3,4},{4,5},{5,6},{6,7},{7,0},{8,9},{9,10},{10,1... | collective-permute-start | bytes 442376 | tf_op jit(solution)/shard_map/ppermute | solution.py:407
  71.0 9.9 %collective-permute-start.15 = (bf16[6,96,128]{2,1,0:T(8,128)(2,1)S(1)}, bf16[6,96,128]{2,1,0:T(8,128)(2,1)S(1)}, u32[]{:S(2)}, u32[]{:S(2)}) collective-permute-start(bf16[6,96,128]{2,1,0:T(8,128)(2,1)S(1)} %add_convert_fusion.1), channel_id=1, source_target_pairs={{0,7},{1,0},{2,1},{3,2},{4,3},{5,4},{6,5},{7,6},{8,15},{9,8},{10,9... | collective-permute-start | bytes 442376 | tf_op jit(solution)/shard_map/ppermute | solution.py:407
  75.1 14.3 %all-to-all-start.1 = ((bf16[16,96,96]{2,1,0:T(8,128)(2,1)}), bf16[16,96,96]{2,1,0:T(8,128)(2,1)S(1)}, u32[]{:S(2)}, u32[]{:S(2)}) async-start(bf16[16,96,96]{2,1,0:T(8,128)(2,1)} %bitcast.3), calls=%async_computation.1 | async-start | bytes 786432 | tf_op jit(solution)/shard_map/all_to_all | solution.py:449
  80.8 6.4 %collective-permute-start.12 = (bf16[6,96,128]{2,1,0:T(8,128)(2,1)S(1)}, bf16[6,96,128]{2,1,0:T(8,128)(2,1)S(1)}, u32[]{:S(2)}, u32[]{:S(2)}) collective-permute-start(bf16[6,96,128]{2,1,0:T(8,128)(2,1)S(1)} %add_convert_fusion.3), channel_id=1, source_target_pairs={{0,1},{1,2},{2,3},{3,4},{4,5},{5,6},{6,7},{7,0},{8,9},{9,10},{10,1... | collective-permute-start | bytes 442376 | tf_op jit(solution)/shard_map/ppermute | solution.py:407
  87.8 5.2 %collective-permute-start.16 = (bf16[6,96,128]{2,1,0:T(8,128)(2,1)S(1)}, bf16[6,96,128]{2,1,0:T(8,128)(2,1)S(1)}, u32[]{:S(2)}, u32[]{:S(2)}) collective-permute-start(bf16[6,96,128]{2,1,0:T(8,128)(2,1)S(1)} %get-tuple-element.53), channel_id=1, source_target_pairs={{0,8},{8,0},{1,9},{9,1},{2,10},{10,2},{3,11},{11,3},{4,12},{12,4},... | collective-permute-start | bytes 442376 | tf_op jit(solution)/shard_map/ppermute | solution.py:411
  (1 other events, 0.7 us)

commit v4 on v3

v4 whole, which is shorter than its diff:
```python
import functools
import math

import jax
import jax.numpy as jnp
from jax import lax
from jax.experimental import pallas as pl
from jax.experimental.pallas import tpu as pltpu
from jax.sharding import Mesh, PartitionSpec as P

H = 2
DH = 32
CHAINS = 8
SCALE = 1.0 / math.sqrt(DH)
MASKED_SCORE = -1e30
F32 = jnp.float32
BF16 = jnp.bfloat16

ROWS = 6
COLS = 96
RING = 8
HALF = RING * COLS
KEYS = 2 * HALF
WIDE = 128
NEAR = (0, 1, 7, 2)
FAR = (3, 6)
LATE = (4, 5)
NC, NF, NL = (2 * len(group) * COLS for group in (NEAR, FAR, LATE))


NT = (((1,), (1,)), ((), ()))
NN = (((1,), (0,)), ((), ()))
TN = (((0,), (0,)), ((), ()))


def mm(a, b, dims):
    return lax.dot_general(a, b, dims, preferred_element_type=F32)


def params(limit=32 << 20):
    return pltpu.CompilerParams(vmem_limit_bytes=limit)


def cost(us):
    return pl.CostEstimate(flops=0, bytes_accessed=int(us * 3e6), transcendentals=0)


def lanes(shape):
    return lax.broadcasted_iota(jnp.int32, shape, len(shape) - 1)


def head_weight(w, h):
    parts = [w[:, (part * H + h) * DH : (part * H + h + 1) * DH] for part in (1, 2, 0, 3)]
    return jnp.concatenate(parts, axis=1)


def project_kernel(
    len_hbm, bias_hbm, pair_hbm, grad_hbm, w_hbm, wout_hbm,
    mine_ref, other_ref, gmine_ref, gother_ref, wanted_ref, lift_ref,
    len_s, bias_s, pair_s, grad_s, w_s, wout_s, sem,
):
    yl = lax.axis_index("yl")
    pairs = (
        (len_hbm, len_s), (bias_hbm, bias_s), (w_hbm, w_s),
        (wout_hbm, wout_s), (pair_hbm, pair_s), (grad_hbm, grad_s),
    )
    copies = [pltpu.make_async_copy(a, b, sem.at[n]) for n, (a, b) in enumerate(pairs)]
    for copy in copies:
        copy.start()
    for copy in copies[:2]:
        copy.wait()
    for h in range(H):
        for n in range(8):
            wanted_ref[n * H + h] = bias_s[h]
    for c in range(CHAINS):
        for half in range(2):
            position = lanes((1, COLS)) + half * COLS
            lift_ref[2 * c + half] = jnp.where(position < len_s[c], 0.0, MASKED_SCORE)
    for copy in copies[2:]:
        copy.wait()
    pair = pair_s[...].reshape(ROWS * COLS, WIDE)
    grad = grad_s[...].reshape(ROWS * COLS, WIDE)
    w = w_s[...]
    wout = wout_s[...]
    lane = lanes((ROWS * COLS, WIDE))
    for h in range(H):
        proj = mm(pair, head_weight(w, h), NN)
        rows = jnp.concatenate(
            [jnp.zeros((WIDE - DH, WIDE), BF16), wout[h * DH : (h + 1) * DH]], axis=0
        )
        d_out = mm(grad, rows, NT)
        gate = jax.nn.sigmoid(proj)
        payload = jnp.where(
            lane < 2 * DH, proj, jnp.where(lane < 3 * DH, proj * SCALE, d_out * gate)
        )
        payload = payload.astype(BF16).reshape(ROWS, COLS, WIDE)
        g = (d_out * gate * (1.0 - gate)).reshape(ROWS, COLS, WIDE)

        @pl.when(yl == h)
        def _():
            mine_ref[...] = payload
            gmine_ref[...] = g

        @pl.when(yl != h)
        def _():
            other_ref[...] = payload
            gother_ref[...] = g


def project(chain_lengths, bias, pair, grad, w, wout):
    shape = (ROWS, COLS, WIDE)
    arrays = (chain_lengths, bias, pair, grad, w, wout)
    arrays = [pltpu.with_memory_space_constraint(array, pltpu.HBM) for array in arrays]
    return pl.pallas_call(
        project_kernel,
        in_specs=[pl.BlockSpec(memory_space=pltpu.HBM)] * 6,
        out_shape=[
            jax.ShapeDtypeStruct(shape, BF16),
            jax.ShapeDtypeStruct(shape, BF16),
            jax.ShapeDtypeStruct(shape, F32),
            jax.ShapeDtypeStruct(shape, F32),
            jax.ShapeDtypeStruct((16, COLS, COLS), BF16),
            jax.ShapeDtypeStruct((2 * CHAINS, 1, COLS), F32),
        ],
        scratch_shapes=[
            pltpu.SMEM((CHAINS,), jnp.int32),
            pltpu.VMEM(bias.shape, BF16),
            pltpu.VMEM(shape, BF16),
            pltpu.VMEM(shape, BF16),
            pltpu.VMEM(w.shape, BF16),
            pltpu.VMEM(wout.shape, BF16),
            pltpu.SemaphoreType.DMA((6,)),
        ],
        compiler_params=params(),
        cost_estimate=cost(2.0),
        name="project",
    )(*arrays)


def pack_kernel(mine_ref, recv_ref, kv_ref, q_ref, da_ref, qt_ref, dat_ref):
    yl = lax.axis_index("yl")
    lane = lanes((COLS, WIDE))

    def write(i, a, b):
        a, b = a.astype(F32), b.astype(F32)
        kv_ref[i] = jnp.where(lane < 2 * DH, a, pltpu.roll(b, 2 * DH, 1)).astype(BF16)
        for part, x in enumerate((a, b)):
            y = pltpu.roll(x, 2 * DH, 1)
            rows = slice(part * COLS, (part + 1) * COLS)
            q_ref[i, rows] = jnp.where(lane < DH, y, 0.0).astype(BF16)
            da_ref[i, rows] = jnp.where((lane >= DH) & (lane < 2 * DH), y, 0.0).astype(BF16)
        turned = jnp.concatenate([a, b], axis=0).T
        qt_ref[i] = turned[2 * DH : 3 * DH].astype(BF16)
        dat_ref[i] = turned[3 * DH :].astype(BF16)

    for i in range(ROWS):

        @pl.when(yl == 0)
        def _():
            write(i, mine_ref[i], recv_ref[i])

        @pl.when(yl != 0)
        def _():
            write(i, recv_ref[i], mine_ref[i])


BLOCK = jax.ShapeDtypeStruct((ROWS, COLS, WIDE), BF16)
STATE = jax.ShapeDtypeStruct((ROWS, 2 * COLS, WIDE), F32)


def pack(mine, recv):
    both = jax.ShapeDtypeStruct((ROWS, 2 * COLS, WIDE), BF16)
    turned = jax.ShapeDtypeStruct((ROWS, DH, 2 * COLS), BF16)
    return pl.pallas_call(
        pack_kernel,
        out_shape=[BLOCK, both, both, turned, turned],
        compiler_params=params(),
        cost_estimate=cost(0.6),
        name="pack",
    )(mine, recv)


def bias_kernel(lift_ref, own_ref, oth_ref, early_ref, late_ref):
    core = lax.axis_index("core")
    z = lax.axis_index("z")
    for group, out_ref, first in (
        (FAR, early_ref, 0), (NEAR, early_ref, NF), (LATE, late_ref, 0),
    ):
        for n, r in enumerate(group):
            at = lax.rem(z + r, RING)
            x, odd = at // 2, lax.rem(at, 2)
            for yh in range(2):
                start = first + (yh * len(group) + n) * COLS
                lift = lift_ref[yh * CHAINS + at]
                for yl in range(2):
                    rows = slice(yl * COLS, (yl + 1) * COLS)
                    both = jnp.where(odd == core, own_ref[yh, x, yl], oth_ref[yh, x, yl])
                    out_ref[rows, start : start + COLS] = both.astype(F32) + lift


def bias_tables(lift, own, oth):
    return pl.pallas_call(
        bias_kernel,
        out_shape=[
            jax.ShapeDtypeStruct((2 * COLS, NF + NC), F32),
            jax.ShapeDtypeStruct((2 * COLS, NL), F32),
        ],
        compiler_params=params(),
        cost_estimate=cost(1.5),
        name="bias_tables",
    )(lift, own, oth)


def stack(refs, i):
    one = jnp.concatenate([ref[i] for ref in refs], axis=0)
    moved = pltpu.roll(one.astype(F32), 2 * DH, 1).astype(BF16)
    return jnp.concatenate([one, moved], axis=0)


def key_gradients(qt, dat, low, p_low, dkv_refs, i):
    dk = mm(qt, low, NN)
    dv = mm(dat, p_low, NN)
    half = dk.shape[1] // 2
    dkv = jnp.concatenate([dk[:, :half], dv[:, :half], dk[:, half:], dv[:, half:]], axis=0).T
    for n, ref in enumerate(dkv_refs):
        ref[i] = dkv[n * COLS : (n + 1) * COLS].astype(BF16)


def wide(value):
    return jnp.broadcast_to(value, (2 * COLS, WIDE))


def across(value, like):
    return jnp.concatenate([value] * (like.shape[1] // WIDE), axis=1)


def add_row(table_ref, i, value):
    if i == 0:
        table_ref[...] = value
    else:
        table_ref[...] += value


def staged(first, second, third):
    held = first(0)
    for i in range(ROWS):
        done = second(i, *held)
        if i + 1 < ROWS:
            following = first(i + 1)
        third(i, *done)
        held = following


def early_kernel(q_ref, da_ref, bias_ref, *refs):
    n = len(FAR) + len(NEAR)
    far_refs, near_refs = refs[: len(FAR)], refs[len(FAR) : n]
    far_e_ref, near_e_ref, acc_ref, total_ref, mass_ref, top_ref = refs[n:]

    def scores(i):
        kv = jnp.concatenate([stack(far_refs, i), stack(near_refs, i)], axis=0)
        return kv, mm(q_ref[i], kv, NT) + bias_ref[...], mm(da_ref[i], kv, NT)

    def weigh(i, kv, s, w):
        top = jnp.max(s, axis=1, keepdims=True)
        e = jnp.exp(s - top)
        low = e.astype(BF16)
        far_e_ref[i] = low[:, :NF]
        near_e_ref[i] = low[:, NF:]
        total_ref[i] = wide(jnp.sum(e, axis=1, keepdims=True))
        mass_ref[i] = wide(jnp.sum(e * w, axis=1, keepdims=True))
        top_ref[i] = wide(top)
        return kv, low

    def gather(i, kv, low):
        acc_ref[i] = mm(low, kv, NN)

    staged(scores, weigh, gather)


def early(q, da, bias, kvs):
    return pl.pallas_call(
        early_kernel,
        out_shape=[
            jax.ShapeDtypeStruct((ROWS, 2 * COLS, NF), BF16),
            jax.ShapeDtypeStruct((ROWS, 2 * COLS, NC), BF16),
        ]
        + [STATE] * 4,
        compiler_params=params(),
        cost_estimate=cost(4.0),
        name="early",
    )(q, da, bias, *[kvs[r] for r in FAR + NEAR])


def turn_kernel(
    q_ref, da_ref, qt_ref, dat_ref, bias_ref, acc_ref, total_ref, mass_ref, top_ref, *refs
):
    n = len(LATE)
    kv_refs, (u_ref, dot_ref, factor_ref) = refs[:n], refs[n : n + 3]
    dkv_refs, table_ref = refs[n + 3 : 2 * n + 3], refs[-1]
    lane = lanes((2 * COLS, WIDE))

    def scores(i):
        kv = stack(kv_refs, i)
        return kv, mm(q_ref[i], kv, NT) + bias_ref[...], mm(da_ref[i], kv, NT)

    def weigh(i, kv, s, w):
        old = top_ref[i]
        top = jnp.maximum(jnp.max(s, axis=1, keepdims=True), old)
        fade = jnp.exp(old - top)
        e = jnp.exp(s - across(top, s))
        inverse = 1.0 / (jnp.sum(e, axis=1, keepdims=True) + total_ref[i] * fade)
        factor = fade * inverse
        dot = (jnp.sum(e * w, axis=1, keepdims=True) + mass_ref[i] * fade) * inverse
        factor_ref[i] = factor
        dot_ref[i] = dot
        p = e * across(inverse, e)
        d = p * (w - across(dot, p))
        add_row(table_ref, i, d)
        return kv, p.astype(BF16), d.astype(BF16), factor

    def gather(i, kv, p_low, low, factor):
        key_gradients(qt_ref[i], dat_ref[i], low, p_low, dkv_refs, i)
        acc = mm(p_low, kv, NN) + acc_ref[i] * factor
        u_ref[i] = jnp.where(lane < DH, mm(low, kv, NN), acc)

    staged(scores, weigh, gather)


def turn(q, da, qt, dat, bias, state, kvs):
    return pl.pallas_call(
        turn_kernel,
        out_shape=[STATE] * 3
        + [BLOCK] * len(LATE)
        + [jax.ShapeDtypeStruct((2 * COLS, NL), F32)],
        compiler_params=params(),
        cost_estimate=cost(3.0),
        name="turn",
    )(q, da, qt, dat, bias, *state, *[kvs[r] for r in LATE])


def backward_kernel(
    group, da_ref, qt_ref, dat_ref, part_ref, dot_ref, factor_ref, e_ref, *refs
):
    n = len(group)
    kv_refs, u_ref, dkv_refs, table_ref = refs[:n], refs[n], refs[n + 1 : 2 * n + 1], refs[2 * n + 1]
    lane = lanes((2 * COLS, WIDE))

    def scores(i):
        kv = stack(kv_refs, i)
        return kv, mm(da_ref[i], kv, NT)

    def weigh(i, kv, w):
        p = e_ref[i].astype(F32)
        p = p * across(factor_ref[i], p)
        d = p * (w - across(dot_ref[i], p))
        add_row(table_ref, i, d)
        return kv, p.astype(BF16), d.astype(BF16)

    def gather(i, kv, p_low, low):
        u = part_ref[i]
        u_ref[i] = jnp.where(lane < DH, u + mm(low, kv, NN), u)
        key_gradients(qt_ref[i], dat_ref[i], low, p_low, dkv_refs, i)

    staged(scores, weigh, gather)


def backward(group, da, qt, dat, state, e, kvs, time):
    n = len(group)
    out = pl.pallas_call(
        functools.partial(backward_kernel, group),
        out_shape=[STATE]
        + [BLOCK] * n
        + [jax.ShapeDtypeStruct((2 * COLS, 2 * n * COLS), F32)],
        compiler_params=params(),
        cost_estimate=cost(time),
        name="backward",
    )(da, qt, dat, *state, e, *[kvs[r] for r in group])
    return out[0], dict(zip(group, out[1 : n + 1])), out[-1]


def split_kernel(near_ref, far_ref, late_ref, keep_ref, send_ref):
    core = lax.axis_index("core")
    z = lax.axis_index("z")
    for group, table in ((NEAR, near_ref), (FAR, far_ref), (LATE, late_ref)):
        for m, r in enumerate(group):
            at = lax.rem(z + r, RING)
            x, odd = at // 2, lax.rem(at, 2)
            for yh in range(2):
                start = (yh * len(group) + m) * COLS
                for yl in range(2):
                    piece = table[yl * COLS : (yl + 1) * COLS, start : start + COLS]

                    @pl.when(odd == core)
                    def _():
                        keep_ref[yh, x, yl] = piece

                    @pl.when(odd != core)
                    def _():
                        send_ref[yh, x, yl] = piece.astype(BF16)


def split_tables(near, far, late):
    blocks = (2, 4, 2, COLS, COLS)
    return pl.pallas_call(
        split_kernel,
        out_shape=[jax.ShapeDtypeStruct(blocks, F32), jax.ShapeDtypeStruct(blocks, BF16)],
        compiler_params=params(),
        cost_estimate=cost(1.0),
        name="split_tables",
    )(near, far, late)


def relay_kernel(up_ref, part_ref, keep_ref, recv_ref, sent_ref, summed_ref):
    sent_ref[...] = (up_ref[...].astype(F32) + part_ref[...].astype(F32)).astype(BF16)
    summed_ref[...] = (keep_ref[...] + recv_ref[...].astype(F32)).astype(BF16)


def relay(up, part, keep, recv):
    return pl.pallas_call(
        relay_kernel,
        out_shape=[BLOCK, jax.ShapeDtypeStruct(keep.shape, BF16)],
        compiler_params=params(),
        cost_estimate=cost(0.8),
        name="relay",
    )(up, part, keep, recv)


def finish_kernel(u_ref, a_ref, b_ref, c_ref, keep_ref, send_ref):
    yl = lax.axis_index("yl")
    lane = lanes((COLS, WIDE))
    lane2 = lanes((2 * COLS, WIDE))
    for i in range(ROWS):
        dkv = a_ref[i].astype(F32) + b_ref[i].astype(F32) + c_ref[i].astype(F32)
        u = jnp.where(lane2 < DH, u_ref[i] * SCALE, u_ref[i])
        u = pltpu.roll(u, 2 * DH, 1)
        first = jnp.where(lane < 2 * DH, dkv, u[:COLS])
        second = jnp.where(lane < 2 * DH, pltpu.roll(dkv, 2 * DH, 1), u[COLS:])

        @pl.when(yl == 0)
        def _():
            keep_ref[i] = first
            send_ref[i] = second.astype(BF16)

        @pl.when(yl != 0)
        def _():
            keep_ref[i] = second
            send_ref[i] = first.astype(BF16)


def finish(u, a, b, c):
    shape = (ROWS, COLS, WIDE)
    return pl.pallas_call(
        finish_kernel,
        out_shape=[jax.ShapeDtypeStruct(shape, F32), jax.ShapeDtypeStruct(shape, BF16)],
        compiler_params=params(),
        name="finish",
    )(u, a, b, c)


def output_kernel(keep_ref, recv_ref, gmine_ref, gother_ref, w_ref, out_ref):
    yl = lax.axis_index("yl")
    flat = (ROWS * COLS, WIDE)
    lane = lanes(flat)
    keep = keep_ref[...].reshape(flat)
    recv = recv_ref[...].reshape(flat).astype(F32)
    mine = jnp.where(lane < 3 * DH, keep, keep * gmine_ref[...].reshape(flat)).astype(BF16)
    other = jnp.where(lane < 3 * DH, recv, recv * gother_ref[...].reshape(flat)).astype(BF16)
    w = w_ref[...]
    w0, w1 = head_weight(w, 0), head_weight(w, 1)

    def write(a, b):
        out_ref[...] = (mm(a, w0, NT) + mm(b, w1, NT)).astype(BF16).reshape(ROWS, COLS, WIDE)

    @pl.when(yl == 0)
    def _():
        write(mine, other)

    @pl.when(yl != 0)
    def _():
        write(other, mine)


def output(keep, recv, gmine, gother, w):
    return pl.pallas_call(
        output_kernel,
        out_shape=jax.ShapeDtypeStruct((ROWS, COLS, WIDE), BF16),
        compiler_params=params(),
        name="output",
    )(keep, recv, gmine, gother, w)


def shift(value, step):
    return lax.ppermute(value, "z", [(z, (z + step) % RING) for z in range(RING)])


def swap(value, axis):
    return lax.ppermute(value, axis, [(0, 1), (1, 0)])


def added(a, b):
    return (a.astype(F32) + b.astype(F32)).astype(BF16)


def body(pair, w_qkvg, w_out, bias, chain_lengths, d_pair_out):
    peers = ("yh", "x", "yl")
    mine, other, gmine, gother, wanted, lift = project(
        chain_lengths, bias, pair, d_pair_out, w_qkvg, w_out
    )
    recv = swap(other, "yl")
    own = lax.all_to_all(wanted, peers, 0, 0, tiled=True)
    kv, q, da, qt, dat = pack(mine, recv)
    oth = swap(own, "core")
    blocks = (2, 4, 2, COLS, COLS)
    bias_early, bias_late = bias_tables(lift, own.reshape(blocks), oth.reshape(blocks))
    kvs = [kv] + [None] * (RING - 1)
    up = down = kv
    for r in range(1, 5):
        down = shift(down, -1)
        kvs[r] = down
        if r < 4:
            up = shift(up, 1)
            kvs[RING - r] = up
    e_far, e_near, *state = early(q, da, bias_early, kvs)
    u, dot, factor, d4, d5, t_late = turn(q, da, qt, dat, bias_late, state, kvs)
    up = shift(d4, 1)
    down = shift(d5, -1)
    u, far, t_far = backward(FAR, da, qt, dat, (u, dot, factor), e_far, kvs, 2.5)
    up = shift(added(up, far[3]), 1)
    down = shift(added(down, far[6]), -1)
    u, near, t_near = backward(NEAR, da, qt, dat, (u, dot, factor), e_near, kvs, 3.0)
    keep_table, send_table = split_tables(t_near, t_far, t_late)
    recv_table = swap(send_table, "core")
    up = shift(added(up, near[2]), 1)
    down = shift(added(down, near[7]), -1)
    up, summed = relay(up, near[1], keep_table, recv_table)
    up = shift(up, 1)
    parts = lax.all_to_all(summed.reshape(16, COLS, COLS), peers, 0, 0, tiled=True)
    keep, send = finish(u, near[0], up, down)
    d_bias = jnp.sum(parts.reshape(8, H, COLS, COLS).astype(F32), axis=0)
    d_pair = output(keep, swap(send, "yl"), gmine, gother, w_qkvg)
    return (d_pair, d_bias)


def solution(mesh):
    split = Mesh(mesh.devices.reshape(2, 4, 2, 2, RING), ("yh", "x", "core", "yl", "z"))
    row, col = ("yh", "x", "core"), ("yl", "z")
    in_specs = (P(row, col, None), P(), P(), P(None, col, row), P(), P(row, col, None))
    out_specs = (P(row, col, None), P(None, col, row))
    return jax.shard_map(body, mesh=split, in_specs=in_specs, out_specs=out_specs, check_vma=False)
```

time: 94.5 us -> 89.8 us (0.950)
  local copies, waits for them, and re-layouts: 3.19 us -> 0.01 us
  waiting for transfers between devices: 25.8 us -> 28.7 us
  Pallas kernels: 20.4 us -> 18.3 us
  starting transfers between devices: 42.1 us -> 40.8 us
    ppermute x14, waiting for transfers between devices: 14.6 us -> 17.7 us  [shift(): lax.ppermute(value, 'z', [(z, (z + step) % RING) for z in range(RING)])]
    pallas_call x3 -> x6, Pallas kernels: 12 us -> 9.52 us  [the longest x2 3.37 us: backward(): pl.pallas_call(functools.partial(backward_kernel, group), out_shape=[STAT...]
    broadcast_in_dim x1 -> x0, local copies, waits for them, and re-layouts: 1.61 us -> none  [body(): jnp.broadcast_to(bias[None], (8,) + bias.shape).reshape(16, COLS, COLS)]
    unnamed x10 -> x2, local copies, waits for them, and re-layouts: 1.58 us -> 0.01 us
    ppermute x14, starting transfers between devices: 25.8 us -> 24.5 us  [shift(): lax.ppermute(value, 'z', [(z, (z + step) % RING) for z in range(RING)])]
  transfers between devices with their start and end apart: 20 -> 20, of which waited for: 6 -> 8; matrix products, arithmetic and copies ran while one was open for 4% -> 1% of each run, Pallas kernels for 11% -> 13%
where the time goes in v4:
time: 89.8 us; the launch traced here: 89.5 us
  starting transfers between devices  40.8 us (45%)
  waiting for transfers between devices  28.7 us (32%)
  Pallas kernels  18.3 us (20%)
    ppermute x14, starting transfers between devices, shift(): lax.ppermute(value, 'z', [(z, (z + step) % RING) for z in range(RING)])  24.5 us
    ppermute x14, waiting for transfers between devices, shift(): lax.ppermute(value, 'z', [(z, (z + step) % RING) for z in range(RING)])  17.7 us
    all_to_all x1, starting transfers between devices, body(): own = lax.all_to_all(wanted, peers, 0, 0, tiled=True)  7.48 us
    ppermute x4, waiting for transfers between devices, swap(): return lax.ppermute(value, axis, [(0, 1), (1, 0)])  6.96 us
    all_to_all x1, starting transfers between devices, body(): lax.all_to_all(summed.reshape(16, COLS, COLS), peers, 0, 0, tiled=True)  5.61 us
    all_to_all x1, waiting for transfers between devices, body(): own = lax.all_to_all(wanted, peers, 0, 0, tiled=True)  4 us
    pallas_call x1, Pallas kernels, early(): pl.pallas_call(early_kernel, out_shape=[jax.ShapeDtypeStruct((ROWS, 2 * C...  3.74 us
    pallas_call x2, Pallas kernels, backward(): pl.pallas_call(functools.partial(backward_kernel, group), out_shape=[STAT...  3.37 us
  transfers between devices with their start and end apart: 20, of which 8 were waited for; matrix products, arithmetic and copies ran while one was open for 1% of the time, Pallas kernels for 13%

profile of v4, /device:TPU:2, one launch (start us, length us, event | category | flops | bytes accessed | tf_op | source)
XLA Modules:
  0.0 89.5 jit_solution(11328679877225415954)
XLA Ops:
  0.6 2.5 %project.1 = (bf16[6,96,128]{2,1,0:T(8,128)(2,1)S(1)}, bf16[6,96,128]{2,1,0:T(8,128)(2,1)S(1)}, f32[6,96,128]{2,1,0:T(8,128)S(1)}, f32[6,96,128]{2,1,0:T(8,128)S...) custom-call(s32[8]{0:T(128)} %len_hbm.1, bf16[2,96,96]{2,1,0:T(8,128)(2,1)} %bias_hbm.1, ...), custom_call_target="tpu_custom_call" | custom-call | bytes 6000000 | tf_op jit(solution)/shard_map/project/pallas_call | solution.py:114
  3.2 1.7 %collective-permute-start = (bf16[6,96,128]{2,1,0:T(8,128)(2,1)S(1)}, bf16[6,96,128]{2,1,0:T(8,128)(2,1)S(1)}, u32[]{:S(2)}, u32[]{:S(2)}) collective-permute-start(bf16[6,96,128]{2,1,0:T(8,128)(2,1)S(1)} %get-tuple-element.44), channel_id=1, source_target_pairs={{0,8},{8,0},{1,9},{9,1},{2,10},{10,2},{3,11},{11,3},{4,12},{12,4},... | collective-permute-start | bytes 442376 | tf_op jit(solution)/shard_map/ppermute | solution.py:497
  4.8 4.0 %collective-permute-done.recv_ref = bf16[6,96,128]{2,1,0:T(8,128)(2,1)S(1)} collective-permute-done((bf16[6,96,128]{2,1,0:T(8,128)(2,1)S(1)}, bf16[6,96,128]{2,1,0:T(8,128)(2,1)S(1)}, u32[]{:S(2)}, u32[]{:S(2)}) %collective-permute-start) | collective-permute-done | bytes 147488 | tf_op jit(solution)/shard_map/ppermute | solution.py:497
  9.7 5.9 %collective-permute-start.2 = (bf16[6,96,128]{2,1,0:T(8,128)(2,1)S(1)}, bf16[6,96,128]{2,1,0:T(8,128)(2,1)S(1)}, u32[]{:S(2)}, u32[]{:S(2)}) collective-permute-start(bf16[6,96,128]{2,1,0:T(8,128)(2,1)S(1)} %get-tuple-element.53.refs_2_.refs_0_), channel_id=1, source_target_pairs={{0,7},{1,0},{2,1},{3,2},{4,3},{5,4},{6,5},{7,6},{8,15},{9,8},{10,9... | collective-permute-start | bytes 442376 | tf_op jit(solution)/shard_map/ppermute | solution.py:493
  15.6 7.5 %all-to-all-start = ((bf16[16,96,96]{2,1,0:T(8,128)(2,1)}), bf16[16,96,96]{2,1,0:T(8,128)(2,1)S(1)}, u32[]{:S(2)}, u32[]{:S(2)}) async-start(bf16[16,96,96]{2,1,0:T(8,128)(2,1)} %get-tuple-element.50), calls=%async_computation | async-start | bytes 786432 | tf_op jit(solution)/shard_map/all_to_all | solution.py:510
  23.1 3.2 %collective-permute-start.3 = (bf16[6,96,128]{2,1,0:T(8,128)(2,1)S(1)}, bf16[6,96,128]{2,1,0:T(8,128)(2,1)S(1)}, u32[]{:S(2)}, u32[]{:S(2)}) collective-permute-start(bf16[6,96,128]{2,1,0:T(8,128)(2,1)S(1)} %collective-permute-done.2.refs_3_.refs_1_), channel_id=1, source_target_pairs={{0,7},{1,0},{2,1},{3,2},{4,3},{5,4},{6,5},{7,6},{8,15},{9,8},{10,9... | collective-permute-start | bytes 442376 | tf_op jit(solution)/shard_map/ppermute | solution.py:493
  26.3 4.0 %all-to-all-done = bf16[16,96,96]{2,1,0:T(8,128)(2,1)S(1)} async-done(((bf16[16,96,96]{2,1,0:T(8,128)(2,1)}), bf16[16,96,96]{2,1,0:T(8,128)(2,1)S(1)}, u32[]{:S(2)}, u32[]{:S(2)}) %all-to-all-start) | async-done | bytes 294944 | tf_op jit(solution)/shard_map/all_to_all | solution.py:510
  30.3 3.2 %collective-permute-start.4 = (bf16[6,96,128]{2,1,0:T(8,128)(2,1)S(1)}, bf16[6,96,128]{2,1,0:T(8,128)(2,1)S(1)}, u32[]{:S(2)}, u32[]{:S(2)}) collective-permute-start(bf16[6,96,128]{2,1,0:T(8,128)(2,1)S(1)} %collective-permute-done.3.refs_5_.refs_3_), channel_id=1, source_target_pairs={{0,7},{1,0},{2,1},{3,2},{4,3},{5,4},{6,5},{7,6},{8,15},{9,8},{10,9... | collective-permute-start | bytes 442376 | tf_op jit(solution)/shard_map/ppermute | solution.py:493
  33.6 4.2 %collective-permute-done.6.refs_1_ = bf16[6,96,128]{2,1,0:T(8,128)(2,1)S(1)} collective-permute-done((bf16[6,96,128]{2,1,0:T(8,128)(2,1)S(1)}, bf16[6,96,128]{2,1,0:T(8,128)(2,1)S(1)}, u32[]{:S(2)}, u32[]{:S(2)}) %collective-permute-start.6) | collective-permute-done | bytes 147488 | tf_op jit(solution)/shard_map/ppermute | solution.py:493
  37.8 3.2 %collective-permute-start.7 = (bf16[6,96,128]{2,1,0:T(8,128)(2,1)S(1)}, bf16[6,96,128]{2,1,0:T(8,128)(2,1)S(1)}, u32[]{:S(2)}, u32[]{:S(2)}) collective-permute-start(bf16[6,96,128]{2,1,0:T(8,128)(2,1)S(1)} %collective-permute-done.4.refs_0_), channel_id=1, source_target_pairs={{0,7},{1,0},{2,1},{3,2},{4,3},{5,4},{6,5},{7,6},{8,15},{9,8},{10,9... | collective-permute-start | bytes 442376 | tf_op jit(solution)/shard_map/ppermute | solution.py:493
  41.4 3.7 %early.1 = (bf16[6,192,384]{2,1,0:T(8,128)(2,1)S(1)}, bf16[6,192,768]{2,1,0:T(8,128)(2,1)S(1)}, f32[6,192,128]{2,1,0:T(8,128)S(1)}, f32[6,192,128]{2,1,0:T(8,128...) custom-call(bf16[6,192,128]{2,1,0:T(8,128)(2,1)S(1)} %get-tuple-element.48.q_ref, ...), custom_call_target="tpu_custom_call" | custom-call | bytes 12000000 | tf_op jit(solution)/shard_map/early/pallas_call | solution.py:281
  45.2 2.6 %turn.1 = (f32[6,192,128]{2,1,0:T(8,128)S(1)}, f32[6,192,128]{2,1,0:T(8,128)S(1)}, f32[6,192,128]{2,1,0:T(8,128)S(1)}, bf16[6,96,128]{2,1,0:T(8,128)(2,1)S(1)}, ...) custom-call(bf16[6,192,128]{2,1,0:T(8,128)(2,1)S(1)} %get-tuple-element.48.q_ref, ...), custom_call_target="tpu_custom_call" | custom-call | bytes 9000000 | tf_op jit(solution)/shard_map/turn/pallas_call | solution.py:330
  47.9 1.4 %backward.2 = (f32[6,192,128]{2,1,0:T(8,128)S(1)}, bf16[6,96,128]{2,1,0:T(8,128)(2,1)S(1)}, bf16[6,96,128]{2,1,0:T(8,128)(2,1)S(1)}, f32[192,384]{1,0:T(8,128)S(1)}) custom-call(bf16[6,192,128]{2,1,0:T(8,128)(2,1)S(1)} %get-tuple-element.45.da_ref, bf16[6,32,192]{2,1,0:T(8,128)(2,1)S(1)} %get-tuple-element.46.qt_ref, ...), custom_call_target="tpu_custom_call" | custom-call | bytes 7500000 | tf_op jit(solution)/shard_map/backward/pallas_call | solution.py:369
  49.3 4.9 %collective-permute-done.9 = bf16[6,96,128]{2,1,0:T(8,128)(2,1)S(1)} collective-permute-done((bf16[6,96,128]{2,1,0:T(8,128)(2,1)S(1)}, bf16[6,96,128]{2,1,0:T(8,128)(2,1)S(1)}, u32[]{:S(2)}, u32[]{:S(2)}) %collective-permute-start.9) | collective-permute-done | bytes 147488 | tf_op jit(solution)/shard_map/ppermute | solution.py:493
  54.3 3.2 %collective-permute-start.14 = (bf16[6,96,128]{2,1,0:T(8,128)(2,1)S(1)}, bf16[6,96,128]{2,1,0:T(8,128)(2,1)S(1)}, u32[]{:S(2)}, u32[]{:S(2)}) collective-permute-start(bf16[6,96,128]{2,1,0:T(8,128)(2,1)S(1)} %get-tuple-element.76), channel_id=1, source_target_pairs={{0,7},{1,0},{2,1},{3,2},{4,3},{5,4},{6,5},{7,6},{8,15},{9,8},{10,9... | collective-permute-start | bytes 442376 | tf_op jit(solution)/shard_map/ppermute | solution.py:493
  57.6 2.0 %backward.3 = (f32[6,192,128]{2,1,0:T(8,128)S(1)}, bf16[6,96,128]{2,1,0:T(8,128)(2,1)S(1)}, bf16[6,96,128]{2,1,0:T(8,128)(2,1)S(1)}, bf16[6,96,128]{2,1,0:T(8,12...) custom-call(bf16[6,192,128]{2,1,0:T(8,128)(2,1)S(1)} %get-tuple-element.45.da_ref, ...), custom_call_target="tpu_custom_call" | custom-call | bytes 9000000 | tf_op jit(solution)/shard_map/backward/pallas_call | solution.py:369
  59.5 2.3 %split_tables.1 = (f32[2,4,2,96,96]{4,3,2,1,0:T(8,128)S(1)}, bf16[2,4,2,96,96]{4,3,2,1,0:T(8,128)(2,1)S(1)}) custom-call(f32[192,768]{1,0:T(8,128)S(1)} %get-tuple-element.70.near_ref, f32[192,384]{1,0:T(8,128)S(1)} %get-tuple-element.71.far_ref, f32[192,384]{1,0:T(8,128)S(1)} %get-tuple-element.72.late_ref), custom_call_target="tpu_custom_call" | custom-call | bytes 3000000 | tf_op jit(solution)/shard_map/split_tables/pallas_call | solution.py:404
  62.1 3.3 %collective-permute-start.15 = (bf16[6,96,128]{2,1,0:T(8,128)(2,1)S(1)}, bf16[6,96,128]{2,1,0:T(8,128)(2,1)S(1)}, u32[]{:S(2)}, u32[]{:S(2)}) collective-permute-start(bf16[6,96,128]{2,1,0:T(8,128)(2,1)S(1)} %add_convert_fusion.1), channel_id=1, source_target_pairs={{0,7},{1,0},{2,1},{3,2},{4,3},{5,4},{6,5},{7,6},{8,15},{9,8},{10,9... | collective-permute-start | bytes 442376 | tf_op jit(solution)/shard_map/ppermute | solution.py:493
  65.4 4.1 %collective-permute-done.11.up_ref = bf16[6,96,128]{2,1,0:T(8,128)(2,1)S(1)} collective-permute-done((bf16[6,96,128]{2,1,0:T(8,128)(2,1)S(1)}, bf16[6,96,128]{2,1,0:T(8,128)(2,1)S(1)}, u32[]{:S(2)}, u32[]{:S(2)}) %collective-permute-start.11) | collective-permute-done | bytes 147488 | tf_op jit(solution)/shard_map/ppermute | solution.py:493
  70.3 5.6 %all-to-all-start.1 = ((bf16[16,96,96]{2,1,0:T(8,128)(2,1)}), bf16[16,96,96]{2,1,0:T(8,128)(2,1)S(1)}, u32[]{:S(2)}, u32[]{:S(2)}) async-start(bf16[16,96,96]{2,1,0:T(8,128)(2,1)} %bitcast.2), calls=%async_computation.1 | async-start | bytes 786432 | tf_op jit(solution)/shard_map/all_to_all | solution.py:537
  76.1 2.0 %collective-permute-start.13 = (bf16[6,96,128]{2,1,0:T(8,128)(2,1)S(1)}, bf16[6,96,128]{2,1,0:T(8,128)(2,1)S(1)}, u32[]{:S(2)}, u32[]{:S(2)}) collective-permute-start(bf16[6,96,128]{2,1,0:T(8,128)(2,1)S(1)} %get-tuple-element.75), channel_id=1, source_target_pairs={{0,1},{1,2},{2,3},{3,4},{4,5},{5,6},{6,7},{7,0},{8,9},{9,10},{10,1... | collective-permute-start | bytes 442376 | tf_op jit(solution)/shard_map/ppermute | solution.py:493
  78.1 3.1 %collective-permute-done.16.c_ref = bf16[6,96,128]{2,1,0:T(8,128)(2,1)S(1)} collective-permute-done((bf16[6,96,128]{2,1,0:T(8,128)(2,1)S(1)}, bf16[6,96,128]{2,1,0:T(8,128)(2,1)S(1)}, u32[]{:S(2)}, u32[]{:S(2)}) %collective-permute-start.16) | collective-permute-done | bytes 147488 | tf_op jit(solution)/shard_map/ppermute | solution.py:493
  83.2 1.6 %collective-permute-start.17 = (bf16[6,96,128]{2,1,0:T(8,128)(2,1)S(1)}, bf16[6,96,128]{2,1,0:T(8,128)(2,1)S(1)}, u32[]{:S(2)}, u32[]{:S(2)}) collective-permute-start(bf16[6,96,128]{2,1,0:T(8,128)(2,1)S(1)} %get-tuple-element.80), channel_id=1, source_target_pairs={{0,8},{8,0},{1,9},{9,1},{2,10},{10,2},{3,11},{11,3},{4,12},{12,4},... | collective-permute-start | bytes 442376 | tf_op jit(solution)/shard_map/ppermute | solution.py:497
  85.5 2.9 %collective-permute-done.17.recv_ref = bf16[6,96,128]{2,1,0:T(8,128)(2,1)S(1)} collective-permute-done((bf16[6,96,128]{2,1,0:T(8,128)(2,1)S(1)}, bf16[6,96,128]{2,1,0:T(8,128)(2,1)S(1)}, u32[]{:S(2)}, u32[]{:S(2)}) %collective-permute-start.17) | collective-permute-done | bytes 147488 | tf_op jit(solution)/shard_map/ppermute | solution.py:497
  (34 shorter events, 6.3 us)
Async XLA Ops:
  3.2 5.7 %collective-permute-start = (bf16[6,96,128]{2,1,0:T(8,128)(2,1)S(1)}, bf16[6,96,128]{2,1,0:T(8,128)(2,1)S(1)}, u32[]{:S(2)}, u32[]{:S(2)}) collective-permute-start(bf16[6,96,128]{2,1,0:T(8,128)(2,1)S(1)} %get-tuple-element.44), channel_id=1, source_target_pairs={{0,8},{8,0},{1,9},{9,1},{2,10},{10,2},{3,11},{11,3},{4,12},{12,4},... | collective-permute-start | bytes 442376 | tf_op jit(solution)/shard_map/ppermute | solution.py:497
  9.7 13.4 %collective-permute-start.2 = (bf16[6,96,128]{2,1,0:T(8,128)(2,1)S(1)}, bf16[6,96,128]{2,1,0:T(8,128)(2,1)S(1)}, u32[]{:S(2)}, u32[]{:S(2)}) collective-permute-start(bf16[6,96,128]{2,1,0:T(8,128)(2,1)S(1)} %get-tuple-element.53.refs_2_.refs_0_), channel_id=1, source_target_pairs={{0,7},{1,0},{2,1},{3,2},{4,3},{5,4},{6,5},{7,6},{8,15},{9,8},{10,9... | collective-permute-start | bytes 442376 | tf_op jit(solution)/shard_map/ppermute | solution.py:493
  15.6 14.7 %all-to-all-start = ((bf16[16,96,96]{2,1,0:T(8,128)(2,1)}), bf16[16,96,96]{2,1,0:T(8,128)(2,1)S(1)}, u32[]{:S(2)}, u32[]{:S(2)}) async-start(bf16[16,96,96]{2,1,0:T(8,128)(2,1)} %get-tuple-element.50), calls=%async_computation | async-start | bytes 786432 | tf_op jit(solution)/shard_map/all_to_all | solution.py:510
  23.1 7.2 %collective-permute-start.5 = (bf16[6,96,128]{2,1,0:T(8,128)(2,1)S(1)}, bf16[6,96,128]{2,1,0:T(8,128)(2,1)S(1)}, u32[]{:S(2)}, u32[]{:S(2)}) collective-permute-start(bf16[6,96,128]{2,1,0:T(8,128)(2,1)S(1)} %get-tuple-element.53.refs_2_.refs_0_), channel_id=1, source_target_pairs={{0,1},{1,2},{2,3},{3,4},{4,5},{5,6},{6,7},{7,0},{8,9},{9,10},{10,1... | collective-permute-start | bytes 442376 | tf_op jit(solution)/shard_map/ppermute | solution.py:493
  23.1 7.2 %collective-permute-start.3 = (bf16[6,96,128]{2,1,0:T(8,128)(2,1)S(1)}, bf16[6,96,128]{2,1,0:T(8,128)(2,1)S(1)}, u32[]{:S(2)}, u32[]{:S(2)}) collective-permute-start(bf16[6,96,128]{2,1,0:T(8,128)(2,1)S(1)} %collective-permute-done.2.refs_3_.refs_1_), channel_id=1, source_target_pairs={{0,7},{1,0},{2,1},{3,2},{4,3},{5,4},{6,5},{7,6},{8,15},{9,8},{10,9... | collective-permute-start | bytes 442376 | tf_op jit(solution)/shard_map/ppermute | solution.py:493
  30.3 10.7 %collective-permute-start.1 = (bf16[16,96,96]{2,1,0:T(8,128)(2,1)S(1)}, bf16[16,96,96]{2,1,0:T(8,128)(2,1)S(1)}, u32[]{:S(2)}, u32[]{:S(2)}) collective-permute-start(bf16[16,96,96]{2,1,0:T(8,128)(2,1)S(1)} %all-to-all-done), channel_id=1, source_target_pairs={{0,16},{16,0},{1,17},{17,1},{2,18},{18,2},{3,19},{19,3},{4,20},{20... | collective-permute-start | bytes 884744 | tf_op jit(solution)/shard_map/ppermute | solution.py:497
  30.3 7.5 %collective-permute-start.6 = (bf16[6,96,128]{2,1,0:T(8,128)(2,1)S(1)}, bf16[6,96,128]{2,1,0:T(8,128)(2,1)S(1)}, u32[]{:S(2)}, u32[]{:S(2)}) collective-permute-start(bf16[6,96,128]{2,1,0:T(8,128)(2,1)S(1)} %collective-permute-done.5.refs_4_.refs_2_), channel_id=1, source_target_pairs={{0,1},{1,2},{2,3},{3,4},{4,5},{5,6},{6,7},{7,0},{8,9},{9,10},{10,1... | collective-permute-start | bytes 442376 | tf_op jit(solution)/shard_map/ppermute | solution.py:493
  30.3 7.5 %collective-permute-start.4 = (bf16[6,96,128]{2,1,0:T(8,128)(2,1)S(1)}, bf16[6,96,128]{2,1,0:T(8,128)(2,1)S(1)}, u32[]{:S(2)}, u32[]{:S(2)}) collective-permute-start(bf16[6,96,128]{2,1,0:T(8,128)(2,1)S(1)} %collective-permute-done.3.refs_5_.refs_3_), channel_id=1, source_target_pairs={{0,7},{1,0},{2,1},{3,2},{4,3},{5,4},{6,5},{7,6},{8,15},{9,8},{10,9... | collective-permute-start | bytes 442376 | tf_op jit(solution)/shard_map/ppermute | solution.py:493
  37.8 7.4 %collective-permute-start.8 = (bf16[6,96,128]{2,1,0:T(8,128)(2,1)S(1)}, bf16[6,96,128]{2,1,0:T(8,128)(2,1)S(1)}, u32[]{:S(2)}, u32[]{:S(2)}) collective-permute-start(bf16[6,96,128]{2,1,0:T(8,128)(2,1)S(1)} %collective-permute-done.6.refs_1_), channel_id=1, source_target_pairs={{0,1},{1,2},{2,3},{3,4},{4,5},{5,6},{6,7},{7,0},{8,9},{9,10},{10,1... | collective-permute-start | bytes 442376 | tf_op jit(solution)/shard_map/ppermute | solution.py:493
  37.8 7.4 %collective-permute-start.7 = (bf16[6,96,128]{2,1,0:T(8,128)(2,1)S(1)}, bf16[6,96,128]{2,1,0:T(8,128)(2,1)S(1)}, u32[]{:S(2)}, u32[]{:S(2)}) collective-permute-start(bf16[6,96,128]{2,1,0:T(8,128)(2,1)S(1)} %collective-permute-done.4.refs_0_), channel_id=1, source_target_pairs={{0,7},{1,0},{2,1},{3,2},{4,3},{5,4},{6,5},{7,6},{8,15},{9,8},{10,9... | collective-permute-start | bytes 442376 | tf_op jit(solution)/shard_map/ppermute | solution.py:493
  47.8 6.4 %collective-permute-start.9 = (bf16[6,96,128]{2,1,0:T(8,128)(2,1)S(1)}, bf16[6,96,128]{2,1,0:T(8,128)(2,1)S(1)}, u32[]{:S(2)}, u32[]{:S(2)}) collective-permute-start(bf16[6,96,128]{2,1,0:T(8,128)(2,1)S(1)} %get-tuple-element.66), channel_id=1, source_target_pairs={{0,1},{1,2},{2,3},{3,4},{4,5},{5,6},{6,7},{7,0},{8,9},{9,10},{10,1... | collective-permute-start | bytes 442376 | tf_op jit(solution)/shard_map/ppermute | solution.py:493
  54.2 7.7 %collective-permute-start.10 = (bf16[6,96,128]{2,1,0:T(8,128)(2,1)S(1)}, bf16[6,96,128]{2,1,0:T(8,128)(2,1)S(1)}, u32[]{:S(2)}, u32[]{:S(2)}) collective-permute-start(bf16[6,96,128]{2,1,0:T(8,128)(2,1)S(1)} %add_convert_fusion.3), channel_id=1, source_target_pairs={{0,1},{1,2},{2,3},{3,4},{4,5},{5,6},{6,7},{7,0},{8,9},{9,10},{10,1... | collective-permute-start | bytes 442376 | tf_op jit(solution)/shard_map/ppermute | solution.py:493
  54.3 7.7 %collective-permute-start.14 = (bf16[6,96,128]{2,1,0:T(8,128)(2,1)S(1)}, bf16[6,96,128]{2,1,0:T(8,128)(2,1)S(1)}, u32[]{:S(2)}, u32[]{:S(2)}) collective-permute-start(bf16[6,96,128]{2,1,0:T(8,128)(2,1)S(1)} %get-tuple-element.76), channel_id=1, source_target_pairs={{0,7},{1,0},{2,1},{3,2},{4,3},{5,4},{6,5},{7,6},{8,15},{9,8},{10,9... | collective-permute-start | bytes 442376 | tf_op jit(solution)/shard_map/ppermute | solution.py:493
  61.9 3.6 %collective-permute-start.12 = (bf16[2,4,2,96,96]{4,3,2,1,0:T(8,128)(2,1)S(1)}, bf16[2,4,2,96,96]{4,3,2,1,0:T(8,128)(2,1)S(1)}, u32[]{:S(2)}, u32[]{:S(2)}) collective-permute-start(bf16[2,4,2,96,96]{4,3,2,1,0:T(8,128)(2,1)S(1)} %get-tuple-element.74), channel_id=1, source_target_pairs={{0,16},{16,0},{1,17},{17,1},{2,18},{18,2},{3,19},{19,3},{4,20},{20... | collective-permute-start | bytes 884744 | tf_op jit(solution)/shard_map/ppermute | solution.py:497
  62.0 7.5 %collective-permute-start.11 = (bf16[6,96,128]{2,1,0:T(8,128)(2,1)S(1)}, bf16[6,96,128]{2,1,0:T(8,128)(2,1)S(1)}, u32[]{:S(2)}, u32[]{:S(2)}) collective-permute-start(bf16[6,96,128]{2,1,0:T(8,128)(2,1)S(1)} %add_convert_fusion.2), channel_id=1, source_target_pairs={{0,1},{1,2},{2,3},{3,4},{4,5},{5,6},{6,7},{7,0},{8,9},{9,10},{10,1... | collective-permute-start | bytes 442376 | tf_op jit(solution)/shard_map/ppermute | solution.py:493
  62.1 13.8 %collective-permute-start.15 = (bf16[6,96,128]{2,1,0:T(8,128)(2,1)S(1)}, bf16[6,96,128]{2,1,0:T(8,128)(2,1)S(1)}, u32[]{:S(2)}, u32[]{:S(2)}) collective-permute-start(bf16[6,96,128]{2,1,0:T(8,128)(2,1)S(1)} %add_convert_fusion.1), channel_id=1, source_target_pairs={{0,7},{1,0},{2,1},{3,2},{4,3},{5,4},{6,5},{7,6},{8,15},{9,8},{10,9... | collective-permute-start | bytes 442376 | tf_op jit(solution)/shard_map/ppermute | solution.py:493
  69.5 18.9 %copy-start = (bf16[128,256]{1,0:T(8,128)(2,1)S(1)}, bf16[128,256]{1,0:T(8,128)(2,1)}, u32[]{:S(2)}) copy-start(bf16[128,256]{1,0:T(8,128)(2,1)} %w_ref.1) | copy-start | bytes 196612
  70.3 14.4 %all-to-all-start.1 = ((bf16[16,96,96]{2,1,0:T(8,128)(2,1)}), bf16[16,96,96]{2,1,0:T(8,128)(2,1)S(1)}, u32[]{:S(2)}, u32[]{:S(2)}) async-start(bf16[16,96,96]{2,1,0:T(8,128)(2,1)} %bitcast.2), calls=%async_computation.1 | async-start | bytes 786432 | tf_op jit(solution)/shard_map/all_to_all | solution.py:537
  76.0 5.2 %collective-permute-start.16 = (bf16[6,96,128]{2,1,0:T(8,128)(2,1)S(1)}, bf16[6,96,128]{2,1,0:T(8,128)(2,1)S(1)}, u32[]{:S(2)}, u32[]{:S(2)}) collective-permute-start(bf16[6,96,128]{2,1,0:T(8,128)(2,1)S(1)} %add_convert_fusion), channel_id=1, source_target_pairs={{0,7},{1,0},{2,1},{3,2},{4,3},{5,4},{6,5},{7,6},{8,15},{9,8},{10,9... | collective-permute-start | bytes 442376 | tf_op jit(solution)/shard_map/ppermute | solution.py:493
  76.1 6.4 %collective-permute-start.13 = (bf16[6,96,128]{2,1,0:T(8,128)(2,1)S(1)}, bf16[6,96,128]{2,1,0:T(8,128)(2,1)S(1)}, u32[]{:S(2)}, u32[]{:S(2)}) collective-permute-start(bf16[6,96,128]{2,1,0:T(8,128)(2,1)S(1)} %get-tuple-element.75), channel_id=1, source_target_pairs={{0,1},{1,2},{2,3},{3,4},{4,5},{5,6},{6,7},{7,0},{8,9},{9,10},{10,1... | collective-permute-start | bytes 442376 | tf_op jit(solution)/shard_map/ppermute | solution.py:493
  83.2 5.2 %collective-permute-start.17 = (bf16[6,96,128]{2,1,0:T(8,128)(2,1)S(1)}, bf16[6,96,128]{2,1,0:T(8,128)(2,1)S(1)}, u32[]{:S(2)}, u32[]{:S(2)}) collective-permute-start(bf16[6,96,128]{2,1,0:T(8,128)(2,1)S(1)} %get-tuple-element.80), channel_id=1, source_target_pairs={{0,8},{8,0},{1,9},{9,1},{2,10},{10,2},{3,11},{11,3},{4,12},{12,4},... | collective-permute-start | bytes 442376 | tf_op jit(solution)/shard_map/ppermute | solution.py:497

commit v5 on v4

v5 whole, which is shorter than its diff:
```python
import functools
import math

import jax
import jax.numpy as jnp
from jax import lax
from jax.experimental import pallas as pl
from jax.experimental.pallas import tpu as pltpu
from jax.sharding import Mesh, PartitionSpec as P

H = 2
DH = 32
CHAINS = 8
SCALE = 1.0 / math.sqrt(DH)
MASKED_SCORE = -1e30
F32 = jnp.float32
BF16 = jnp.bfloat16

ROWS = 6
COLS = 96
RING = 8
HALF = RING * COLS
KEYS = 2 * HALF
WIDE = 128
NEAR = (0, 1, 7, 2)
FAR = (3, 6)
LATE = (4, 5)
NC, NF, NL = (2 * len(group) * COLS for group in (NEAR, FAR, LATE))


NT = (((1,), (1,)), ((), ()))
NN = (((1,), (0,)), ((), ()))
TN = (((0,), (0,)), ((), ()))


def mm(a, b, dims):
    return lax.dot_general(a, b, dims, preferred_element_type=F32)


def params(limit=32 << 20):
    return pltpu.CompilerParams(vmem_limit_bytes=limit)


def cost(us):
    return pl.CostEstimate(flops=0, bytes_accessed=int(us * 1e5), transcendentals=0)


def lanes(shape):
    return lax.broadcasted_iota(jnp.int32, shape, len(shape) - 1)


def head_weight(w, h):
    parts = [w[:, (part * H + h) * DH : (part * H + h + 1) * DH] for part in (1, 2, 0, 3)]
    return jnp.concatenate(parts, axis=1)


def project_kernel(
    len_hbm, pair_hbm, grad_hbm, w_hbm, wout_hbm,
    mine_ref, other_ref, lift_ref,
    len_s, pair_s, grad_s, w_s, wout_s, sem,
):
    yl = lax.axis_index("yl")
    pairs = (
        (len_hbm, len_s), (w_hbm, w_s), (wout_hbm, wout_s),
        (pair_hbm, pair_s), (grad_hbm, grad_s),
    )
    copies = [pltpu.make_async_copy(a, b, sem.at[n]) for n, (a, b) in enumerate(pairs)]
    for copy in copies:
        copy.start()
    copies[0].wait()
    for c in range(CHAINS):
        for half in range(2):
            position = lanes((1, COLS)) + half * COLS
            lift_ref[2 * c + half] = jnp.where(position < len_s[c], 0.0, MASKED_SCORE)
    for copy in copies[1:]:
        copy.wait()
    pair = pair_s[...].reshape(ROWS * COLS, WIDE)
    grad = grad_s[...].reshape(ROWS * COLS, WIDE)
    w = w_s[...]
    wout = wout_s[...]
    lane = lanes((ROWS * COLS, WIDE))
    for h in range(H):
        proj = mm(pair, head_weight(w, h), NN)
        rows = jnp.concatenate(
            [jnp.zeros((WIDE - DH, WIDE), BF16), wout[h * DH : (h + 1) * DH]], axis=0
        )
        d_out = mm(grad, rows, NT)
        gate = jax.nn.sigmoid(proj)
        payload = jnp.where(
            lane < 2 * DH, proj, jnp.where(lane < 3 * DH, proj * SCALE, d_out * gate)
        )
        payload = payload.astype(BF16).reshape(ROWS, COLS, WIDE)

        @pl.when(yl == h)
        def _():
            mine_ref[...] = payload

        @pl.when(yl != h)
        def _():
            other_ref[...] = payload


def project(chain_lengths, pair, grad, w, wout):
    shape = (ROWS, COLS, WIDE)
    arrays = (chain_lengths, pair, grad, w, wout)
    arrays = [pltpu.with_memory_space_constraint(array, pltpu.HBM) for array in arrays]
    return pl.pallas_call(
        project_kernel,
        in_specs=[pl.BlockSpec(memory_space=pltpu.HBM)] * 5,
        out_shape=[
            jax.ShapeDtypeStruct(shape, BF16),
            jax.ShapeDtypeStruct(shape, BF16),
            jax.ShapeDtypeStruct((2 * CHAINS, 1, COLS), F32),
        ],
        scratch_shapes=[
            pltpu.SMEM((CHAINS,), jnp.int32),
            pltpu.VMEM(shape, BF16),
            pltpu.VMEM(shape, BF16),
            pltpu.VMEM(w.shape, BF16),
            pltpu.VMEM(wout.shape, BF16),
            pltpu.SemaphoreType.DMA((5,)),
        ],
        compiler_params=params(),
        cost_estimate=cost(2.0),
        name="project",
    )(*arrays)


def slope_kernel(
    _, pair_hbm, grad_hbm, w_hbm, wout_hbm, gmine_ref, gother_ref, pair_s, grad_s, w_s, wout_s, sem
):
    yl = lax.axis_index("yl")
    pairs = ((w_hbm, w_s), (wout_hbm, wout_s), (pair_hbm, pair_s), (grad_hbm, grad_s))
    copies = [pltpu.make_async_copy(a, b, sem.at[n]) for n, (a, b) in enumerate(pairs)]
    for copy in copies:
        copy.start()
    for copy in copies:
        copy.wait()
    pair = pair_s[...].reshape(ROWS * COLS, WIDE)
    grad = grad_s[...].reshape(ROWS * COLS, WIDE)
    zeros = jnp.zeros((WIDE - DH, WIDE), BF16)
    for h in range(H):
        gate = jax.nn.sigmoid(mm(pair, head_weight(w_s[...], h), NN))
        rows = jnp.concatenate([zeros, wout_s[h * DH : (h + 1) * DH]], axis=0)
        g = mm(grad, rows, NT) * gate * (1.0 - gate)

        @pl.when(yl == h)
        def _():
            gmine_ref[...] = g.reshape(ROWS, COLS, WIDE)

        @pl.when(yl != h)
        def _():
            gother_ref[...] = g.reshape(ROWS, COLS, WIDE)


def slopes(after, pair, grad, w, wout):
    shape = (ROWS, COLS, WIDE)
    arrays = [pltpu.with_memory_space_constraint(array, pltpu.HBM) for array in (pair, grad, w, wout)]
    return pl.pallas_call(
        slope_kernel,
        in_specs=[pl.BlockSpec(memory_space=pl.ANY)] + [pl.BlockSpec(memory_space=pltpu.HBM)] * 4,
        out_shape=[jax.ShapeDtypeStruct(shape, F32)] * 2,
        scratch_shapes=[
            pltpu.VMEM(shape, BF16),
            pltpu.VMEM(shape, BF16),
            pltpu.VMEM(w.shape, BF16),
            pltpu.VMEM(wout.shape, BF16),
            pltpu.SemaphoreType.DMA((4,)),
        ],
        compiler_params=params(),
        cost_estimate=cost(2.0),
        name="slopes",
    )(after, *arrays)


def pack_kernel(mine_ref, recv_ref, _, kv_ref, q_ref, da_ref, qt_ref, dat_ref):
    yl = lax.axis_index("yl")
    lane = lanes((COLS, WIDE))

    def write(i, a, b):
        a, b = a.astype(F32), b.astype(F32)
        kv_ref[i] = jnp.where(lane < 2 * DH, a, pltpu.roll(b, 2 * DH, 1)).astype(BF16)
        for part, x in enumerate((a, b)):
            y = pltpu.roll(x, 2 * DH, 1)
            rows = slice(part * COLS, (part + 1) * COLS)
            q_ref[i, rows] = jnp.where(lane < DH, y, 0.0).astype(BF16)
            da_ref[i, rows] = jnp.where((lane >= DH) & (lane < 2 * DH), y, 0.0).astype(BF16)
        turned = jnp.concatenate([a, b], axis=0).T
        qt_ref[i] = turned[2 * DH : 3 * DH].astype(BF16)
        dat_ref[i] = turned[3 * DH :].astype(BF16)

    for i in range(ROWS):

        @pl.when(yl == 0)
        def _():
            write(i, mine_ref[i], recv_ref[i])

        @pl.when(yl != 0)
        def _():
            write(i, recv_ref[i], mine_ref[i])


BLOCK = jax.ShapeDtypeStruct((ROWS, COLS, WIDE), BF16)
STATE = jax.ShapeDtypeStruct((ROWS, 2 * COLS, WIDE), F32)


def pack(mine, recv, after):
    both = jax.ShapeDtypeStruct((ROWS, 2 * COLS, WIDE), BF16)
    turned = jax.ShapeDtypeStruct((ROWS, DH, 2 * COLS), BF16)
    return pl.pallas_call(
        pack_kernel,
        in_specs=[pl.BlockSpec(memory_space=pltpu.VMEM)] * 2 + [pl.BlockSpec(memory_space=pl.ANY)],
        out_shape=[BLOCK, both, both, turned, turned],
        compiler_params=params(),
        cost_estimate=cost(0.6),
        name="pack",
    )(mine, recv, after)


EXCHANGE = jax.ShapeDtypeStruct((16, 2, COLS, COLS), BF16)


def want_kernel(own_ref, oth_ref, out_ref):
    core = lax.axis_index("core")
    for h in range(H):
        for n in range(8):
            out_ref[n * H + h, core] = own_ref[h]
            out_ref[n * H + h, 1 - core] = oth_ref[h]


def want(own, oth):
    return pl.pallas_call(
        want_kernel,
        out_shape=EXCHANGE,
        compiler_params=params(),
        cost_estimate=cost(0.4),
        name="want",
    )(own, oth)


def bias_kernel(lift_ref, all_ref, near_ref, far_ref, late_ref):
    z = lax.axis_index("z")
    for group, out_ref in ((NEAR, near_ref), (FAR, far_ref), (LATE, late_ref)):
        for n, r in enumerate(group):
            at = lax.rem(z + r, RING)
            x, odd = at // 2, lax.rem(at, 2)
            for yh in range(2):
                start = (yh * len(group) + n) * COLS
                lift = lift_ref[yh * CHAINS + at]
                for yl in range(2):
                    rows = slice(yl * COLS, (yl + 1) * COLS)
                    block = all_ref[(yh * 4 + x) * 2 + yl, odd].astype(F32)
                    out_ref[rows, start : start + COLS] = block + lift


def bias_tables(lift, everything):
    return pl.pallas_call(
        bias_kernel,
        out_shape=[
            jax.ShapeDtypeStruct((2 * COLS, NC), F32),
            jax.ShapeDtypeStruct((2 * COLS, NF), F32),
            jax.ShapeDtypeStruct((2 * COLS, NL), F32),
        ],
        compiler_params=params(),
        cost_estimate=cost(0.5),
        name="bias_tables",
    )(lift, everything)


def join_kernel(block_ref, _, out_ref):
    out_ref[...] = block_ref[...]


def join(block, after):
    return pl.pallas_call(
        join_kernel,
        in_specs=[pl.BlockSpec(memory_space=pltpu.VMEM), pl.BlockSpec(memory_space=pl.ANY)],
        out_shape=BLOCK,
        compiler_params=params(),
        cost_estimate=cost(0.2),
        name="join",
    )(block, after)


def stack(refs, i):
    one = jnp.concatenate([ref[i] for ref in refs], axis=0)
    moved = pltpu.roll(one.astype(F32), 2 * DH, 1).astype(BF16)
    return jnp.concatenate([one, moved], axis=0)


def key_gradients(qt, dat, low, p_low, dkv_refs, i):
    dk = mm(qt, low, NN)
    dv = mm(dat, p_low, NN)
    half = dk.shape[1] // 2
    dkv = jnp.concatenate([dk[:, :half], dv[:, :half], dk[:, half:], dv[:, half:]], axis=0).T
    for n, ref in enumerate(dkv_refs):
        ref[i] = dkv[n * COLS : (n + 1) * COLS].astype(BF16)


def wide(value):
    return jnp.broadcast_to(value, (2 * COLS, WIDE))


def across(value, like):
    return jnp.concatenate([value] * (like.shape[1] // WIDE), axis=1)


def add_row(table_ref, i, value):
    if i == 0:
        table_ref[...] = value
    else:
        table_ref[...] += value


def staged(first, second, third):
    held = first(0)
    for i in range(ROWS):
        done = second(i, *held)
        if i + 1 < ROWS:
            following = first(i + 1)
        third(i, *done)
        held = following


def early_kernel(group, q_ref, da_ref, bias_ref, *refs):
    n = len(group)
    kv_refs, old_refs, (e_ref, *new_refs) = refs[:n], refs[n:-5], refs[-5:]
    acc_ref, total_ref, mass_ref, top_ref = new_refs

    def scores(i):
        kv = stack(kv_refs, i)
        return kv, mm(q_ref[i], kv, NT) + bias_ref[...], mm(da_ref[i], kv, NT)

    def weigh(i, kv, s, w):
        top = jnp.max(s, axis=1, keepdims=True)
        if old_refs:
            old = old_refs[3][i]
            top = jnp.maximum(top, old)
            fade = jnp.exp(old - top)
            e = jnp.exp(s - across(top, s))
        else:
            fade = None
            e = jnp.exp(s - top)
            top = wide(top)
        low = e.astype(BF16)
        e_ref[i] = low
        total = jnp.sum(e, axis=1, keepdims=True)
        mass = jnp.sum(e * w, axis=1, keepdims=True)
        if old_refs:
            total = total + old_refs[1][i] * fade
            mass = mass + old_refs[2][i] * fade
        total_ref[i] = wide(total)
        mass_ref[i] = wide(mass)
        top_ref[i] = top
        return kv, low, fade

    def gather(i, kv, low, fade):
        acc = mm(low, kv, NN)
        acc_ref[i] = acc + old_refs[0][i] * fade if old_refs else acc

    staged(scores, weigh, gather)


def early(group, q, da, bias, kvs, state):
    return pl.pallas_call(
        functools.partial(early_kernel, group),
        out_shape=[jax.ShapeDtypeStruct((ROWS, 2 * COLS, 2 * len(group) * COLS), BF16)]
        + [STATE] * 4,
        compiler_params=params(),
        cost_estimate=cost(4.0),
        name="early",
    )(q, da, bias, *[kvs[r] for r in group], *state)


def turn_kernel(
    q_ref, da_ref, qt_ref, dat_ref, bias_ref, near_top_ref,
    acc_ref, total_ref, mass_ref, top_ref, *refs,
):
    n = len(LATE)
    kv_refs, (u_ref, dot_ref, factor_ref, near_factor_ref) = refs[:n], refs[n : n + 4]
    dkv_refs, table_ref = refs[n + 4 : 2 * n + 4], refs[-1]
    lane = lanes((2 * COLS, WIDE))

    def scores(i):
        kv = stack(kv_refs, i)
        return kv, mm(q_ref[i], kv, NT) + bias_ref[...], mm(da_ref[i], kv, NT)

    def weigh(i, kv, s, w):
        old = top_ref[i]
        top = jnp.maximum(jnp.max(s, axis=1, keepdims=True), old)
        fade = jnp.exp(old - top)
        e = jnp.exp(s - across(top, s))
        inverse = 1.0 / (jnp.sum(e, axis=1, keepdims=True) + total_ref[i] * fade)
        factor = fade * inverse
        dot = (jnp.sum(e * w, axis=1, keepdims=True) + mass_ref[i] * fade) * inverse
        factor_ref[i] = factor
        near_factor_ref[i] = jnp.exp(near_top_ref[i] - top) * inverse
        dot_ref[i] = dot
        p = e * across(inverse, e)
        d = p * (w - across(dot, p))
        add_row(table_ref, i, d)
        return kv, p.astype(BF16), d.astype(BF16), factor

    def gather(i, kv, p_low, low, factor):
        key_gradients(qt_ref[i], dat_ref[i], low, p_low, dkv_refs, i)
        acc = mm(p_low, kv, NN) + acc_ref[i] * factor
        u_ref[i] = jnp.where(lane < DH, mm(low, kv, NN), acc)

    staged(scores, weigh, gather)


def turn(q, da, qt, dat, bias, near_top, state, kvs):
    return pl.pallas_call(
        turn_kernel,
        out_shape=[STATE] * 4
        + [BLOCK] * len(LATE)
        + [jax.ShapeDtypeStruct((2 * COLS, NL), F32)],
        compiler_params=params(),
        cost_estimate=cost(3.0),
        name="turn",
    )(q, da, qt, dat, bias, near_top, *state, *[kvs[r] for r in LATE])


def backward_kernel(
    group, _, da_ref, qt_ref, dat_ref, part_ref, dot_ref, factor_ref, e_ref, *refs
):
    n = len(group)
    kv_refs, u_ref, dkv_refs, table_ref = refs[:n], refs[n], refs[n + 1 : 2 * n + 1], refs[2 * n + 1]
    lane = lanes((2 * COLS, WIDE))

    def scores(i):
        kv = stack(kv_refs, i)
        return kv, mm(da_ref[i], kv, NT)

    def weigh(i, kv, w):
        p = e_ref[i].astype(F32)
        p = p * across(factor_ref[i], p)
        d = p * (w - across(dot_ref[i], p))
        add_row(table_ref, i, d)
        return kv, p.astype(BF16), d.astype(BF16)

    def gather(i, kv, p_low, low):
        u = part_ref[i]
        u_ref[i] = jnp.where(lane < DH, u + mm(low, kv, NN), u)
        key_gradients(qt_ref[i], dat_ref[i], low, p_low, dkv_refs, i)

    staged(scores, weigh, gather)


def backward(group, after, da, qt, dat, state, e, kvs, time):
    n = len(group)
    out = pl.pallas_call(
        functools.partial(backward_kernel, group),
        in_specs=[pl.BlockSpec(memory_space=pl.ANY)]
        + [pl.BlockSpec(memory_space=pltpu.VMEM)] * (7 + n),
        out_shape=[STATE]
        + [BLOCK] * n
        + [jax.ShapeDtypeStruct((2 * COLS, 2 * n * COLS), F32)],
        compiler_params=params(),
        cost_estimate=cost(time),
        name="backward",
    )(after, da, qt, dat, *state, e, *[kvs[r] for r in group])
    return out[0], dict(zip(group, out[1 : n + 1])), out[-1]


def split_kernel(near_ref, far_ref, late_ref, keep_ref, send_ref):
    core = lax.axis_index("core")
    z = lax.axis_index("z")

    def write(even_ref, odd_ref):
        for group, table in ((NEAR, near_ref), (FAR, far_ref), (LATE, late_ref)):
            for m, r in enumerate(group):
                ref = odd_ref if r % 2 else even_ref
                x = lax.rem(z + r, RING) // 2
                for yh in range(2):
                    start = (yh * len(group) + m) * COLS
                    for yl in range(2):
                        piece = table[yl * COLS : (yl + 1) * COLS, start : start + COLS]
                        ref[yh, x, yl] = piece.astype(ref.dtype)

    @pl.when(lax.rem(z + core, 2) == 0)
    def _():
        write(keep_ref, send_ref)

    @pl.when(lax.rem(z + core, 2) != 0)
    def _():
        write(send_ref, keep_ref)


def split_tables(near, far, late):
    blocks = (2, 4, 2, COLS, COLS)
    return pl.pallas_call(
        split_kernel,
        out_shape=[jax.ShapeDtypeStruct(blocks, F32), jax.ShapeDtypeStruct(blocks, BF16)],
        compiler_params=params(),
        cost_estimate=cost(1.0),
        name="split_tables",
    )(near, far, late)


def relay_kernel(up_ref, part_ref, keep_ref, recv_ref, sent_ref, summed_ref):
    sent_ref[...] = (up_ref[...].astype(F32) + part_ref[...].astype(F32)).astype(BF16)
    summed_ref[...] = (keep_ref[...] + recv_ref[...].astype(F32)).astype(BF16)


def relay(up, part, keep, recv):
    return pl.pallas_call(
        relay_kernel,
        out_shape=[BLOCK, jax.ShapeDtypeStruct(keep.shape, BF16)],
        compiler_params=params(),
        cost_estimate=cost(0.8),
        name="relay",
    )(up, part, keep, recv)


def gather_kernel(u_ref, a_ref, b_ref, near_ref, far_ref):
    lane = lanes((COLS, WIDE))
    lane2 = lanes((2 * COLS, WIDE))
    for i in range(ROWS):
        dkv = a_ref[i].astype(F32) + b_ref[i].astype(F32)
        u = jnp.where(lane2 < DH, u_ref[i] * SCALE, u_ref[i])
        u = pltpu.roll(u, 2 * DH, 1)
        near_ref[i] = jnp.where(lane < 2 * DH, dkv, u[:COLS])
        far_ref[i] = jnp.where(lane < 2 * DH, pltpu.roll(dkv, 2 * DH, 1), u[COLS:])


def gather_parts(u, a, b):
    shape = jax.ShapeDtypeStruct((ROWS, COLS, WIDE), F32)
    return pl.pallas_call(
        gather_kernel,
        out_shape=[shape, shape],
        compiler_params=params(),
        cost_estimate=cost(0.5),
        name="gather_parts",
    )(u, a, b)


def finish_kernel(first_ref, second_ref, last_ref, keep_ref, send_ref):
    yl = lax.axis_index("yl")
    lane = lanes((COLS, WIDE))

    def write(first_out, second_out):
        for i in range(ROWS):
            last = last_ref[i].astype(F32)
            first = first_ref[i] + jnp.where(lane < 2 * DH, last, 0.0)
            second = second_ref[i] + jnp.where(lane < 2 * DH, pltpu.roll(last, 2 * DH, 1), 0.0)
            first_out[i] = first.astype(first_out.dtype)
            second_out[i] = second.astype(second_out.dtype)

    @pl.when(yl == 0)
    def _():
        write(keep_ref, send_ref)

    @pl.when(yl != 0)
    def _():
        write(send_ref, keep_ref)


def finish(first, second, last):
    shape = (ROWS, COLS, WIDE)
    return pl.pallas_call(
        finish_kernel,
        out_shape=[jax.ShapeDtypeStruct(shape, F32), jax.ShapeDtypeStruct(shape, BF16)],
        compiler_params=params(),
        cost_estimate=cost(0.8),
        name="finish",
    )(first, second, last)


def product(value, gate, w, h):
    flat = (ROWS * COLS, WIDE)
    value = value.reshape(flat).astype(F32)
    value = jnp.where(lanes(flat) < 3 * DH, value, value * gate.reshape(flat)).astype(BF16)
    weight = jnp.where(h == 0, head_weight(w, 0).astype(F32), head_weight(w, 1).astype(F32))
    return mm(value, weight.astype(BF16), NT)


def keep_kernel(keep_ref, gate_ref, w_ref, out_ref):
    yl = lax.axis_index("yl")
    out_ref[...] = product(keep_ref[...], gate_ref[...], w_ref[...], yl)


def keep_product(keep, gate, w):
    return pl.pallas_call(
        keep_kernel,
        out_shape=jax.ShapeDtypeStruct((ROWS * COLS, WIDE), F32),
        compiler_params=params(),
        cost_estimate=cost(0.5),
        name="keep_product",
    )(keep, gate, w)


def table_kernel(parts_ref, bias_ref):
    for h in range(H):
        bias_ref[h] = sum(parts_ref[n * H + h].astype(F32) for n in range(8))


def table_sum(parts):
    return pl.pallas_call(
        table_kernel,
        out_shape=jax.ShapeDtypeStruct((H, COLS, COLS), F32),
        compiler_params=params(),
        cost_estimate=cost(0.3),
        name="table_sum",
    )(parts)


def output_kernel(kept_ref, recv_ref, gate_ref, w_ref, out_ref):
    yl = lax.axis_index("yl")
    other = product(recv_ref[...], gate_ref[...], w_ref[...], 1 - yl)
    out_ref[...] = (kept_ref[...] + other).astype(BF16).reshape(ROWS, COLS, WIDE)


def output(kept, recv, gate, w):
    return pl.pallas_call(
        output_kernel,
        out_shape=BLOCK,
        compiler_params=params(),
        cost_estimate=cost(0.5),
        name="output",
    )(kept, recv, gate, w)


def shift(value, step):
    return lax.ppermute(value, "z", [(z, (z + step) % RING) for z in range(RING)])


def swap(value, axis):
    return lax.ppermute(value, axis, [(0, 1), (1, 0)])


def added(a, b):
    return (a.astype(F32) + b.astype(F32)).astype(BF16)


def body(pair, w_qkvg, w_out, bias, chain_lengths, d_pair_out):
    peers = ("yh", "x", "yl")
    oth = swap(bias, "core")
    mine, other, lift = project(chain_lengths, pair, d_pair_out, w_qkvg, w_out)
    recv = swap(other, "yl")
    wanted = want(bias, oth)
    everything = lax.all_to_all(wanted, peers, 0, 0, tiled=True)
    kv, q, da, qt, dat = pack(mine, recv, wanted)
    kvs = [kv] + [None] * (RING - 1)
    kvs[1] = shift(kv, -1)
    kvs[7] = shift(kv, 1)
    kvs[2] = shift(kvs[1], -1)
    kvs[6] = shift(kvs[7], 1)
    kvs[3] = shift(kvs[2], -1)
    bias_near, bias_far, bias_late = bias_tables(lift, everything)
    e_near, *state = early(NEAR, q, da, bias_near, kvs, ())
    near_top = state[-1]
    kvs[4] = shift(join(kvs[3], near_top), -1)
    kvs[5] = shift(kvs[6], 1)
    e_far, *state = early(FAR, q, da, bias_far, kvs, state)
    u, dot, factor, near_factor, d4, d5, t_late = turn(
        q, da, qt, dat, bias_late, near_top, state, kvs
    )
    up = shift(d4, 1)
    down = shift(d5, -1)
    u, far, t_far = backward(FAR, d4, da, qt, dat, (u, dot, factor), e_far, kvs, 2.5)
    sent = added(up, far[3])
    up = shift(sent, 1)
    down = shift(added(down, far[6]), -1)
    u, near, t_near = backward(NEAR, sent, da, qt, dat, (u, dot, near_factor), e_near, kvs, 3.0)
    keep_table, send_table = split_tables(t_near, t_far, t_late)
    recv_table = swap(send_table, "core")
    sent3 = added(up, near[2])
    up = shift(sent3, 1)
    down = shift(added(down, near[7]), -1)
    up, summed = relay(up, near[1], keep_table, recv_table)
    up = shift(up, 1)
    parts = lax.all_to_all(summed.reshape(16, COLS, COLS), peers, 0, 0, tiled=True)
    gmine, gother = slopes(sent3, pair, d_pair_out, w_qkvg, w_out)
    first, second = gather_parts(u, near[0], down)
    keep, send = finish(first, second, up)
    recv = swap(send, "yl")
    kept = keep_product(keep, gmine, w_qkvg)
    return output(kept, recv, gother, w_qkvg), table_sum(parts)


def solution(mesh):
    split = Mesh(mesh.devices.reshape(2, 4, 2, 2, RING), ("yh", "x", "core", "yl", "z"))
    row, col = ("yh", "x", "core"), ("yl", "z")
    in_specs = (P(row, col, None), P(), P(), P(None, col, row), P(), P(row, col, None))
    out_specs = (P(row, col, None), P(None, col, row))
    return jax.shard_map(body, mesh=split, in_specs=in_specs, out_specs=out_specs, check_vma=False)
```

time: 89.8 us -> 84.8 us (0.944)
  waiting for transfers between devices: 28.7 us -> 17.5 us
  starting transfers between devices: 40.8 us -> 46.4 us
    ppermute x4, waiting for transfers between devices: 6.96 us -> 0.54 us  [swap(): return lax.ppermute(value, axis, [(0, 1), (1, 0)])]
    ppermute x14, waiting for transfers between devices: 17.7 us -> 13.6 us  [shift(): lax.ppermute(value, 'z', [(z, (z + step) % RING) for z in range(RING)])]
    all_to_all x1, waiting for transfers between devices: 4 us -> 0.01 us  [body(): everything = lax.all_to_all(wanted, peers, 0, 0, tiled=True)]
    ppermute x14, starting transfers between devices: 24.5 us -> 28.4 us  [shift(): lax.ppermute(value, 'z', [(z, (z + step) % RING) for z in range(RING)])]
    pallas_call x7 -> x14, Pallas kernels: 11.9 us -> 15.6 us  [the longest x2 3.54 us: early(): pl.pallas_call(functools.partial(early_kernel, group), out_shape=[jax.Sha...]
    all_to_all x1, waiting for transfers between devices: 0.01 us -> 3.33 us  [body(): lax.all_to_all(summed.reshape(16, COLS, COLS), peers, 0, 0, tiled=True)]
    pallas_call x1, Pallas kernels: 2.33 us -> 0.44 us  [split_tables(): pl.pallas_call(split_kernel, out_shape=[jax.ShapeDtypeStruct(blocks, F32)...]
    all_to_all x1, starting transfers between devices: 5.61 us -> 7.35 us  [body(): lax.all_to_all(summed.reshape(16, COLS, COLS), peers, 0, 0, tiled=True)]
  transfers between devices with their start and end apart: 20 -> 20, of which waited for: 8 -> 9; matrix products, arithmetic and copies ran while one was open for 1% -> 0% of each run, Pallas kernels for 13% -> 18%
where the time goes in v5:
time: 84.8 us; the launch traced here: 84.4 us
  starting transfers between devices  46.4 us (55%)
  Pallas kernels  18.7 us (22%)
  waiting for transfers between devices  17.5 us (21%)
    ppermute x14, starting transfers between devices, shift(): lax.ppermute(value, 'z', [(z, (z + step) % RING) for z in range(RING)])  28.4 us
    ppermute x14, waiting for transfers between devices, shift(): lax.ppermute(value, 'z', [(z, (z + step) % RING) for z in range(RING)])  13.6 us
    all_to_all x1, starting transfers between devices, body(): lax.all_to_all(summed.reshape(16, COLS, COLS), peers, 0, 0, tiled=True)  7.35 us
    all_to_all x1, starting transfers between devices, body(): everything = lax.all_to_all(wanted, peers, 0, 0, tiled=True)  7.19 us
    pallas_call x2, Pallas kernels, early(): pl.pallas_call(functools.partial(early_kernel, group), out_shape=[jax.Sha...  3.54 us
    ppermute x4, starting transfers between devices, swap(): return lax.ppermute(value, axis, [(0, 1), (1, 0)])  3.4 us
    pallas_call x2, Pallas kernels, backward(): pl.pallas_call(functools.partial(backward_kernel, group), in_specs=[pl.Bl...  3.39 us
    all_to_all x1, waiting for transfers between devices, body(): lax.all_to_all(summed.reshape(16, COLS, COLS), peers, 0, 0, tiled=True)  3.33 us
  transfers between devices with their start and end apart: 20, of which 9 were waited for; matrix products, arithmetic and copies ran while one was open for 0% of the time, Pallas kernels for 18%

profile of v5, /device:TPU:2, one launch (start us, length us, event | category | flops | bytes accessed | tf_op | source)
XLA Modules:
  0.0 84.4 jit_solution(13564202083688765147)
XLA Ops:
  0.7 1.7 %project.1 = (bf16[6,96,128]{2,1,0:T(8,128)(2,1)S(1)}, bf16[6,96,128]{2,1,0:T(8,128)(2,1)S(1)}, f32[16,1,96]{2,1,0:T(1,128)S(1)}) custom-call(s32[8]{0:T(128)} %len_hbm.1, bf16[6,96,128]{2,1,0:T(8,128)(2,1)} %pair_hbm.3, bf16[6,96,128]{2,1,0:T(8,128)(2,1)} %grad_hbm.3, bf16[128,256]{1,0:T(8,128)(2,1)} %w_ref.3, bf16[64,128]{1,0:T(8,128)(2,1)} %wout_hbm.3), custom_call_target="tpu_custom_call" | custom-call | bytes 200000 | tf_op jit(solution)/shard_map/project/pallas_call | solution.py:107
  2.4 1.7 %collective-permute-start = (bf16[6,96,128]{2,1,0:T(8,128)(2,1)S(1)}, bf16[6,96,128]{2,1,0:T(8,128)(2,1)S(1)}, u32[]{:S(2)}, u32[]{:S(2)}) collective-permute-start(bf16[6,96,128]{2,1,0:T(8,128)(2,1)S(1)} %get-tuple-element.51), channel_id=1, source_target_pairs={{0,8},{8,0},{1,9},{9,1},{2,10},{10,2},{3,11},{11,3},{4,12},{12,4},... | collective-permute-start | bytes 442376 | tf_op jit(solution)/shard_map/ppermute | solution.py:629
  5.9 7.2 %all-to-all-start = ((bf16[16,2,96,96]{3,2,1,0:T(8,128)(2,1)}), bf16[16,2,96,96]{3,2,1,0:T(8,128)(2,1)S(1)}, u32[]{:S(2)}, u32[]{:S(2)}) async-start(bf16[16,2,96,96]{3,2,1,0:T(8,128)(2,1)} %want.1._), calls=%async_computation | async-start | bytes 1572864 | tf_op jit(solution)/shard_map/all_to_all | solution.py:642
  13.9 5.9 %collective-permute-start.2 = (bf16[6,96,128]{2,1,0:T(8,128)(2,1)S(1)}, bf16[6,96,128]{2,1,0:T(8,128)(2,1)S(1)}, u32[]{:S(2)}, u32[]{:S(2)}) collective-permute-start(bf16[6,96,128]{2,1,0:T(8,128)(2,1)S(1)} %get-tuple-element.59.refs_0_), channel_id=1, source_target_pairs={{0,7},{1,0},{2,1},{3,2},{4,3},{5,4},{6,5},{7,6},{8,15},{9,8},{10,9... | collective-permute-start | bytes 442376 | tf_op jit(solution)/shard_map/ppermute | solution.py:625
  19.8 2.9 %collective-permute-done.2.refs_1_ = bf16[6,96,128]{2,1,0:T(8,128)(2,1)S(1)} collective-permute-done((bf16[6,96,128]{2,1,0:T(8,128)(2,1)S(1)}, bf16[6,96,128]{2,1,0:T(8,128)(2,1)S(1)}, u32[]{:S(2)}, u32[]{:S(2)}) %collective-permute-start.2) | collective-permute-done | bytes 147488 | tf_op jit(solution)/shard_map/ppermute | solution.py:625
  22.8 3.7 %collective-permute-start.4 = (bf16[6,96,128]{2,1,0:T(8,128)(2,1)S(1)}, bf16[6,96,128]{2,1,0:T(8,128)(2,1)S(1)}, u32[]{:S(2)}, u32[]{:S(2)}) collective-permute-start(bf16[6,96,128]{2,1,0:T(8,128)(2,1)S(1)} %collective-permute-done.2.refs_1_), channel_id=1, source_target_pairs={{0,7},{1,0},{2,1},{3,2},{4,3},{5,4},{6,5},{7,6},{8,15},{9,8},{10,9... | collective-permute-start | bytes 442376 | tf_op jit(solution)/shard_map/ppermute | solution.py:625
  26.5 2.7 %collective-permute-done.4.refs_3_ = bf16[6,96,128]{2,1,0:T(8,128)(2,1)S(1)} collective-permute-done((bf16[6,96,128]{2,1,0:T(8,128)(2,1)S(1)}, bf16[6,96,128]{2,1,0:T(8,128)(2,1)S(1)}, u32[]{:S(2)}, u32[]{:S(2)}) %collective-permute-start.4) | collective-permute-done | bytes 147488 | tf_op jit(solution)/shard_map/ppermute | solution.py:625
  29.1 3.7 %collective-permute-start.5 = (bf16[6,96,128]{2,1,0:T(8,128)(2,1)S(1)}, bf16[6,96,128]{2,1,0:T(8,128)(2,1)S(1)}, u32[]{:S(2)}, u32[]{:S(2)}) collective-permute-start(bf16[6,96,128]{2,1,0:T(8,128)(2,1)S(1)} %collective-permute-done.4.refs_3_), channel_id=1, source_target_pairs={{0,7},{1,0},{2,1},{3,2},{4,3},{5,4},{6,5},{7,6},{8,15},{9,8},{10,9... | collective-permute-start | bytes 442376 | tf_op jit(solution)/shard_map/ppermute | solution.py:625
  33.2 2.1 %early.2 = (bf16[6,192,768]{2,1,0:T(8,128)(2,1)S(1)}, f32[6,192,128]{2,1,0:T(8,128)S(1)}, f32[6,192,128]{2,1,0:T(8,128)S(1)}, f32[6,192,128]{2,1,0:T(8,128)S(1)}, f32[6,192,128]{2,1,0:T(8,128)S(1)}) custom-call(bf16[6,192,128]{2,1,0:T(8,128)(2,1)S(1)} %get-tuple-element.52.q_ref, bf16[6,192,128]{2,1,0:T(8,128)(2,1)S(1)} %get-tuple-element.53.da_ref, ...), custom_call_target="tpu_custom_call" | custom-call | bytes 400000 | tf_op jit(solution)/shard_map/early/pallas_call | solution.py:365
  35.5 3.9 %collective-permute-start.7 = (bf16[6,96,128]{2,1,0:T(8,128)(2,1)S(1)}, bf16[6,96,128]{2,1,0:T(8,128)(2,1)S(1)}, u32[]{:S(2)}, u32[]{:S(2)}) collective-permute-start(bf16[6,96,128]{2,1,0:T(8,128)(2,1)S(1)} %join.1), channel_id=1, source_target_pairs={{0,7},{1,0},{2,1},{3,2},{4,3},{5,4},{6,5},{7,6},{8,15},{9,8},{10,9... | collective-permute-start | bytes 442376 | tf_op jit(solution)/shard_map/ppermute | solution.py:625
  39.4 1.4 %early.3 = (bf16[6,192,384]{2,1,0:T(8,128)(2,1)S(1)}, f32[6,192,128]{2,1,0:T(8,128)S(1)}, f32[6,192,128]{2,1,0:T(8,128)S(1)}, f32[6,192,128]{2,1,0:T(8,128)S(1)}, f32[6,192,128]{2,1,0:T(8,128)S(1)}) custom-call(bf16[6,192,128]{2,1,0:T(8,128)(2,1)S(1)} %get-tuple-element.52.q_ref, bf16[6,192,128]{2,1,0:T(8,128)(2,1)S(1)} %get-tuple-element.53.da_ref, ...), custom_call_target="tpu_custom_call" | custom-call | bytes 400000 | tf_op jit(solution)/shard_map/early/pallas_call | solution.py:365
  40.9 1.3 %collective-permute-done.7.refs_0_ = bf16[6,96,128]{2,1,0:T(8,128)(2,1)S(1)} collective-permute-done((bf16[6,96,128]{2,1,0:T(8,128)(2,1)S(1)}, bf16[6,96,128]{2,1,0:T(8,128)(2,1)S(1)}, u32[]{:S(2)}, u32[]{:S(2)}) %collective-permute-start.7) | collective-permute-done | bytes 147488 | tf_op jit(solution)/shard_map/ppermute | solution.py:625
  42.1 2.6 %turn.1 = (f32[6,192,128]{2,1,0:T(8,128)S(1)}, f32[6,192,128]{2,1,0:T(8,128)S(1)}, f32[6,192,128]{2,1,0:T(8,128)S(1)}, f32[6,192,128]{2,1,0:T(8,128)S(1)}, bf16[...) custom-call(bf16[6,192,128]{2,1,0:T(8,128)(2,1)S(1)} %get-tuple-element.52.q_ref, ...), custom_call_target="tpu_custom_call" | custom-call | bytes 300000 | tf_op jit(solution)/shard_map/turn/pallas_call | solution.py:413
  44.8 3.8 %collective-permute-start.10 = (bf16[6,96,128]{2,1,0:T(8,128)(2,1)S(1)}, bf16[6,96,128]{2,1,0:T(8,128)(2,1)S(1)}, u32[]{:S(2)}, u32[]{:S(2)}) collective-permute-start(bf16[6,96,128]{2,1,0:T(8,128)(2,1)S(1)} %get-tuple-element.80), channel_id=1, source_target_pairs={{0,7},{1,0},{2,1},{3,2},{4,3},{5,4},{6,5},{7,6},{8,15},{9,8},{10,9... | collective-permute-start | bytes 442376 | tf_op jit(solution)/shard_map/ppermute | solution.py:625
  48.6 1.4 %backward.2 = (f32[6,192,128]{2,1,0:T(8,128)S(1)}, bf16[6,96,128]{2,1,0:T(8,128)(2,1)S(1)}, bf16[6,96,128]{2,1,0:T(8,128)(2,1)S(1)}, f32[192,384]{1,0:T(8,128)S(1)}) custom-call(bf16[6,96,128]{2,1,0:T(8,128)(2,1)S(1)} %get-tuple-element.69._, bf16[6,192,128]{2,1,0:T(8,128)(2,1)S(1)} %get-tuple-element.53.da_ref, ...), custom_call_target="tpu_custom_call" | custom-call | bytes 250000 | tf_op jit(solution)/shard_map/backward/pallas_call | solution.py:452
  50.0 3.0 %collective-permute-done.9 = bf16[6,96,128]{2,1,0:T(8,128)(2,1)S(1)} collective-permute-done((bf16[6,96,128]{2,1,0:T(8,128)(2,1)S(1)}, bf16[6,96,128]{2,1,0:T(8,128)(2,1)S(1)}, u32[]{:S(2)}, u32[]{:S(2)}) %collective-permute-start.9) | collective-permute-done | bytes 147488 | tf_op jit(solution)/shard_map/ppermute | solution.py:625
  53.2 3.5 %collective-permute-start.11 = (bf16[6,96,128]{2,1,0:T(8,128)(2,1)S(1)}, bf16[6,96,128]{2,1,0:T(8,128)(2,1)S(1)}, u32[]{:S(2)}, u32[]{:S(2)}) collective-permute-start(bf16[6,96,128]{2,1,0:T(8,128)(2,1)S(1)} %add_convert_fusion.2), channel_id=1, source_target_pairs={{0,7},{1,0},{2,1},{3,2},{4,3},{5,4},{6,5},{7,6},{8,15},{9,8},{10,9... | collective-permute-start | bytes 442376 | tf_op jit(solution)/shard_map/ppermute | solution.py:625
  56.6 2.0 %backward.3 = (f32[6,192,128]{2,1,0:T(8,128)S(1)}, bf16[6,96,128]{2,1,0:T(8,128)(2,1)S(1)}, bf16[6,96,128]{2,1,0:T(8,128)(2,1)S(1)}, bf16[6,96,128]{2,1,0:T(8,12...) custom-call(bf16[6,96,128]{2,1,0:T(8,128)(2,1)S(1)} %add_convert_fusion.3._, ...), custom_call_target="tpu_custom_call" | custom-call | bytes 300000 | tf_op jit(solution)/shard_map/backward/pallas_call | solution.py:452
  59.6 3.7 %collective-permute-start.12 = (bf16[6,96,128]{2,1,0:T(8,128)(2,1)S(1)}, bf16[6,96,128]{2,1,0:T(8,128)(2,1)S(1)}, u32[]{:S(2)}, u32[]{:S(2)}) collective-permute-start(bf16[6,96,128]{2,1,0:T(8,128)(2,1)S(1)} %add_convert_fusion.1), channel_id=1, source_target_pairs={{0,7},{1,0},{2,1},{3,2},{4,3},{5,4},{6,5},{7,6},{8,15},{9,8},{10,9... | collective-permute-start | bytes 442376 | tf_op jit(solution)/shard_map/ppermute | solution.py:625
  63.3 3.4 %collective-permute-done.14.up_ref = bf16[6,96,128]{2,1,0:T(8,128)(2,1)S(1)} collective-permute-done((bf16[6,96,128]{2,1,0:T(8,128)(2,1)S(1)}, bf16[6,96,128]{2,1,0:T(8,128)(2,1)S(1)}, u32[]{:S(2)}, u32[]{:S(2)}) %collective-permute-start.14) | collective-permute-done | bytes 147488 | tf_op jit(solution)/shard_map/ppermute | solution.py:625
  67.6 7.3 %all-to-all-start.1 = ((bf16[16,96,96]{2,1,0:T(8,128)(2,1)}), bf16[16,96,96]{2,1,0:T(8,128)(2,1)S(1)}, u32[]{:S(2)}, u32[]{:S(2)}) async-start(bf16[16,96,96]{2,1,0:T(8,128)(2,1)} %bitcast), calls=%async_computation.1 | async-start | bytes 786432 | tf_op jit(solution)/shard_map/all_to_all | solution.py:673
  75.4 1.5 %collective-permute-start.17 = (bf16[6,96,128]{2,1,0:T(8,128)(2,1)S(1)}, bf16[6,96,128]{2,1,0:T(8,128)(2,1)S(1)}, u32[]{:S(2)}, u32[]{:S(2)}) collective-permute-start(bf16[6,96,128]{2,1,0:T(8,128)(2,1)S(1)} %get-tuple-element.95), channel_id=1, source_target_pairs={{0,8},{8,0},{1,9},{9,1},{2,10},{10,2},{3,11},{11,3},{4,12},{12,4},... | collective-permute-start | bytes 442376 | tf_op jit(solution)/shard_map/ppermute | solution.py:629
  76.9 1.7 %slopes.1 = (f32[6,96,128]{2,1,0:T(8,128)S(1)}, f32[6,96,128]{2,1,0:T(8,128)S(1)}) custom-call(bf16[6,96,128]{2,1,0:T(8,128)(2,1)S(1)} %add_convert_fusion._, bf16[6,96,128]{2,1,0:T(8,128)(2,1)} %pair_hbm.3, bf16[6,96,128]{2,1,0:T(8,128)(2,1)} %grad_hbm.3, bf16[128,256]{1,0:T(8,128)(2,1)} %w_ref.3, bf16[64,128]{1,0:T(8,128)(2,1)} %wout_hbm.3), custom_call_target="tpu_custom_call" | custom-call | bytes 200000 | tf_op jit(solution)/shard_map/slopes/pallas_call | solution.py:159
  78.9 3.3 %all-to-all-done.1.parts_ref = bf16[16,96,96]{2,1,0:T(8,128)(2,1)S(1)} async-done(((bf16[16,96,96]{2,1,0:T(8,128)(2,1)}), bf16[16,96,96]{2,1,0:T(8,128)(2,1)S(1)}, u32[]{:S(2)}, u32[]{:S(2)}) %all-to-all-start.1) | async-done | bytes 294944 | tf_op jit(solution)/shard_map/all_to_all | solution.py:673
  (42 shorter events, 8.2 us)
Async XLA Ops:
  0.6 3.5 %collective-permute-start.1 = (bf16[2,96,96]{2,1,0:T(8,128)(2,1)}, bf16[2,96,96]{2,1,0:T(8,128)(2,1)S(1)}, u32[]{:S(2)}, u32[]{:S(2)}) collective-permute-start(bf16[2,96,96]{2,1,0:T(8,128)(2,1)} %own_ref.1), channel_id=1, source_target_pairs={{0,16},{16,0},{1,17},{17,1},{2,18},{18,2},{3,19},{19,3},{4,20},{20... | collective-permute-start | bytes 110600 | tf_op jit(solution)/shard_map/ppermute | solution.py:629
  2.4 10.7 %collective-permute-start = (bf16[6,96,128]{2,1,0:T(8,128)(2,1)S(1)}, bf16[6,96,128]{2,1,0:T(8,128)(2,1)S(1)}, u32[]{:S(2)}, u32[]{:S(2)}) collective-permute-start(bf16[6,96,128]{2,1,0:T(8,128)(2,1)S(1)} %get-tuple-element.51), channel_id=1, source_target_pairs={{0,8},{8,0},{1,9},{9,1},{2,10},{10,2},{3,11},{11,3},{4,12},{12,4},... | collective-permute-start | bytes 442376 | tf_op jit(solution)/shard_map/ppermute | solution.py:629
  4.1 0.8 copy-start.1
  5.9 26.9 %all-to-all-start = ((bf16[16,2,96,96]{3,2,1,0:T(8,128)(2,1)}), bf16[16,2,96,96]{3,2,1,0:T(8,128)(2,1)S(1)}, u32[]{:S(2)}, u32[]{:S(2)}) async-start(bf16[16,2,96,96]{3,2,1,0:T(8,128)(2,1)} %want.1._), calls=%async_computation | async-start | bytes 1572864 | tf_op jit(solution)/shard_map/all_to_all | solution.py:642
  13.9 8.9 %collective-permute-start.2 = (bf16[6,96,128]{2,1,0:T(8,128)(2,1)S(1)}, bf16[6,96,128]{2,1,0:T(8,128)(2,1)S(1)}, u32[]{:S(2)}, u32[]{:S(2)}) collective-permute-start(bf16[6,96,128]{2,1,0:T(8,128)(2,1)S(1)} %get-tuple-element.59.refs_0_), channel_id=1, source_target_pairs={{0,7},{1,0},{2,1},{3,2},{4,3},{5,4},{6,5},{7,6},{8,15},{9,8},{10,9... | collective-permute-start | bytes 442376 | tf_op jit(solution)/shard_map/ppermute | solution.py:625
  19.8 6.6 %collective-permute-start.3 = (bf16[6,96,128]{2,1,0:T(8,128)(2,1)S(1)}, bf16[6,96,128]{2,1,0:T(8,128)(2,1)S(1)}, u32[]{:S(2)}, u32[]{:S(2)}) collective-permute-start(bf16[6,96,128]{2,1,0:T(8,128)(2,1)S(1)} %get-tuple-element.59.refs_0_), channel_id=1, source_target_pairs={{0,1},{1,2},{2,3},{3,4},{4,5},{5,6},{6,7},{7,0},{8,9},{9,10},{10,1... | collective-permute-start | bytes 442376 | tf_op jit(solution)/shard_map/ppermute | solution.py:625
  22.8 6.4 %collective-permute-start.4 = (bf16[6,96,128]{2,1,0:T(8,128)(2,1)S(1)}, bf16[6,96,128]{2,1,0:T(8,128)(2,1)S(1)}, u32[]{:S(2)}, u32[]{:S(2)}) collective-permute-start(bf16[6,96,128]{2,1,0:T(8,128)(2,1)S(1)} %collective-permute-done.2.refs_1_), channel_id=1, source_target_pairs={{0,7},{1,0},{2,1},{3,2},{4,3},{5,4},{6,5},{7,6},{8,15},{9,8},{10,9... | collective-permute-start | bytes 442376 | tf_op jit(solution)/shard_map/ppermute | solution.py:625
  26.5 6.4 %collective-permute-start.6 = (bf16[6,96,128]{2,1,0:T(8,128)(2,1)S(1)}, bf16[6,96,128]{2,1,0:T(8,128)(2,1)S(1)}, u32[]{:S(2)}, u32[]{:S(2)}) collective-permute-start(bf16[6,96,128]{2,1,0:T(8,128)(2,1)S(1)} %collective-permute-done.3.refs_2_), channel_id=1, source_target_pairs={{0,1},{1,2},{2,3},{3,4},{4,5},{5,6},{6,7},{7,0},{8,9},{9,10},{10,1... | collective-permute-start | bytes 442376 | tf_op jit(solution)/shard_map/ppermute | solution.py:625
  29.1 6.4 %collective-permute-start.5 = (bf16[6,96,128]{2,1,0:T(8,128)(2,1)S(1)}, bf16[6,96,128]{2,1,0:T(8,128)(2,1)S(1)}, u32[]{:S(2)}, u32[]{:S(2)}) collective-permute-start(bf16[6,96,128]{2,1,0:T(8,128)(2,1)S(1)} %collective-permute-done.4.refs_3_), channel_id=1, source_target_pairs={{0,7},{1,0},{2,1},{3,2},{4,3},{5,4},{6,5},{7,6},{8,15},{9,8},{10,9... | collective-permute-start | bytes 442376 | tf_op jit(solution)/shard_map/ppermute | solution.py:625
  32.8 8.0 %collective-permute-start.8 = (bf16[6,96,128]{2,1,0:T(8,128)(2,1)S(1)}, bf16[6,96,128]{2,1,0:T(8,128)(2,1)S(1)}, u32[]{:S(2)}, u32[]{:S(2)}) collective-permute-start(bf16[6,96,128]{2,1,0:T(8,128)(2,1)S(1)} %collective-permute-done.6.refs_1_), channel_id=1, source_target_pairs={{0,1},{1,2},{2,3},{3,4},{4,5},{5,6},{6,7},{7,0},{8,9},{9,10},{10,1... | collective-permute-start | bytes 442376 | tf_op jit(solution)/shard_map/ppermute | solution.py:625
  35.5 6.6 %collective-permute-start.7 = (bf16[6,96,128]{2,1,0:T(8,128)(2,1)S(1)}, bf16[6,96,128]{2,1,0:T(8,128)(2,1)S(1)}, u32[]{:S(2)}, u32[]{:S(2)}) collective-permute-start(bf16[6,96,128]{2,1,0:T(8,128)(2,1)S(1)} %join.1), channel_id=1, source_target_pairs={{0,7},{1,0},{2,1},{3,2},{4,3},{5,4},{6,5},{7,6},{8,15},{9,8},{10,9... | collective-permute-start | bytes 442376 | tf_op jit(solution)/shard_map/ppermute | solution.py:625
  44.7 8.2 %collective-permute-start.9 = (bf16[6,96,128]{2,1,0:T(8,128)(2,1)S(1)}, bf16[6,96,128]{2,1,0:T(8,128)(2,1)S(1)}, u32[]{:S(2)}, u32[]{:S(2)}) collective-permute-start(bf16[6,96,128]{2,1,0:T(8,128)(2,1)S(1)} %get-tuple-element.69._), channel_id=1, source_target_pairs={{0,1},{1,2},{2,3},{3,4},{4,5},{5,6},{6,7},{7,0},{8,9},{9,10},{10,1... | collective-permute-start | bytes 442376 | tf_op jit(solution)/shard_map/ppermute | solution.py:625
  44.8 8.3 %collective-permute-start.10 = (bf16[6,96,128]{2,1,0:T(8,128)(2,1)S(1)}, bf16[6,96,128]{2,1,0:T(8,128)(2,1)S(1)}, u32[]{:S(2)}, u32[]{:S(2)}) collective-permute-start(bf16[6,96,128]{2,1,0:T(8,128)(2,1)S(1)} %get-tuple-element.80), channel_id=1, source_target_pairs={{0,7},{1,0},{2,1},{3,2},{4,3},{5,4},{6,5},{7,6},{8,15},{9,8},{10,9... | collective-permute-start | bytes 442376 | tf_op jit(solution)/shard_map/ppermute | solution.py:625
  53.0 6.4 %collective-permute-start.13 = (bf16[6,96,128]{2,1,0:T(8,128)(2,1)S(1)}, bf16[6,96,128]{2,1,0:T(8,128)(2,1)S(1)}, u32[]{:S(2)}, u32[]{:S(2)}) collective-permute-start(bf16[6,96,128]{2,1,0:T(8,128)(2,1)S(1)} %add_convert_fusion.3._), channel_id=1, source_target_pairs={{0,1},{1,2},{2,3},{3,4},{4,5},{5,6},{6,7},{7,0},{8,9},{9,10},{10,1... | collective-permute-start | bytes 442376 | tf_op jit(solution)/shard_map/ppermute | solution.py:625
  53.2 6.4 %collective-permute-start.11 = (bf16[6,96,128]{2,1,0:T(8,128)(2,1)S(1)}, bf16[6,96,128]{2,1,0:T(8,128)(2,1)S(1)}, u32[]{:S(2)}, u32[]{:S(2)}) collective-permute-start(bf16[6,96,128]{2,1,0:T(8,128)(2,1)S(1)} %add_convert_fusion.2), channel_id=1, source_target_pairs={{0,7},{1,0},{2,1},{3,2},{4,3},{5,4},{6,5},{7,6},{8,15},{9,8},{10,9... | collective-permute-start | bytes 442376 | tf_op jit(solution)/shard_map/ppermute | solution.py:625
  59.1 7.7 %collective-permute-start.15 = (bf16[2,4,2,96,96]{4,3,2,1,0:T(8,128)(2,1)S(1)}, bf16[2,4,2,96,96]{4,3,2,1,0:T(8,128)(2,1)S(1)}, u32[]{:S(2)}, u32[]{:S(2)}) collective-permute-start(bf16[2,4,2,96,96]{4,3,2,1,0:T(8,128)(2,1)S(1)} %get-tuple-element.91), channel_id=1, source_target_pairs={{0,16},{16,0},{1,17},{17,1},{2,18},{18,2},{3,19},{19,3},{4,20},{20... | collective-permute-start | bytes 884744 | tf_op jit(solution)/shard_map/ppermute | solution.py:629
  59.5 7.3 %collective-permute-start.14 = (bf16[6,96,128]{2,1,0:T(8,128)(2,1)S(1)}, bf16[6,96,128]{2,1,0:T(8,128)(2,1)S(1)}, u32[]{:S(2)}, u32[]{:S(2)}) collective-permute-start(bf16[6,96,128]{2,1,0:T(8,128)(2,1)S(1)} %add_convert_fusion._), channel_id=1, source_target_pairs={{0,1},{1,2},{2,3},{3,4},{4,5},{5,6},{6,7},{7,0},{8,9},{9,10},{10,1... | collective-permute-start | bytes 442376 | tf_op jit(solution)/shard_map/ppermute | solution.py:625
  59.6 15.3 %collective-permute-start.12 = (bf16[6,96,128]{2,1,0:T(8,128)(2,1)S(1)}, bf16[6,96,128]{2,1,0:T(8,128)(2,1)S(1)}, u32[]{:S(2)}, u32[]{:S(2)}) collective-permute-start(bf16[6,96,128]{2,1,0:T(8,128)(2,1)S(1)} %add_convert_fusion.1), channel_id=1, source_target_pairs={{0,7},{1,0},{2,1},{3,2},{4,3},{5,4},{6,5},{7,6},{8,15},{9,8},{10,9... | collective-permute-start | bytes 442376 | tf_op jit(solution)/shard_map/ppermute | solution.py:625
  67.6 11.0 %copy-start = (bf16[128,256]{1,0:T(8,128)(2,1)S(1)}, bf16[128,256]{1,0:T(8,128)(2,1)}, u32[]{:S(2)}) copy-start(bf16[128,256]{1,0:T(8,128)(2,1)} %w_ref.3) | copy-start | bytes 196612
  67.6 7.7 %collective-permute-start.16 = (bf16[6,96,128]{2,1,0:T(8,128)(2,1)S(1)}, bf16[6,96,128]{2,1,0:T(8,128)(2,1)S(1)}, u32[]{:S(2)}, u32[]{:S(2)}) collective-permute-start(bf16[6,96,128]{2,1,0:T(8,128)(2,1)S(1)} %get-tuple-element.92), channel_id=1, source_target_pairs={{0,1},{1,2},{2,3},{3,4},{4,5},{5,6},{6,7},{7,0},{8,9},{9,10},{10,1... | collective-permute-start | bytes 442376 | tf_op jit(solution)/shard_map/ppermute | solution.py:625
  67.6 14.6 %all-to-all-start.1 = ((bf16[16,96,96]{2,1,0:T(8,128)(2,1)}), bf16[16,96,96]{2,1,0:T(8,128)(2,1)S(1)}, u32[]{:S(2)}, u32[]{:S(2)}) async-start(bf16[16,96,96]{2,1,0:T(8,128)(2,1)} %bitcast), calls=%async_computation.1 | async-start | bytes 786432 | tf_op jit(solution)/shard_map/all_to_all | solution.py:673
  75.4 8.1 %collective-permute-start.17 = (bf16[6,96,128]{2,1,0:T(8,128)(2,1)S(1)}, bf16[6,96,128]{2,1,0:T(8,128)(2,1)S(1)}, u32[]{:S(2)}, u32[]{:S(2)}) collective-permute-start(bf16[6,96,128]{2,1,0:T(8,128)(2,1)S(1)} %get-tuple-element.95), channel_id=1, source_target_pairs={{0,8},{8,0},{1,9},{9,1},{2,10},{10,2},{3,11},{11,3},{4,12},{12,4},... | collective-permute-start | bytes 442376 | tf_op jit(solution)/shard_map/ppermute | solution.py:629

commit v6 on v5

--- a/solution.py
+++ b/solution.py
@@ -22,10 +22,9 @@
 HALF = RING * COLS
 KEYS = 2 * HALF
 WIDE = 128
-NEAR = (0, 1, 7, 2)
-FAR = (3, 6)
-LATE = (4, 5)
-NC, NF, NL = (2 * len(group) * COLS for group in (NEAR, FAR, LATE))
+NEAR = (0, 1, 7, 2, 6)
+LATE = (3, 4, 5)
+NC, NL = (2 * len(group) * COLS for group in (NEAR, LATE))
 
 
 NT = (((1,), (1,)), ((), ()))
@@ -238,9 +237,9 @@
     )(own, oth)
 
 
-def bias_kernel(lift_ref, all_ref, near_ref, far_ref, late_ref):
+def bias_kernel(lift_ref, all_ref, near_ref, late_ref):
     z = lax.axis_index("z")
-    for group, out_ref in ((NEAR, near_ref), (FAR, far_ref), (LATE, late_ref)):
+    for group, out_ref in ((NEAR, near_ref), (LATE, late_ref)):
         for n, r in enumerate(group):
             at = lax.rem(z + r, RING)
             x, odd = at // 2, lax.rem(at, 2)
@@ -258,7 +257,6 @@
         bias_kernel,
         out_shape=[
             jax.ShapeDtypeStruct((2 * COLS, NC), F32),
-            jax.ShapeDtypeStruct((2 * COLS, NF), F32),
             jax.ShapeDtypeStruct((2 * COLS, NL), F32),
         ],
         compiler_params=params(),
@@ -302,7 +300,8 @@
 
 
 def across(value, like):
-    return jnp.concatenate([value] * (like.shape[1] // WIDE), axis=1)
+    width = like.shape[1]
+    return jnp.concatenate([value] * pl.cdiv(width, WIDE), axis=1)[:, :width]
 
 
 def add_row(table_ref, i, value):
@@ -322,10 +321,9 @@
         held = following
 
 
-def early_kernel(group, q_ref, da_ref, bias_ref, *refs):
-    n = len(group)
-    kv_refs, old_refs, (e_ref, *new_refs) = refs[:n], refs[n:-5], refs[-5:]
-    acc_ref, total_ref, mass_ref, top_ref = new_refs
+def early_kernel(q_ref, da_ref, bias_ref, *refs):
+    n = len(NEAR)
+    kv_refs, (e_ref, acc_ref, total_ref, mass_ref, top_ref) = refs[:n], refs[n:]
 
     def scores(i):
         kv = stack(kv_refs, i)
@@ -333,52 +331,36 @@
 
     def weigh(i, kv, s, w):
         top = jnp.max(s, axis=1, keepdims=True)
-        if old_refs:
-            old = old_refs[3][i]
-            top = jnp.maximum(top, old)
-            fade = jnp.exp(old - top)
-            e = jnp.exp(s - across(top, s))
-        else:
-            fade = None
-            e = jnp.exp(s - top)
-            top = wide(top)
+        e = jnp.exp(s - top)
         low = e.astype(BF16)
         e_ref[i] = low
-        total = jnp.sum(e, axis=1, keepdims=True)
-        mass = jnp.sum(e * w, axis=1, keepdims=True)
-        if old_refs:
-            total = total + old_refs[1][i] * fade
-            mass = mass + old_refs[2][i] * fade
-        total_ref[i] = wide(total)
-        mass_ref[i] = wide(mass)
-        top_ref[i] = top
-        return kv, low, fade
-
-    def gather(i, kv, low, fade):
-        acc = mm(low, kv, NN)
-        acc_ref[i] = acc + old_refs[0][i] * fade if old_refs else acc
+        total_ref[i] = wide(jnp.sum(e, axis=1, keepdims=True))
+        mass_ref[i] = wide(jnp.sum(e * w, axis=1, keepdims=True))
+        top_ref[i] = wide(top)
+        return kv, low
+
+    def gather(i, kv, low):
+        acc_ref[i] = mm(low, kv, NN)
 
     staged(scores, weigh, gather)
 
 
-def early(group, q, da, bias, kvs, state):
-    return pl.pallas_call(
-        functools.partial(early_kernel, group),
-        out_shape=[jax.ShapeDtypeStruct((ROWS, 2 * COLS, 2 * len(group) * COLS), BF16)]
-        + [STATE] * 4,
+def early(q, da, bias, kvs):
+    return pl.pallas_call(
+        early_kernel,
+        out_shape=[jax.ShapeDtypeStruct((ROWS, 2 * COLS, NC), BF16)] + [STATE] * 4,
         compiler_params=params(),
         cost_estimate=cost(4.0),
         name="early",
-    )(q, da, bias, *[kvs[r] for r in group], *state)
+    )(q, da, bias, *[kvs[r] for r in NEAR])
 
 
 def turn_kernel(
-    q_ref, da_ref, qt_ref, dat_ref, bias_ref, near_top_ref,
-    acc_ref, total_ref, mass_ref, top_ref, *refs,
+    q_ref, da_ref, qt_ref, dat_ref, bias_ref, acc_ref, total_ref, mass_ref, top_ref, *refs
 ):
     n = len(LATE)
-    kv_refs, (u_ref, dot_ref, factor_ref, near_factor_ref) = refs[:n], refs[n : n + 4]
-    dkv_refs, table_ref = refs[n + 4 : 2 * n + 4], refs[-1]
+    kv_refs, (u_ref, dot_ref, factor_ref) = refs[:n], refs[n : n + 3]
+    dkv_refs, table_ref = refs[n + 3 : 2 * n + 3], refs[-1]
     lane = lanes((2 * COLS, WIDE))
 
     def scores(i):
@@ -394,7 +376,6 @@
         factor = fade * inverse
         dot = (jnp.sum(e * w, axis=1, keepdims=True) + mass_ref[i] * fade) * inverse
         factor_ref[i] = factor
-        near_factor_ref[i] = jnp.exp(near_top_ref[i] - top) * inverse
         dot_ref[i] = dot
         p = e * across(inverse, e)
         d = p * (w - across(dot, p))
@@ -409,16 +390,16 @@
     staged(scores, weigh, gather)
 
 
-def turn(q, da, qt, dat, bias, near_top, state, kvs):
+def turn(q, da, qt, dat, bias, state, kvs):
     return pl.pallas_call(
         turn_kernel,
-        out_shape=[STATE] * 4
+        out_shape=[STATE] * 3
         + [BLOCK] * len(LATE)
         + [jax.ShapeDtypeStruct((2 * COLS, NL), F32)],
         compiler_params=params(),
         cost_estimate=cost(3.0),
         name="turn",
-    )(q, da, qt, dat, bias, near_top, *state, *[kvs[r] for r in LATE])
+    )(q, da, qt, dat, bias, *state, *[kvs[r] for r in LATE])
 
 
 def backward_kernel(
@@ -463,12 +444,12 @@
     return out[0], dict(zip(group, out[1 : n + 1])), out[-1]
 
 
-def split_kernel(near_ref, far_ref, late_ref, keep_ref, send_ref):
+def split_kernel(near_ref, late_ref, keep_ref, send_ref):
     core = lax.axis_index("core")
     z = lax.axis_index("z")
 
     def write(even_ref, odd_ref):
-        for group, table in ((NEAR, near_ref), (FAR, far_ref), (LATE, late_ref)):
+        for group, table in ((NEAR, near_ref), (LATE, late_ref)):
             for m, r in enumerate(group):
                 ref = odd_ref if r % 2 else even_ref
                 x = lax.rem(z + r, RING) // 2
@@ -487,7 +468,7 @@
         write(send_ref, keep_ref)
 
 
-def split_tables(near, far, late):
+def split_tables(near, late):
     blocks = (2, 4, 2, COLS, COLS)
     return pl.pallas_call(
         split_kernel,
@@ -495,22 +476,25 @@
         compiler_params=params(),
         cost_estimate=cost(1.0),
         name="split_tables",
-    )(near, far, late)
-
-
-def relay_kernel(up_ref, part_ref, keep_ref, recv_ref, sent_ref, summed_ref):
-    sent_ref[...] = (up_ref[...].astype(F32) + part_ref[...].astype(F32)).astype(BF16)
+    )(near, late)
+
+
+def relay_kernel(
+    up_ref, near_ref, down_ref, far_ref, keep_ref, recv_ref, up_out, down_out, summed_ref
+):
+    up_out[...] = (up_ref[...].astype(F32) + near_ref[...].astype(F32)).astype(BF16)
+    down_out[...] = (down_ref[...].astype(F32) + far_ref[...].astype(F32)).astype(BF16)
     summed_ref[...] = (keep_ref[...] + recv_ref[...].astype(F32)).astype(BF16)
 
 
-def relay(up, part, keep, recv):
+def relay(up, near, down, far, keep, recv):
     return pl.pallas_call(
         relay_kernel,
-        out_shape=[BLOCK, jax.ShapeDtypeStruct(keep.shape, BF16)],
+        out_shape=[BLOCK, BLOCK, jax.ShapeDtypeStruct(keep.shape, BF16)],
         compiler_params=params(),
         cost_estimate=cost(0.8),
         name="relay",
-    )(up, part, keep, recv)
+    )(up, near, down, far, keep, recv)
 
 
 def gather_kernel(u_ref, a_ref, b_ref, near_ref, far_ref):
@@ -629,8 +613,8 @@
     return lax.ppermute(value, axis, [(0, 1), (1, 0)])
 
 
-def added(a, b):
-    return (a.astype(F32) + b.astype(F32)).astype(BF16)
+def added(*parts):
+    return sum(part.astype(F32) for part in parts).astype(BF16)
 
 
 def body(pair, w_qkvg, w_out, bias, chain_lengths, d_pair_out):
@@ -647,31 +631,22 @@
     kvs[2] = shift(kvs[1], -1)
     kvs[6] = shift(kvs[7], 1)
     kvs[3] = shift(kvs[2], -1)
-    bias_near, bias_far, bias_late = bias_tables(lift, everything)
-    e_near, *state = early(NEAR, q, da, bias_near, kvs, ())
-    near_top = state[-1]
-    kvs[4] = shift(join(kvs[3], near_top), -1)
+    kvs[4] = shift(kvs[2], -2)
     kvs[5] = shift(kvs[6], 1)
-    e_far, *state = early(FAR, q, da, bias_far, kvs, state)
-    u, dot, factor, near_factor, d4, d5, t_late = turn(
-        q, da, qt, dat, bias_late, near_top, state, kvs
-    )
-    up = shift(d4, 1)
-    down = shift(d5, -1)
-    u, far, t_far = backward(FAR, d4, da, qt, dat, (u, dot, factor), e_far, kvs, 2.5)
-    sent = added(up, far[3])
+    bias_near, bias_late = bias_tables(lift, everything)
+    e, *state = early(q, da, bias_near, kvs)
+    u, dot, factor, d3, d4, d5, t_late = turn(q, da, qt, dat, bias_late, state, kvs)
+    up, far, down = shift(d3, 1), shift(d4, 2), shift(d5, -1)
+    u, near, t_near = backward(NEAR, d4, da, qt, dat, (u, dot, factor), e, kvs, 3.0)
+    keep_table, send_table = split_tables(t_near, t_late)
+    recv_table = swap(send_table, "core")
+    sent = added(up, far, near[2])
     up = shift(sent, 1)
-    down = shift(added(down, far[6]), -1)
-    u, near, t_near = backward(NEAR, sent, da, qt, dat, (u, dot, near_factor), e_near, kvs, 3.0)
-    keep_table, send_table = split_tables(t_near, t_far, t_late)
-    recv_table = swap(send_table, "core")
-    sent3 = added(up, near[2])
-    up = shift(sent3, 1)
-    down = shift(added(down, near[7]), -1)
-    up, summed = relay(up, near[1], keep_table, recv_table)
-    up = shift(up, 1)
+    down = shift(added(down, near[6]), -1)
+    up, down, summed = relay(up, near[1], down, near[7], keep_table, recv_table)
+    gmine, gother = slopes(up, pair, d_pair_out, w_qkvg, w_out)
+    up, down = shift(up, 1), shift(down, -1)
     parts = lax.all_to_all(summed.reshape(16, COLS, COLS), peers, 0, 0, tiled=True)
-    gmine, gother = slopes(sent3, pair, d_pair_out, w_qkvg, w_out)
     first, second = gather_parts(u, near[0], down)
     keep, send = finish(first, second, up)
     recv = swap(send, "yl")

time: 84.8 us -> 82.5 us (0.973)
  starting transfers between devices: 46.4 us -> 39.7 us
  waiting for transfers between devices: 17.5 us -> 21.9 us
    ppermute x14, starting transfers between devices: 28.4 us -> 22.1 us  [shift(): lax.ppermute(value, 'z', [(z, (z + step) % RING) for z in range(RING)])]
    ppermute x14, waiting for transfers between devices: 13.6 us -> 18.6 us  [shift(): lax.ppermute(value, 'z', [(z, (z + step) % RING) for z in range(RING)])]
    pallas_call x2 -> x1, Pallas kernels: 3.39 us -> 2.53 us  [backward(): pl.pallas_call(functools.partial(backward_kernel, group), in_specs=[pl.Bl...]
    pallas_call x5 -> x3, Pallas kernels: 7 us -> 7.29 us  [the longest x1 3.42 us: turn(): pl.pallas_call(turn_kernel, out_shape=[STATE] * 3 + [BLOCK] * len(LATE) +...]
  transfers between devices with their start and end apart: 20 -> 20, of which waited for: 9 -> 8; matrix products, arithmetic and copies ran while one was open for 0% -> 0% of each run, Pallas kernels for 18% -> 16%
where the time goes in v6:
time: 82.5 us; the launch traced here: 81.6 us
  starting transfers between devices  39.7 us (48%)
  waiting for transfers between devices  21.9 us (27%)
  Pallas kernels  18.3 us (22%)
    ppermute x14, starting transfers between devices, shift(): lax.ppermute(value, 'z', [(z, (z + step) % RING) for z in range(RING)])  22.1 us
    ppermute x14, waiting for transfers between devices, shift(): lax.ppermute(value, 'z', [(z, (z + step) % RING) for z in range(RING)])  18.6 us
    all_to_all x1, starting transfers between devices, body(): everything = lax.all_to_all(wanted, peers, 0, 0, tiled=True)  7.19 us
    all_to_all x1, starting transfers between devices, body(): lax.all_to_all(summed.reshape(16, COLS, COLS), peers, 0, 0, tiled=True)  6.98 us
    pallas_call x1, Pallas kernels, turn(): pl.pallas_call(turn_kernel, out_shape=[STATE] * 3 + [BLOCK] * len(LATE) +...  3.42 us
    ppermute x4, starting transfers between devices, swap(): return lax.ppermute(value, axis, [(0, 1), (1, 0)])  3.4 us
    all_to_all x1, waiting for transfers between devices, body(): lax.all_to_all(summed.reshape(16, COLS, COLS), peers, 0, 0, tiled=True)  3.29 us
    pallas_call x1, Pallas kernels, early(): pl.pallas_call(early_kernel, out_shape=[jax.ShapeDtypeStruct((ROWS, 2 * C...  3.04 us
  transfers between devices with their start and end apart: 20, of which 8 were waited for; matrix products, arithmetic and copies ran while one was open for 0% of the time, Pallas kernels for 16%

profile of v6, /device:TPU:2, one launch (start us, length us, event | category | flops | bytes accessed | tf_op | source)
XLA Modules:
  0.0 81.6 jit_solution(9145387297413907427)
XLA Ops:
  0.7 1.7 %project.1 = (bf16[6,96,128]{2,1,0:T(8,128)(2,1)S(1)}, bf16[6,96,128]{2,1,0:T(8,128)(2,1)S(1)}, f32[16,1,96]{2,1,0:T(1,128)S(1)}) custom-call(s32[8]{0:T(128)} %len_hbm.1, bf16[6,96,128]{2,1,0:T(8,128)(2,1)} %pair_hbm.3, bf16[6,96,128]{2,1,0:T(8,128)(2,1)} %grad_hbm.3, bf16[128,256]{1,0:T(8,128)(2,1)} %w_ref.3, bf16[64,128]{1,0:T(8,128)(2,1)} %wout_hbm.3), custom_call_target="tpu_custom_call" | custom-call | bytes 200000 | tf_op jit(solution)/shard_map/project/pallas_call | solution.py:106
  2.4 1.7 %collective-permute-start = (bf16[6,96,128]{2,1,0:T(8,128)(2,1)S(1)}, bf16[6,96,128]{2,1,0:T(8,128)(2,1)S(1)}, u32[]{:S(2)}, u32[]{:S(2)}) collective-permute-start(bf16[6,96,128]{2,1,0:T(8,128)(2,1)S(1)} %get-tuple-element.43), channel_id=1, source_target_pairs={{0,8},{8,0},{1,9},{9,1},{2,10},{10,2},{3,11},{11,3},{4,12},{12,4},... | collective-permute-start | bytes 442376 | tf_op jit(solution)/shard_map/ppermute | solution.py:613
  5.9 7.2 %all-to-all-start = ((bf16[16,2,96,96]{3,2,1,0:T(8,128)(2,1)}), bf16[16,2,96,96]{3,2,1,0:T(8,128)(2,1)S(1)}, u32[]{:S(2)}, u32[]{:S(2)}) async-start(bf16[16,2,96,96]{3,2,1,0:T(8,128)(2,1)} %want.1._), calls=%async_computation | async-start | bytes 1572864 | tf_op jit(solution)/shard_map/all_to_all | solution.py:626
  13.9 2.0 %collective-permute-start.3 = (bf16[6,96,128]{2,1,0:T(8,128)(2,1)S(1)}, bf16[6,96,128]{2,1,0:T(8,128)(2,1)S(1)}, u32[]{:S(2)}, u32[]{:S(2)}) collective-permute-start(bf16[6,96,128]{2,1,0:T(8,128)(2,1)S(1)} %get-tuple-element.51.refs_0_), channel_id=1, source_target_pairs={{0,1},{1,2},{2,3},{3,4},{4,5},{5,6},{6,7},{7,0},{8,9},{9,10},{10,1... | collective-permute-start | bytes 442376 | tf_op jit(solution)/shard_map/ppermute | solution.py:609
  15.9 4.0 %collective-permute-start.2 = (bf16[6,96,128]{2,1,0:T(8,128)(2,1)S(1)}, bf16[6,96,128]{2,1,0:T(8,128)(2,1)S(1)}, u32[]{:S(2)}, u32[]{:S(2)}) collective-permute-start(bf16[6,96,128]{2,1,0:T(8,128)(2,1)S(1)} %get-tuple-element.51.refs_0_), channel_id=1, source_target_pairs={{0,7},{1,0},{2,1},{3,2},{4,3},{5,4},{6,5},{7,6},{8,15},{9,8},{10,9... | collective-permute-start | bytes 442376 | tf_op jit(solution)/shard_map/ppermute | solution.py:609
  20.0 3.6 %collective-permute-done.3.refs_2_ = bf16[6,96,128]{2,1,0:T(8,128)(2,1)S(1)} collective-permute-done((bf16[6,96,128]{2,1,0:T(8,128)(2,1)S(1)}, bf16[6,96,128]{2,1,0:T(8,128)(2,1)S(1)}, u32[]{:S(2)}, u32[]{:S(2)}) %collective-permute-start.3) | collective-permute-done | bytes 147488 | tf_op jit(solution)/shard_map/ppermute | solution.py:609
  23.5 3.2 %collective-permute-start.4 = (bf16[6,96,128]{2,1,0:T(8,128)(2,1)S(1)}, bf16[6,96,128]{2,1,0:T(8,128)(2,1)S(1)}, u32[]{:S(2)}, u32[]{:S(2)}) collective-permute-start(bf16[6,96,128]{2,1,0:T(8,128)(2,1)S(1)} %collective-permute-done.2.refs_1_), channel_id=1, source_target_pairs={{0,7},{1,0},{2,1},{3,2},{4,3},{5,4},{6,5},{7,6},{8,15},{9,8},{10,9... | collective-permute-start | bytes 442376 | tf_op jit(solution)/shard_map/ppermute | solution.py:609
  26.8 3.1 %collective-permute-done.5.refs_4_ = bf16[6,96,128]{2,1,0:T(8,128)(2,1)S(1)} collective-permute-done((bf16[6,96,128]{2,1,0:T(8,128)(2,1)S(1)}, bf16[6,96,128]{2,1,0:T(8,128)(2,1)S(1)}, u32[]{:S(2)}, u32[]{:S(2)}) %collective-permute-start.5) | collective-permute-done | bytes 147488 | tf_op jit(solution)/shard_map/ppermute | solution.py:609
  29.9 2.0 %collective-permute-start.7 = (bf16[6,96,128]{2,1,0:T(8,128)(2,1)S(1)}, bf16[6,96,128]{2,1,0:T(8,128)(2,1)S(1)}, u32[]{:S(2)}, u32[]{:S(2)}) collective-permute-start(bf16[6,96,128]{2,1,0:T(8,128)(2,1)S(1)} %collective-permute-done.4.refs_3_), channel_id=1, source_target_pairs={{0,6},{1,7},{2,0},{3,1},{4,2},{5,3},{6,4},{7,5},{8,14},{9,15},{10,... | collective-permute-start | bytes 442376 | tf_op jit(solution)/shard_map/ppermute | solution.py:609
  33.5 3.0 %early.1 = (bf16[6,192,960]{2,1,0:T(8,128)(2,1)S(1)}, f32[6,192,128]{2,1,0:T(8,128)S(1)}, f32[6,192,128]{2,1,0:T(8,128)S(1)}, f32[6,192,128]{2,1,0:T(8,128)S(1)}, f32[6,192,128]{2,1,0:T(8,128)S(1)}) custom-call(bf16[6,192,128]{2,1,0:T(8,128)(2,1)S(1)} %get-tuple-element.44.q_ref, bf16[6,192,128]{2,1,0:T(8,128)(2,1)S(1)} %get-tuple-element.45.da_ref, ...), custom_call_target="tpu_custom_call" | custom-call | bytes 400000 | tf_op jit(solution)/shard_map/early/pallas_call | solution.py:349
  36.5 2.8 %collective-permute-done.7.refs_1_ = bf16[6,96,128]{2,1,0:T(8,128)(2,1)S(1)} collective-permute-done((bf16[6,96,128]{2,1,0:T(8,128)(2,1)S(1)}, bf16[6,96,128]{2,1,0:T(8,128)(2,1)S(1)}, u32[]{:S(2)}, u32[]{:S(2)}) %collective-permute-start.7) | collective-permute-done | bytes 147488 | tf_op jit(solution)/shard_map/ppermute | solution.py:609
  39.3 1.6 %collective-permute-done.6.refs_0_ = bf16[6,96,128]{2,1,0:T(8,128)(2,1)S(1)} collective-permute-done((bf16[6,96,128]{2,1,0:T(8,128)(2,1)S(1)}, bf16[6,96,128]{2,1,0:T(8,128)(2,1)S(1)}, u32[]{:S(2)}, u32[]{:S(2)}) %collective-permute-start.6) | collective-permute-done | bytes 147488 | tf_op jit(solution)/shard_map/ppermute | solution.py:609
  40.8 3.4 %turn.1 = (f32[6,192,128]{2,1,0:T(8,128)S(1)}, f32[6,192,128]{2,1,0:T(8,128)S(1)}, f32[6,192,128]{2,1,0:T(8,128)S(1)}, bf16[6,96,128]{2,1,0:T(8,128)(2,1)S(1)}, ...) custom-call(bf16[6,192,128]{2,1,0:T(8,128)(2,1)S(1)} %get-tuple-element.44.q_ref, ...), custom_call_target="tpu_custom_call" | custom-call | bytes 300000 | tf_op jit(solution)/shard_map/turn/pallas_call | solution.py:394
  44.3 2.1 %collective-permute-start.12 = (bf16[6,96,128]{2,1,0:T(8,128)(2,1)S(1)}, bf16[6,96,128]{2,1,0:T(8,128)(2,1)S(1)}, u32[]{:S(2)}, u32[]{:S(2)}) collective-permute-start(bf16[6,96,128]{2,1,0:T(8,128)(2,1)S(1)} %get-tuple-element.66), channel_id=1, source_target_pairs={{0,7},{1,0},{2,1},{3,2},{4,3},{5,4},{6,5},{7,6},{8,15},{9,8},{10,9... | collective-permute-start | bytes 442376 | tf_op jit(solution)/shard_map/ppermute | solution.py:609
  46.4 2.4 %collective-permute-start.10 = (bf16[6,96,128]{2,1,0:T(8,128)(2,1)S(1)}, bf16[6,96,128]{2,1,0:T(8,128)(2,1)S(1)}, u32[]{:S(2)}, u32[]{:S(2)}) collective-permute-start(bf16[6,96,128]{2,1,0:T(8,128)(2,1)S(1)} %get-tuple-element.56._), channel_id=1, source_target_pairs={{0,2},{1,3},{2,4},{3,5},{4,6},{5,7},{6,0},{7,1},{8,10},{9,11},{10,... | collective-permute-start | bytes 442376 | tf_op jit(solution)/shard_map/ppermute | solution.py:609
  48.8 2.5 %backward.1 = (f32[6,192,128]{2,1,0:T(8,128)S(1)}, bf16[6,96,128]{2,1,0:T(8,128)(2,1)S(1)}, bf16[6,96,128]{2,1,0:T(8,128)(2,1)S(1)}, bf16[6,96,128]{2,1,0:T(8,12...) custom-call(bf16[6,96,128]{2,1,0:T(8,128)(2,1)S(1)} %get-tuple-element.56._, ...), custom_call_target="tpu_custom_call" | custom-call | bytes 300000 | tf_op jit(solution)/shard_map/backward/pallas_call | solution.py:433
  53.6 2.8 %collective-permute-done.10 = bf16[6,96,128]{2,1,0:T(8,128)(2,1)S(1)} collective-permute-done((bf16[6,96,128]{2,1,0:T(8,128)(2,1)S(1)}, bf16[6,96,128]{2,1,0:T(8,128)(2,1)S(1)}, u32[]{:S(2)}, u32[]{:S(2)}) %collective-permute-start.10) | collective-permute-done | bytes 147488 | tf_op jit(solution)/shard_map/ppermute | solution.py:609
  56.5 1.7 %collective-permute-start.11 = (bf16[6,96,128]{2,1,0:T(8,128)(2,1)S(1)}, bf16[6,96,128]{2,1,0:T(8,128)(2,1)S(1)}, u32[]{:S(2)}, u32[]{:S(2)}) collective-permute-start(bf16[6,96,128]{2,1,0:T(8,128)(2,1)S(1)} %add_convert_fusion.1), channel_id=1, source_target_pairs={{0,1},{1,2},{2,3},{3,4},{4,5},{5,6},{6,7},{7,0},{8,9},{9,10},{10,1... | collective-permute-start | bytes 442376 | tf_op jit(solution)/shard_map/ppermute | solution.py:609
  59.5 3.4 %collective-permute-done.11.up_ref = bf16[6,96,128]{2,1,0:T(8,128)(2,1)S(1)} collective-permute-done((bf16[6,96,128]{2,1,0:T(8,128)(2,1)S(1)}, bf16[6,96,128]{2,1,0:T(8,128)(2,1)S(1)}, u32[]{:S(2)}, u32[]{:S(2)}) %collective-permute-start.11) | collective-permute-done | bytes 147488 | tf_op jit(solution)/shard_map/ppermute | solution.py:609
  63.7 2.0 %collective-permute-start.16 = (bf16[6,96,128]{2,1,0:T(8,128)(2,1)S(1)}, bf16[6,96,128]{2,1,0:T(8,128)(2,1)S(1)}, u32[]{:S(2)}, u32[]{:S(2)}) collective-permute-start(bf16[6,96,128]{2,1,0:T(8,128)(2,1)S(1)} %get-tuple-element.76._), channel_id=1, source_target_pairs={{0,1},{1,2},{2,3},{3,4},{4,5},{5,6},{6,7},{7,0},{8,9},{9,10},{10,1... | collective-permute-start | bytes 442376 | tf_op jit(solution)/shard_map/ppermute | solution.py:609
  65.8 7.0 %all-to-all-start.1 = ((bf16[16,96,96]{2,1,0:T(8,128)(2,1)}), bf16[16,96,96]{2,1,0:T(8,128)(2,1)S(1)}, u32[]{:S(2)}, u32[]{:S(2)}) async-start(bf16[16,96,96]{2,1,0:T(8,128)(2,1)} %bitcast), calls=%async_computation.1 | async-start | bytes 786432 | tf_op jit(solution)/shard_map/all_to_all | solution.py:649
  73.2 1.5 %collective-permute-start.17 = (bf16[6,96,128]{2,1,0:T(8,128)(2,1)S(1)}, bf16[6,96,128]{2,1,0:T(8,128)(2,1)S(1)}, u32[]{:S(2)}, u32[]{:S(2)}) collective-permute-start(bf16[6,96,128]{2,1,0:T(8,128)(2,1)S(1)} %get-tuple-element.79), channel_id=1, source_target_pairs={{0,8},{8,0},{1,9},{9,1},{2,10},{10,2},{3,11},{11,3},{4,12},{12,4},... | collective-permute-start | bytes 442376 | tf_op jit(solution)/shard_map/ppermute | solution.py:613
  74.7 1.7 %slopes.1 = (f32[6,96,128]{2,1,0:T(8,128)S(1)}, f32[6,96,128]{2,1,0:T(8,128)S(1)}) custom-call(bf16[6,96,128]{2,1,0:T(8,128)(2,1)S(1)} %get-tuple-element.76._, bf16[6,96,128]{2,1,0:T(8,128)(2,1)} %pair_hbm.3, bf16[6,96,128]{2,1,0:T(8,128)(2,1)} %grad_hbm.3, bf16[128,256]{1,0:T(8,128)(2,1)} %w_ref.3, bf16[64,128]{1,0:T(8,128)(2,1)} %wout_hbm.3), custom_call_target="tpu_custom_call" | custom-call | bytes 200000 | tf_op jit(solution)/shard_map/slopes/pallas_call | solution.py:158
  76.7 3.3 %all-to-all-done.1.parts_ref = bf16[16,96,96]{2,1,0:T(8,128)(2,1)S(1)} async-done(((bf16[16,96,96]{2,1,0:T(8,128)(2,1)}), bf16[16,96,96]{2,1,0:T(8,128)(2,1)S(1)}, u32[]{:S(2)}, u32[]{:S(2)}) %all-to-all-start.1) | async-done | bytes 294944 | tf_op jit(solution)/shard_map/all_to_all | solution.py:649
  (37 shorter events, 11.2 us)
Async XLA Ops:
  0.6 3.5 %collective-permute-start.1 = (bf16[2,96,96]{2,1,0:T(8,128)(2,1)}, bf16[2,96,96]{2,1,0:T(8,128)(2,1)S(1)}, u32[]{:S(2)}, u32[]{:S(2)}) collective-permute-start(bf16[2,96,96]{2,1,0:T(8,128)(2,1)} %own_ref.1), channel_id=1, source_target_pairs={{0,16},{16,0},{1,17},{17,1},{2,18},{18,2},{3,19},{19,3},{4,20},{20... | collective-permute-start | bytes 110600 | tf_op jit(solution)/shard_map/ppermute | solution.py:613
  2.4 10.7 %collective-permute-start = (bf16[6,96,128]{2,1,0:T(8,128)(2,1)S(1)}, bf16[6,96,128]{2,1,0:T(8,128)(2,1)S(1)}, u32[]{:S(2)}, u32[]{:S(2)}) collective-permute-start(bf16[6,96,128]{2,1,0:T(8,128)(2,1)S(1)} %get-tuple-element.43), channel_id=1, source_target_pairs={{0,8},{8,0},{1,9},{9,1},{2,10},{10,2},{3,11},{11,3},{4,12},{12,4},... | collective-permute-start | bytes 442376 | tf_op jit(solution)/shard_map/ppermute | solution.py:613
  4.1 0.8 copy-start.1
  5.9 27.2 %all-to-all-start = ((bf16[16,2,96,96]{3,2,1,0:T(8,128)(2,1)}), bf16[16,2,96,96]{3,2,1,0:T(8,128)(2,1)S(1)}, u32[]{:S(2)}, u32[]{:S(2)}) async-start(bf16[16,2,96,96]{3,2,1,0:T(8,128)(2,1)} %want.1._), calls=%async_computation | async-start | bytes 1572864 | tf_op jit(solution)/shard_map/all_to_all | solution.py:626
  13.9 9.6 %collective-permute-start.3 = (bf16[6,96,128]{2,1,0:T(8,128)(2,1)S(1)}, bf16[6,96,128]{2,1,0:T(8,128)(2,1)S(1)}, u32[]{:S(2)}, u32[]{:S(2)}) collective-permute-start(bf16[6,96,128]{2,1,0:T(8,128)(2,1)S(1)} %get-tuple-element.51.refs_0_), channel_id=1, source_target_pairs={{0,1},{1,2},{2,3},{3,4},{4,5},{5,6},{6,7},{7,0},{8,9},{9,10},{10,1... | collective-permute-start | bytes 442376 | tf_op jit(solution)/shard_map/ppermute | solution.py:609
  15.9 7.6 %collective-permute-start.2 = (bf16[6,96,128]{2,1,0:T(8,128)(2,1)S(1)}, bf16[6,96,128]{2,1,0:T(8,128)(2,1)S(1)}, u32[]{:S(2)}, u32[]{:S(2)}) collective-permute-start(bf16[6,96,128]{2,1,0:T(8,128)(2,1)S(1)} %get-tuple-element.51.refs_0_), channel_id=1, source_target_pairs={{0,7},{1,0},{2,1},{3,2},{4,3},{5,4},{6,5},{7,6},{8,15},{9,8},{10,9... | collective-permute-start | bytes 442376 | tf_op jit(solution)/shard_map/ppermute | solution.py:609
  23.5 6.4 %collective-permute-start.5 = (bf16[6,96,128]{2,1,0:T(8,128)(2,1)S(1)}, bf16[6,96,128]{2,1,0:T(8,128)(2,1)S(1)}, u32[]{:S(2)}, u32[]{:S(2)}) collective-permute-start(bf16[6,96,128]{2,1,0:T(8,128)(2,1)S(1)} %collective-permute-done.3.refs_2_), channel_id=1, source_target_pairs={{0,1},{1,2},{2,3},{3,4},{4,5},{5,6},{6,7},{7,0},{8,9},{9,10},{10,1... | collective-permute-start | bytes 442376 | tf_op jit(solution)/shard_map/ppermute | solution.py:609
  23.5 6.4 %collective-permute-start.4 = (bf16[6,96,128]{2,1,0:T(8,128)(2,1)S(1)}, bf16[6,96,128]{2,1,0:T(8,128)(2,1)S(1)}, u32[]{:S(2)}, u32[]{:S(2)}) collective-permute-start(bf16[6,96,128]{2,1,0:T(8,128)(2,1)S(1)} %collective-permute-done.2.refs_1_), channel_id=1, source_target_pairs={{0,7},{1,0},{2,1},{3,2},{4,3},{5,4},{6,5},{7,6},{8,15},{9,8},{10,9... | collective-permute-start | bytes 442376 | tf_op jit(solution)/shard_map/ppermute | solution.py:609
  29.9 6.7 %collective-permute-start.8 = (bf16[6,96,128]{2,1,0:T(8,128)(2,1)S(1)}, bf16[6,96,128]{2,1,0:T(8,128)(2,1)S(1)}, u32[]{:S(2)}, u32[]{:S(2)}) collective-permute-start(bf16[6,96,128]{2,1,0:T(8,128)(2,1)S(1)} %collective-permute-done.5.refs_4_), channel_id=1, source_target_pairs={{0,1},{1,2},{2,3},{3,4},{4,5},{5,6},{6,7},{7,0},{8,9},{9,10},{10,1... | collective-permute-start | bytes 442376 | tf_op jit(solution)/shard_map/ppermute | solution.py:609
  29.9 9.4 %collective-permute-start.7 = (bf16[6,96,128]{2,1,0:T(8,128)(2,1)S(1)}, bf16[6,96,128]{2,1,0:T(8,128)(2,1)S(1)}, u32[]{:S(2)}, u32[]{:S(2)}) collective-permute-start(bf16[6,96,128]{2,1,0:T(8,128)(2,1)S(1)} %collective-permute-done.4.refs_3_), channel_id=1, source_target_pairs={{0,6},{1,7},{2,0},{3,1},{4,2},{5,3},{6,4},{7,5},{8,14},{9,15},{10,... | collective-permute-start | bytes 442376 | tf_op jit(solution)/shard_map/ppermute | solution.py:609
  31.9 9.0 %collective-permute-start.6 = (bf16[6,96,128]{2,1,0:T(8,128)(2,1)S(1)}, bf16[6,96,128]{2,1,0:T(8,128)(2,1)S(1)}, u32[]{:S(2)}, u32[]{:S(2)}) collective-permute-start(bf16[6,96,128]{2,1,0:T(8,128)(2,1)S(1)} %collective-permute-done.4.refs_3_), channel_id=1, source_target_pairs={{0,7},{1,0},{2,1},{3,2},{4,3},{5,4},{6,5},{7,6},{8,15},{9,8},{10,9... | collective-permute-start | bytes 442376 | tf_op jit(solution)/shard_map/ppermute | solution.py:609
  44.3 7.8 %collective-permute-start.12 = (bf16[6,96,128]{2,1,0:T(8,128)(2,1)S(1)}, bf16[6,96,128]{2,1,0:T(8,128)(2,1)S(1)}, u32[]{:S(2)}, u32[]{:S(2)}) collective-permute-start(bf16[6,96,128]{2,1,0:T(8,128)(2,1)S(1)} %get-tuple-element.66), channel_id=1, source_target_pairs={{0,7},{1,0},{2,1},{3,2},{4,3},{5,4},{6,5},{7,6},{8,15},{9,8},{10,9... | collective-permute-start | bytes 442376 | tf_op jit(solution)/shard_map/ppermute | solution.py:609
  46.3 7.2 %collective-permute-start.9 = (bf16[6,96,128]{2,1,0:T(8,128)(2,1)S(1)}, bf16[6,96,128]{2,1,0:T(8,128)(2,1)S(1)}, u32[]{:S(2)}, u32[]{:S(2)}) collective-permute-start(bf16[6,96,128]{2,1,0:T(8,128)(2,1)S(1)} %get-tuple-element.63), channel_id=1, source_target_pairs={{0,1},{1,2},{2,3},{3,4},{4,5},{5,6},{6,7},{7,0},{8,9},{9,10},{10,1... | collective-permute-start | bytes 442376 | tf_op jit(solution)/shard_map/ppermute | solution.py:609
  46.4 10.0 %collective-permute-start.10 = (bf16[6,96,128]{2,1,0:T(8,128)(2,1)S(1)}, bf16[6,96,128]{2,1,0:T(8,128)(2,1)S(1)}, u32[]{:S(2)}, u32[]{:S(2)}) collective-permute-start(bf16[6,96,128]{2,1,0:T(8,128)(2,1)S(1)} %get-tuple-element.56._), channel_id=1, source_target_pairs={{0,2},{1,3},{2,4},{3,5},{4,6},{5,7},{6,0},{7,1},{8,10},{9,11},{10,... | collective-permute-start | bytes 442376 | tf_op jit(solution)/shard_map/ppermute | solution.py:609
  52.0 10.9 %collective-permute-start.14 = (bf16[2,4,2,96,96]{4,3,2,1,0:T(8,128)(2,1)S(1)}, bf16[2,4,2,96,96]{4,3,2,1,0:T(8,128)(2,1)S(1)}, u32[]{:S(2)}, u32[]{:S(2)}) collective-permute-start(bf16[2,4,2,96,96]{4,3,2,1,0:T(8,128)(2,1)S(1)} %get-tuple-element.72), channel_id=1, source_target_pairs={{0,16},{16,0},{1,17},{17,1},{2,18},{18,2},{3,19},{19,3},{4,20},{20... | collective-permute-start | bytes 884744 | tf_op jit(solution)/shard_map/ppermute | solution.py:613
  52.2 7.4 %collective-permute-start.13 = (bf16[6,96,128]{2,1,0:T(8,128)(2,1)S(1)}, bf16[6,96,128]{2,1,0:T(8,128)(2,1)S(1)}, u32[]{:S(2)}, u32[]{:S(2)}) collective-permute-start(bf16[6,96,128]{2,1,0:T(8,128)(2,1)S(1)} %add_convert_fusion), channel_id=1, source_target_pairs={{0,7},{1,0},{2,1},{3,2},{4,3},{5,4},{6,5},{7,6},{8,15},{9,8},{10,9... | collective-permute-start | bytes 442376 | tf_op jit(solution)/shard_map/ppermute | solution.py:609
  56.5 6.4 %collective-permute-start.11 = (bf16[6,96,128]{2,1,0:T(8,128)(2,1)S(1)}, bf16[6,96,128]{2,1,0:T(8,128)(2,1)S(1)}, u32[]{:S(2)}, u32[]{:S(2)}) collective-permute-start(bf16[6,96,128]{2,1,0:T(8,128)(2,1)S(1)} %add_convert_fusion.1), channel_id=1, source_target_pairs={{0,1},{1,2},{2,3},{3,4},{4,5},{5,6},{6,7},{7,0},{8,9},{9,10},{10,1... | collective-permute-start | bytes 442376 | tf_op jit(solution)/shard_map/ppermute | solution.py:609
  62.9 13.5 %copy-start = (bf16[128,256]{1,0:T(8,128)(2,1)S(1)}, bf16[128,256]{1,0:T(8,128)(2,1)}, u32[]{:S(2)}) copy-start(bf16[128,256]{1,0:T(8,128)(2,1)} %w_ref.3) | copy-start | bytes 196612
  63.7 9.0 %collective-permute-start.15 = (bf16[6,96,128]{2,1,0:T(8,128)(2,1)S(1)}, bf16[6,96,128]{2,1,0:T(8,128)(2,1)S(1)}, u32[]{:S(2)}, u32[]{:S(2)}) collective-permute-start(bf16[6,96,128]{2,1,0:T(8,128)(2,1)S(1)} %get-tuple-element.73), channel_id=1, source_target_pairs={{0,7},{1,0},{2,1},{3,2},{4,3},{5,4},{6,5},{7,6},{8,15},{9,8},{10,9... | collective-permute-start | bytes 442376 | tf_op jit(solution)/shard_map/ppermute | solution.py:609
  63.7 9.3 %collective-permute-start.16 = (bf16[6,96,128]{2,1,0:T(8,128)(2,1)S(1)}, bf16[6,96,128]{2,1,0:T(8,128)(2,1)S(1)}, u32[]{:S(2)}, u32[]{:S(2)}) collective-permute-start(bf16[6,96,128]{2,1,0:T(8,128)(2,1)S(1)} %get-tuple-element.76._), channel_id=1, source_target_pairs={{0,1},{1,2},{2,3},{3,4},{4,5},{5,6},{6,7},{7,0},{8,9},{9,10},{10,1... | collective-permute-start | bytes 442376 | tf_op jit(solution)/shard_map/ppermute | solution.py:609
  65.8 14.2 %all-to-all-start.1 = ((bf16[16,96,96]{2,1,0:T(8,128)(2,1)}), bf16[16,96,96]{2,1,0:T(8,128)(2,1)S(1)}, u32[]{:S(2)}, u32[]{:S(2)}) async-start(bf16[16,96,96]{2,1,0:T(8,128)(2,1)} %bitcast), calls=%async_computation.1 | async-start | bytes 786432 | tf_op jit(solution)/shard_map/all_to_all | solution.py:649
  73.2 7.5 %collective-permute-start.17 = (bf16[6,96,128]{2,1,0:T(8,128)(2,1)S(1)}, bf16[6,96,128]{2,1,0:T(8,128)(2,1)S(1)}, u32[]{:S(2)}, u32[]{:S(2)}) collective-permute-start(bf16[6,96,128]{2,1,0:T(8,128)(2,1)S(1)} %get-tuple-element.79), channel_id=1, source_target_pairs={{0,8},{8,0},{1,9},{9,1},{2,10},{10,2},{3,11},{11,3},{4,12},{12,4},... | collective-permute-start | bytes 442376 | tf_op jit(solution)/shard_map/ppermute | solution.py:613

commit v7 on v6

--- a/solution.py
+++ b/solution.py
@@ -54,14 +54,14 @@
 
 
 def project_kernel(
-    len_hbm, pair_hbm, grad_hbm, w_hbm, wout_hbm,
-    mine_ref, other_ref, lift_ref,
+    len_hbm, bias_hbm, pair_hbm, grad_hbm, w_hbm, wout_hbm,
+    mine_ref, other_ref, lift_ref, bias_ref,
     len_s, pair_s, grad_s, w_s, wout_s, sem,
 ):
     yl = lax.axis_index("yl")
     pairs = (
         (len_hbm, len_s), (w_hbm, w_s), (wout_hbm, wout_s),
-        (pair_hbm, pair_s), (grad_hbm, grad_s),
+        (pair_hbm, pair_s), (grad_hbm, grad_s), (bias_hbm, bias_ref),
     )
     copies = [pltpu.make_async_copy(a, b, sem.at[n]) for n, (a, b) in enumerate(pairs)]
     for copy in copies:
@@ -99,17 +99,18 @@
             other_ref[...] = payload
 
 
-def project(chain_lengths, pair, grad, w, wout):
+def project(chain_lengths, bias, pair, grad, w, wout):
     shape = (ROWS, COLS, WIDE)
-    arrays = (chain_lengths, pair, grad, w, wout)
+    arrays = (chain_lengths, bias, pair, grad, w, wout)
     arrays = [pltpu.with_memory_space_constraint(array, pltpu.HBM) for array in arrays]
     return pl.pallas_call(
         project_kernel,
-        in_specs=[pl.BlockSpec(memory_space=pltpu.HBM)] * 5,
+        in_specs=[pl.BlockSpec(memory_space=pltpu.HBM)] * 6,
         out_shape=[
             jax.ShapeDtypeStruct(shape, BF16),
             jax.ShapeDtypeStruct(shape, BF16),
             jax.ShapeDtypeStruct((2 * CHAINS, 1, COLS), F32),
+            jax.ShapeDtypeStruct(bias.shape, BF16),
         ],
         scratch_shapes=[
             pltpu.SMEM((CHAINS,), jnp.int32),
@@ -117,7 +118,7 @@
             pltpu.VMEM(shape, BF16),
             pltpu.VMEM(w.shape, BF16),
             pltpu.VMEM(wout.shape, BF16),
-            pltpu.SemaphoreType.DMA((5,)),
+            pltpu.SemaphoreType.DMA((6,)),
         ],
         compiler_params=params(),
         cost_estimate=cost(2.0),
@@ -497,18 +498,18 @@
     )(up, near, down, far, keep, recv)
 
 
-def gather_kernel(u_ref, a_ref, b_ref, near_ref, far_ref):
+def gather_kernel(u_ref, a_ref, b_ref, c_ref, near_ref, far_ref):
     lane = lanes((COLS, WIDE))
     lane2 = lanes((2 * COLS, WIDE))
     for i in range(ROWS):
-        dkv = a_ref[i].astype(F32) + b_ref[i].astype(F32)
+        dkv = a_ref[i].astype(F32) + b_ref[i].astype(F32) + c_ref[i].astype(F32)
         u = jnp.where(lane2 < DH, u_ref[i] * SCALE, u_ref[i])
         u = pltpu.roll(u, 2 * DH, 1)
         near_ref[i] = jnp.where(lane < 2 * DH, dkv, u[:COLS])
         far_ref[i] = jnp.where(lane < 2 * DH, pltpu.roll(dkv, 2 * DH, 1), u[COLS:])
 
 
-def gather_parts(u, a, b):
+def gather_parts(u, a, b, c):
     shape = jax.ShapeDtypeStruct((ROWS, COLS, WIDE), F32)
     return pl.pallas_call(
         gather_kernel,
@@ -516,7 +517,7 @@
         compiler_params=params(),
         cost_estimate=cost(0.5),
         name="gather_parts",
-    )(u, a, b)
+    )(u, a, b, c)
 
 
 def finish_kernel(first_ref, second_ref, last_ref, keep_ref, send_ref):
@@ -620,38 +621,40 @@
 def body(pair, w_qkvg, w_out, bias, chain_lengths, d_pair_out):
     peers = ("yh", "x", "yl")
     oth = swap(bias, "core")
-    mine, other, lift = project(chain_lengths, pair, d_pair_out, w_qkvg, w_out)
+    mine, other, lift, bias = project(chain_lengths, bias, pair, d_pair_out, w_qkvg, w_out)
     recv = swap(other, "yl")
     wanted = want(bias, oth)
     everything = lax.all_to_all(wanted, peers, 0, 0, tiled=True)
     kv, q, da, qt, dat = pack(mine, recv, wanted)
     kvs = [kv] + [None] * (RING - 1)
+    kvs[2] = shift(kv, -2)
+    kvs[7] = shift(kv, 1)
     kvs[1] = shift(kv, -1)
-    kvs[7] = shift(kv, 1)
-    kvs[2] = shift(kvs[1], -1)
+    kvs[3] = shift(kvs[2], -1)
     kvs[6] = shift(kvs[7], 1)
-    kvs[3] = shift(kvs[2], -1)
-    kvs[4] = shift(kvs[2], -2)
+    kvs[4] = shift(kvs[3], -1)
     kvs[5] = shift(kvs[6], 1)
     bias_near, bias_late = bias_tables(lift, everything)
     e, *state = early(q, da, bias_near, kvs)
-    u, dot, factor, d3, d4, d5, t_late = turn(q, da, qt, dat, bias_late, state, kvs)
-    up, far, down = shift(d3, 1), shift(d4, 2), shift(d5, -1)
-    u, near, t_near = backward(NEAR, d4, da, qt, dat, (u, dot, factor), e, kvs, 3.0)
+    u, dot, factor, *late, t_late = turn(q, da, qt, dat, bias_late, state, kvs)
+    late = dict(zip(LATE, late))
+    up, down = shift(late[4], 1), shift(late[5], -1)
+    u, near, t_near = backward(NEAR, late[4], da, qt, dat, (u, dot, factor), e, kvs, 3.0)
+    parts = {**near, **late}
     keep_table, send_table = split_tables(t_near, t_late)
     recv_table = swap(send_table, "core")
-    sent = added(up, far, near[2])
-    up = shift(sent, 1)
-    down = shift(added(down, near[6]), -1)
-    up, down, summed = relay(up, near[1], down, near[7], keep_table, recv_table)
-    gmine, gother = slopes(up, pair, d_pair_out, w_qkvg, w_out)
-    up, down = shift(up, 1), shift(down, -1)
-    parts = lax.all_to_all(summed.reshape(16, COLS, COLS), peers, 0, 0, tiled=True)
-    first, second = gather_parts(u, near[0], down)
+    up = shift(added(up, parts[3]), 1)
+    down = shift(added(down, parts[6]), -1)
+    step = shift(parts[1], 1)
+    up, down, summed = relay(up, parts[2], down, parts[7], keep_table, recv_table)
+    up, down = shift(up, 2), shift(down, -1)
+    tables = lax.all_to_all(summed.reshape(16, COLS, COLS), peers, 0, 0, tiled=True)
+    gmine, gother = slopes(step, pair, d_pair_out, w_qkvg, w_out)
+    first, second = gather_parts(u, parts[0], step, down)
     keep, send = finish(first, second, up)
     recv = swap(send, "yl")
     kept = keep_product(keep, gmine, w_qkvg)
-    return output(kept, recv, gother, w_qkvg), table_sum(parts)
+    return output(kept, recv, gother, w_qkvg), table_sum(tables)
 
 
 def solution(mesh):

time: 82.5 us -> 80.5 us (0.976)
  the two profiles are of different devices: /device:TPU:2 before, /device:TPU:1 now
where the time goes in v7:
time: 80.5 us; the launch traced here: 80.2 us
  starting transfers between devices  41.2 us (51%)
  waiting for transfers between devices  19.9 us (25%)
  Pallas kernels  18.2 us (23%)
  between operations  0.82 us (1%)
    ppermute x14, starting transfers between devices, shift(): lax.ppermute(value, 'z', [(z, (z + step) % RING) for z in range(RING)])  19.6 us
    ppermute x14, waiting for transfers between devices, shift(): lax.ppermute(value, 'z', [(z, (z + step) % RING) for z in range(RING)])  15.2 us
    ppermute x4, starting transfers between devices, swap(): return lax.ppermute(value, axis, [(0, 1), (1, 0)])  8.97 us
    all_to_all x1, starting transfers between devices, body(): lax.all_to_all(summed.reshape(16, COLS, COLS), peers, 0, 0, tiled=True)  6.65 us
    all_to_all x1, starting transfers between devices, body(): everything = lax.all_to_all(wanted, peers, 0, 0, tiled=True)  6 us
    pallas_call x1, Pallas kernels, turn(): pl.pallas_call(turn_kernel, out_shape=[STATE] * 3 + [BLOCK] * len(LATE) +...  3.42 us
    pallas_call x1, Pallas kernels, early(): pl.pallas_call(early_kernel, out_shape=[jax.ShapeDtypeStruct((ROWS, 2 * C...  3.05 us
    pallas_call x1, Pallas kernels, backward(): pl.pallas_call(functools.partial(backward_kernel, group), in_specs=[pl.Bl...  2.53 us
  transfers between devices with their start and end apart: 20, of which 7 were waited for; matrix products, arithmetic and copies ran while one was open for 0% of the time, Pallas kernels for 17%

profile of v7, /device:TPU:1, one launch (start us, length us, event | category | flops | bytes accessed | tf_op | source)
XLA Modules:
  0.0 80.2 jit_solution(15603365466617009592)
XLA Ops:
  0.6 3.3 %collective-permute-start.1 = (bf16[2,96,96]{2,1,0:T(8,128)(2,1)}, bf16[2,96,96]{2,1,0:T(8,128)(2,1)S(1)}, u32[]{:S(2)}, u32[]{:S(2)}) collective-permute-start(bf16[2,96,96]{2,1,0:T(8,128)(2,1)} %bias_hbm.1), channel_id=1, source_target_pairs={{0,16},{16,0},{1,17},{17,1},{2,18},{18,2},{3,19},{19,3},{4,20},{20... | collective-permute-start | bytes 110600 | tf_op jit(solution)/shard_map/ppermute | solution.py:614
  4.0 1.7 %project.1 = (bf16[6,96,128]{2,1,0:T(8,128)(2,1)S(1)}, bf16[6,96,128]{2,1,0:T(8,128)(2,1)S(1)}, f32[16,1,96]{2,1,0:T(1,128)S(1)}, bf16[2,96,96]{2,1,0:T(8,128)(2,1)S(1)}) custom-call(s32[8]{0:T(128)} %len_hbm.1, bf16[2,96,96]{2,1,0:T(8,128)(2,1)} %bias_hbm.1, bf16[6,96,128]{2,1,0:T(8,128)(2,1)} %pair_hbm.3, bf16[6,96,128]{2,1,0:T(8,128)(2,1)} %grad_hbm.3, ...), custom_call_target="tpu_custom_call" | custom-call | bytes 200000 | tf_op jit(solution)/shard_map/project/pallas_call | solution.py:106
  5.8 1.0 %want.1._ = bf16[16,2,96,96]{3,2,1,0:T(8,128)(2,1)} custom-call(bf16[2,96,96]{2,1,0:T(8,128)(2,1)S(1)} %get-tuple-element.45.own_ref, bf16[2,96,96]{2,1,0:T(8,128)(2,1)S(1)} %collective-permute-done.1.oth_ref), custom_call_target="tpu_custom_call" | custom-call | bytes 40000 | tf_op jit(solution)/shard_map/want/pallas_call | solution.py:232
  6.8 6.0 %all-to-all-start = ((bf16[16,2,96,96]{3,2,1,0:T(8,128)(2,1)}), bf16[16,2,96,96]{3,2,1,0:T(8,128)(2,1)S(1)}, u32[]{:S(2)}, u32[]{:S(2)}) async-start(bf16[16,2,96,96]{3,2,1,0:T(8,128)(2,1)} %want.1._), calls=%async_computation | async-start | bytes 1572864 | tf_op jit(solution)/shard_map/all_to_all | solution.py:627
  13.6 6.1 %collective-permute-start.4 = (bf16[6,96,128]{2,1,0:T(8,128)(2,1)S(1)}, bf16[6,96,128]{2,1,0:T(8,128)(2,1)S(1)}, u32[]{:S(2)}, u32[]{:S(2)}) collective-permute-start(bf16[6,96,128]{2,1,0:T(8,128)(2,1)S(1)} %get-tuple-element.53.refs_0_), channel_id=1, source_target_pairs={{0,6},{1,7},{2,0},{3,1},{4,2},{5,3},{6,4},{7,5},{8,14},{9,15},{10,... | collective-permute-start | bytes 442376 | tf_op jit(solution)/shard_map/ppermute | solution.py:610
  20.5 5.3 %collective-permute-done.4.refs_3_ = bf16[6,96,128]{2,1,0:T(8,128)(2,1)S(1)} collective-permute-done((bf16[6,96,128]{2,1,0:T(8,128)(2,1)S(1)}, bf16[6,96,128]{2,1,0:T(8,128)(2,1)S(1)}, u32[]{:S(2)}, u32[]{:S(2)}) %collective-permute-start.4) | collective-permute-done | bytes 147488 | tf_op jit(solution)/shard_map/ppermute | solution.py:610
  25.8 2.8 %collective-permute-start.6 = (bf16[6,96,128]{2,1,0:T(8,128)(2,1)S(1)}, bf16[6,96,128]{2,1,0:T(8,128)(2,1)S(1)}, u32[]{:S(2)}, u32[]{:S(2)}) collective-permute-start(bf16[6,96,128]{2,1,0:T(8,128)(2,1)S(1)} %collective-permute-done.4.refs_3_), channel_id=1, source_target_pairs={{0,7},{1,0},{2,1},{3,2},{4,3},{5,4},{6,5},{7,6},{8,15},{9,8},{10,9... | collective-permute-start | bytes 442376 | tf_op jit(solution)/shard_map/ppermute | solution.py:610
  28.6 2.7 %collective-permute-start.2 = (bf16[6,96,128]{2,1,0:T(8,128)(2,1)S(1)}, bf16[6,96,128]{2,1,0:T(8,128)(2,1)S(1)}, u32[]{:S(2)}, u32[]{:S(2)}) collective-permute-start(bf16[6,96,128]{2,1,0:T(8,128)(2,1)S(1)} %get-tuple-element.53.refs_0_), channel_id=1, source_target_pairs={{0,7},{1,0},{2,1},{3,2},{4,3},{5,4},{6,5},{7,6},{8,15},{9,8},{10,9... | collective-permute-start | bytes 442376 | tf_op jit(solution)/shard_map/ppermute | solution.py:610
  31.2 3.1 %collective-permute-start.7 = (bf16[6,96,128]{2,1,0:T(8,128)(2,1)S(1)}, bf16[6,96,128]{2,1,0:T(8,128)(2,1)S(1)}, u32[]{:S(2)}, u32[]{:S(2)}) collective-permute-start(bf16[6,96,128]{2,1,0:T(8,128)(2,1)S(1)} %collective-permute-done.6.refs_0_), channel_id=1, source_target_pairs={{0,7},{1,0},{2,1},{3,2},{4,3},{5,4},{6,5},{7,6},{8,15},{9,8},{10,9... | collective-permute-start | bytes 442376 | tf_op jit(solution)/shard_map/ppermute | solution.py:610
  34.7 3.1 %early.1 = (bf16[6,192,960]{2,1,0:T(8,128)(2,1)S(1)}, f32[6,192,128]{2,1,0:T(8,128)S(1)}, f32[6,192,128]{2,1,0:T(8,128)S(1)}, f32[6,192,128]{2,1,0:T(8,128)S(1)}, f32[6,192,128]{2,1,0:T(8,128)S(1)}) custom-call(bf16[6,192,128]{2,1,0:T(8,128)(2,1)S(1)} %get-tuple-element.46.q_ref, bf16[6,192,128]{2,1,0:T(8,128)(2,1)S(1)} %get-tuple-element.47.da_ref, ...), custom_call_target="tpu_custom_call" | custom-call | bytes 400000 | tf_op jit(solution)/shard_map/early/pallas_call | solution.py:350
  37.8 1.7 %collective-permute-done.8.refs_2_ = bf16[6,96,128]{2,1,0:T(8,128)(2,1)S(1)} collective-permute-done((bf16[6,96,128]{2,1,0:T(8,128)(2,1)S(1)}, bf16[6,96,128]{2,1,0:T(8,128)(2,1)S(1)}, u32[]{:S(2)}, u32[]{:S(2)}) %collective-permute-start.8) | collective-permute-done | bytes 147488 | tf_op jit(solution)/shard_map/ppermute | solution.py:610
  39.5 3.4 %turn.1 = (f32[6,192,128]{2,1,0:T(8,128)S(1)}, f32[6,192,128]{2,1,0:T(8,128)S(1)}, f32[6,192,128]{2,1,0:T(8,128)S(1)}, bf16[6,96,128]{2,1,0:T(8,128)(2,1)S(1)}, ...) custom-call(bf16[6,192,128]{2,1,0:T(8,128)(2,1)S(1)} %get-tuple-element.46.q_ref, ...), custom_call_target="tpu_custom_call" | custom-call | bytes 300000 | tf_op jit(solution)/shard_map/turn/pallas_call | solution.py:395
  43.0 1.0 %collective-permute-start.12 = (bf16[6,96,128]{2,1,0:T(8,128)(2,1)S(1)}, bf16[6,96,128]{2,1,0:T(8,128)(2,1)S(1)}, u32[]{:S(2)}, u32[]{:S(2)}) collective-permute-start(bf16[6,96,128]{2,1,0:T(8,128)(2,1)S(1)} %get-tuple-element.68), channel_id=1, source_target_pairs={{0,7},{1,0},{2,1},{3,2},{4,3},{5,4},{6,5},{7,6},{8,15},{9,8},{10,9... | collective-permute-start | bytes 442376 | tf_op jit(solution)/shard_map/ppermute | solution.py:610
  44.5 2.5 %backward.1 = (f32[6,192,128]{2,1,0:T(8,128)S(1)}, bf16[6,96,128]{2,1,0:T(8,128)(2,1)S(1)}, bf16[6,96,128]{2,1,0:T(8,128)(2,1)S(1)}, bf16[6,96,128]{2,1,0:T(8,12...) custom-call(bf16[6,96,128]{2,1,0:T(8,128)(2,1)S(1)} %get-tuple-element.58._, ...), custom_call_target="tpu_custom_call" | custom-call | bytes 300000 | tf_op jit(solution)/shard_map/backward/pallas_call | solution.py:434
  47.5 4.2 %collective-permute-start.14 = (bf16[2,4,2,96,96]{4,3,2,1,0:T(8,128)(2,1)S(1)}, bf16[2,4,2,96,96]{4,3,2,1,0:T(8,128)(2,1)S(1)}, u32[]{:S(2)}, u32[]{:S(2)}) collective-permute-start(bf16[2,4,2,96,96]{4,3,2,1,0:T(8,128)(2,1)S(1)} %get-tuple-element.74), channel_id=1, source_target_pairs={{0,16},{16,0},{1,17},{17,1},{2,18},{18,2},{3,19},{19,3},{4,20},{20... | collective-permute-start | bytes 884744 | tf_op jit(solution)/shard_map/ppermute | solution.py:614
  51.7 2.2 %collective-permute-start.13 = (bf16[6,96,128]{2,1,0:T(8,128)(2,1)S(1)}, bf16[6,96,128]{2,1,0:T(8,128)(2,1)S(1)}, u32[]{:S(2)}, u32[]{:S(2)}) collective-permute-start(bf16[6,96,128]{2,1,0:T(8,128)(2,1)S(1)} %add_convert_fusion), channel_id=1, source_target_pairs={{0,7},{1,0},{2,1},{3,2},{4,3},{5,4},{6,5},{7,6},{8,15},{9,8},{10,9... | collective-permute-start | bytes 442376 | tf_op jit(solution)/shard_map/ppermute | solution.py:610
  54.2 3.3 %collective-permute-done.13.down_ref = bf16[6,96,128]{2,1,0:T(8,128)(2,1)S(1)} collective-permute-done((bf16[6,96,128]{2,1,0:T(8,128)(2,1)S(1)}, bf16[6,96,128]{2,1,0:T(8,128)(2,1)S(1)}, u32[]{:S(2)}, u32[]{:S(2)}) %collective-permute-start.13) | collective-permute-done | bytes 147488 | tf_op jit(solution)/shard_map/ppermute | solution.py:610
  57.5 3.0 %collective-permute-done.11.up_ref = bf16[6,96,128]{2,1,0:T(8,128)(2,1)S(1)} collective-permute-done((bf16[6,96,128]{2,1,0:T(8,128)(2,1)S(1)}, bf16[6,96,128]{2,1,0:T(8,128)(2,1)S(1)}, u32[]{:S(2)}, u32[]{:S(2)}) %collective-permute-start.11) | collective-permute-done | bytes 147488 | tf_op jit(solution)/shard_map/ppermute | solution.py:610
  61.6 6.7 %all-to-all-start.1 = ((bf16[16,96,96]{2,1,0:T(8,128)(2,1)}), bf16[16,96,96]{2,1,0:T(8,128)(2,1)S(1)}, u32[]{:S(2)}, u32[]{:S(2)}) async-start(bf16[16,96,96]{2,1,0:T(8,128)(2,1)} %bitcast), calls=%async_computation.1 | async-start | bytes 786432 | tf_op jit(solution)/shard_map/all_to_all | solution.py:651
  68.6 1.9 %collective-permute-done.16.last_ref = bf16[6,96,128]{2,1,0:T(8,128)(2,1)S(1)} collective-permute-done((bf16[6,96,128]{2,1,0:T(8,128)(2,1)S(1)}, bf16[6,96,128]{2,1,0:T(8,128)(2,1)S(1)}, u32[]{:S(2)}, u32[]{:S(2)}) %collective-permute-start.16) | collective-permute-done | bytes 147488 | tf_op jit(solution)/shard_map/ppermute | solution.py:610
  70.6 1.4 %collective-permute-start.17 = (bf16[6,96,128]{2,1,0:T(8,128)(2,1)S(1)}, bf16[6,96,128]{2,1,0:T(8,128)(2,1)S(1)}, u32[]{:S(2)}, u32[]{:S(2)}) collective-permute-start(bf16[6,96,128]{2,1,0:T(8,128)(2,1)S(1)} %get-tuple-element.81), channel_id=1, source_target_pairs={{0,8},{8,0},{1,9},{9,1},{2,10},{10,2},{3,11},{11,3},{4,12},{12,4},... | collective-permute-start | bytes 442376 | tf_op jit(solution)/shard_map/ppermute | solution.py:614
  72.0 1.7 %slopes.1 = (f32[6,96,128]{2,1,0:T(8,128)S(1)}, f32[6,96,128]{2,1,0:T(8,128)S(1)}) custom-call(bf16[6,96,128]{2,1,0:T(8,128)(2,1)S(1)} %collective-permute-done.9.b_ref._, bf16[6,96,128]{2,1,0:T(8,128)(2,1)} %pair_hbm.3, bf16[6,96,128]{2,1,0:T(8,128)(2,1)} %grad_hbm.3, bf16[128,256]{1,0:T(8,128)(2,1)} %w_ref.3, bf16[64,128]{1,0:T(8,128)(2,1)} %wout_hbm.3), custom_call_target="tpu_custom_call" | custom-call | bytes 200000 | tf_op jit(solution)/shard_map/slopes/pallas_call | solution.py:159
  73.9 2.5 %all-to-all-done.1.parts_ref = bf16[16,96,96]{2,1,0:T(8,128)(2,1)S(1)} async-done(((bf16[16,96,96]{2,1,0:T(8,128)(2,1)}), bf16[16,96,96]{2,1,0:T(8,128)(2,1)S(1)}, u32[]{:S(2)}, u32[]{:S(2)}) %all-to-all-start.1) | async-done | bytes 294944 | tf_op jit(solution)/shard_map/all_to_all | solution.py:651
  77.1 2.1 %collective-permute-done.17.recv_ref = bf16[6,96,128]{2,1,0:T(8,128)(2,1)S(1)} collective-permute-done((bf16[6,96,128]{2,1,0:T(8,128)(2,1)S(1)}, bf16[6,96,128]{2,1,0:T(8,128)(2,1)S(1)}, u32[]{:S(2)}, u32[]{:S(2)}) %collective-permute-start.17) | collective-permute-done | bytes 147488 | tf_op jit(solution)/shard_map/ppermute | solution.py:614
  (35 shorter events, 6.8 us)
Async XLA Ops:
  0.6 5.1 %collective-permute-start.1 = (bf16[2,96,96]{2,1,0:T(8,128)(2,1)}, bf16[2,96,96]{2,1,0:T(8,128)(2,1)S(1)}, u32[]{:S(2)}, u32[]{:S(2)}) collective-permute-start(bf16[2,96,96]{2,1,0:T(8,128)(2,1)} %bias_hbm.1), channel_id=1, source_target_pairs={{0,16},{16,0},{1,17},{17,1},{2,18},{18,2},{3,19},{19,3},{4,20},{20... | collective-permute-start | bytes 110600 | tf_op jit(solution)/shard_map/ppermute | solution.py:614
  5.7 7.1 %collective-permute-start = (bf16[6,96,128]{2,1,0:T(8,128)(2,1)S(1)}, bf16[6,96,128]{2,1,0:T(8,128)(2,1)S(1)}, u32[]{:S(2)}, u32[]{:S(2)}) collective-permute-start(bf16[6,96,128]{2,1,0:T(8,128)(2,1)S(1)} %get-tuple-element.44), channel_id=1, source_target_pairs={{0,8},{8,0},{1,9},{9,1},{2,10},{10,2},{3,11},{11,3},{4,12},{12,4},... | collective-permute-start | bytes 442376 | tf_op jit(solution)/shard_map/ppermute | solution.py:614
  6.8 27.5 %all-to-all-start = ((bf16[16,2,96,96]{3,2,1,0:T(8,128)(2,1)}), bf16[16,2,96,96]{3,2,1,0:T(8,128)(2,1)S(1)}, u32[]{:S(2)}, u32[]{:S(2)}) async-start(bf16[16,2,96,96]{3,2,1,0:T(8,128)(2,1)} %want.1._), calls=%async_computation | async-start | bytes 1572864 | tf_op jit(solution)/shard_map/all_to_all | solution.py:627
  13.6 12.2 %collective-permute-start.4 = (bf16[6,96,128]{2,1,0:T(8,128)(2,1)S(1)}, bf16[6,96,128]{2,1,0:T(8,128)(2,1)S(1)}, u32[]{:S(2)}, u32[]{:S(2)}) collective-permute-start(bf16[6,96,128]{2,1,0:T(8,128)(2,1)S(1)} %get-tuple-element.53.refs_0_), channel_id=1, source_target_pairs={{0,6},{1,7},{2,0},{3,1},{4,2},{5,3},{6,4},{7,5},{8,14},{9,15},{10,... | collective-permute-start | bytes 442376 | tf_op jit(solution)/shard_map/ppermute | solution.py:610
  19.7 8.8 %collective-permute-start.3 = (bf16[6,96,128]{2,1,0:T(8,128)(2,1)S(1)}, bf16[6,96,128]{2,1,0:T(8,128)(2,1)S(1)}, u32[]{:S(2)}, u32[]{:S(2)}) collective-permute-start(bf16[6,96,128]{2,1,0:T(8,128)(2,1)S(1)} %get-tuple-element.53.refs_0_), channel_id=1, source_target_pairs={{0,1},{1,2},{2,3},{3,4},{4,5},{5,6},{6,7},{7,0},{8,9},{9,10},{10,1... | collective-permute-start | bytes 442376 | tf_op jit(solution)/shard_map/ppermute | solution.py:610
  25.8 5.4 %collective-permute-start.6 = (bf16[6,96,128]{2,1,0:T(8,128)(2,1)S(1)}, bf16[6,96,128]{2,1,0:T(8,128)(2,1)S(1)}, u32[]{:S(2)}, u32[]{:S(2)}) collective-permute-start(bf16[6,96,128]{2,1,0:T(8,128)(2,1)S(1)} %collective-permute-done.4.refs_3_), channel_id=1, source_target_pairs={{0,7},{1,0},{2,1},{3,2},{4,3},{5,4},{6,5},{7,6},{8,15},{9,8},{10,9... | collective-permute-start | bytes 442376 | tf_op jit(solution)/shard_map/ppermute | solution.py:610
  28.6 5.8 %collective-permute-start.5 = (bf16[6,96,128]{2,1,0:T(8,128)(2,1)S(1)}, bf16[6,96,128]{2,1,0:T(8,128)(2,1)S(1)}, u32[]{:S(2)}, u32[]{:S(2)}) collective-permute-start(bf16[6,96,128]{2,1,0:T(8,128)(2,1)S(1)} %collective-permute-done.3.refs_2_), channel_id=1, source_target_pairs={{0,1},{1,2},{2,3},{3,4},{4,5},{5,6},{6,7},{7,0},{8,9},{9,10},{10,1... | collective-permute-start | bytes 442376 | tf_op jit(solution)/shard_map/ppermute | solution.py:610
  28.6 6.1 %collective-permute-start.2 = (bf16[6,96,128]{2,1,0:T(8,128)(2,1)S(1)}, bf16[6,96,128]{2,1,0:T(8,128)(2,1)S(1)}, u32[]{:S(2)}, u32[]{:S(2)}) collective-permute-start(bf16[6,96,128]{2,1,0:T(8,128)(2,1)S(1)} %get-tuple-element.53.refs_0_), channel_id=1, source_target_pairs={{0,7},{1,0},{2,1},{3,2},{4,3},{5,4},{6,5},{7,6},{8,15},{9,8},{10,9... | collective-permute-start | bytes 442376 | tf_op jit(solution)/shard_map/ppermute | solution.py:610
  31.2 6.5 %collective-permute-start.7 = (bf16[6,96,128]{2,1,0:T(8,128)(2,1)S(1)}, bf16[6,96,128]{2,1,0:T(8,128)(2,1)S(1)}, u32[]{:S(2)}, u32[]{:S(2)}) collective-permute-start(bf16[6,96,128]{2,1,0:T(8,128)(2,1)S(1)} %collective-permute-done.6.refs_0_), channel_id=1, source_target_pairs={{0,7},{1,0},{2,1},{3,2},{4,3},{5,4},{6,5},{7,6},{8,15},{9,8},{10,9... | collective-permute-start | bytes 442376 | tf_op jit(solution)/shard_map/ppermute | solution.py:610
  34.3 5.2 %collective-permute-start.8 = (bf16[6,96,128]{2,1,0:T(8,128)(2,1)S(1)}, bf16[6,96,128]{2,1,0:T(8,128)(2,1)S(1)}, u32[]{:S(2)}, u32[]{:S(2)}) collective-permute-start(bf16[6,96,128]{2,1,0:T(8,128)(2,1)S(1)} %collective-permute-done.5.refs_4_), channel_id=1, source_target_pairs={{0,1},{1,2},{2,3},{3,4},{4,5},{5,6},{6,7},{7,0},{8,9},{9,10},{10,1... | collective-permute-start | bytes 442376 | tf_op jit(solution)/shard_map/ppermute | solution.py:610
  43.0 8.7 %collective-permute-start.12 = (bf16[6,96,128]{2,1,0:T(8,128)(2,1)S(1)}, bf16[6,96,128]{2,1,0:T(8,128)(2,1)S(1)}, u32[]{:S(2)}, u32[]{:S(2)}) collective-permute-start(bf16[6,96,128]{2,1,0:T(8,128)(2,1)S(1)} %get-tuple-element.68), channel_id=1, source_target_pairs={{0,7},{1,0},{2,1},{3,2},{4,3},{5,4},{6,5},{7,6},{8,15},{9,8},{10,9... | collective-permute-start | bytes 442376 | tf_op jit(solution)/shard_map/ppermute | solution.py:610
  44.0 10.0 %collective-permute-start.10 = (bf16[6,96,128]{2,1,0:T(8,128)(2,1)S(1)}, bf16[6,96,128]{2,1,0:T(8,128)(2,1)S(1)}, u32[]{:S(2)}, u32[]{:S(2)}) collective-permute-start(bf16[6,96,128]{2,1,0:T(8,128)(2,1)S(1)} %get-tuple-element.58._), channel_id=1, source_target_pairs={{0,1},{1,2},{2,3},{3,4},{4,5},{5,6},{6,7},{7,0},{8,9},{9,10},{10,1... | collective-permute-start | bytes 442376 | tf_op jit(solution)/shard_map/ppermute | solution.py:610
  47.5 12.9 %collective-permute-start.14 = (bf16[2,4,2,96,96]{4,3,2,1,0:T(8,128)(2,1)S(1)}, bf16[2,4,2,96,96]{4,3,2,1,0:T(8,128)(2,1)S(1)}, u32[]{:S(2)}, u32[]{:S(2)}) collective-permute-start(bf16[2,4,2,96,96]{4,3,2,1,0:T(8,128)(2,1)S(1)} %get-tuple-element.74), channel_id=1, source_target_pairs={{0,16},{16,0},{1,17},{17,1},{2,18},{18,2},{3,19},{19,3},{4,20},{20... | collective-permute-start | bytes 884744 | tf_op jit(solution)/shard_map/ppermute | solution.py:614
  51.7 5.7 %collective-permute-start.13 = (bf16[6,96,128]{2,1,0:T(8,128)(2,1)S(1)}, bf16[6,96,128]{2,1,0:T(8,128)(2,1)S(1)}, u32[]{:S(2)}, u32[]{:S(2)}) collective-permute-start(bf16[6,96,128]{2,1,0:T(8,128)(2,1)S(1)} %add_convert_fusion), channel_id=1, source_target_pairs={{0,7},{1,0},{2,1},{3,2},{4,3},{5,4},{6,5},{7,6},{8,15},{9,8},{10,9... | collective-permute-start | bytes 442376 | tf_op jit(solution)/shard_map/ppermute | solution.py:610
  54.0 6.4 %collective-permute-start.11 = (bf16[6,96,128]{2,1,0:T(8,128)(2,1)S(1)}, bf16[6,96,128]{2,1,0:T(8,128)(2,1)S(1)}, u32[]{:S(2)}, u32[]{:S(2)}) collective-permute-start(bf16[6,96,128]{2,1,0:T(8,128)(2,1)S(1)} %add_convert_fusion.1), channel_id=1, source_target_pairs={{0,1},{1,2},{2,3},{3,4},{4,5},{5,6},{6,7},{7,0},{8,9},{9,10},{10,1... | collective-permute-start | bytes 442376 | tf_op jit(solution)/shard_map/ppermute | solution.py:610
  54.1 14.1 %collective-permute-start.9 = (bf16[6,96,128]{2,1,0:T(8,128)(2,1)S(1)}, bf16[6,96,128]{2,1,0:T(8,128)(2,1)S(1)}, u32[]{:S(2)}, u32[]{:S(2)}) collective-permute-start(bf16[6,96,128]{2,1,0:T(8,128)(2,1)S(1)} %get-tuple-element.65), channel_id=1, source_target_pairs={{0,1},{1,2},{2,3},{3,4},{4,5},{5,6},{6,7},{7,0},{8,9},{9,10},{10,1... | collective-permute-start | bytes 442376 | tf_op jit(solution)/shard_map/ppermute | solution.py:610
  60.5 13.2 %copy-start = (bf16[128,256]{1,0:T(8,128)(2,1)S(1)}, bf16[128,256]{1,0:T(8,128)(2,1)}, u32[]{:S(2)}) copy-start(bf16[128,256]{1,0:T(8,128)(2,1)} %w_ref.3) | copy-start | bytes 196612
  61.3 7.0 %collective-permute-start.15 = (bf16[6,96,128]{2,1,0:T(8,128)(2,1)S(1)}, bf16[6,96,128]{2,1,0:T(8,128)(2,1)S(1)}, u32[]{:S(2)}, u32[]{:S(2)}) collective-permute-start(bf16[6,96,128]{2,1,0:T(8,128)(2,1)S(1)} %get-tuple-element.75), channel_id=1, source_target_pairs={{0,7},{1,0},{2,1},{3,2},{4,3},{5,4},{6,5},{7,6},{8,15},{9,8},{10,9... | collective-permute-start | bytes 442376 | tf_op jit(solution)/shard_map/ppermute | solution.py:610
  61.5 9.0 %collective-permute-start.16 = (bf16[6,96,128]{2,1,0:T(8,128)(2,1)S(1)}, bf16[6,96,128]{2,1,0:T(8,128)(2,1)S(1)}, u32[]{:S(2)}, u32[]{:S(2)}) collective-permute-start(bf16[6,96,128]{2,1,0:T(8,128)(2,1)S(1)} %get-tuple-element.78), channel_id=1, source_target_pairs={{0,2},{1,3},{2,4},{3,5},{4,6},{5,7},{6,0},{7,1},{8,10},{9,11},{10,... | collective-permute-start | bytes 442376 | tf_op jit(solution)/shard_map/ppermute | solution.py:610
  61.6 14.9 %all-to-all-start.1 = ((bf16[16,96,96]{2,1,0:T(8,128)(2,1)}), bf16[16,96,96]{2,1,0:T(8,128)(2,1)S(1)}, u32[]{:S(2)}, u32[]{:S(2)}) async-start(bf16[16,96,96]{2,1,0:T(8,128)(2,1)} %bitcast), calls=%async_computation.1 | async-start | bytes 786432 | tf_op jit(solution)/shard_map/all_to_all | solution.py:651
  70.6 8.7 %collective-permute-start.17 = (bf16[6,96,128]{2,1,0:T(8,128)(2,1)S(1)}, bf16[6,96,128]{2,1,0:T(8,128)(2,1)S(1)}, u32[]{:S(2)}, u32[]{:S(2)}) collective-permute-start(bf16[6,96,128]{2,1,0:T(8,128)(2,1)S(1)} %get-tuple-element.81), channel_id=1, source_target_pairs={{0,8},{8,0},{1,9},{9,1},{2,10},{10,2},{3,11},{11,3},{4,12},{12,4},... | collective-permute-start | bytes 442376 | tf_op jit(solution)/shard_map/ppermute | solution.py:614

commit v8 on v7

--- a/solution.py
+++ b/solution.py
@@ -481,21 +481,20 @@
 
 
 def relay_kernel(
-    up_ref, near_ref, down_ref, far_ref, keep_ref, recv_ref, up_out, down_out, summed_ref
+    down_ref, far_ref, keep_ref, recv_ref, down_out, summed_ref
 ):
-    up_out[...] = (up_ref[...].astype(F32) + near_ref[...].astype(F32)).astype(BF16)
     down_out[...] = (down_ref[...].astype(F32) + far_ref[...].astype(F32)).astype(BF16)
     summed_ref[...] = (keep_ref[...] + recv_ref[...].astype(F32)).astype(BF16)
 
 
-def relay(up, near, down, far, keep, recv):
+def relay(down, far, keep, recv):
     return pl.pallas_call(
         relay_kernel,
-        out_shape=[BLOCK, BLOCK, jax.ShapeDtypeStruct(keep.shape, BF16)],
+        out_shape=[BLOCK, jax.ShapeDtypeStruct(keep.shape, BF16)],
         compiler_params=params(),
         cost_estimate=cost(0.8),
         name="relay",
-    )(up, near, down, far, keep, recv)
+    )(down, far, keep, recv)
 
 
 def gather_kernel(u_ref, a_ref, b_ref, c_ref, near_ref, far_ref):
@@ -638,16 +637,18 @@
     e, *state = early(q, da, bias_near, kvs)
     u, dot, factor, *late, t_late = turn(q, da, qt, dat, bias_late, state, kvs)
     late = dict(zip(LATE, late))
-    up, down = shift(late[4], 1), shift(late[5], -1)
+    up = shift(late[4], 1)
     u, near, t_near = backward(NEAR, late[4], da, qt, dat, (u, dot, factor), e, kvs, 3.0)
     parts = {**near, **late}
+    down = shift(join(late[5], t_near), -1)
     keep_table, send_table = split_tables(t_near, t_late)
     recv_table = swap(send_table, "core")
     up = shift(added(up, parts[3]), 1)
     down = shift(added(down, parts[6]), -1)
     step = shift(parts[1], 1)
-    up, down, summed = relay(up, parts[2], down, parts[7], keep_table, recv_table)
-    up, down = shift(up, 2), shift(down, -1)
+    up = shift(added(up, parts[2]), 2)
+    down, summed = relay(down, parts[7], keep_table, recv_table)
+    down = shift(down, -1)
     tables = lax.all_to_all(summed.reshape(16, COLS, COLS), peers, 0, 0, tiled=True)
     gmine, gother = slopes(step, pair, d_pair_out, w_qkvg, w_out)
     first, second = gather_parts(u, parts[0], step, down)

time: 80.5 us -> 79.7 us (0.990)
  the two profiles are of different devices: /device:TPU:1 before, /device:TPU:2 now
where the time goes in v8:
time: 79.7 us; the launch traced here: 78.9 us
  starting transfers between devices  43.1 us (54%)
  Pallas kernels  18.2 us (23%)
  waiting for transfers between devices  16.7 us (21%)
  between operations  0.82 us (1%)
    ppermute x14, starting transfers between devices, shift(): lax.ppermute(value, 'z', [(z, (z + step) % RING) for z in range(RING)])  25.3 us
    ppermute x14, waiting for transfers between devices, shift(): lax.ppermute(value, 'z', [(z, (z + step) % RING) for z in range(RING)])  13.4 us
    all_to_all x1, starting transfers between devices, body(): lax.all_to_all(summed.reshape(16, COLS, COLS), peers, 0, 0, tiled=True)  7.24 us
    all_to_all x1, starting transfers between devices, body(): everything = lax.all_to_all(wanted, peers, 0, 0, tiled=True)  7.18 us
    pallas_call x1, Pallas kernels, turn(): pl.pallas_call(turn_kernel, out_shape=[STATE] * 3 + [BLOCK] * len(LATE) +...  3.43 us
    ppermute x4, starting transfers between devices, swap(): return lax.ppermute(value, axis, [(0, 1), (1, 0)])  3.4 us
    all_to_all x1, waiting for transfers between devices, body(): lax.all_to_all(summed.reshape(16, COLS, COLS), peers, 0, 0, tiled=True)  3.28 us
    pallas_call x1, Pallas kernels, early(): pl.pallas_call(early_kernel, out_shape=[jax.ShapeDtypeStruct((ROWS, 2 * C...  3.05 us
  transfers between devices with their start and end apart: 20, of which 6 were waited for; matrix products, arithmetic and copies ran while one was open for 0% of the time, Pallas kernels for 14%

profile of v8, /device:TPU:2, one launch (start us, length us, event | category | flops | bytes accessed | tf_op | source)
XLA Modules:
  0.0 78.9 jit_solution(13826527800088575915)
XLA Ops:
  0.7 1.7 %project.1 = (bf16[6,96,128]{2,1,0:T(8,128)(2,1)S(1)}, bf16[6,96,128]{2,1,0:T(8,128)(2,1)S(1)}, f32[16,1,96]{2,1,0:T(1,128)S(1)}, bf16[2,96,96]{2,1,0:T(8,128)(2,1)S(1)}) custom-call(s32[8]{0:T(128)} %len_hbm.1, bf16[2,96,96]{2,1,0:T(8,128)(2,1)} %bias_hbm.1, bf16[6,96,128]{2,1,0:T(8,128)(2,1)} %pair_hbm.3, bf16[6,96,128]{2,1,0:T(8,128)(2,1)} %grad_hbm.3, ...), custom_call_target="tpu_custom_call" | custom-call | bytes 200000 | tf_op jit(solution)/shard_map/project/pallas_call | solution.py:106
  2.4 1.7 %collective-permute-start = (bf16[6,96,128]{2,1,0:T(8,128)(2,1)S(1)}, bf16[6,96,128]{2,1,0:T(8,128)(2,1)S(1)}, u32[]{:S(2)}, u32[]{:S(2)}) collective-permute-start(bf16[6,96,128]{2,1,0:T(8,128)(2,1)S(1)} %get-tuple-element.43), channel_id=1, source_target_pairs={{0,8},{8,0},{1,9},{9,1},{2,10},{10,2},{3,11},{11,3},{4,12},{12,4},... | collective-permute-start | bytes 442376 | tf_op jit(solution)/shard_map/ppermute | solution.py:613
  4.1 1.0 %want.1._ = bf16[16,2,96,96]{3,2,1,0:T(8,128)(2,1)} custom-call(bf16[2,96,96]{2,1,0:T(8,128)(2,1)S(1)} %get-tuple-element.44.own_ref, bf16[2,96,96]{2,1,0:T(8,128)(2,1)S(1)} %collective-permute-done.1.oth_ref), custom_call_target="tpu_custom_call" | custom-call | bytes 40000 | tf_op jit(solution)/shard_map/want/pallas_call | solution.py:232
  5.1 7.2 %all-to-all-start = ((bf16[16,2,96,96]{3,2,1,0:T(8,128)(2,1)}), bf16[16,2,96,96]{3,2,1,0:T(8,128)(2,1)S(1)}, u32[]{:S(2)}, u32[]{:S(2)}) async-start(bf16[16,2,96,96]{3,2,1,0:T(8,128)(2,1)} %want.1._), calls=%async_computation | async-start | bytes 1572864 | tf_op jit(solution)/shard_map/all_to_all | solution.py:626
  13.1 6.4 %collective-permute-start.4 = (bf16[6,96,128]{2,1,0:T(8,128)(2,1)S(1)}, bf16[6,96,128]{2,1,0:T(8,128)(2,1)S(1)}, u32[]{:S(2)}, u32[]{:S(2)}) collective-permute-start(bf16[6,96,128]{2,1,0:T(8,128)(2,1)S(1)} %get-tuple-element.52.refs_0_), channel_id=1, source_target_pairs={{0,6},{1,7},{2,0},{3,1},{4,2},{5,3},{6,4},{7,5},{8,14},{9,15},{10,... | collective-permute-start | bytes 442376 | tf_op jit(solution)/shard_map/ppermute | solution.py:609
  19.5 1.0 %collective-permute-start.3 = (bf16[6,96,128]{2,1,0:T(8,128)(2,1)S(1)}, bf16[6,96,128]{2,1,0:T(8,128)(2,1)S(1)}, u32[]{:S(2)}, u32[]{:S(2)}) collective-permute-start(bf16[6,96,128]{2,1,0:T(8,128)(2,1)S(1)} %get-tuple-element.52.refs_0_), channel_id=1, source_target_pairs={{0,1},{1,2},{2,3},{3,4},{4,5},{5,6},{6,7},{7,0},{8,9},{9,10},{10,1... | collective-permute-start | bytes 442376 | tf_op jit(solution)/shard_map/ppermute | solution.py:609
  20.5 5.1 %collective-permute-done.4.refs_3_ = bf16[6,96,128]{2,1,0:T(8,128)(2,1)S(1)} collective-permute-done((bf16[6,96,128]{2,1,0:T(8,128)(2,1)S(1)}, bf16[6,96,128]{2,1,0:T(8,128)(2,1)S(1)}, u32[]{:S(2)}, u32[]{:S(2)}) %collective-permute-start.4) | collective-permute-done | bytes 147488 | tf_op jit(solution)/shard_map/ppermute | solution.py:609
  25.6 2.7 %collective-permute-start.6 = (bf16[6,96,128]{2,1,0:T(8,128)(2,1)S(1)}, bf16[6,96,128]{2,1,0:T(8,128)(2,1)S(1)}, u32[]{:S(2)}, u32[]{:S(2)}) collective-permute-start(bf16[6,96,128]{2,1,0:T(8,128)(2,1)S(1)} %collective-permute-done.4.refs_3_), channel_id=1, source_target_pairs={{0,7},{1,0},{2,1},{3,2},{4,3},{5,4},{6,5},{7,6},{8,15},{9,8},{10,9... | collective-permute-start | bytes 442376 | tf_op jit(solution)/shard_map/ppermute | solution.py:609
  28.3 3.2 %collective-permute-start.2 = (bf16[6,96,128]{2,1,0:T(8,128)(2,1)S(1)}, bf16[6,96,128]{2,1,0:T(8,128)(2,1)S(1)}, u32[]{:S(2)}, u32[]{:S(2)}) collective-permute-start(bf16[6,96,128]{2,1,0:T(8,128)(2,1)S(1)} %get-tuple-element.52.refs_0_), channel_id=1, source_target_pairs={{0,7},{1,0},{2,1},{3,2},{4,3},{5,4},{6,5},{7,6},{8,15},{9,8},{10,9... | collective-permute-start | bytes 442376 | tf_op jit(solution)/shard_map/ppermute | solution.py:609
  31.6 3.7 %collective-permute-start.7 = (bf16[6,96,128]{2,1,0:T(8,128)(2,1)S(1)}, bf16[6,96,128]{2,1,0:T(8,128)(2,1)S(1)}, u32[]{:S(2)}, u32[]{:S(2)}) collective-permute-start(bf16[6,96,128]{2,1,0:T(8,128)(2,1)S(1)} %collective-permute-done.6.refs_0_), channel_id=1, source_target_pairs={{0,7},{1,0},{2,1},{3,2},{4,3},{5,4},{6,5},{7,6},{8,15},{9,8},{10,9... | collective-permute-start | bytes 442376 | tf_op jit(solution)/shard_map/ppermute | solution.py:609
  35.7 3.1 %early.1 = (bf16[6,192,960]{2,1,0:T(8,128)(2,1)S(1)}, f32[6,192,128]{2,1,0:T(8,128)S(1)}, f32[6,192,128]{2,1,0:T(8,128)S(1)}, f32[6,192,128]{2,1,0:T(8,128)S(1)}, f32[6,192,128]{2,1,0:T(8,128)S(1)}) custom-call(bf16[6,192,128]{2,1,0:T(8,128)(2,1)S(1)} %get-tuple-element.45.q_ref, bf16[6,192,128]{2,1,0:T(8,128)(2,1)S(1)} %get-tuple-element.46.da_ref, ...), custom_call_target="tpu_custom_call" | custom-call | bytes 400000 | tf_op jit(solution)/shard_map/early/pallas_call | solution.py:350
  38.8 2.9 %collective-permute-done.8.refs_2_ = bf16[6,96,128]{2,1,0:T(8,128)(2,1)S(1)} collective-permute-done((bf16[6,96,128]{2,1,0:T(8,128)(2,1)S(1)}, bf16[6,96,128]{2,1,0:T(8,128)(2,1)S(1)}, u32[]{:S(2)}, u32[]{:S(2)}) %collective-permute-start.8) | collective-permute-done | bytes 147488 | tf_op jit(solution)/shard_map/ppermute | solution.py:609
  41.7 3.4 %turn.1 = (f32[6,192,128]{2,1,0:T(8,128)S(1)}, f32[6,192,128]{2,1,0:T(8,128)S(1)}, f32[6,192,128]{2,1,0:T(8,128)S(1)}, bf16[6,96,128]{2,1,0:T(8,128)(2,1)S(1)}, ...) custom-call(bf16[6,192,128]{2,1,0:T(8,128)(2,1)S(1)} %get-tuple-element.45.q_ref, ...), custom_call_target="tpu_custom_call" | custom-call | bytes 300000 | tf_op jit(solution)/shard_map/turn/pallas_call | solution.py:395
  45.1 2.5 %backward.1 = (f32[6,192,128]{2,1,0:T(8,128)S(1)}, bf16[6,96,128]{2,1,0:T(8,128)(2,1)S(1)}, bf16[6,96,128]{2,1,0:T(8,128)(2,1)S(1)}, bf16[6,96,128]{2,1,0:T(8,12...) custom-call(bf16[6,96,128]{2,1,0:T(8,128)(2,1)S(1)} %get-tuple-element.57._, ...), custom_call_target="tpu_custom_call" | custom-call | bytes 300000 | tf_op jit(solution)/shard_map/backward/pallas_call | solution.py:434
  47.7 1.1 %collective-permute-start.10 = (bf16[6,96,128]{2,1,0:T(8,128)(2,1)S(1)}, bf16[6,96,128]{2,1,0:T(8,128)(2,1)S(1)}, u32[]{:S(2)}, u32[]{:S(2)}) collective-permute-start(bf16[6,96,128]{2,1,0:T(8,128)(2,1)S(1)} %join.1), channel_id=1, source_target_pairs={{0,7},{1,0},{2,1},{3,2},{4,3},{5,4},{6,5},{7,6},{8,15},{9,8},{10,9... | collective-permute-start | bytes 442376 | tf_op jit(solution)/shard_map/ppermute | solution.py:609
  48.8 1.0 %collective-permute-start.14 = (bf16[6,96,128]{2,1,0:T(8,128)(2,1)S(1)}, bf16[6,96,128]{2,1,0:T(8,128)(2,1)S(1)}, u32[]{:S(2)}, u32[]{:S(2)}) collective-permute-start(bf16[6,96,128]{2,1,0:T(8,128)(2,1)S(1)} %get-tuple-element.57._), channel_id=1, source_target_pairs={{0,1},{1,2},{2,3},{3,4},{4,5},{5,6},{6,7},{7,0},{8,9},{9,10},{10,1... | collective-permute-start | bytes 442376 | tf_op jit(solution)/shard_map/ppermute | solution.py:609
  50.3 2.6 %collective-permute-done.10 = bf16[6,96,128]{2,1,0:T(8,128)(2,1)S(1)} collective-permute-done((bf16[6,96,128]{2,1,0:T(8,128)(2,1)S(1)}, bf16[6,96,128]{2,1,0:T(8,128)(2,1)S(1)}, u32[]{:S(2)}, u32[]{:S(2)}) %collective-permute-start.10) | collective-permute-done | bytes 147488 | tf_op jit(solution)/shard_map/ppermute | solution.py:609
  52.9 2.5 %collective-permute-start.11 = (bf16[6,96,128]{2,1,0:T(8,128)(2,1)S(1)}, bf16[6,96,128]{2,1,0:T(8,128)(2,1)S(1)}, u32[]{:S(2)}, u32[]{:S(2)}) collective-permute-start(bf16[6,96,128]{2,1,0:T(8,128)(2,1)S(1)} %add_convert_fusion.2), channel_id=1, source_target_pairs={{0,7},{1,0},{2,1},{3,2},{4,3},{5,4},{6,5},{7,6},{8,15},{9,8},{10,9... | collective-permute-start | bytes 442376 | tf_op jit(solution)/shard_map/ppermute | solution.py:609
  55.7 2.7 %collective-permute-done.11.down_ref = bf16[6,96,128]{2,1,0:T(8,128)(2,1)S(1)} collective-permute-done((bf16[6,96,128]{2,1,0:T(8,128)(2,1)S(1)}, bf16[6,96,128]{2,1,0:T(8,128)(2,1)S(1)}, u32[]{:S(2)}, u32[]{:S(2)}) %collective-permute-start.11) | collective-permute-done | bytes 147488 | tf_op jit(solution)/shard_map/ppermute | solution.py:609
  59.2 3.4 %collective-permute-start.13 = (bf16[6,96,128]{2,1,0:T(8,128)(2,1)S(1)}, bf16[6,96,128]{2,1,0:T(8,128)(2,1)S(1)}, u32[]{:S(2)}, u32[]{:S(2)}) collective-permute-start(bf16[6,96,128]{2,1,0:T(8,128)(2,1)S(1)} %get-tuple-element.72), channel_id=1, source_target_pairs={{0,7},{1,0},{2,1},{3,2},{4,3},{5,4},{6,5},{7,6},{8,15},{9,8},{10,9... | collective-permute-start | bytes 442376 | tf_op jit(solution)/shard_map/ppermute | solution.py:609
  62.8 7.2 %all-to-all-start.1 = ((bf16[16,96,96]{2,1,0:T(8,128)(2,1)}), bf16[16,96,96]{2,1,0:T(8,128)(2,1)S(1)}, u32[]{:S(2)}, u32[]{:S(2)}) async-start(bf16[16,96,96]{2,1,0:T(8,128)(2,1)} %bitcast), calls=%async_computation.1 | async-start | bytes 786432 | tf_op jit(solution)/shard_map/all_to_all | solution.py:652
  70.5 1.5 %collective-permute-start.17 = (bf16[6,96,128]{2,1,0:T(8,128)(2,1)S(1)}, bf16[6,96,128]{2,1,0:T(8,128)(2,1)S(1)}, u32[]{:S(2)}, u32[]{:S(2)}) collective-permute-start(bf16[6,96,128]{2,1,0:T(8,128)(2,1)S(1)} %get-tuple-element.79), channel_id=1, source_target_pairs={{0,8},{8,0},{1,9},{9,1},{2,10},{10,2},{3,11},{11,3},{4,12},{12,4},... | collective-permute-start | bytes 442376 | tf_op jit(solution)/shard_map/ppermute | solution.py:613
  72.1 1.7 %slopes.1 = (f32[6,96,128]{2,1,0:T(8,128)S(1)}, f32[6,96,128]{2,1,0:T(8,128)S(1)}) custom-call(bf16[6,96,128]{2,1,0:T(8,128)(2,1)S(1)} %collective-permute-done.9.b_ref._, bf16[6,96,128]{2,1,0:T(8,128)(2,1)} %pair_hbm.3, bf16[6,96,128]{2,1,0:T(8,128)(2,1)} %grad_hbm.3, bf16[128,256]{1,0:T(8,128)(2,1)} %w_ref.3, bf16[64,128]{1,0:T(8,128)(2,1)} %wout_hbm.3), custom_call_target="tpu_custom_call" | custom-call | bytes 200000 | tf_op jit(solution)/shard_map/slopes/pallas_call | solution.py:159
  74.0 3.3 %all-to-all-done.1.parts_ref = bf16[16,96,96]{2,1,0:T(8,128)(2,1)S(1)} async-done(((bf16[16,96,96]{2,1,0:T(8,128)(2,1)}), bf16[16,96,96]{2,1,0:T(8,128)(2,1)S(1)}, u32[]{:S(2)}, u32[]{:S(2)}) %all-to-all-start.1) | async-done | bytes 294944 | tf_op jit(solution)/shard_map/all_to_all | solution.py:652
  (37 shorter events, 5.5 us)
Async XLA Ops:
  0.6 3.5 %collective-permute-start.1 = (bf16[2,96,96]{2,1,0:T(8,128)(2,1)}, bf16[2,96,96]{2,1,0:T(8,128)(2,1)S(1)}, u32[]{:S(2)}, u32[]{:S(2)}) collective-permute-start(bf16[2,96,96]{2,1,0:T(8,128)(2,1)} %bias_hbm.1), channel_id=1, source_target_pairs={{0,16},{16,0},{1,17},{17,1},{2,18},{18,2},{3,19},{19,3},{4,20},{20... | collective-permute-start | bytes 110600 | tf_op jit(solution)/shard_map/ppermute | solution.py:613
  2.4 9.9 %collective-permute-start = (bf16[6,96,128]{2,1,0:T(8,128)(2,1)S(1)}, bf16[6,96,128]{2,1,0:T(8,128)(2,1)S(1)}, u32[]{:S(2)}, u32[]{:S(2)}) collective-permute-start(bf16[6,96,128]{2,1,0:T(8,128)(2,1)S(1)} %get-tuple-element.43), channel_id=1, source_target_pairs={{0,8},{8,0},{1,9},{9,1},{2,10},{10,2},{3,11},{11,3},{4,12},{12,4},... | collective-permute-start | bytes 442376 | tf_op jit(solution)/shard_map/ppermute | solution.py:613
  5.1 30.2 %all-to-all-start = ((bf16[16,2,96,96]{3,2,1,0:T(8,128)(2,1)}), bf16[16,2,96,96]{3,2,1,0:T(8,128)(2,1)S(1)}, u32[]{:S(2)}, u32[]{:S(2)}) async-start(bf16[16,2,96,96]{3,2,1,0:T(8,128)(2,1)} %want.1._), calls=%async_computation | async-start | bytes 1572864 | tf_op jit(solution)/shard_map/all_to_all | solution.py:626
  13.1 12.5 %collective-permute-start.4 = (bf16[6,96,128]{2,1,0:T(8,128)(2,1)S(1)}, bf16[6,96,128]{2,1,0:T(8,128)(2,1)S(1)}, u32[]{:S(2)}, u32[]{:S(2)}) collective-permute-start(bf16[6,96,128]{2,1,0:T(8,128)(2,1)S(1)} %get-tuple-element.52.refs_0_), channel_id=1, source_target_pairs={{0,6},{1,7},{2,0},{3,1},{4,2},{5,3},{6,4},{7,5},{8,14},{9,15},{10,... | collective-permute-start | bytes 442376 | tf_op jit(solution)/shard_map/ppermute | solution.py:609
  19.5 8.8 %collective-permute-start.3 = (bf16[6,96,128]{2,1,0:T(8,128)(2,1)S(1)}, bf16[6,96,128]{2,1,0:T(8,128)(2,1)S(1)}, u32[]{:S(2)}, u32[]{:S(2)}) collective-permute-start(bf16[6,96,128]{2,1,0:T(8,128)(2,1)S(1)} %get-tuple-element.52.refs_0_), channel_id=1, source_target_pairs={{0,1},{1,2},{2,3},{3,4},{4,5},{5,6},{6,7},{7,0},{8,9},{9,10},{10,1... | collective-permute-start | bytes 442376 | tf_op jit(solution)/shard_map/ppermute | solution.py:609
  25.6 6.0 %collective-permute-start.6 = (bf16[6,96,128]{2,1,0:T(8,128)(2,1)S(1)}, bf16[6,96,128]{2,1,0:T(8,128)(2,1)S(1)}, u32[]{:S(2)}, u32[]{:S(2)}) collective-permute-start(bf16[6,96,128]{2,1,0:T(8,128)(2,1)S(1)} %collective-permute-done.4.refs_3_), channel_id=1, source_target_pairs={{0,7},{1,0},{2,1},{3,2},{4,3},{5,4},{6,5},{7,6},{8,15},{9,8},{10,9... | collective-permute-start | bytes 442376 | tf_op jit(solution)/shard_map/ppermute | solution.py:609
  28.3 7.0 %collective-permute-start.5 = (bf16[6,96,128]{2,1,0:T(8,128)(2,1)S(1)}, bf16[6,96,128]{2,1,0:T(8,128)(2,1)S(1)}, u32[]{:S(2)}, u32[]{:S(2)}) collective-permute-start(bf16[6,96,128]{2,1,0:T(8,128)(2,1)S(1)} %collective-permute-done.3.refs_2_), channel_id=1, source_target_pairs={{0,1},{1,2},{2,3},{3,4},{4,5},{5,6},{6,7},{7,0},{8,9},{9,10},{10,1... | collective-permute-start | bytes 442376 | tf_op jit(solution)/shard_map/ppermute | solution.py:609
  28.3 7.4 %collective-permute-start.2 = (bf16[6,96,128]{2,1,0:T(8,128)(2,1)S(1)}, bf16[6,96,128]{2,1,0:T(8,128)(2,1)S(1)}, u32[]{:S(2)}, u32[]{:S(2)}) collective-permute-start(bf16[6,96,128]{2,1,0:T(8,128)(2,1)S(1)} %get-tuple-element.52.refs_0_), channel_id=1, source_target_pairs={{0,7},{1,0},{2,1},{3,2},{4,3},{5,4},{6,5},{7,6},{8,15},{9,8},{10,9... | collective-permute-start | bytes 442376 | tf_op jit(solution)/shard_map/ppermute | solution.py:609
  31.6 7.1 %collective-permute-start.7 = (bf16[6,96,128]{2,1,0:T(8,128)(2,1)S(1)}, bf16[6,96,128]{2,1,0:T(8,128)(2,1)S(1)}, u32[]{:S(2)}, u32[]{:S(2)}) collective-permute-start(bf16[6,96,128]{2,1,0:T(8,128)(2,1)S(1)} %collective-permute-done.6.refs_0_), channel_id=1, source_target_pairs={{0,7},{1,0},{2,1},{3,2},{4,3},{5,4},{6,5},{7,6},{8,15},{9,8},{10,9... | collective-permute-start | bytes 442376 | tf_op jit(solution)/shard_map/ppermute | solution.py:609
  35.3 6.4 %collective-permute-start.8 = (bf16[6,96,128]{2,1,0:T(8,128)(2,1)S(1)}, bf16[6,96,128]{2,1,0:T(8,128)(2,1)S(1)}, u32[]{:S(2)}, u32[]{:S(2)}) collective-permute-start(bf16[6,96,128]{2,1,0:T(8,128)(2,1)S(1)} %collective-permute-done.5.refs_4_), channel_id=1, source_target_pairs={{0,1},{1,2},{2,3},{3,4},{4,5},{5,6},{6,7},{7,0},{8,9},{9,10},{10,1... | collective-permute-start | bytes 442376 | tf_op jit(solution)/shard_map/ppermute | solution.py:609
  47.7 5.2 %collective-permute-start.10 = (bf16[6,96,128]{2,1,0:T(8,128)(2,1)S(1)}, bf16[6,96,128]{2,1,0:T(8,128)(2,1)S(1)}, u32[]{:S(2)}, u32[]{:S(2)}) collective-permute-start(bf16[6,96,128]{2,1,0:T(8,128)(2,1)S(1)} %join.1), channel_id=1, source_target_pairs={{0,7},{1,0},{2,1},{3,2},{4,3},{5,4},{6,5},{7,6},{8,15},{9,8},{10,9... | collective-permute-start | bytes 442376 | tf_op jit(solution)/shard_map/ppermute | solution.py:609
  48.8 6.7 %collective-permute-start.14 = (bf16[6,96,128]{2,1,0:T(8,128)(2,1)S(1)}, bf16[6,96,128]{2,1,0:T(8,128)(2,1)S(1)}, u32[]{:S(2)}, u32[]{:S(2)}) collective-permute-start(bf16[6,96,128]{2,1,0:T(8,128)(2,1)S(1)} %get-tuple-element.57._), channel_id=1, source_target_pairs={{0,1},{1,2},{2,3},{3,4},{4,5},{5,6},{6,7},{7,0},{8,9},{9,10},{10,1... | collective-permute-start | bytes 442376 | tf_op jit(solution)/shard_map/ppermute | solution.py:609
  50.2 8.2 %collective-permute-start.12 = (bf16[2,4,2,96,96]{4,3,2,1,0:T(8,128)(2,1)S(1)}, bf16[2,4,2,96,96]{4,3,2,1,0:T(8,128)(2,1)S(1)}, u32[]{:S(2)}, u32[]{:S(2)}) collective-permute-start(bf16[2,4,2,96,96]{4,3,2,1,0:T(8,128)(2,1)S(1)} %get-tuple-element.71), channel_id=1, source_target_pairs={{0,16},{16,0},{1,17},{17,1},{2,18},{18,2},{3,19},{19,3},{4,20},{20... | collective-permute-start | bytes 884744 | tf_op jit(solution)/shard_map/ppermute | solution.py:613
  52.9 5.4 %collective-permute-start.11 = (bf16[6,96,128]{2,1,0:T(8,128)(2,1)S(1)}, bf16[6,96,128]{2,1,0:T(8,128)(2,1)S(1)}, u32[]{:S(2)}, u32[]{:S(2)}) collective-permute-start(bf16[6,96,128]{2,1,0:T(8,128)(2,1)S(1)} %add_convert_fusion.2), channel_id=1, source_target_pairs={{0,7},{1,0},{2,1},{3,2},{4,3},{5,4},{6,5},{7,6},{8,15},{9,8},{10,9... | collective-permute-start | bytes 442376 | tf_op jit(solution)/shard_map/ppermute | solution.py:609
  55.5 7.2 %collective-permute-start.15 = (bf16[6,96,128]{2,1,0:T(8,128)(2,1)S(1)}, bf16[6,96,128]{2,1,0:T(8,128)(2,1)S(1)}, u32[]{:S(2)}, u32[]{:S(2)}) collective-permute-start(bf16[6,96,128]{2,1,0:T(8,128)(2,1)S(1)} %add_convert_fusion.1), channel_id=1, source_target_pairs={{0,1},{1,2},{2,3},{3,4},{4,5},{5,6},{6,7},{7,0},{8,9},{9,10},{10,1... | collective-permute-start | bytes 442376 | tf_op jit(solution)/shard_map/ppermute | solution.py:609
  55.6 14.5 %collective-permute-start.9 = (bf16[6,96,128]{2,1,0:T(8,128)(2,1)S(1)}, bf16[6,96,128]{2,1,0:T(8,128)(2,1)S(1)}, u32[]{:S(2)}, u32[]{:S(2)}) collective-permute-start(bf16[6,96,128]{2,1,0:T(8,128)(2,1)S(1)} %get-tuple-element.64), channel_id=1, source_target_pairs={{0,1},{1,2},{2,3},{3,4},{4,5},{5,6},{6,7},{7,0},{8,9},{9,10},{10,1... | collective-permute-start | bytes 442376 | tf_op jit(solution)/shard_map/ppermute | solution.py:609
  58.4 15.4 %copy-start = (bf16[128,256]{1,0:T(8,128)(2,1)S(1)}, bf16[128,256]{1,0:T(8,128)(2,1)}, u32[]{:S(2)}) copy-start(bf16[128,256]{1,0:T(8,128)(2,1)} %w_ref.3) | copy-start | bytes 196612
  59.2 10.9 %collective-permute-start.13 = (bf16[6,96,128]{2,1,0:T(8,128)(2,1)S(1)}, bf16[6,96,128]{2,1,0:T(8,128)(2,1)S(1)}, u32[]{:S(2)}, u32[]{:S(2)}) collective-permute-start(bf16[6,96,128]{2,1,0:T(8,128)(2,1)S(1)} %get-tuple-element.72), channel_id=1, source_target_pairs={{0,7},{1,0},{2,1},{3,2},{4,3},{5,4},{6,5},{7,6},{8,15},{9,8},{10,9... | collective-permute-start | bytes 442376 | tf_op jit(solution)/shard_map/ppermute | solution.py:609
  62.7 7.6 %collective-permute-start.16 = (bf16[6,96,128]{2,1,0:T(8,128)(2,1)S(1)}, bf16[6,96,128]{2,1,0:T(8,128)(2,1)S(1)}, u32[]{:S(2)}, u32[]{:S(2)}) collective-permute-start(bf16[6,96,128]{2,1,0:T(8,128)(2,1)S(1)} %add_convert_fusion), channel_id=1, source_target_pairs={{0,2},{1,3},{2,4},{3,5},{4,6},{5,7},{6,0},{7,1},{8,10},{9,11},{10,... | collective-permute-start | bytes 442376 | tf_op jit(solution)/shard_map/ppermute | solution.py:609
  62.8 14.5 %all-to-all-start.1 = ((bf16[16,96,96]{2,1,0:T(8,128)(2,1)}), bf16[16,96,96]{2,1,0:T(8,128)(2,1)S(1)}, u32[]{:S(2)}, u32[]{:S(2)}) async-start(bf16[16,96,96]{2,1,0:T(8,128)(2,1)} %bitcast), calls=%async_computation.1 | async-start | bytes 786432 | tf_op jit(solution)/shard_map/all_to_all | solution.py:652
  70.5 7.5 %collective-permute-start.17 = (bf16[6,96,128]{2,1,0:T(8,128)(2,1)S(1)}, bf16[6,96,128]{2,1,0:T(8,128)(2,1)S(1)}, u32[]{:S(2)}, u32[]{:S(2)}) collective-permute-start(bf16[6,96,128]{2,1,0:T(8,128)(2,1)S(1)} %get-tuple-element.79), channel_id=1, source_target_pairs={{0,8},{8,0},{1,9},{9,1},{2,10},{10,2},{3,11},{11,3},{4,12},{12,4},... | collective-permute-start | bytes 442376 | tf_op jit(solution)/shard_map/ppermute | solution.py:613

commit v9 on v8

--- a/solution.py
+++ b/solution.py
@@ -574,35 +574,22 @@
     )(keep, gate, w)
 
 
-def table_kernel(parts_ref, bias_ref):
+def output_kernel(kept_ref, recv_ref, gate_ref, w_ref, parts_ref, out_ref, bias_ref):
+    yl = lax.axis_index("yl")
     for h in range(H):
         bias_ref[h] = sum(parts_ref[n * H + h].astype(F32) for n in range(8))
-
-
-def table_sum(parts):
-    return pl.pallas_call(
-        table_kernel,
-        out_shape=jax.ShapeDtypeStruct((H, COLS, COLS), F32),
-        compiler_params=params(),
-        cost_estimate=cost(0.3),
-        name="table_sum",
-    )(parts)
-
-
-def output_kernel(kept_ref, recv_ref, gate_ref, w_ref, out_ref):
-    yl = lax.axis_index("yl")
     other = product(recv_ref[...], gate_ref[...], w_ref[...], 1 - yl)
     out_ref[...] = (kept_ref[...] + other).astype(BF16).reshape(ROWS, COLS, WIDE)
 
 
-def output(kept, recv, gate, w):
+def output(kept, recv, gate, w, parts):
     return pl.pallas_call(
         output_kernel,
-        out_shape=BLOCK,
+        out_shape=[BLOCK, jax.ShapeDtypeStruct((H, COLS, COLS), F32)],
         compiler_params=params(),
         cost_estimate=cost(0.5),
         name="output",
-    )(kept, recv, gate, w)
+    )(kept, recv, gate, w, parts)
 
 
 def shift(value, step):
@@ -655,7 +642,7 @@
     keep, send = finish(first, second, up)
     recv = swap(send, "yl")
     kept = keep_product(keep, gmine, w_qkvg)
-    return output(kept, recv, gother, w_qkvg), table_sum(tables)
+    return output(kept, recv, gother, w_qkvg, tables)
 
 
 def solution(mesh):

time: 79.7 us -> 79 us (level)
    pallas_call x2 -> x1, Pallas kernels: 1.63 us -> 0.95 us  [output(): pl.pallas_call(output_kernel, out_shape=[BLOCK, jax.ShapeDtypeStruct((H,...]
  transfers between devices with their start and end apart: 20 -> 20, of which waited for: 6 -> 6; matrix products, arithmetic and copies ran while one was open for 0% -> 0% of each run, Pallas kernels for 14% -> 13%
where the time goes in v9:
time: 79 us; the launch traced here: 78.3 us
  starting transfers between devices  43.1 us (55%)
  Pallas kernels  17.5 us (22%)
  waiting for transfers between devices  16.7 us (21%)
  between operations  0.82 us (1%)
    ppermute x14, starting transfers between devices, shift(): lax.ppermute(value, 'z', [(z, (z + step) % RING) for z in range(RING)])  25.3 us
    ppermute x14, waiting for transfers between devices, shift(): lax.ppermute(value, 'z', [(z, (z + step) % RING) for z in range(RING)])  13.4 us
    all_to_all x1, starting transfers between devices, body(): lax.all_to_all(summed.reshape(16, COLS, COLS), peers, 0, 0, tiled=True)  7.24 us
    all_to_all x1, starting transfers between devices, body(): everything = lax.all_to_all(wanted, peers, 0, 0, tiled=True)  7.18 us
    pallas_call x1, Pallas kernels, turn(): pl.pallas_call(turn_kernel, out_shape=[STATE] * 3 + [BLOCK] * len(LATE) +...  3.43 us
    ppermute x4, starting transfers between devices, swap(): return lax.ppermute(value, axis, [(0, 1), (1, 0)])  3.4 us
    all_to_all x1, waiting for transfers between devices, body(): lax.all_to_all(summed.reshape(16, COLS, COLS), peers, 0, 0, tiled=True)  3.28 us
    pallas_call x1, Pallas kernels, early(): pl.pallas_call(early_kernel, out_shape=[jax.ShapeDtypeStruct((ROWS, 2 * C...  3.05 us
  transfers between devices with their start and end apart: 20, of which 6 were waited for; matrix products, arithmetic and copies ran while one was open for 0% of the time, Pallas kernels for 13%

profile of v9, /device:TPU:2, one launch (start us, length us, event | category | flops | bytes accessed | tf_op | source)
XLA Modules:
  0.0 78.3 jit_solution(4006433005207391292)
XLA Ops:
  0.7 1.7 %project.1 = (bf16[6,96,128]{2,1,0:T(8,128)(2,1)S(1)}, bf16[6,96,128]{2,1,0:T(8,128)(2,1)S(1)}, f32[16,1,96]{2,1,0:T(1,128)S(1)}, bf16[2,96,96]{2,1,0:T(8,128)(2,1)S(1)}) custom-call(s32[8]{0:T(128)} %len_hbm.1, bf16[2,96,96]{2,1,0:T(8,128)(2,1)} %bias_hbm.1, bf16[6,96,128]{2,1,0:T(8,128)(2,1)} %pair_hbm.3, bf16[6,96,128]{2,1,0:T(8,128)(2,1)} %grad_hbm.3, ...), custom_call_target="tpu_custom_call" | custom-call | bytes 200000 | tf_op jit(solution)/shard_map/project/pallas_call | solution.py:106
  2.4 1.7 %collective-permute-start = (bf16[6,96,128]{2,1,0:T(8,128)(2,1)S(1)}, bf16[6,96,128]{2,1,0:T(8,128)(2,1)S(1)}, u32[]{:S(2)}, u32[]{:S(2)}) collective-permute-start(bf16[6,96,128]{2,1,0:T(8,128)(2,1)S(1)} %get-tuple-element.43), channel_id=1, source_target_pairs={{0,8},{8,0},{1,9},{9,1},{2,10},{10,2},{3,11},{11,3},{4,12},{12,4},... | collective-permute-start | bytes 442376 | tf_op jit(solution)/shard_map/ppermute | solution.py:600
  4.1 1.0 %want.1._ = bf16[16,2,96,96]{3,2,1,0:T(8,128)(2,1)} custom-call(bf16[2,96,96]{2,1,0:T(8,128)(2,1)S(1)} %get-tuple-element.44.own_ref, bf16[2,96,96]{2,1,0:T(8,128)(2,1)S(1)} %collective-permute-done.1.oth_ref), custom_call_target="tpu_custom_call" | custom-call | bytes 40000 | tf_op jit(solution)/shard_map/want/pallas_call | solution.py:232
  5.1 7.2 %all-to-all-start = ((bf16[16,2,96,96]{3,2,1,0:T(8,128)(2,1)}), bf16[16,2,96,96]{3,2,1,0:T(8,128)(2,1)S(1)}, u32[]{:S(2)}, u32[]{:S(2)}) async-start(bf16[16,2,96,96]{3,2,1,0:T(8,128)(2,1)} %want.1._), calls=%async_computation | async-start | bytes 1572864 | tf_op jit(solution)/shard_map/all_to_all | solution.py:613
  13.1 6.4 %collective-permute-start.4 = (bf16[6,96,128]{2,1,0:T(8,128)(2,1)S(1)}, bf16[6,96,128]{2,1,0:T(8,128)(2,1)S(1)}, u32[]{:S(2)}, u32[]{:S(2)}) collective-permute-start(bf16[6,96,128]{2,1,0:T(8,128)(2,1)S(1)} %get-tuple-element.52.refs_0_), channel_id=1, source_target_pairs={{0,6},{1,7},{2,0},{3,1},{4,2},{5,3},{6,4},{7,5},{8,14},{9,15},{10,... | collective-permute-start | bytes 442376 | tf_op jit(solution)/shard_map/ppermute | solution.py:596
  19.5 1.0 %collective-permute-start.3 = (bf16[6,96,128]{2,1,0:T(8,128)(2,1)S(1)}, bf16[6,96,128]{2,1,0:T(8,128)(2,1)S(1)}, u32[]{:S(2)}, u32[]{:S(2)}) collective-permute-start(bf16[6,96,128]{2,1,0:T(8,128)(2,1)S(1)} %get-tuple-element.52.refs_0_), channel_id=1, source_target_pairs={{0,1},{1,2},{2,3},{3,4},{4,5},{5,6},{6,7},{7,0},{8,9},{9,10},{10,1... | collective-permute-start | bytes 442376 | tf_op jit(solution)/shard_map/ppermute | solution.py:596
  20.5 5.1 %collective-permute-done.4.refs_3_ = bf16[6,96,128]{2,1,0:T(8,128)(2,1)S(1)} collective-permute-done((bf16[6,96,128]{2,1,0:T(8,128)(2,1)S(1)}, bf16[6,96,128]{2,1,0:T(8,128)(2,1)S(1)}, u32[]{:S(2)}, u32[]{:S(2)}) %collective-permute-start.4) | collective-permute-done | bytes 147488 | tf_op jit(solution)/shard_map/ppermute | solution.py:596
  25.6 2.7 %collective-permute-start.6 = (bf16[6,96,128]{2,1,0:T(8,128)(2,1)S(1)}, bf16[6,96,128]{2,1,0:T(8,128)(2,1)S(1)}, u32[]{:S(2)}, u32[]{:S(2)}) collective-permute-start(bf16[6,96,128]{2,1,0:T(8,128)(2,1)S(1)} %collective-permute-done.4.refs_3_), channel_id=1, source_target_pairs={{0,7},{1,0},{2,1},{3,2},{4,3},{5,4},{6,5},{7,6},{8,15},{9,8},{10,9... | collective-permute-start | bytes 442376 | tf_op jit(solution)/shard_map/ppermute | solution.py:596
  28.3 3.2 %collective-permute-start.2 = (bf16[6,96,128]{2,1,0:T(8,128)(2,1)S(1)}, bf16[6,96,128]{2,1,0:T(8,128)(2,1)S(1)}, u32[]{:S(2)}, u32[]{:S(2)}) collective-permute-start(bf16[6,96,128]{2,1,0:T(8,128)(2,1)S(1)} %get-tuple-element.52.refs_0_), channel_id=1, source_target_pairs={{0,7},{1,0},{2,1},{3,2},{4,3},{5,4},{6,5},{7,6},{8,15},{9,8},{10,9... | collective-permute-start | bytes 442376 | tf_op jit(solution)/shard_map/ppermute | solution.py:596
  31.6 3.7 %collective-permute-start.7 = (bf16[6,96,128]{2,1,0:T(8,128)(2,1)S(1)}, bf16[6,96,128]{2,1,0:T(8,128)(2,1)S(1)}, u32[]{:S(2)}, u32[]{:S(2)}) collective-permute-start(bf16[6,96,128]{2,1,0:T(8,128)(2,1)S(1)} %collective-permute-done.6.refs_0_), channel_id=1, source_target_pairs={{0,7},{1,0},{2,1},{3,2},{4,3},{5,4},{6,5},{7,6},{8,15},{9,8},{10,9... | collective-permute-start | bytes 442376 | tf_op jit(solution)/shard_map/ppermute | solution.py:596
  35.7 3.1 %early.1 = (bf16[6,192,960]{2,1,0:T(8,128)(2,1)S(1)}, f32[6,192,128]{2,1,0:T(8,128)S(1)}, f32[6,192,128]{2,1,0:T(8,128)S(1)}, f32[6,192,128]{2,1,0:T(8,128)S(1)}, f32[6,192,128]{2,1,0:T(8,128)S(1)}) custom-call(bf16[6,192,128]{2,1,0:T(8,128)(2,1)S(1)} %get-tuple-element.45.q_ref, bf16[6,192,128]{2,1,0:T(8,128)(2,1)S(1)} %get-tuple-element.46.da_ref, ...), custom_call_target="tpu_custom_call" | custom-call | bytes 400000 | tf_op jit(solution)/shard_map/early/pallas_call | solution.py:350
  38.8 2.9 %collective-permute-done.8.refs_2_ = bf16[6,96,128]{2,1,0:T(8,128)(2,1)S(1)} collective-permute-done((bf16[6,96,128]{2,1,0:T(8,128)(2,1)S(1)}, bf16[6,96,128]{2,1,0:T(8,128)(2,1)S(1)}, u32[]{:S(2)}, u32[]{:S(2)}) %collective-permute-start.8) | collective-permute-done | bytes 147488 | tf_op jit(solution)/shard_map/ppermute | solution.py:596
  41.7 3.4 %turn.1 = (f32[6,192,128]{2,1,0:T(8,128)S(1)}, f32[6,192,128]{2,1,0:T(8,128)S(1)}, f32[6,192,128]{2,1,0:T(8,128)S(1)}, bf16[6,96,128]{2,1,0:T(8,128)(2,1)S(1)}, ...) custom-call(bf16[6,192,128]{2,1,0:T(8,128)(2,1)S(1)} %get-tuple-element.45.q_ref, ...), custom_call_target="tpu_custom_call" | custom-call | bytes 300000 | tf_op jit(solution)/shard_map/turn/pallas_call | solution.py:395
  45.1 2.5 %backward.1 = (f32[6,192,128]{2,1,0:T(8,128)S(1)}, bf16[6,96,128]{2,1,0:T(8,128)(2,1)S(1)}, bf16[6,96,128]{2,1,0:T(8,128)(2,1)S(1)}, bf16[6,96,128]{2,1,0:T(8,12...) custom-call(bf16[6,96,128]{2,1,0:T(8,128)(2,1)S(1)} %get-tuple-element.57._, ...), custom_call_target="tpu_custom_call" | custom-call | bytes 300000 | tf_op jit(solution)/shard_map/backward/pallas_call | solution.py:434
  47.7 1.1 %collective-permute-start.10 = (bf16[6,96,128]{2,1,0:T(8,128)(2,1)S(1)}, bf16[6,96,128]{2,1,0:T(8,128)(2,1)S(1)}, u32[]{:S(2)}, u32[]{:S(2)}) collective-permute-start(bf16[6,96,128]{2,1,0:T(8,128)(2,1)S(1)} %join.1), channel_id=1, source_target_pairs={{0,7},{1,0},{2,1},{3,2},{4,3},{5,4},{6,5},{7,6},{8,15},{9,8},{10,9... | collective-permute-start | bytes 442376 | tf_op jit(solution)/shard_map/ppermute | solution.py:596
  48.8 1.0 %collective-permute-start.14 = (bf16[6,96,128]{2,1,0:T(8,128)(2,1)S(1)}, bf16[6,96,128]{2,1,0:T(8,128)(2,1)S(1)}, u32[]{:S(2)}, u32[]{:S(2)}) collective-permute-start(bf16[6,96,128]{2,1,0:T(8,128)(2,1)S(1)} %get-tuple-element.57._), channel_id=1, source_target_pairs={{0,1},{1,2},{2,3},{3,4},{4,5},{5,6},{6,7},{7,0},{8,9},{9,10},{10,1... | collective-permute-start | bytes 442376 | tf_op jit(solution)/shard_map/ppermute | solution.py:596
  50.3 2.6 %collective-permute-done.10 = bf16[6,96,128]{2,1,0:T(8,128)(2,1)S(1)} collective-permute-done((bf16[6,96,128]{2,1,0:T(8,128)(2,1)S(1)}, bf16[6,96,128]{2,1,0:T(8,128)(2,1)S(1)}, u32[]{:S(2)}, u32[]{:S(2)}) %collective-permute-start.10) | collective-permute-done | bytes 147488 | tf_op jit(solution)/shard_map/ppermute | solution.py:596
  52.9 2.5 %collective-permute-start.11 = (bf16[6,96,128]{2,1,0:T(8,128)(2,1)S(1)}, bf16[6,96,128]{2,1,0:T(8,128)(2,1)S(1)}, u32[]{:S(2)}, u32[]{:S(2)}) collective-permute-start(bf16[6,96,128]{2,1,0:T(8,128)(2,1)S(1)} %add_convert_fusion.2), channel_id=1, source_target_pairs={{0,7},{1,0},{2,1},{3,2},{4,3},{5,4},{6,5},{7,6},{8,15},{9,8},{10,9... | collective-permute-start | bytes 442376 | tf_op jit(solution)/shard_map/ppermute | solution.py:596
  55.7 2.7 %collective-permute-done.11.down_ref = bf16[6,96,128]{2,1,0:T(8,128)(2,1)S(1)} collective-permute-done((bf16[6,96,128]{2,1,0:T(8,128)(2,1)S(1)}, bf16[6,96,128]{2,1,0:T(8,128)(2,1)S(1)}, u32[]{:S(2)}, u32[]{:S(2)}) %collective-permute-start.11) | collective-permute-done | bytes 147488 | tf_op jit(solution)/shard_map/ppermute | solution.py:596
  59.2 3.4 %collective-permute-start.13 = (bf16[6,96,128]{2,1,0:T(8,128)(2,1)S(1)}, bf16[6,96,128]{2,1,0:T(8,128)(2,1)S(1)}, u32[]{:S(2)}, u32[]{:S(2)}) collective-permute-start(bf16[6,96,128]{2,1,0:T(8,128)(2,1)S(1)} %get-tuple-element.72), channel_id=1, source_target_pairs={{0,7},{1,0},{2,1},{3,2},{4,3},{5,4},{6,5},{7,6},{8,15},{9,8},{10,9... | collective-permute-start | bytes 442376 | tf_op jit(solution)/shard_map/ppermute | solution.py:596
  62.8 7.2 %all-to-all-start.1 = ((bf16[16,96,96]{2,1,0:T(8,128)(2,1)}), bf16[16,96,96]{2,1,0:T(8,128)(2,1)S(1)}, u32[]{:S(2)}, u32[]{:S(2)}) async-start(bf16[16,96,96]{2,1,0:T(8,128)(2,1)} %bitcast), calls=%async_computation.1 | async-start | bytes 786432 | tf_op jit(solution)/shard_map/all_to_all | solution.py:639
  70.5 1.5 %collective-permute-start.17 = (bf16[6,96,128]{2,1,0:T(8,128)(2,1)S(1)}, bf16[6,96,128]{2,1,0:T(8,128)(2,1)S(1)}, u32[]{:S(2)}, u32[]{:S(2)}) collective-permute-start(bf16[6,96,128]{2,1,0:T(8,128)(2,1)S(1)} %get-tuple-element.79), channel_id=1, source_target_pairs={{0,8},{8,0},{1,9},{9,1},{2,10},{10,2},{3,11},{11,3},{4,12},{12,4},... | collective-permute-start | bytes 442376 | tf_op jit(solution)/shard_map/ppermute | solution.py:600
  72.1 1.7 %slopes.1 = (f32[6,96,128]{2,1,0:T(8,128)S(1)}, f32[6,96,128]{2,1,0:T(8,128)S(1)}) custom-call(bf16[6,96,128]{2,1,0:T(8,128)(2,1)S(1)} %collective-permute-done.9.b_ref._, bf16[6,96,128]{2,1,0:T(8,128)(2,1)} %pair_hbm.3, bf16[6,96,128]{2,1,0:T(8,128)(2,1)} %grad_hbm.3, bf16[128,256]{1,0:T(8,128)(2,1)} %w_ref.3, bf16[64,128]{1,0:T(8,128)(2,1)} %wout_hbm.3), custom_call_target="tpu_custom_call" | custom-call | bytes 200000 | tf_op jit(solution)/shard_map/slopes/pallas_call | solution.py:159
  74.0 3.3 %all-to-all-done.1.parts_ref = bf16[16,96,96]{2,1,0:T(8,128)(2,1)S(1)} async-done(((bf16[16,96,96]{2,1,0:T(8,128)(2,1)}), bf16[16,96,96]{2,1,0:T(8,128)(2,1)S(1)}, u32[]{:S(2)}, u32[]{:S(2)}) %all-to-all-start.1) | async-done | bytes 294944 | tf_op jit(solution)/shard_map/all_to_all | solution.py:639
  (36 shorter events, 4.8 us)
Async XLA Ops:
  0.6 3.5 %collective-permute-start.1 = (bf16[2,96,96]{2,1,0:T(8,128)(2,1)}, bf16[2,96,96]{2,1,0:T(8,128)(2,1)S(1)}, u32[]{:S(2)}, u32[]{:S(2)}) collective-permute-start(bf16[2,96,96]{2,1,0:T(8,128)(2,1)} %bias_hbm.1), channel_id=1, source_target_pairs={{0,16},{16,0},{1,17},{17,1},{2,18},{18,2},{3,19},{19,3},{4,20},{20... | collective-permute-start | bytes 110600 | tf_op jit(solution)/shard_map/ppermute | solution.py:600
  2.4 9.9 %collective-permute-start = (bf16[6,96,128]{2,1,0:T(8,128)(2,1)S(1)}, bf16[6,96,128]{2,1,0:T(8,128)(2,1)S(1)}, u32[]{:S(2)}, u32[]{:S(2)}) collective-permute-start(bf16[6,96,128]{2,1,0:T(8,128)(2,1)S(1)} %get-tuple-element.43), channel_id=1, source_target_pairs={{0,8},{8,0},{1,9},{9,1},{2,10},{10,2},{3,11},{11,3},{4,12},{12,4},... | collective-permute-start | bytes 442376 | tf_op jit(solution)/shard_map/ppermute | solution.py:600
  5.1 30.2 %all-to-all-start = ((bf16[16,2,96,96]{3,2,1,0:T(8,128)(2,1)}), bf16[16,2,96,96]{3,2,1,0:T(8,128)(2,1)S(1)}, u32[]{:S(2)}, u32[]{:S(2)}) async-start(bf16[16,2,96,96]{3,2,1,0:T(8,128)(2,1)} %want.1._), calls=%async_computation | async-start | bytes 1572864 | tf_op jit(solution)/shard_map/all_to_all | solution.py:613
  13.1 12.5 %collective-permute-start.4 = (bf16[6,96,128]{2,1,0:T(8,128)(2,1)S(1)}, bf16[6,96,128]{2,1,0:T(8,128)(2,1)S(1)}, u32[]{:S(2)}, u32[]{:S(2)}) collective-permute-start(bf16[6,96,128]{2,1,0:T(8,128)(2,1)S(1)} %get-tuple-element.52.refs_0_), channel_id=1, source_target_pairs={{0,6},{1,7},{2,0},{3,1},{4,2},{5,3},{6,4},{7,5},{8,14},{9,15},{10,... | collective-permute-start | bytes 442376 | tf_op jit(solution)/shard_map/ppermute | solution.py:596
  19.5 8.8 %collective-permute-start.3 = (bf16[6,96,128]{2,1,0:T(8,128)(2,1)S(1)}, bf16[6,96,128]{2,1,0:T(8,128)(2,1)S(1)}, u32[]{:S(2)}, u32[]{:S(2)}) collective-permute-start(bf16[6,96,128]{2,1,0:T(8,128)(2,1)S(1)} %get-tuple-element.52.refs_0_), channel_id=1, source_target_pairs={{0,1},{1,2},{2,3},{3,4},{4,5},{5,6},{6,7},{7,0},{8,9},{9,10},{10,1... | collective-permute-start | bytes 442376 | tf_op jit(solution)/shard_map/ppermute | solution.py:596
  25.6 6.0 %collective-permute-start.6 = (bf16[6,96,128]{2,1,0:T(8,128)(2,1)S(1)}, bf16[6,96,128]{2,1,0:T(8,128)(2,1)S(1)}, u32[]{:S(2)}, u32[]{:S(2)}) collective-permute-start(bf16[6,96,128]{2,1,0:T(8,128)(2,1)S(1)} %collective-permute-done.4.refs_3_), channel_id=1, source_target_pairs={{0,7},{1,0},{2,1},{3,2},{4,3},{5,4},{6,5},{7,6},{8,15},{9,8},{10,9... | collective-permute-start | bytes 442376 | tf_op jit(solution)/shard_map/ppermute | solution.py:596
  28.3 7.0 %collective-permute-start.5 = (bf16[6,96,128]{2,1,0:T(8,128)(2,1)S(1)}, bf16[6,96,128]{2,1,0:T(8,128)(2,1)S(1)}, u32[]{:S(2)}, u32[]{:S(2)}) collective-permute-start(bf16[6,96,128]{2,1,0:T(8,128)(2,1)S(1)} %collective-permute-done.3.refs_2_), channel_id=1, source_target_pairs={{0,1},{1,2},{2,3},{3,4},{4,5},{5,6},{6,7},{7,0},{8,9},{9,10},{10,1... | collective-permute-start | bytes 442376 | tf_op jit(solution)/shard_map/ppermute | solution.py:596
  28.3 7.4 %collective-permute-start.2 = (bf16[6,96,128]{2,1,0:T(8,128)(2,1)S(1)}, bf16[6,96,128]{2,1,0:T(8,128)(2,1)S(1)}, u32[]{:S(2)}, u32[]{:S(2)}) collective-permute-start(bf16[6,96,128]{2,1,0:T(8,128)(2,1)S(1)} %get-tuple-element.52.refs_0_), channel_id=1, source_target_pairs={{0,7},{1,0},{2,1},{3,2},{4,3},{5,4},{6,5},{7,6},{8,15},{9,8},{10,9... | collective-permute-start | bytes 442376 | tf_op jit(solution)/shard_map/ppermute | solution.py:596
  31.6 7.1 %collective-permute-start.7 = (bf16[6,96,128]{2,1,0:T(8,128)(2,1)S(1)}, bf16[6,96,128]{2,1,0:T(8,128)(2,1)S(1)}, u32[]{:S(2)}, u32[]{:S(2)}) collective-permute-start(bf16[6,96,128]{2,1,0:T(8,128)(2,1)S(1)} %collective-permute-done.6.refs_0_), channel_id=1, source_target_pairs={{0,7},{1,0},{2,1},{3,2},{4,3},{5,4},{6,5},{7,6},{8,15},{9,8},{10,9... | collective-permute-start | bytes 442376 | tf_op jit(solution)/shard_map/ppermute | solution.py:596
  35.3 6.4 %collective-permute-start.8 = (bf16[6,96,128]{2,1,0:T(8,128)(2,1)S(1)}, bf16[6,96,128]{2,1,0:T(8,128)(2,1)S(1)}, u32[]{:S(2)}, u32[]{:S(2)}) collective-permute-start(bf16[6,96,128]{2,1,0:T(8,128)(2,1)S(1)} %collective-permute-done.5.refs_4_), channel_id=1, source_target_pairs={{0,1},{1,2},{2,3},{3,4},{4,5},{5,6},{6,7},{7,0},{8,9},{9,10},{10,1... | collective-permute-start | bytes 442376 | tf_op jit(solution)/shard_map/ppermute | solution.py:596
  47.7 5.2 %collective-permute-start.10 = (bf16[6,96,128]{2,1,0:T(8,128)(2,1)S(1)}, bf16[6,96,128]{2,1,0:T(8,128)(2,1)S(1)}, u32[]{:S(2)}, u32[]{:S(2)}) collective-permute-start(bf16[6,96,128]{2,1,0:T(8,128)(2,1)S(1)} %join.1), channel_id=1, source_target_pairs={{0,7},{1,0},{2,1},{3,2},{4,3},{5,4},{6,5},{7,6},{8,15},{9,8},{10,9... | collective-permute-start | bytes 442376 | tf_op jit(solution)/shard_map/ppermute | solution.py:596
  48.8 6.7 %collective-permute-start.14 = (bf16[6,96,128]{2,1,0:T(8,128)(2,1)S(1)}, bf16[6,96,128]{2,1,0:T(8,128)(2,1)S(1)}, u32[]{:S(2)}, u32[]{:S(2)}) collective-permute-start(bf16[6,96,128]{2,1,0:T(8,128)(2,1)S(1)} %get-tuple-element.57._), channel_id=1, source_target_pairs={{0,1},{1,2},{2,3},{3,4},{4,5},{5,6},{6,7},{7,0},{8,9},{9,10},{10,1... | collective-permute-start | bytes 442376 | tf_op jit(solution)/shard_map/ppermute | solution.py:596
  50.2 8.2 %collective-permute-start.12 = (bf16[2,4,2,96,96]{4,3,2,1,0:T(8,128)(2,1)S(1)}, bf16[2,4,2,96,96]{4,3,2,1,0:T(8,128)(2,1)S(1)}, u32[]{:S(2)}, u32[]{:S(2)}) collective-permute-start(bf16[2,4,2,96,96]{4,3,2,1,0:T(8,128)(2,1)S(1)} %get-tuple-element.71), channel_id=1, source_target_pairs={{0,16},{16,0},{1,17},{17,1},{2,18},{18,2},{3,19},{19,3},{4,20},{20... | collective-permute-start | bytes 884744 | tf_op jit(solution)/shard_map/ppermute | solution.py:600
  52.9 5.4 %collective-permute-start.11 = (bf16[6,96,128]{2,1,0:T(8,128)(2,1)S(1)}, bf16[6,96,128]{2,1,0:T(8,128)(2,1)S(1)}, u32[]{:S(2)}, u32[]{:S(2)}) collective-permute-start(bf16[6,96,128]{2,1,0:T(8,128)(2,1)S(1)} %add_convert_fusion.2), channel_id=1, source_target_pairs={{0,7},{1,0},{2,1},{3,2},{4,3},{5,4},{6,5},{7,6},{8,15},{9,8},{10,9... | collective-permute-start | bytes 442376 | tf_op jit(solution)/shard_map/ppermute | solution.py:596
  55.5 7.2 %collective-permute-start.15 = (bf16[6,96,128]{2,1,0:T(8,128)(2,1)S(1)}, bf16[6,96,128]{2,1,0:T(8,128)(2,1)S(1)}, u32[]{:S(2)}, u32[]{:S(2)}) collective-permute-start(bf16[6,96,128]{2,1,0:T(8,128)(2,1)S(1)} %add_convert_fusion.1), channel_id=1, source_target_pairs={{0,1},{1,2},{2,3},{3,4},{4,5},{5,6},{6,7},{7,0},{8,9},{9,10},{10,1... | collective-permute-start | bytes 442376 | tf_op jit(solution)/shard_map/ppermute | solution.py:596
  55.6 14.5 %collective-permute-start.9 = (bf16[6,96,128]{2,1,0:T(8,128)(2,1)S(1)}, bf16[6,96,128]{2,1,0:T(8,128)(2,1)S(1)}, u32[]{:S(2)}, u32[]{:S(2)}) collective-permute-start(bf16[6,96,128]{2,1,0:T(8,128)(2,1)S(1)} %get-tuple-element.64), channel_id=1, source_target_pairs={{0,1},{1,2},{2,3},{3,4},{4,5},{5,6},{6,7},{7,0},{8,9},{9,10},{10,1... | collective-permute-start | bytes 442376 | tf_op jit(solution)/shard_map/ppermute | solution.py:596
  58.4 15.4 %copy-start = (bf16[128,256]{1,0:T(8,128)(2,1)S(1)}, bf16[128,256]{1,0:T(8,128)(2,1)}, u32[]{:S(2)}) copy-start(bf16[128,256]{1,0:T(8,128)(2,1)} %w_ref.3) | copy-start | bytes 196612
  59.2 10.9 %collective-permute-start.13 = (bf16[6,96,128]{2,1,0:T(8,128)(2,1)S(1)}, bf16[6,96,128]{2,1,0:T(8,128)(2,1)S(1)}, u32[]{:S(2)}, u32[]{:S(2)}) collective-permute-start(bf16[6,96,128]{2,1,0:T(8,128)(2,1)S(1)} %get-tuple-element.72), channel_id=1, source_target_pairs={{0,7},{1,0},{2,1},{3,2},{4,3},{5,4},{6,5},{7,6},{8,15},{9,8},{10,9... | collective-permute-start | bytes 442376 | tf_op jit(solution)/shard_map/ppermute | solution.py:596
  62.7 7.6 %collective-permute-start.16 = (bf16[6,96,128]{2,1,0:T(8,128)(2,1)S(1)}, bf16[6,96,128]{2,1,0:T(8,128)(2,1)S(1)}, u32[]{:S(2)}, u32[]{:S(2)}) collective-permute-start(bf16[6,96,128]{2,1,0:T(8,128)(2,1)S(1)} %add_convert_fusion), channel_id=1, source_target_pairs={{0,2},{1,3},{2,4},{3,5},{4,6},{5,7},{6,0},{7,1},{8,10},{9,11},{10,... | collective-permute-start | bytes 442376 | tf_op jit(solution)/shard_map/ppermute | solution.py:596
  62.8 14.5 %all-to-all-start.1 = ((bf16[16,96,96]{2,1,0:T(8,128)(2,1)}), bf16[16,96,96]{2,1,0:T(8,128)(2,1)S(1)}, u32[]{:S(2)}, u32[]{:S(2)}) async-start(bf16[16,96,96]{2,1,0:T(8,128)(2,1)} %bitcast), calls=%async_computation.1 | async-start | bytes 786432 | tf_op jit(solution)/shard_map/all_to_all | solution.py:639
  70.5 6.8 %collective-permute-start.17 = (bf16[6,96,128]{2,1,0:T(8,128)(2,1)S(1)}, bf16[6,96,128]{2,1,0:T(8,128)(2,1)S(1)}, u32[]{:S(2)}, u32[]{:S(2)}) collective-permute-start(bf16[6,96,128]{2,1,0:T(8,128)(2,1)S(1)} %get-tuple-element.79), channel_id=1, source_target_pairs={{0,8},{8,0},{1,9},{9,1},{2,10},{10,2},{3,11},{11,3},{4,12},{12,4},... | collective-permute-start | bytes 442376 | tf_op jit(solution)/shard_map/ppermute | solution.py:600
